TPU v7x, 128 devices: a whole 4x4x4 slice. The times are simulated.
128 devices in a mesh: seq: 32 (over x, z, core), val: 4 (over y).
Axes of the slice: x: 4, y: 4, z: 4, core: 2. Of those that a mesh axis runs over, the one named last changes fastest.
Arguments:
- tokens: bfloat16 [12288, 4096], P('seq', 'val'), may hold values from -6 to 6
- w_query: bfloat16 [4096, 2048], P(None, 'val'), may hold values from -0.09375 to 0.09375
- w_key: bfloat16 [4096, 2048], P(None, 'val'), may hold values from -0.09375 to 0.09375
- w_value: bfloat16 [4096, 8, 512], P(None, None, 'val'), may hold values from -0.09375 to 0.09375
- w_gate: bfloat16 [4096, 2, 8], replicated, may hold values from -0.09375 to 0.09375
- gate_bias: float32 [2, 8], replicated, as said below
- norm_gain: float32 [8, 512], P(None, 'val'), may hold values from 0.1 to 1.9
- w_out: bfloat16 [8, 512, 4096], P(None, 'val'), may hold values from -0.09375 to 0.09375
Outputs:
- layer_out: bfloat16 [12288, 4096], P('seq', 'val')
Inputs may be any that keep to these rules, and one draw needn't show every extreme that they name: `gate_bias`: row 0 holds input gate biases; row 1 holds forget gate biases, all positive.
All inputs are finite; a program needn't handle non-finite values.
Results may differ from a plain program's by a relative error of at most 0.015.
Values may be sent and summed in bfloat16 or wider, within the bound.
No kernel may reach another device: no remote copies, remote signals or barrier semaphores. Data moves between devices by JAX's collectives and lax.ppermute only.
A program may use at most 128 MiB of HBM per device.

v0:
```python
import jax
import jax.numpy as jnp
from jax import lax
from jax.sharding import PartitionSpec as P

DV = 512


def passed_along(block, axis, distance):
    devices = range(lax.axis_size(axis))
    route = [(i - distance, i) for i in devices if i - distance in devices]
    return lax.ppermute(block, axis, route)


def combine(early, late):
    ce, ne, me, be = early
    cl, nl, ml, bl = late
    top = jnp.maximum(me + bl, ml)
    fe = jnp.exp(me + bl - top)
    fl = jnp.exp(ml - top)
    return (
        fe[:, None, None] * ce + fl[:, None, None] * cl,
        fe[:, None] * ne + fl[:, None] * nl,
        top,
        be + bl,
    )


def summary(keys, values, igate, cumb):
    total = cumb[-1]
    weight_log = total[None] - cumb + igate
    top = jnp.max(weight_log, axis=0)
    wts = jnp.exp(weight_log - top[None])
    kw = (keys.astype(jnp.float32) * wts[:, :, None]).astype(jnp.bfloat16)
    state = jnp.einsum("thd,the->hde", kw, values, preferred_element_type=jnp.float32)
    norm = jnp.sum(kw.astype(jnp.float32), axis=0)
    return (state, norm, top, total)


def block_output(queries, keys, values, igate, cumb, prefix):
    scale = queries.shape[-1] ** (-0.5)
    rows = queries.shape[0]
    scores = jnp.einsum("thd,shd->hts", queries, keys, preferred_element_type=jnp.float32) * scale
    position = jnp.arange(rows)
    causal = position[:, None] >= position[None, :]
    cumh = cumb.T
    logd = cumh[:, :, None] - cumh[:, None, :] + igate.T[:, None, :]
    logd = jnp.where(causal[None], logd, jnp.float32(-1e30))
    rowmax = jnp.max(logd, axis=-1)
    state, norm, ptop, ptotal = prefix
    top = jnp.maximum(cumh + ptop[:, None], rowmax)
    wts = jnp.where(causal[None], jnp.exp(logd - top[:, :, None]) * scores, 0.0).astype(
        jnp.bfloat16
    )
    numer = jnp.einsum("hts,she->the", wts, values, preferred_element_type=jnp.float32)
    denom = jnp.sum(wts.astype(jnp.float32), axis=-1)
    decay = jnp.exp(cumh + ptop[:, None] - top)
    qf = queries.astype(jnp.float32)
    inter = jnp.einsum("thd,hde->the", qf, state, precision=lax.Precision.HIGHEST)
    numer = numer + inter * (scale * decay.T)[:, :, None]
    denom = (
        denom + jnp.einsum("thd,hd->ht", qf, norm, precision=lax.Precision.HIGHEST) * scale * decay
    )
    return numer / jnp.maximum(jnp.abs(denom), 1.0).T[:, :, None]


def reset_start(got, empty):
    return (got[0], got[1], jnp.where(empty, jnp.float32(-1e30), got[2]), got[3])


def per_device(tokens, w_query, w_key, w_value, w_gate, gate_bias, norm_gain, w_out):
    whole = lax.all_gather(tokens, "val", axis=1, tiled=True)
    rows = whole.shape[0]
    width = whole.shape[1]
    heads = w_value.shape[1]
    vlocal = w_value.shape[2]
    q_part = jnp.dot(whole, w_query, preferred_element_type=jnp.float32).astype(jnp.bfloat16)
    k_part = jnp.dot(whole, w_key, preferred_element_type=jnp.float32).astype(jnp.bfloat16)
    queries, keys = (
        lax.all_gather(q_part, "val", axis=1, tiled=True),
        lax.all_gather(k_part, "val", axis=1, tiled=True),
    )
    queries = queries.reshape(rows, heads, -1)
    keys = keys.reshape(rows, heads, -1)
    values = jnp.dot(
        whole, w_value.reshape(width, heads * vlocal), preferred_element_type=jnp.float32
    )
    values = values.astype(jnp.bfloat16).reshape(rows, heads, vlocal)
    gates = jnp.dot(
        whole, w_gate.reshape(width, 2 * heads), preferred_element_type=jnp.float32
    ).reshape(rows, 2, heads)
    gates = gates + gate_bias[None]
    igate = gates[:, 0]
    cumb = jnp.cumsum(jax.nn.log_sigmoid(gates[:, 1]), axis=0)
    local = summary(keys, values, igate, cumb)
    qsize = keys.shape[-1]
    start = (
        jnp.zeros((heads, qsize, vlocal), jnp.float32),
        jnp.zeros((heads, qsize), jnp.float32),
        jnp.full((heads,), -1e30, jnp.float32),
        jnp.zeros((heads,), jnp.float32),
    )
    position = lax.axis_index("seq")
    blocks = lax.axis_size("seq")

    def turn(step, before):
        joined = combine(before, local)
        got = passed_along((joined[0], joined[1], joined[2], joined[3]), "seq", 1)
        return reset_start(got, position < 1)

    prefix = lax.fori_loop(0, blocks - 1, turn, start)
    hidden = block_output(queries, keys, values, igate, cumb, prefix)
    totals, squares = lax.psum((jnp.sum(hidden, axis=-1), jnp.sum(hidden * hidden, axis=-1)), "val")
    mean = totals / DV
    msq = squares / DV
    normed = (
        (hidden - mean[..., None])
        * lax.rsqrt(msq - mean * mean + 1e-06)[..., None]
        * norm_gain[None]
    ).astype(jnp.bfloat16)
    partial_value = jnp.dot(
        normed.reshape(rows, heads * vlocal),
        w_out.reshape(heads * vlocal, -1),
        preferred_element_type=jnp.float32,
    )
    return lax.psum_scatter(
        partial_value.astype(jnp.bfloat16), "val", scatter_dimension=1, tiled=True
    )


def solution(mesh):
    placed = (
        P("seq", "val"),
        P(None, "val"),
        P(None, "val"),
        P(None, None, "val"),
        P(),
        P(),
        P(None, "val"),
        P(None, "val", None),
    )
    return jax.shard_map(
        per_device, mesh=mesh, in_specs=placed, out_specs=P("seq", "val"), check_vma=False
    )
```

profile of v0, /device:TPU:1, one launch (start us, length us, event | category | flops | bytes accessed | tf_op | source)
XLA Modules:
  0.0 744.7 jit_solution(3138549592570780363)
XLA Ops:
  7.4 44.4 %all-gather.4.cloned.1.call-done = bf16[384,4096]{1,0:T(8,128)(2,1)} async-done(((bf16[384,1024]{1,0:T(8,128)(2,1)}), bf16[384,4096]{1,0:T(8,128)(2,1)}) %all-gather.4.cloned.1.call-update) | async-done | bytes 3145744 | tf_op jit(solution)/shard_map/all_gather | solution.py:72
  65.5 8.6 %fusion.17 = bf16[384,1024]{1,0:T(8,128)(2,1)} fusion(bf16[384,4096]{1,0:T(8,128)(2,1)} %all-gather.4.cloned.1.call-done, bf16[512,8,8,128]{3,2,1,0:T(8,128)(2,1)} %bitcast.102), kind=kOutput, calls=%fused_computation.33 | convolution fusion | flops 3221618688 | bytes 12320768 | tf_op jit(solution)/shard_map/dot_general | solution.py:85
  94.1 552.9 %while.17 = (s32[]{:T(128)}, f32[8,256,128]{2,1,0:T(8,128)S(1)}, f32[8,256]{1,0:T(8,128)S(1)}, f32[8]{0:T(128)S(1)}, f32[8]{0:T(128)S(1)}, /*index=5*/f32[8]{0:T...) while((s32[]{:T(128)}, f32[8,256,128]{2,1,0:T(8,128)S(1)}, ...), condition=%wide.region_5.6_spmd.clone, body=%wide.region_4.5_spmd.clone.sunk | while | flops 792627 | bytes 7398192 | solution.py:111
  231.9 6.5 collective-permute-start.1
  250.4 6.5 collective-permute-start.1
  268.9 6.5 collective-permute-start.1
  276.4 6.5 collective-permute-start
  287.5 6.5 collective-permute-start.1
  295.0 6.5 collective-permute-start
  306.0 6.5 collective-permute-start.1
  313.5 6.5 collective-permute-start
  324.6 6.5 collective-permute-start.1
  332.0 6.5 collective-permute-start
  343.1 6.5 collective-permute-start.1
  350.6 6.5 collective-permute-start
  361.6 6.5 collective-permute-start.1
  369.1 6.5 collective-permute-start
  380.2 6.5 collective-permute-start.1
  387.7 6.5 collective-permute-start
  398.7 6.5 collective-permute-start.1
  406.2 6.5 collective-permute-start
  417.3 6.5 collective-permute-start.1
  424.7 6.5 collective-permute-start
  435.8 6.5 collective-permute-start.1
  443.3 6.5 collective-permute-start
  454.3 6.5 collective-permute-start.1
  461.8 6.5 collective-permute-start
  472.9 6.5 collective-permute-start.1
  480.4 6.5 collective-permute-start
  491.4 6.5 collective-permute-start.1
  498.9 6.5 collective-permute-start
  509.9 6.5 collective-permute-start.1
  517.4 6.5 collective-permute-start
  528.5 6.5 collective-permute-start.1
  536.0 6.5 collective-permute-start
  547.0 6.5 collective-permute-start.1
  554.5 6.5 collective-permute-start
  565.6 6.5 collective-permute-start.1
  573.0 6.5 collective-permute-start
  584.1 6.5 collective-permute-start.1
  591.6 6.5 collective-permute-start
  602.6 6.5 collective-permute-start.1
  610.1 6.5 collective-permute-start
  621.2 6.5 collective-permute-start.1
  628.7 6.5 collective-permute-start
  656.1 12.2 %all-reduce = (f32[384,8]{0,1:T(8,128)S(1)}, f32[384,8]{0,1:T(8,128)S(1)}) all-reduce(f32[384,8]{0,1:T(8,128)S(1)} %get-tuple-element.146, f32[384,8]{0,1:T(8,128)S(1)} %get-tuple-element.145), channel_id=1, replica_groups=mesh['seq'=32,'val'=4] {'val'}, use_global_device_ids=true, to_apply=%region_11.12 | all-reduce | flops 6144 | bytes 49152 | tf_op jit(solution)/shard_map/psum | solution.py:113
  668.3 8.7 %bitcast_convert_fusion = bf16[384,4096]{1,0:T(8,128)(2,1)} fusion(bf16[8,128,4096]{2,1,0:T(8,128)(2,1)} %param.17, f32[384,8,128]{0,2,1:T(8,128)S(1)} %get-tuple-element.177, f32[8,128]{1,0:T(8,128)S(1)} %copy-done.5, f32[384,8]{0,1:T(8,128)S(1)} %get-tuple-element.174, f32[384,8]{0,1:T(8,128)S(1)} %get-tuple-element.173), kind=kOutput, calls=%fused_computation.11 | convolution fusion | flops 3224371200 | bytes 13135872 | tf_op jit(solution)/shard_map/dot_general | solution.py:121
  677.0 61.2 %reduce-scatter.2.cloned.1.call-done = bf16[384,1024]{1,0:T(8,128)(2,1)} async-done(((bf16[384,4096]{1,0:T(8,128)(2,1)}), bf16[384,1024]{1,0:T(8,128)(2,1)}) %reduce-scatter.2.cloned.1.call-update) | async-done | bytes 786448 | tf_op jit(solution)/shard_map/reduce_scatter | solution.py:126
  (352 shorter events, 322.4 us)
Async XLA Ops:
  6.5 45.3 %all-gather.4.cloned.1.call-start = ((), (), s32[]{:S(2)}) async-start(), calls=%async_computation.1 | async-start | bytes 3932160 | tf_op jit(solution)/shard_map/all_gather | solution.py:72
  7.3 80.2 %all-gather.6.cloned.1.call-start = ((), (), s32[]{:S(2)}) async-start(), calls=%async_computation.2 | async-start | bytes 1966080 | tf_op jit(solution)/shard_map/all_gather | solution.py:81
  60.6 586.4 %all-gather.8.cloned.1.call-start = ((), (), s32[]{:S(2)}) async-start(), calls=%async_computation.3 | async-start | bytes 1966080 | tf_op jit(solution)/shard_map/all_gather | solution.py:80
  82.2 656.0 %reduce-scatter.2.cloned.1.call-start = ((), (), s32[]{:S(2)}) async-start(), calls=%async_computation.4 | async-start | bytes 3932160 | tf_op jit(solution)/shard_map/reduce_scatter | solution.py:126
  94.3 15.6 %collective-permute-start = (f32[8,256,128]{2,1,0:T(8,128)S(1)}, f32[8,256,128]{2,1,0:T(8,128)S(1)}, u32[]{:S(2)}, u32[]{:S(2)}) collective-permute-start(f32[8,256,128]{2,1,0:T(8,128)S(1)} %multiply_add_fusion.4), channel_id=1, source_target_pairs={{0,4},{4,8},{8,12},{12,16},{16,20},{20,24},{24,28},{28,32},{32,36}... | collective-permute-start | bytes 3145736 | tf_op jit(solution)/shard_map/while/body/eval_jaxpr/ppermute | solution.py:12
  98.1 11.8 %collective-permute-start.2 = (f32[8]{0:T(128)S(1)}, f32[8]{0:T(128)S(1)}, u32[]{:S(2)}, u32[]{:S(2)}) collective-permute-start(f32[8]{0:T(128)S(1)} %get-tuple-element.235), channel_id=1, source_target_pairs={{0,4},{4,8},{8,12},{12,16},{16,20},{20,24},{24,28},{28,32},{32,36}... | collective-permute-start | bytes 104 | tf_op jit(solution)/shard_map/while/body/eval_jaxpr/ppermute | solution.py:12
  110.1 16.2 %collective-permute-start = (f32[8,256,128]{2,1,0:T(8,128)S(1)}, f32[8,256,128]{2,1,0:T(8,128)S(1)}, u32[]{:S(2)}, u32[]{:S(2)}) collective-permute-start(f32[8,256,128]{2,1,0:T(8,128)S(1)} %multiply_add_fusion.4), channel_id=1, source_target_pairs={{0,4},{4,8},{8,12},{12,16},{16,20},{20,24},{24,28},{28,32},{32,36}... | collective-permute-start | bytes 3145736 | tf_op jit(solution)/shard_map/while/body/eval_jaxpr/ppermute | solution.py:12
  114.5 11.8 %collective-permute-start.2 = (f32[8]{0:T(128)S(1)}, f32[8]{0:T(128)S(1)}, u32[]{:S(2)}, u32[]{:S(2)}) collective-permute-start(f32[8]{0:T(128)S(1)} %get-tuple-element.235), channel_id=1, source_target_pairs={{0,4},{4,8},{8,12},{12,16},{16,20},{20,24},{24,28},{28,32},{32,36}... | collective-permute-start | bytes 104 | tf_op jit(solution)/shard_map/while/body/eval_jaxpr/ppermute | solution.py:12
  126.5 16.2 %collective-permute-start = (f32[8,256,128]{2,1,0:T(8,128)S(1)}, f32[8,256,128]{2,1,0:T(8,128)S(1)}, u32[]{:S(2)}, u32[]{:S(2)}) collective-permute-start(f32[8,256,128]{2,1,0:T(8,128)S(1)} %multiply_add_fusion.4), channel_id=1, source_target_pairs={{0,4},{4,8},{8,12},{12,16},{16,20},{20,24},{24,28},{28,32},{32,36}... | collective-permute-start | bytes 3145736 | tf_op jit(solution)/shard_map/while/body/eval_jaxpr/ppermute | solution.py:12
  130.9 11.8 %collective-permute-start.2 = (f32[8]{0:T(128)S(1)}, f32[8]{0:T(128)S(1)}, u32[]{:S(2)}, u32[]{:S(2)}) collective-permute-start(f32[8]{0:T(128)S(1)} %get-tuple-element.235), channel_id=1, source_target_pairs={{0,4},{4,8},{8,12},{12,16},{16,20},{20,24},{24,28},{28,32},{32,36}... | collective-permute-start | bytes 104 | tf_op jit(solution)/shard_map/while/body/eval_jaxpr/ppermute | solution.py:12
  143.0 16.2 %collective-permute-start = (f32[8,256,128]{2,1,0:T(8,128)S(1)}, f32[8,256,128]{2,1,0:T(8,128)S(1)}, u32[]{:S(2)}, u32[]{:S(2)}) collective-permute-start(f32[8,256,128]{2,1,0:T(8,128)S(1)} %multiply_add_fusion.4), channel_id=1, source_target_pairs={{0,4},{4,8},{8,12},{12,16},{16,20},{20,24},{24,28},{28,32},{32,36}... | collective-permute-start | bytes 3145736 | tf_op jit(solution)/shard_map/while/body/eval_jaxpr/ppermute | solution.py:12
  147.4 11.8 %collective-permute-start.2 = (f32[8]{0:T(128)S(1)}, f32[8]{0:T(128)S(1)}, u32[]{:S(2)}, u32[]{:S(2)}) collective-permute-start(f32[8]{0:T(128)S(1)} %get-tuple-element.235), channel_id=1, source_target_pairs={{0,4},{4,8},{8,12},{12,16},{16,20},{20,24},{24,28},{28,32},{32,36}... | collective-permute-start | bytes 104 | tf_op jit(solution)/shard_map/while/body/eval_jaxpr/ppermute | solution.py:12
  159.4 16.2 %collective-permute-start = (f32[8,256,128]{2,1,0:T(8,128)S(1)}, f32[8,256,128]{2,1,0:T(8,128)S(1)}, u32[]{:S(2)}, u32[]{:S(2)}) collective-permute-start(f32[8,256,128]{2,1,0:T(8,128)S(1)} %multiply_add_fusion.4), channel_id=1, source_target_pairs={{0,4},{4,8},{8,12},{12,16},{16,20},{20,24},{24,28},{28,32},{32,36}... | collective-permute-start | bytes 3145736 | tf_op jit(solution)/shard_map/while/body/eval_jaxpr/ppermute | solution.py:12
  163.8 11.8 %collective-permute-start.2 = (f32[8]{0:T(128)S(1)}, f32[8]{0:T(128)S(1)}, u32[]{:S(2)}, u32[]{:S(2)}) collective-permute-start(f32[8]{0:T(128)S(1)} %get-tuple-element.235), channel_id=1, source_target_pairs={{0,4},{4,8},{8,12},{12,16},{16,20},{20,24},{24,28},{28,32},{32,36}... | collective-permute-start | bytes 104 | tf_op jit(solution)/shard_map/while/body/eval_jaxpr/ppermute | solution.py:12
  175.8 16.2 %collective-permute-start = (f32[8,256,128]{2,1,0:T(8,128)S(1)}, f32[8,256,128]{2,1,0:T(8,128)S(1)}, u32[]{:S(2)}, u32[]{:S(2)}) collective-permute-start(f32[8,256,128]{2,1,0:T(8,128)S(1)} %multiply_add_fusion.4), channel_id=1, source_target_pairs={{0,4},{4,8},{8,12},{12,16},{16,20},{20,24},{24,28},{28,32},{32,36}... | collective-permute-start | bytes 3145736 | tf_op jit(solution)/shard_map/while/body/eval_jaxpr/ppermute | solution.py:12
  192.2 16.2 %collective-permute-start = (f32[8,256,128]{2,1,0:T(8,128)S(1)}, f32[8,256,128]{2,1,0:T(8,128)S(1)}, u32[]{:S(2)}, u32[]{:S(2)}) collective-permute-start(f32[8,256,128]{2,1,0:T(8,128)S(1)} %multiply_add_fusion.4), channel_id=1, source_target_pairs={{0,4},{4,8},{8,12},{12,16},{16,20},{20,24},{24,28},{28,32},{32,36}... | collective-permute-start | bytes 3145736 | tf_op jit(solution)/shard_map/while/body/eval_jaxpr/ppermute | solution.py:12
  196.6 11.8 %collective-permute-start.2 = (f32[8]{0:T(128)S(1)}, f32[8]{0:T(128)S(1)}, u32[]{:S(2)}, u32[]{:S(2)}) collective-permute-start(f32[8]{0:T(128)S(1)} %get-tuple-element.235), channel_id=1, source_target_pairs={{0,4},{4,8},{8,12},{12,16},{16,20},{20,24},{24,28},{28,32},{32,36}... | collective-permute-start | bytes 104 | tf_op jit(solution)/shard_map/while/body/eval_jaxpr/ppermute | solution.py:12
  208.7 16.2 %collective-permute-start = (f32[8,256,128]{2,1,0:T(8,128)S(1)}, f32[8,256,128]{2,1,0:T(8,128)S(1)}, u32[]{:S(2)}, u32[]{:S(2)}) collective-permute-start(f32[8,256,128]{2,1,0:T(8,128)S(1)} %multiply_add_fusion.4), channel_id=1, source_target_pairs={{0,4},{4,8},{8,12},{12,16},{16,20},{20,24},{24,28},{28,32},{32,36}... | collective-permute-start | bytes 3145736 | tf_op jit(solution)/shard_map/while/body/eval_jaxpr/ppermute | solution.py:12
  225.1 16.2 %collective-permute-start = (f32[8,256,128]{2,1,0:T(8,128)S(1)}, f32[8,256,128]{2,1,0:T(8,128)S(1)}, u32[]{:S(2)}, u32[]{:S(2)}) collective-permute-start(f32[8,256,128]{2,1,0:T(8,128)S(1)} %multiply_add_fusion.4), channel_id=1, source_target_pairs={{0,4},{4,8},{8,12},{12,16},{16,20},{20,24},{24,28},{28,32},{32,36}... | collective-permute-start | bytes 3145736 | tf_op jit(solution)/shard_map/while/body/eval_jaxpr/ppermute | solution.py:12
  241.5 16.2 %collective-permute-start = (f32[8,256,128]{2,1,0:T(8,128)S(1)}, f32[8,256,128]{2,1,0:T(8,128)S(1)}, u32[]{:S(2)}, u32[]{:S(2)}) collective-permute-start(f32[8,256,128]{2,1,0:T(8,128)S(1)} %multiply_add_fusion.4), channel_id=1, source_target_pairs={{0,4},{4,8},{8,12},{12,16},{16,20},{20,24},{24,28},{28,32},{32,36}... | collective-permute-start | bytes 3145736 | tf_op jit(solution)/shard_map/while/body/eval_jaxpr/ppermute | solution.py:12
  245.9 11.8 %collective-permute-start.2 = (f32[8]{0:T(128)S(1)}, f32[8]{0:T(128)S(1)}, u32[]{:S(2)}, u32[]{:S(2)}) collective-permute-start(f32[8]{0:T(128)S(1)} %get-tuple-element.235), channel_id=1, source_target_pairs={{0,4},{4,8},{8,12},{12,16},{16,20},{20,24},{24,28},{28,32},{32,36}... | collective-permute-start | bytes 104 | tf_op jit(solution)/shard_map/while/body/eval_jaxpr/ppermute | solution.py:12
  258.0 18.3 %collective-permute-start = (f32[8,256,128]{2,1,0:T(8,128)S(1)}, f32[8,256,128]{2,1,0:T(8,128)S(1)}, u32[]{:S(2)}, u32[]{:S(2)}) collective-permute-start(f32[8,256,128]{2,1,0:T(8,128)S(1)} %multiply_add_fusion.4), channel_id=1, source_target_pairs={{0,4},{4,8},{8,12},{12,16},{16,20},{20,24},{24,28},{28,32},{32,36}... | collective-permute-start | bytes 3145736 | tf_op jit(solution)/shard_map/while/body/eval_jaxpr/ppermute | solution.py:12
  276.4 18.3 %collective-permute-start = (f32[8,256,128]{2,1,0:T(8,128)S(1)}, f32[8,256,128]{2,1,0:T(8,128)S(1)}, u32[]{:S(2)}, u32[]{:S(2)}) collective-permute-start(f32[8,256,128]{2,1,0:T(8,128)S(1)} %multiply_add_fusion.4), channel_id=1, source_target_pairs={{0,4},{4,8},{8,12},{12,16},{16,20},{20,24},{24,28},{28,32},{32,36}... | collective-permute-start | bytes 3145736 | tf_op jit(solution)/shard_map/while/body/eval_jaxpr/ppermute | solution.py:12
  295.0 18.3 %collective-permute-start = (f32[8,256,128]{2,1,0:T(8,128)S(1)}, f32[8,256,128]{2,1,0:T(8,128)S(1)}, u32[]{:S(2)}, u32[]{:S(2)}) collective-permute-start(f32[8,256,128]{2,1,0:T(8,128)S(1)} %multiply_add_fusion.4), channel_id=1, source_target_pairs={{0,4},{4,8},{8,12},{12,16},{16,20},{20,24},{24,28},{28,32},{32,36}... | collective-permute-start | bytes 3145736 | tf_op jit(solution)/shard_map/while/body/eval_jaxpr/ppermute | solution.py:12
  313.5 18.3 %collective-permute-start = (f32[8,256,128]{2,1,0:T(8,128)S(1)}, f32[8,256,128]{2,1,0:T(8,128)S(1)}, u32[]{:S(2)}, u32[]{:S(2)}) collective-permute-start(f32[8,256,128]{2,1,0:T(8,128)S(1)} %multiply_add_fusion.4), channel_id=1, source_target_pairs={{0,4},{4,8},{8,12},{12,16},{16,20},{20,24},{24,28},{28,32},{32,36}... | collective-permute-start | bytes 3145736 | tf_op jit(solution)/shard_map/while/body/eval_jaxpr/ppermute | solution.py:12
  332.0 18.3 %collective-permute-start = (f32[8,256,128]{2,1,0:T(8,128)S(1)}, f32[8,256,128]{2,1,0:T(8,128)S(1)}, u32[]{:S(2)}, u32[]{:S(2)}) collective-permute-start(f32[8,256,128]{2,1,0:T(8,128)S(1)} %multiply_add_fusion.4), channel_id=1, source_target_pairs={{0,4},{4,8},{8,12},{12,16},{16,20},{20,24},{24,28},{28,32},{32,36}... | collective-permute-start | bytes 3145736 | tf_op jit(solution)/shard_map/while/body/eval_jaxpr/ppermute | solution.py:12
  350.6 18.3 %collective-permute-start = (f32[8,256,128]{2,1,0:T(8,128)S(1)}, f32[8,256,128]{2,1,0:T(8,128)S(1)}, u32[]{:S(2)}, u32[]{:S(2)}) collective-permute-start(f32[8,256,128]{2,1,0:T(8,128)S(1)} %multiply_add_fusion.4), channel_id=1, source_target_pairs={{0,4},{4,8},{8,12},{12,16},{16,20},{20,24},{24,28},{28,32},{32,36}... | collective-permute-start | bytes 3145736 | tf_op jit(solution)/shard_map/while/body/eval_jaxpr/ppermute | solution.py:12
  369.1 18.3 %collective-permute-start = (f32[8,256,128]{2,1,0:T(8,128)S(1)}, f32[8,256,128]{2,1,0:T(8,128)S(1)}, u32[]{:S(2)}, u32[]{:S(2)}) collective-permute-start(f32[8,256,128]{2,1,0:T(8,128)S(1)} %multiply_add_fusion.4), channel_id=1, source_target_pairs={{0,4},{4,8},{8,12},{12,16},{16,20},{20,24},{24,28},{28,32},{32,36}... | collective-permute-start | bytes 3145736 | tf_op jit(solution)/shard_map/while/body/eval_jaxpr/ppermute | solution.py:12
  387.7 18.3 %collective-permute-start = (f32[8,256,128]{2,1,0:T(8,128)S(1)}, f32[8,256,128]{2,1,0:T(8,128)S(1)}, u32[]{:S(2)}, u32[]{:S(2)}) collective-permute-start(f32[8,256,128]{2,1,0:T(8,128)S(1)} %multiply_add_fusion.4), channel_id=1, source_target_pairs={{0,4},{4,8},{8,12},{12,16},{16,20},{20,24},{24,28},{28,32},{32,36}... | collective-permute-start | bytes 3145736 | tf_op jit(solution)/shard_map/while/body/eval_jaxpr/ppermute | solution.py:12
  406.2 18.3 %collective-permute-start = (f32[8,256,128]{2,1,0:T(8,128)S(1)}, f32[8,256,128]{2,1,0:T(8,128)S(1)}, u32[]{:S(2)}, u32[]{:S(2)}) collective-permute-start(f32[8,256,128]{2,1,0:T(8,128)S(1)} %multiply_add_fusion.4), channel_id=1, source_target_pairs={{0,4},{4,8},{8,12},{12,16},{16,20},{20,24},{24,28},{28,32},{32,36}... | collective-permute-start | bytes 3145736 | tf_op jit(solution)/shard_map/while/body/eval_jaxpr/ppermute | solution.py:12
  424.7 18.3 %collective-permute-start = (f32[8,256,128]{2,1,0:T(8,128)S(1)}, f32[8,256,128]{2,1,0:T(8,128)S(1)}, u32[]{:S(2)}, u32[]{:S(2)}) collective-permute-start(f32[8,256,128]{2,1,0:T(8,128)S(1)} %multiply_add_fusion.4), channel_id=1, source_target_pairs={{0,4},{4,8},{8,12},{12,16},{16,20},{20,24},{24,28},{28,32},{32,36}... | collective-permute-start | bytes 3145736 | tf_op jit(solution)/shard_map/while/body/eval_jaxpr/ppermute | solution.py:12
  431.2 11.8 %collective-permute-start.2 = (f32[8]{0:T(128)S(1)}, f32[8]{0:T(128)S(1)}, u32[]{:S(2)}, u32[]{:S(2)}) collective-permute-start(f32[8]{0:T(128)S(1)} %get-tuple-element.235), channel_id=1, source_target_pairs={{0,4},{4,8},{8,12},{12,16},{16,20},{20,24},{24,28},{28,32},{32,36}... | collective-permute-start | bytes 104 | tf_op jit(solution)/shard_map/while/body/eval_jaxpr/ppermute | solution.py:12
  443.3 18.3 %collective-permute-start = (f32[8,256,128]{2,1,0:T(8,128)S(1)}, f32[8,256,128]{2,1,0:T(8,128)S(1)}, u32[]{:S(2)}, u32[]{:S(2)}) collective-permute-start(f32[8,256,128]{2,1,0:T(8,128)S(1)} %multiply_add_fusion.4), channel_id=1, source_target_pairs={{0,4},{4,8},{8,12},{12,16},{16,20},{20,24},{24,28},{28,32},{32,36}... | collective-permute-start | bytes 3145736 | tf_op jit(solution)/shard_map/while/body/eval_jaxpr/ppermute | solution.py:12
  449.8 11.8 %collective-permute-start.2 = (f32[8]{0:T(128)S(1)}, f32[8]{0:T(128)S(1)}, u32[]{:S(2)}, u32[]{:S(2)}) collective-permute-start(f32[8]{0:T(128)S(1)} %get-tuple-element.235), channel_id=1, source_target_pairs={{0,4},{4,8},{8,12},{12,16},{16,20},{20,24},{24,28},{28,32},{32,36}... | collective-permute-start | bytes 104 | tf_op jit(solution)/shard_map/while/body/eval_jaxpr/ppermute | solution.py:12
  461.8 18.3 %collective-permute-start = (f32[8,256,128]{2,1,0:T(8,128)S(1)}, f32[8,256,128]{2,1,0:T(8,128)S(1)}, u32[]{:S(2)}, u32[]{:S(2)}) collective-permute-start(f32[8,256,128]{2,1,0:T(8,128)S(1)} %multiply_add_fusion.4), channel_id=1, source_target_pairs={{0,4},{4,8},{8,12},{12,16},{16,20},{20,24},{24,28},{28,32},{32,36}... | collective-permute-start | bytes 3145736 | tf_op jit(solution)/shard_map/while/body/eval_jaxpr/ppermute | solution.py:12
  468.3 11.8 %collective-permute-start.2 = (f32[8]{0:T(128)S(1)}, f32[8]{0:T(128)S(1)}, u32[]{:S(2)}, u32[]{:S(2)}) collective-permute-start(f32[8]{0:T(128)S(1)} %get-tuple-element.235), channel_id=1, source_target_pairs={{0,4},{4,8},{8,12},{12,16},{16,20},{20,24},{24,28},{28,32},{32,36}... | collective-permute-start | bytes 104 | tf_op jit(solution)/shard_map/while/body/eval_jaxpr/ppermute | solution.py:12
  480.4 18.3 %collective-permute-start = (f32[8,256,128]{2,1,0:T(8,128)S(1)}, f32[8,256,128]{2,1,0:T(8,128)S(1)}, u32[]{:S(2)}, u32[]{:S(2)}) collective-permute-start(f32[8,256,128]{2,1,0:T(8,128)S(1)} %multiply_add_fusion.4), channel_id=1, source_target_pairs={{0,4},{4,8},{8,12},{12,16},{16,20},{20,24},{24,28},{28,32},{32,36}... | collective-permute-start | bytes 3145736 | tf_op jit(solution)/shard_map/while/body/eval_jaxpr/ppermute | solution.py:12
  486.9 11.8 %collective-permute-start.2 = (f32[8]{0:T(128)S(1)}, f32[8]{0:T(128)S(1)}, u32[]{:S(2)}, u32[]{:S(2)}) collective-permute-start(f32[8]{0:T(128)S(1)} %get-tuple-element.235), channel_id=1, source_target_pairs={{0,4},{4,8},{8,12},{12,16},{16,20},{20,24},{24,28},{28,32},{32,36}... | collective-permute-start | bytes 104 | tf_op jit(solution)/shard_map/while/body/eval_jaxpr/ppermute | solution.py:12
  498.9 18.3 %collective-permute-start = (f32[8,256,128]{2,1,0:T(8,128)S(1)}, f32[8,256,128]{2,1,0:T(8,128)S(1)}, u32[]{:S(2)}, u32[]{:S(2)}) collective-permute-start(f32[8,256,128]{2,1,0:T(8,128)S(1)} %multiply_add_fusion.4), channel_id=1, source_target_pairs={{0,4},{4,8},{8,12},{12,16},{16,20},{20,24},{24,28},{28,32},{32,36}... | collective-permute-start | bytes 3145736 | tf_op jit(solution)/shard_map/while/body/eval_jaxpr/ppermute | solution.py:12
  505.4 11.8 %collective-permute-start.2 = (f32[8]{0:T(128)S(1)}, f32[8]{0:T(128)S(1)}, u32[]{:S(2)}, u32[]{:S(2)}) collective-permute-start(f32[8]{0:T(128)S(1)} %get-tuple-element.235), channel_id=1, source_target_pairs={{0,4},{4,8},{8,12},{12,16},{16,20},{20,24},{24,28},{28,32},{32,36}... | collective-permute-start | bytes 104 | tf_op jit(solution)/shard_map/while/body/eval_jaxpr/ppermute | solution.py:12
  517.4 18.3 %collective-permute-start = (f32[8,256,128]{2,1,0:T(8,128)S(1)}, f32[8,256,128]{2,1,0:T(8,128)S(1)}, u32[]{:S(2)}, u32[]{:S(2)}) collective-permute-start(f32[8,256,128]{2,1,0:T(8,128)S(1)} %multiply_add_fusion.4), channel_id=1, source_target_pairs={{0,4},{4,8},{8,12},{12,16},{16,20},{20,24},{24,28},{28,32},{32,36}... | collective-permute-start | bytes 3145736 | tf_op jit(solution)/shard_map/while/body/eval_jaxpr/ppermute | solution.py:12
  523.9 11.8 %collective-permute-start.2 = (f32[8]{0:T(128)S(1)}, f32[8]{0:T(128)S(1)}, u32[]{:S(2)}, u32[]{:S(2)}) collective-permute-start(f32[8]{0:T(128)S(1)} %get-tuple-element.235), channel_id=1, source_target_pairs={{0,4},{4,8},{8,12},{12,16},{16,20},{20,24},{24,28},{28,32},{32,36}... | collective-permute-start | bytes 104 | tf_op jit(solution)/shard_map/while/body/eval_jaxpr/ppermute | solution.py:12
  536.0 18.3 %collective-permute-start = (f32[8,256,128]{2,1,0:T(8,128)S(1)}, f32[8,256,128]{2,1,0:T(8,128)S(1)}, u32[]{:S(2)}, u32[]{:S(2)}) collective-permute-start(f32[8,256,128]{2,1,0:T(8,128)S(1)} %multiply_add_fusion.4), channel_id=1, source_target_pairs={{0,4},{4,8},{8,12},{12,16},{16,20},{20,24},{24,28},{28,32},{32,36}... | collective-permute-start | bytes 3145736 | tf_op jit(solution)/shard_map/while/body/eval_jaxpr/ppermute | solution.py:12
  554.5 18.3 %collective-permute-start = (f32[8,256,128]{2,1,0:T(8,128)S(1)}, f32[8,256,128]{2,1,0:T(8,128)S(1)}, u32[]{:S(2)}, u32[]{:S(2)}) collective-permute-start(f32[8,256,128]{2,1,0:T(8,128)S(1)} %multiply_add_fusion.4), channel_id=1, source_target_pairs={{0,4},{4,8},{8,12},{12,16},{16,20},{20,24},{24,28},{28,32},{32,36}... | collective-permute-start | bytes 3145736 | tf_op jit(solution)/shard_map/while/body/eval_jaxpr/ppermute | solution.py:12
  573.0 18.3 %collective-permute-start = (f32[8,256,128]{2,1,0:T(8,128)S(1)}, f32[8,256,128]{2,1,0:T(8,128)S(1)}, u32[]{:S(2)}, u32[]{:S(2)}) collective-permute-start(f32[8,256,128]{2,1,0:T(8,128)S(1)} %multiply_add_fusion.4), channel_id=1, source_target_pairs={{0,4},{4,8},{8,12},{12,16},{16,20},{20,24},{24,28},{28,32},{32,36}... | collective-permute-start | bytes 3145736 | tf_op jit(solution)/shard_map/while/body/eval_jaxpr/ppermute | solution.py:12
  591.6 18.3 %collective-permute-start = (f32[8,256,128]{2,1,0:T(8,128)S(1)}, f32[8,256,128]{2,1,0:T(8,128)S(1)}, u32[]{:S(2)}, u32[]{:S(2)}) collective-permute-start(f32[8,256,128]{2,1,0:T(8,128)S(1)} %multiply_add_fusion.4), channel_id=1, source_target_pairs={{0,4},{4,8},{8,12},{12,16},{16,20},{20,24},{24,28},{28,32},{32,36}... | collective-permute-start | bytes 3145736 | tf_op jit(solution)/shard_map/while/body/eval_jaxpr/ppermute | solution.py:12
  610.1 18.3 %collective-permute-start = (f32[8,256,128]{2,1,0:T(8,128)S(1)}, f32[8,256,128]{2,1,0:T(8,128)S(1)}, u32[]{:S(2)}, u32[]{:S(2)}) collective-permute-start(f32[8,256,128]{2,1,0:T(8,128)S(1)} %multiply_add_fusion.4), channel_id=1, source_target_pairs={{0,4},{4,8},{8,12},{12,16},{16,20},{20,24},{24,28},{28,32},{32,36}... | collective-permute-start | bytes 3145736 | tf_op jit(solution)/shard_map/while/body/eval_jaxpr/ppermute | solution.py:12
  628.7 18.3 %collective-permute-start = (f32[8,256,128]{2,1,0:T(8,128)S(1)}, f32[8,256,128]{2,1,0:T(8,128)S(1)}, u32[]{:S(2)}, u32[]{:S(2)}) collective-permute-start(f32[8,256,128]{2,1,0:T(8,128)S(1)} %multiply_add_fusion.4), channel_id=1, source_target_pairs={{0,4},{4,8},{8,12},{12,16},{16,20},{20,24},{24,28},{28,32},{32,36}... | collective-permute-start | bytes 3145736 | tf_op jit(solution)/shard_map/while/body/eval_jaxpr/ppermute | solution.py:12
  (55 other events, 532.8 us)
Sparse Core Ops, SparseCore 0:
  9.0 42.7 all-gather.3
  60.7 26.7 all-gather.5
  89.2 26.5 all-gather.7
  677.1 61.0 reduce-scatter.1
where the time goes:
time: 748 us; the launch traced here: 745 us
  starting transfers between devices  475 us (64%)
  waiting for transfers between devices  179 us (24%)
  matrix products  41.6 us (6%)
  between operations  13.3 us (2%)
  other arithmetic  13 us (2%)
  blocking collectives  12.2 us (2%)
  local copies, waits for them, and re-layouts  9.69 us (1%)
    ppermute x93, starting transfers between devices, passed_along(): return lax.ppermute(block, axis, route)  474 us
    ppermute x93, waiting for transfers between devices, passed_along(): return lax.ppermute(block, axis, route)  68.6 us
    reduce_scatter x1, waiting for transfers between devices, per_device(): lax.psum_scatter(partial_value.astype(jnp.bfloat16), 'val', scatter_dimen...  61.2 us
    all_gather x1, waiting for transfers between devices, per_device(): whole = lax.all_gather(tokens, 'val', axis=1, tiled=True)  44.4 us
  transfers between devices with their start and end apart: 97, of which 34 were waited for; matrix products, arithmetic and copies ran while one was open for 5% of the time, Pallas kernels for 0%

commit v1 on v0

v1 whole, which is shorter than its diff:
```python
import jax
import jax.numpy as jnp
from jax import lax
from jax.sharding import PartitionSpec as P

F32 = jnp.float32
BF16 = jnp.bfloat16


def around(x, distance):
    n = lax.axis_size("val")
    return lax.ppermute(x, "val", [(i, (i + distance) % n) for i in range(n)])


def split3(x):
    hi = lax.reduce_precision(x, 8, 7)
    mid = lax.reduce_precision(x - hi, 8, 7)
    return [hi, mid, x - hi - mid]


def rows_of(w, chunk, size):
    return lax.dynamic_slice_in_dim(w, chunk * size, size, axis=0)


def per_device(tokens, w_query, w_key, w_value, w_gate, gate_bias, norm_gain, w_out):
    me = lax.axis_index("val")
    nval = lax.axis_size("val")
    place = lax.axis_index("seq")
    blocks = lax.axis_size("seq")
    rows, chunk = tokens.shape
    width = w_query.shape[0]
    heads, vlocal = w_value.shape[1:]
    own = heads // nval
    qsize = w_query.shape[1] // own
    vsize = vlocal * nval

    part = heads * vlocal // blocks
    wo = rows_of(w_out.reshape(heads * vlocal, -1), place, part)
    wo = wo.reshape(part, nval, chunk).transpose(1, 0, 2)
    wo = lax.all_to_all(wo, "val", 0, 0)
    wo = lax.all_gather(wo, "seq", axis=0)
    wo = wo.reshape(heads, blocks // heads, nval, part, chunk).transpose(0, 2, 1, 3, 4)
    wo = wo.reshape(heads * vsize, chunk)

    pieces = [tokens, around(tokens, 1), around(tokens, -1), around(tokens, 2)]
    index = [(me + d) % nval for d in (0, nval - 1, 1, 2)]

    wv = w_value.reshape(width, heads * vlocal)
    wg = lax.dynamic_slice_in_dim(w_gate, me * own, own, axis=2).reshape(width, 2 * own)

    def project(w):
        return sum(
            jnp.dot(x, rows_of(w, i, chunk), preferred_element_type=F32)
            for x, i in zip(pieces, index)
        )

    values = project(wv).astype(BF16).reshape(rows, nval, own, vlocal)
    values = lax.all_to_all(values, "val", 1, 0)
    values = values.transpose(1, 2, 0, 3).reshape(rows, own, vsize)
    queries = project(w_query).astype(BF16).reshape(rows, own, qsize)
    keys = project(w_key).astype(BF16).reshape(rows, own, qsize)
    gates = project(wg).reshape(rows, 2, own)
    gates = gates + lax.dynamic_slice_in_dim(gate_bias, me * own, own, axis=1)[None]
    igate = gates[:, 0].T
    logf = jax.nn.log_sigmoid(gates[:, 1]).T
    position = jnp.arange(rows)
    causal = position[:, None] >= position[None, :]
    cumb = jnp.dot(logf, causal.T.astype(F32), precision=lax.Precision.HIGHEST)
    total = cumb[:, -1]

    weight_log = total[:, None] - cumb + igate
    top = jnp.max(weight_log, axis=1)
    wts = jnp.exp(weight_log - top[:, None])
    kw = (keys.astype(F32) * wts.T[:, :, None]).astype(BF16)
    state = jnp.einsum("thd,the->hde", kw, values, preferred_element_type=F32)
    norm = jnp.sum(kw.astype(F32), axis=0)
    extra = [norm[:, :, None]] + [
        jnp.broadcast_to(x[:, None, None], (own, qsize, 1)) for x in split3(top) + split3(total)
    ]
    extra = jnp.concatenate(extra + [jnp.zeros((own, qsize, 128 - len(extra)), F32)], axis=2)
    sent = jnp.concatenate([state.astype(BF16), extra.astype(BF16)], axis=2)
    cut = own * qsize // blocks
    sent = sent.reshape(blocks, cut, vsize + 128)
    got = lax.all_to_all(sent, "seq", 0, 0)

    scale = qsize ** (-0.5)
    scores = jnp.einsum("thd,shd->hts", queries, keys, preferred_element_type=F32) * scale
    logd = cumb[:, :, None] - cumb[:, None, :] + igate[:, None, :]
    logd = jnp.where(causal[None], logd, F32(-1e30))
    rowmax = jnp.max(logd, axis=-1)
    wts = jnp.where(causal[None], jnp.exp(logd - rowmax[:, :, None]) * scores, 0.0).astype(BF16)
    numer = jnp.einsum("hts,she->hte", wts, values, preferred_element_type=F32)
    denom = jnp.sum(wts.astype(F32), axis=-1)

    small = got[:, 0, vsize : vsize + 128].astype(F32)
    tops = small[:, 1] + small[:, 2] + small[:, 3]
    totals = small[:, 4] + small[:, 5] + small[:, 6]
    body = got.astype(F32)
    held = jnp.zeros((cut, vsize + 128), F32)
    ptop = F32(-1e30)
    prefixes, ptops = [], []
    for b in range(blocks):
        prefixes.append(held)
        ptops.append(ptop)
        new = jnp.maximum(ptop + totals[b], tops[b])
        held = jnp.exp(ptop + totals[b] - new) * held + jnp.exp(tops[b] - new) * body[b]
        ptop = new
    lane = jnp.arange(vsize + 128)
    back = []
    for held, ptop in zip(prefixes, ptops):
        for k, x in enumerate(split3(ptop)):
            held = jnp.where(lane == vsize + 1 + k, x, held)
        back.append(held.astype(BF16))
    prefix = lax.all_to_all(jnp.stack(back), "seq", 0, 0)
    prefix = prefix.reshape(own, qsize, vsize + 128)
    ptop = prefix[:, 0, vsize + 1 : vsize + 4].astype(F32).sum(axis=1)
    inter = jnp.einsum("thd,hde->hte", queries, prefix, preferred_element_type=F32)
    top = jnp.maximum(cumb + ptop[:, None], rowmax)
    decay = jnp.exp(cumb + ptop[:, None] - top) * scale
    fade = jnp.exp(rowmax - top)
    numer = numer * fade[:, :, None] + inter[:, :, :vsize] * decay[:, :, None]
    denom = denom * fade + inter[:, :, vsize] * decay
    hidden = numer / jnp.maximum(jnp.abs(denom), 1.0)[:, :, None]
    mean = jnp.mean(hidden, axis=-1)
    msq = jnp.mean(hidden * hidden, axis=-1)
    gain = lax.all_gather(norm_gain, "val", axis=1, tiled=True)
    gain = lax.dynamic_slice_in_dim(gain, me * own, own, axis=0)
    normed = (hidden - mean[..., None]) * lax.rsqrt(msq - mean * mean + 1e-06)[..., None]
    normed = (normed * gain[:, None, :]).astype(BF16)
    normed = normed.transpose(1, 0, 2).reshape(rows, own * vsize)

    pieces = [normed, around(normed, 1), around(normed, -1), around(normed, 2)]
    return project_out(pieces, index, wo, chunk).astype(BF16)


def project_out(pieces, index, wo, chunk):
    return sum(
        jnp.dot(x, rows_of(wo, i, chunk), preferred_element_type=F32)
        for x, i in zip(pieces, index)
    )


def solution(mesh):
    placed = (
        P("seq", "val"),
        P(None, "val"),
        P(None, "val"),
        P(None, None, "val"),
        P(),
        P(),
        P(None, "val"),
        P(None, "val", None),
    )
    return jax.shard_map(
        per_device, mesh=mesh, in_specs=placed, out_specs=P("seq", "val"), check_vma=False
    )
```

time: 748 us -> 404 us (0.54)
  starting transfers between devices: 475 us -> 34.6 us
  between operations: 13.3 us -> 147 us
  waiting for transfers between devices: 179 us -> 55.9 us
  other arithmetic: 13 us -> 62.5 us
  local copies, waits for them, and re-layouts: 9.69 us -> 40.9 us
  matrix products: 41.6 us -> 51.2 us
    ppermute x93 -> x6, starting transfers between devices: 474 us -> 9.72 us  [around(): return lax.ppermute(x, 'val', [(i, (i + distance) % n) for i in range(n)])]
    reduce_scatter x1 -> x0, waiting for transfers between devices: 61.2 us -> none  [per_device(): lax.psum_scatter(partial_value.astype(jnp.bfloat16), 'val', scatter_dimen...]
    unnamed x1 -> x31, other arithmetic: 0.01 us -> 56.6 us
    ppermute x93 -> x6, waiting for transfers between devices: 68.6 us -> 19.2 us  [around(): return lax.ppermute(x, 'val', [(i, (i + distance) % n) for i in range(n)])]
    all_gather x3 -> x1, waiting for transfers between devices: 48.5 us -> 0.01 us  [per_device(): wo = lax.all_gather(wo, 'seq', axis=0)]
    all_to_all x0 -> x4, waiting for transfers between devices: none -> 36.6 us  [the longest x1 20.9 us: per_device(): wo = lax.all_to_all(wo, 'val', 0, 0)]
    all_to_all x0 -> x4, starting transfers between devices: none -> 24.8 us  [the longest x1 13.1 us: per_device(): got = lax.all_to_all(sent, 'seq', 0, 0)]
    psum x1 -> x0, blocking collectives: 12.2 us -> none  [per_device(): lax.psum((jnp.sum(hidden, axis=-1), jnp.sum(hidden * hidden, axis=-1)), '...]
  transfers between devices with their start and end apart: 97 -> 11, of which waited for: 34 -> 5; matrix products, arithmetic and copies ran while one was open for 5% -> 37% of each run, Pallas kernels for 0% -> 0%
where the time goes in v1:
time: 404 us; the launch traced here: 401 us
  between operations  147 us (36%)
  other arithmetic  62.5 us (15%)
  waiting for transfers between devices  55.9 us (14%)
  matrix products  51.2 us (13%)
  local copies, waits for them, and re-layouts  40.9 us (10%)
  starting transfers between devices  34.6 us (9%)
  blocking collectives  9.03 us (2%)
    unnamed x31, other arithmetic  56.6 us
    dot_general x16, matrix products, project(): jnp.dot(x, rows_of(w, i, chunk), preferred_element_type=F32)  35.6 us
    all_to_all x1, waiting for transfers between devices, per_device(): wo = lax.all_to_all(wo, 'val', 0, 0)  20.9 us
    ppermute x6, waiting for transfers between devices, around(): return lax.ppermute(x, 'val', [(i, (i + distance) % n) for i in range(n)])  19.2 us
    all_to_all x1, starting transfers between devices, per_device(): got = lax.all_to_all(sent, 'seq', 0, 0)  13.1 us
    unnamed x32, local copies, waits for them, and re-layouts  11.9 us
    ppermute x6, starting transfers between devices, around(): return lax.ppermute(x, 'val', [(i, (i + distance) % n) for i in range(n)])  9.72 us
    all_gather x1, blocking collectives, per_device(): gain = lax.all_gather(norm_gain, 'val', axis=1, tiled=True)  9.03 us
  transfers between devices with their start and end apart: 11, of which 5 were waited for; matrix products, arithmetic and copies ran while one was open for 37% of the time, Pallas kernels for 0%

profile of v1, /device:TPU:1, one launch (start us, length us, event | category | flops | bytes accessed | tf_op | source)
XLA Modules:
  0.0 400.6 jit_solution(4611584995979273099)
XLA Ops:
  6.5 2.1 collective-permute-start
  8.7 2.6 collective-permute-start.2
  15.9 3.4 all-to-all-start.3
  20.9 2.9 fusion.32
  23.8 2.9 fusion.38
  27.0 20.9 %all-to-all-done.3 = bf16[4,32,1024]{2,1,0:T(8,128)(2,1)S(1)} async-done(((bf16[4,32,1024]{2,1,0:T(8,128)(2,1)}), bf16[4,32,1024]{2,1,0:T(8,128)(2,1)S(1)}, u32[]{:S(2)}, u32[]{:S(2)}) %all-to-all-start.3) | async-done | bytes 262176 | tf_op jit(solution)/shard_map/all_to_all | solution.py:40
  49.2 9.0 %all_gather.9 = f32[8,512]{1,0:T(8,128)S(1)} all-gather(f32[8,128]{1,0:T(8,128)S(1)} %copy-done.13), channel_id=1, replica_groups=mesh['seq'=32,'val'=4] {'val'}, dimensions={1}, use_global_device_ids=true | all-gather | bytes 20480 | tf_op jit(solution)/shard_map/all_gather | solution.py:126
  58.4 9.0 %copy.60 = bf16[512,8,8,128]{3,1,2,0:T(8,128)(2,1)} copy(bf16[512,8,8,128]{3,2,1,0:T(8,128)(2,1)} %bitcast.172) | data formatting | bytes 16777216
  67.3 4.1 %fusion.14 = f32[1024,384]{1,0:T(8,128)} fusion(bf16[384,1024]{1,0:T(8,128)(2,1)S(1)} %copy-done.3, bf16[4096,1024]{1,0:T(8,128)(2,1)} %bitcast.164, s32[]{:T(128)S(6)} %select_n.467), kind=kOutput, calls=%fused_computation.15 | convolution fusion | flops 805306368 | bytes 4456452 | tf_op jit(solution)/shard_map/dot_general | solution.py:53
  72.4 2.9 fusion.10
  75.3 3.0 fusion.12
  78.3 3.8 add_convert_fusion.1
  82.2 3.7 all-to-all-start
  86.6 2.0 fusion.28
  88.5 2.1 convolution_add_fusion.1
  90.8 2.8 fusion.42
  97.5 2.3 convolution_convert_fusion
  104.9 3.2 concatenate.6
  108.1 13.1 %all-to-all-start.1 = ((bf16[32,16,640]{2,1,0:T(8,128)(2,1)}), bf16[32,16,640]{2,1,0:T(8,128)(2,1)}, u32[]{:S(2)}, u32[]{:S(2)}) async-start(bf16[32,16,640]{2,1,0:T(8,128)(2,1)} %bitcast.175), calls=%async_computation.1 | async-start | bytes 1310720 | tf_op jit(solution)/shard_map/all_to_all | solution.py:84
  121.2 2.9 fusion.34
  124.2 2.9 convolution_add_fusion.3
  127.1 7.1 %all-to-all-done.1 = bf16[32,16,640]{2,1,0:T(8,128)(2,1)} async-done(((bf16[32,16,640]{2,1,0:T(8,128)(2,1)}), bf16[32,16,640]{2,1,0:T(8,128)(2,1)}, u32[]{:S(2)}, u32[]{:S(2)}) %all-to-all-start.1) | async-done | bytes 655392 | tf_op jit(solution)/shard_map/all_to_all | solution.py:84
  271.7 2.0 constant_dynamic-update-slice_fusion.30
  273.7 1.9 constant_dynamic-update-slice_fusion.29
  279.2 1.9 constant_dynamic-update-slice_fusion.26
  284.7 1.9 constant_dynamic-update-slice_fusion.23
  288.3 2.0 constant_dynamic-update-slice_fusion.21
  292.1 1.9 constant_dynamic-update-slice_fusion.19
  295.7 1.9 constant_dynamic-update-slice_fusion.17
  299.4 2.0 constant_dynamic-update-slice_fusion.15
  303.3 1.9 constant_dynamic-update-slice_fusion.13
  307.0 1.9 constant_dynamic-update-slice_fusion.11
  308.9 1.9 constant_dynamic-update-slice_fusion.10
  310.8 1.9 constant_dynamic-update-slice_fusion.9
  314.5 2.0 constant_dynamic-update-slice_fusion.7
  321.9 2.0 constant_dynamic-update-slice_fusion.3
  323.9 1.9 constant_dynamic-update-slice_fusion.2
  325.8 1.9 constant_dynamic-update-slice_fusion.1
  329.5 4.6 %all-to-all-start.2 = ((bf16[32,16,640]{2,1,0:T(8,128)(2,1)}), bf16[32,16,640]{2,1,0:T(8,128)(2,1)}, u32[]{:S(2)}, u32[]{:S(2)}) async-start(bf16[32,16,640]{2,1,0:T(8,128)(2,1)} %constant_dynamic-update-slice_fusion), calls=%async_computation.2 | async-start | bytes 1310720 | tf_op jit(solution)/shard_map/all_to_all | solution.py:114
  334.5 2.0 fusion.24
  338.0 8.6 %all-to-all-done.2 = bf16[32,16,640]{2,1,0:T(8,128)(2,1)} async-done(((bf16[32,16,640]{2,1,0:T(8,128)(2,1)}), bf16[32,16,640]{2,1,0:T(8,128)(2,1)}, u32[]{:S(2)}, u32[]{:S(2)}) %all-to-all-start.2) | async-done | bytes 655392 | tf_op jit(solution)/shard_map/all_to_all | solution.py:114
  350.8 2.4 fusion.133
  357.8 8.5 %copy.52 = bf16[8,4,4,32,1024]{4,3,2,1,0:T(8,128)(2,1)} copy(bf16[8,4,4,32,1024]{4,3,1,2,0:T(8,128)(2,1)} %bitcast.173) | data formatting | bytes 16777216 | tf_op jit(solution)/shard_map/transpose | solution.py:42
  366.3 2.7 fusion.6
  369.0 5.4 %collective-permute-done.3 = bf16[384,1024]{0,1:T(8,128)(2,1)S(1)} collective-permute-done((bf16[384,1024]{0,1:T(8,128)(2,1)S(1)}, bf16[384,1024]{0,1:T(8,128)(2,1)S(1)}, u32[]{:S(2)}, u32[]{:S(2)}) %collective-permute-start.3) | collective-permute-done | bytes 786464 | tf_op jit(solution)/shard_map/ppermute | solution.py:12
  374.5 2.6 fusion.4
  378.1 13.8 %collective-permute-done.5 = bf16[384,1024]{0,1:T(8,128)(2,1)S(1)} collective-permute-done((bf16[384,1024]{0,1:T(8,128)(2,1)S(1)}, bf16[384,1024]{0,1:T(8,128)(2,1)S(1)}, u32[]{:S(2)}, u32[]{:S(2)}) %collective-permute-start.5) | collective-permute-done | bytes 786464 | tf_op jit(solution)/shard_map/ppermute | solution.py:12
  391.9 1.9 add_convert_fusion
  (110 shorter events, 62.1 us)
Async XLA Ops:
  6.5 12.9 %copy-start = (bf16[4096,2,8]{0,2,1:T(8,128)(2,1)S(1)}, bf16[4096,2,8]{0,2,1:T(8,128)(2,1)}, u32[]{:S(2)}) copy-start(bf16[4096,2,8]{0,2,1:T(8,128)(2,1)} %param.12) | copy-start | bytes 393220
  6.5 14.4 %copy-start.3 = (bf16[384,1024]{1,0:T(8,128)(2,1)S(1)}, bf16[384,1024]{1,0:T(8,128)(2,1)}, u32[]{:S(2)}) copy-start(bf16[384,1024]{1,0:T(8,128)(2,1)} %param.8) | copy-start | bytes 2359300
  6.5 65.2 %collective-permute-start = (bf16[384,1024]{1,0:T(8,128)(2,1)}, bf16[384,1024]{1,0:T(8,128)(2,1)S(1)}, u32[]{:S(2)}, u32[]{:S(2)}) collective-permute-start(bf16[384,1024]{1,0:T(8,128)(2,1)} %param.8), channel_id=1, source_target_pairs={{0,1},{1,2},{2,3},{3,0},{4,5},{5,6},{6,7},{7,4},{8,9},{9,10},{10,1... | collective-permute-start | bytes 2359304 | tf_op jit(solution)/shard_map/ppermute | solution.py:12
  8.7 62.7 %collective-permute-start.2 = (bf16[384,1024]{1,0:T(8,128)(2,1)}, bf16[384,1024]{1,0:T(8,128)(2,1)S(1)}, u32[]{:S(2)}, u32[]{:S(2)}) collective-permute-start(bf16[384,1024]{1,0:T(8,128)(2,1)} %param.8), channel_id=1, source_target_pairs={{0,2},{1,3},{2,0},{3,1},{4,6},{5,7},{6,4},{7,5},{8,10},{9,11},{10,... | collective-permute-start | bytes 2359304 | tf_op jit(solution)/shard_map/ppermute | solution.py:12
  11.3 60.7 %collective-permute-start.1 = (bf16[384,1024]{1,0:T(8,128)(2,1)}, bf16[384,1024]{1,0:T(8,128)(2,1)S(1)}, u32[]{:S(2)}, u32[]{:S(2)}) collective-permute-start(bf16[384,1024]{1,0:T(8,128)(2,1)} %param.8), channel_id=1, source_target_pairs={{0,3},{1,0},{2,1},{3,2},{4,7},{5,4},{6,5},{7,6},{8,11},{9,8},{10,9... | collective-permute-start | bytes 2359304 | tf_op jit(solution)/shard_map/ppermute | solution.py:12
  15.9 31.9 %all-to-all-start.3 = ((bf16[4,32,1024]{2,1,0:T(8,128)(2,1)}), bf16[4,32,1024]{2,1,0:T(8,128)(2,1)S(1)}, u32[]{:S(2)}, u32[]{:S(2)}) async-start(bf16[4,32,1024]{2,1,0:T(8,128)(2,1)} %copy.51), calls=%async_computation.3 | async-start | bytes 524288 | tf_op jit(solution)/shard_map/all_to_all | solution.py:40
  19.3 338.4 %all-gather.3.cloned.1.call-start = ((), (), s32[]{:S(2)}) async-start(), calls=%async_computation.4 | async-start | bytes 8650752 | tf_op jit(solution)/shard_map/all_gather | solution.py:41
  23.8 25.4 %copy-start.13 = (f32[8,128]{1,0:T(8,128)S(1)}, f32[8,128]{1,0:T(8,128)}, u32[]{:S(2)}) copy-start(f32[8,128]{1,0:T(8,128)} %param.14) | copy-start | bytes 12292
  23.8 34.5 %copy-start.14 = (f32[2,8]{1,0:T(2,128)S(1)}, f32[2,8]{1,0:T(2,128)}, u32[]{:S(2)}) copy-start(f32[2,8]{1,0:T(2,128)} %param.13) | copy-start | bytes 196
  47.9 0.7 copy-start.12
  75.3 3.0 copy-start.9
  82.2 12.3 %all-to-all-start = ((bf16[1,384,4,2,128]{1,4,3,0,2:T(8,128)(2,1)}), bf16[1,384,4,2,128]{1,4,3,0,2:T(8,128)(2,1)S(1)}, u32[]{:S(2)}, u32[]{:S(2)}) async-start(bf16[1,384,4,2,128]{1,4,3,0,2:T(8,128)(2,1)} %bitcast.10), calls=%async_computation | async-start | bytes 1572864 | tf_op jit(solution)/shard_map/all_to_all | solution.py:58
  85.8 2.7 copy-start.5
  108.1 26.1 %all-to-all-start.1 = ((bf16[32,16,640]{2,1,0:T(8,128)(2,1)}), bf16[32,16,640]{2,1,0:T(8,128)(2,1)}, u32[]{:S(2)}, u32[]{:S(2)}) async-start(bf16[32,16,640]{2,1,0:T(8,128)(2,1)} %bitcast.175), calls=%async_computation.1 | async-start | bytes 1310720 | tf_op jit(solution)/shard_map/all_to_all | solution.py:84
  121.2 3.0 copy-start.4
  308.9 25.6 %copy-start.6 = (f32[512,384]{1,0:T(8,128)S(1)}, f32[512,384]{1,0:T(8,128)}, u32[]{:S(2)}) copy-start(f32[512,384]{1,0:T(8,128)} %fusion.34) | copy-start | bytes 2359300
  308.9 25.6 %copy-start.7 = (f32[512,384]{1,0:T(8,128)S(1)}, f32[512,384]{1,0:T(8,128)}, u32[]{:S(2)}) copy-start(f32[512,384]{1,0:T(8,128)} %convolution_add_fusion.3) | copy-start | bytes 2359300
  329.5 17.1 %all-to-all-start.2 = ((bf16[32,16,640]{2,1,0:T(8,128)(2,1)}), bf16[32,16,640]{2,1,0:T(8,128)(2,1)}, u32[]{:S(2)}, u32[]{:S(2)}) async-start(bf16[32,16,640]{2,1,0:T(8,128)(2,1)} %constant_dynamic-update-slice_fusion), calls=%async_computation.2 | async-start | bytes 1310720 | tf_op jit(solution)/shard_map/all_to_all | solution.py:114
  334.5 2.8 copy-start.10
  336.5 0.7 copy-start.11
  348.4 1.3 copy-start.8
  353.9 20.6 %collective-permute-start.3 = (bf16[384,1024]{0,1:T(8,128)(2,1)S(1)}, bf16[384,1024]{0,1:T(8,128)(2,1)S(1)}, u32[]{:S(2)}, u32[]{:S(2)}) collective-permute-start(bf16[384,1024]{0,1:T(8,128)(2,1)S(1)} %bitcast.182), channel_id=1, source_target_pairs={{0,1},{1,2},{2,3},{3,0},{4,5},{5,6},{6,7},{7,4},{8,9},{9,10},{10,1... | collective-permute-start | bytes 2359304 | tf_op jit(solution)/shard_map/ppermute | solution.py:12
  354.8 22.2 %collective-permute-start.4 = (bf16[384,1024]{0,1:T(8,128)(2,1)S(1)}, bf16[384,1024]{0,1:T(8,128)(2,1)S(1)}, u32[]{:S(2)}, u32[]{:S(2)}) collective-permute-start(bf16[384,1024]{0,1:T(8,128)(2,1)S(1)} %bitcast.183), channel_id=1, source_target_pairs={{0,3},{1,0},{2,1},{3,2},{4,7},{5,4},{6,5},{7,6},{8,11},{9,8},{10,9... | collective-permute-start | bytes 2359304 | tf_op jit(solution)/shard_map/ppermute | solution.py:12
  356.6 35.3 %collective-permute-start.5 = (bf16[384,1024]{0,1:T(8,128)(2,1)S(1)}, bf16[384,1024]{0,1:T(8,128)(2,1)S(1)}, u32[]{:S(2)}, u32[]{:S(2)}) collective-permute-start(bf16[384,1024]{0,1:T(8,128)(2,1)S(1)} %bitcast.184), channel_id=1, source_target_pairs={{0,2},{1,3},{2,0},{3,1},{4,6},{5,7},{6,4},{7,5},{8,10},{9,11},{10,... | collective-permute-start | bytes 2359304 | tf_op jit(solution)/shard_map/ppermute | solution.py:12
  366.3 10.8 %copy-start.2 = (bf16[8,4,4,32,1024]{4,3,2,1,0:T(8,128)(2,1)S(1)}, bf16[8,4,4,32,1024]{4,3,2,1,0:T(8,128)(2,1)}, u32[]{:S(2)}) copy-start(bf16[8,4,4,32,1024]{4,3,2,1,0:T(8,128)(2,1)} %copy.52) | copy-start | bytes 25165828
  391.9 1.9 copy-start.1
Sparse Core Ops, SparseCore 0:
  48.7 55.8 all-gather.2

commit v2 on v1

v2 whole, which is shorter than its diff:
```python
import functools

import jax
import jax.numpy as jnp
from jax import lax
from jax.experimental import pallas as pl
from jax.experimental.pallas import tpu as pltpu
from jax.sharding import PartitionSpec as P

F32 = jnp.float32
BF16 = jnp.bfloat16
LANES = 128
NEVER = -1e30
BLOCK = 256


def around(x, distance):
    n = lax.axis_size("val")
    return lax.ppermute(x, "val", [(i, (i + distance) % n) for i in range(n)])


def params():
    return pltpu.CompilerParams(vmem_limit_bytes=48 * 1024 * 1024)


def cost(flops, nbytes, exps=0):
    return pl.CostEstimate(flops=flops, bytes_accessed=nbytes, transcendentals=exps)


def ring_gather(x):
    half = x.shape[0] // 2
    left = around(x, 1)
    right = around(x, -1)
    upper = around(left[:half], 1)
    lower = around(right[half:], -1)
    return x, left, right, upper, lower


def product_kernel(counts, with_total, scalars, *refs):
    refs = list(refs)
    total = None
    weights = refs[sum(counts) : sum(counts) + len(counts)]
    at = 0
    for n, w_ref in zip(counts, weights):
        x = refs[at][...] if n == 1 else jnp.concatenate([r[...] for r in refs[at : at + n]], axis=0)
        at += n
        term = jnp.dot(x, w_ref[...], preferred_element_type=F32)
        total = term if total is None else total + term
    at += len(counts)
    if with_total:
        total = total + refs[at][...]
        at += 1
    outs = refs[at:]
    if len(outs) == 1:
        outs[0][...] = total.astype(outs[0].dtype)
        return
    step = pl.program_id(0)
    own, _, vlocal = outs[0].shape
    for k, out in enumerate(outs):

        @pl.when(step == k)
        def _():
            for h in range(own):
                out[h] = total[:, h * vlocal : (h + 1) * vlocal].astype(out.dtype)


def product(groups, index, w, total, dtype, turned=None, own=2):
    rows = sum(x.shape[0] for x in groups[0])
    chunk = groups[0][0].shape[1]
    cols = w.shape[1]
    block = min(BLOCK, cols)
    steps = cols // block
    scalars = jnp.stack(list(index) + [turned if turned is not None else jnp.int32(0)])
    last = len(groups)

    def column(j, s):
        return j if turned is None else lax.rem(j + s[last], steps)

    flat = [x for g in groups for x in g]
    in_specs = [pl.BlockSpec(x.shape, lambda j, s: (0, 0)) for x in flat]
    for g in range(len(groups)):
        in_specs.append(pl.BlockSpec((chunk, block), lambda j, s, g=g: (s[g], column(j, s))))
    args = flat + [w] * len(groups)
    if total is not None:
        in_specs.append(pl.BlockSpec((rows, block), lambda j, s: (0, column(j, s))))
        args.append(total)
    if turned is None:
        out_specs = pl.BlockSpec((rows, block), lambda j, s: (0, j))
        out_shape = jax.ShapeDtypeStruct((rows, cols), dtype)
    else:
        shape = (own, rows, block // own)
        out_specs = [pl.BlockSpec(shape, lambda j, s: (0, 0, 0))] * steps
        out_shape = [jax.ShapeDtypeStruct(shape, dtype)] * steps
    flops = 2 * rows * chunk * len(groups) * cols
    nbytes = 2 * chunk * len(groups) * (cols + rows) + 4 * rows * cols
    return pl.pallas_call(
        functools.partial(product_kernel, [len(g) for g in groups], total is not None),
        grid_spec=pltpu.PrefetchScalarGridSpec(
            num_scalar_prefetch=1, grid=(steps,), in_specs=in_specs, out_specs=out_specs
        ),
        out_shape=out_shape,
        compiler_params=params(),
        cost_estimate=cost(flops, nbytes),
    )(scalars, *args)


def within_kernel(q_ref, k_ref, g_ref, bias_ref, kwt_ref, p_ref, stat_ref, mark_ref):
    own, rows, _ = p_ref.shape
    qsize = q_ref.shape[1] // own
    g = g_ref[...] + bias_ref[...]
    logf = jnp.minimum(g, 0.0) - jnp.log1p(jnp.exp(-jnp.abs(g)))
    late = lax.broadcasted_iota(jnp.int32, (rows, rows), 0)
    early = lax.broadcasted_iota(jnp.int32, (rows, rows), 1)
    causal = late >= early
    cumb = jnp.dot(
        causal.astype(F32), logf, precision=lax.Precision.HIGHEST, preferred_element_type=F32
    )
    cumb = pltpu.roll(cumb, LANES - own, axis=1)
    gap = g - cumb
    gap_rows = gap.T
    most = jnp.max(gap, axis=0, keepdims=True)
    total = cumb[rows - 1 : rows]
    mark_ref[...] = jnp.concatenate([total + most, total, jnp.zeros((6, LANES), F32)], axis=0)
    lane = lax.broadcasted_iota(jnp.int32, (rows, LANES), 1)
    stat = jnp.zeros((rows, LANES), F32)
    for h in range(own):
        q = q_ref[:, h * qsize : (h + 1) * qsize]
        k = k_ref[:, h * qsize : (h + 1) * qsize]
        seen = jnp.where(causal, gap_rows[h : h + 1, :], F32(NEVER))
        high = jnp.max(seen, axis=1, keepdims=True)
        score = lax.dot_general(q, k, (((1,), (1,)), ((), ())), preferred_element_type=F32)
        wts = jnp.exp(seen - high) * (score * qsize ** (-0.5))
        wts = jnp.where(causal, wts, 0.0).astype(BF16)
        p_ref[h] = wts
        denom = jnp.sum(wts.astype(F32), axis=1, keepdims=True)
        stat = jnp.where(lane == h, high, jnp.where(lane == own + h, denom, stat))
        fall = jnp.exp(gap[:, h : h + 1] - most[:, h : h + 1])
        kw = (k.astype(F32) * fall).astype(BF16)
        kwt_ref[h * qsize : (h + 1) * qsize] = kw.astype(F32).T.astype(BF16)
    stat_ref[...] = stat


def within(q, k, g, bias, own):
    rows, width = q.shape
    return pl.pallas_call(
        within_kernel,
        out_shape=[
            jax.ShapeDtypeStruct((width, rows), BF16),
            jax.ShapeDtypeStruct((own, rows, rows), BF16),
            jax.ShapeDtypeStruct((rows, LANES), F32),
            jax.ShapeDtypeStruct((8, LANES), F32),
        ],
        compiler_params=params(),
        cost_estimate=cost(2 * rows * rows * width, 4 * rows * width, own * rows * rows),
    )(q, k, g, bias)


def parts_of(x):
    hi = x.astype(BF16).astype(F32)
    mid = (x - hi).astype(BF16).astype(F32)
    return [hi, mid, x - hi - mid]


def summary_kernel(scalars, kwt_ref, mark_ref, v0, v1, v2, v3, sent_ref, v_ref):
    own, rows, vlocal = v0.shape
    vsize = v_ref.shape[2]
    qsize = kwt_ref.shape[0] // own
    for n, ref in enumerate((v0, v1, v2, v3)):
        at = pl.multiple_of(scalars[n] * vlocal, vlocal)
        for h in range(own):
            v_ref[h, :, pl.ds(at, vlocal)] = ref[h]
    lane = lax.broadcasted_iota(jnp.int32, (qsize, LANES), 1)
    for h in range(own):
        kwt = kwt_ref[h * qsize : (h + 1) * qsize]
        state = jnp.dot(kwt, v_ref[h], preferred_element_type=F32)
        extra = jnp.where(lane == 0, jnp.sum(kwt.astype(F32), axis=1, keepdims=True), 0.0)
        marks = parts_of(mark_ref[0:1, h : h + 1]) + parts_of(mark_ref[1:2, h : h + 1])
        for n, x in enumerate(marks):
            extra = jnp.where(lane == 1 + n, x, extra)
        sent_ref[h * qsize : (h + 1) * qsize, :vsize] = state.astype(BF16)
        sent_ref[h * qsize : (h + 1) * qsize, vsize:] = extra.astype(BF16)


def summary(index, kwt, mark, pieces):
    own, rows, vlocal = pieces[0].shape
    vsize = vlocal * len(pieces)
    whole = lambda shape: pl.BlockSpec(shape, lambda j, s: (0,) * len(shape))
    return pl.pallas_call(
        summary_kernel,
        grid_spec=pltpu.PrefetchScalarGridSpec(
            num_scalar_prefetch=1,
            grid=(1,),
            in_specs=[whole(kwt.shape), whole(mark.shape)] + [whole(x.shape) for x in pieces],
            out_specs=[whole((kwt.shape[0], vsize + LANES)), whole((own, rows, vsize))],
        ),
        out_shape=[
            jax.ShapeDtypeStruct((kwt.shape[0], vsize + LANES), BF16),
            jax.ShapeDtypeStruct((own, rows, vsize), BF16),
        ],
        compiler_params=params(),
        cost_estimate=cost(2 * kwt.size * vsize, 3 * own * rows * vsize * 2),
    )(jnp.stack(index), kwt, mark, *pieces)


def inside_kernel(p_ref, v_ref, out_ref):
    for h in range(p_ref.shape[0]):
        out_ref[h] = jnp.dot(p_ref[h], v_ref[h], preferred_element_type=F32)


def inside(p, v):
    return pl.pallas_call(
        inside_kernel,
        out_shape=jax.ShapeDtypeStruct(v.shape, F32),
        compiler_params=params(),
        cost_estimate=cost(2 * p.size * v.shape[2], 6 * v.size),
    )(p, v)


def prefix_kernel(got_ref, out_ref):
    blocks, cut, width = got_ref.shape
    body = width - LANES
    lane = lax.broadcasted_iota(jnp.int32, (cut, LANES), 1)
    state = jnp.zeros((cut, body), F32)
    extra = jnp.zeros((cut, LANES), F32)
    ptop = jnp.full((cut, 1), NEVER, F32)
    for b in range(blocks):
        held = extra
        for n, x in enumerate(parts_of(ptop)):
            held = jnp.where(lane == 1 + n, x, held)
        out_ref[b, :, :body] = state.astype(BF16)
        out_ref[b, :, body:] = held.astype(BF16)
        if b == blocks - 1:
            break
        ext = got_ref[b, :, body:].astype(F32)
        top = ext[:, 1:2] + ext[:, 2:3] + ext[:, 3:4]
        total = ext[:, 4:5] + ext[:, 5:6] + ext[:, 6:7]
        new = jnp.maximum(ptop + total, top)
        keep = jnp.exp(ptop + total - new)
        add = jnp.exp(top - new)
        state = keep * state + add * got_ref[b, :, :body].astype(F32)
        extra = keep * extra + add * ext
        ptop = new


def prefixes(got):
    return pl.pallas_call(
        prefix_kernel,
        out_shape=jax.ShapeDtypeStruct(got.shape, BF16),
        compiler_params=params(),
        cost_estimate=cost(4 * got.size, 4 * got.size),
    )(got)


def finish_kernel(q_ref, prefix_ref, numer_ref, stat_ref, gain_ref, out_ref):
    own, rows, vsize = numer_ref.shape
    qsize = q_ref.shape[1] // own
    for h in range(own):
        inter = jnp.dot(
            q_ref[:, h * qsize : (h + 1) * qsize], prefix_ref[h], preferred_element_type=F32
        )
        ext = prefix_ref[h, 0:16, vsize:].astype(F32)[0:1]
        ptop = ext[:, 1:2] + ext[:, 2:3] + ext[:, 3:4]
        high = stat_ref[:, h : h + 1]
        top = jnp.maximum(high, ptop)
        fade = jnp.exp(high - top)
        decay = jnp.exp(ptop - top) * qsize ** (-0.5)
        denom = stat_ref[:, own + h : own + h + 1] * fade + inter[:, vsize : vsize + 1] * decay
        share = 1.0 / jnp.maximum(jnp.abs(denom), 1.0)
        hidden = numer_ref[h] * (fade * share) + inter[:, :vsize] * (decay * share)
        mean = jnp.mean(hidden, axis=1, keepdims=True)
        msq = jnp.mean(hidden * hidden, axis=1, keepdims=True)
        normed = (hidden - mean) * lax.rsqrt(msq - mean * mean + 1e-06) * gain_ref[h : h + 1]
        out_ref[:, h * vsize : (h + 1) * vsize] = normed.astype(BF16)


def finish(q, prefix, numer, stat, gain):
    own, rows, vsize = numer.shape
    return pl.pallas_call(
        finish_kernel,
        out_shape=jax.ShapeDtypeStruct((rows, own * vsize), BF16),
        compiler_params=params(),
        cost_estimate=cost(2 * q.size * vsize, 8 * numer.size),
    )(q, prefix, numer, stat, gain)


def per_device(tokens, w_query, w_key, w_value, w_gate, gate_bias, norm_gain, w_out):
    me = lax.axis_index("val")
    nval = lax.axis_size("val")
    place = lax.axis_index("seq")
    blocks = lax.axis_size("seq")
    rows, chunk = tokens.shape
    width = w_query.shape[0]
    heads, vlocal = w_value.shape[1:]
    own = heads // nval
    qsize = w_query.shape[1] // own
    vsize = vlocal * nval
    index = [(me + d) % nval for d in (0, nval - 1, 1, 2)]

    x, left, right, upper, lower = ring_gather(tokens)

    part = heads * vlocal // blocks
    wo = lax.dynamic_slice_in_dim(w_out.reshape(heads * vlocal, -1), place * part, part, axis=0)

    def exchanged(cut):
        kept = [cut((me + d) % nval) for d in range(nval)]
        return [kept[0], around(kept[1], 1), around(kept[3], -1), around(kept[2], 2)]

    def by_source(pieces):
        out = jnp.zeros((nval,) + pieces[0].shape, pieces[0].dtype)
        for i, piece in zip(index, pieces):
            out = lax.dynamic_update_index_in_dim(out, piece, i, axis=0)
        return out

    wo = by_source(
        exchanged(lambda to: lax.dynamic_slice_in_dim(wo, to * chunk, chunk, axis=1))
    )
    gain = by_source(
        exchanged(lambda to: lax.dynamic_slice_in_dim(norm_gain, to * own, own, axis=0))
    )
    gain = gain.transpose(1, 0, 2).reshape(own, vsize)
    wo = lax.all_gather(wo, "seq", axis=0)
    wo = wo.reshape(heads, blocks // heads, nval, part, chunk).transpose(0, 2, 1, 3, 4)
    wo = wo.reshape(heads * vsize, chunk)

    wv = w_value.reshape(width, heads * vlocal)
    wg = lax.dynamic_slice_in_dim(w_gate, me * own, own, axis=2).reshape(width, 2 * own)
    wg = jnp.pad(wg, ((0, 0), (0, LANES - 2 * own)))
    bias = lax.dynamic_slice_in_dim(gate_bias, me * own, own, axis=1).reshape(1, 2 * own)
    bias = jnp.pad(bias, ((0, 0), (0, LANES - 2 * own)))

    first, last = [(x,), (left,), (right,)], [(upper, lower)]

    def early(w):
        return product(first, index[:3], w, None, F32)

    v_acc, q_acc, k_acc, g_acc = early(wv), early(w_query), early(w_key), early(wg)
    v0, v1, v2, v3 = product(last, index[3:], wv, v_acc, BF16, turned=me, own=own)
    values = [v0, around(v1, 1), around(v3, -1), around(v2, 2)]
    q = product(last, index[3:], w_query, q_acc, BF16)
    k = product(last, index[3:], w_key, k_acc, BF16)
    g = product(last, index[3:], wg, g_acc, F32)
    kwt, p, stat, mark = within(q, k, g, bias, own)
    sent, v = summary(index, kwt, mark, values)
    got = lax.all_to_all(sent.reshape(blocks, -1, vsize + LANES), "seq", 0, 0)
    numer = inside(p, v)
    prefix = lax.all_to_all(prefixes(got), "seq", 0, 0)
    normed = finish(q, prefix.reshape(own, qsize, vsize + LANES), numer, stat, gain)

    x, left, right, upper, lower = ring_gather(normed)
    acc = product([(x,), (left,), (right,)], index[:3], wo, None, F32)
    return product([(upper, lower)], index[3:], wo, acc, BF16)


def solution(mesh):
    placed = (
        P("seq", "val"),
        P(None, "val"),
        P(None, "val"),
        P(None, None, "val"),
        P(),
        P(),
        P(None, "val"),
        P(None, "val", None),
    )
    return jax.shard_map(
        per_device, mesh=mesh, in_specs=placed, out_specs=P("seq", "val"), check_vma=False
    )
```

time: 404 us -> 190 us (0.47)
  between operations: 147 us -> 13.8 us
  other arithmetic: 62.5 us -> 0.23 us
  matrix products: 51.2 us -> 0 us
  Pallas kernels: 0 us -> 48 us
  blocking collectives: 9.03 us -> 24.8 us
  waiting for transfers between devices: 55.9 us -> 42 us
  local copies, waits for them, and re-layouts: 40.9 us -> 33.2 us
  starting transfers between devices: 34.6 us -> 27.1 us
    unnamed x31 -> x0, other arithmetic: 56.6 us -> none
    dot_general x25 -> x0, matrix products: 51.2 us -> none  [the longest x16 35.6 us: project(): jnp.dot(x, rows_of(w, i, chunk), preferred_element_type=F32)]
    pallas_call x0 -> x15, Pallas kernels: none -> 48 us  [the longest x10 37.7 us: product(): pl.pallas_call(functools.partial(product_kernel, [len(g) for g in groups]...]
    all_to_all x4 -> x1, waiting for transfers between devices: 36.6 us -> 4.24 us  [per_device(): prefix = lax.all_to_all(prefixes(got), 'seq', 0, 0)]
    all_to_all x0 -> x1, blocking collectives: none -> 24.8 us  [per_device(): got = lax.all_to_all(sent.reshape(blocks, -1, vsize + LANES), 'seq', 0, 0)]
    all_to_all x4 -> x1, starting transfers between devices: 24.8 us -> 3.72 us  [per_device(): prefix = lax.all_to_all(prefixes(got), 'seq', 0, 0)]
    ppermute x6 -> x17, waiting for transfers between devices: 19.2 us -> 37.8 us  [around(): return lax.ppermute(x, 'val', [(i, (i + distance) % n) for i in range(n)])]
    ppermute x6 -> x17, starting transfers between devices: 9.72 us -> 23.4 us  [around(): return lax.ppermute(x, 'val', [(i, (i + distance) % n) for i in range(n)])]
  transfers between devices with their start and end apart: 11 -> 19, of which waited for: 5 -> 5; matrix products, arithmetic and copies ran while one was open for 37% -> 14% of each run, Pallas kernels for 0% -> 23%
where the time goes in v2:
time: 190 us; the launch traced here: 189 us
  Pallas kernels  48 us (25%)
  waiting for transfers between devices  42 us (22%)
  local copies, waits for them, and re-layouts  33.2 us (17%)
  starting transfers between devices  27.1 us (14%)
  blocking collectives  24.8 us (13%)
  between operations  13.8 us (7%)
    ppermute x17, waiting for transfers between devices, around(): return lax.ppermute(x, 'val', [(i, (i + distance) % n) for i in range(n)])  37.8 us
    pallas_call x10, Pallas kernels, product(): pl.pallas_call(functools.partial(product_kernel, [len(g) for g in groups]...  37.7 us
    all_to_all x1, blocking collectives, per_device(): got = lax.all_to_all(sent.reshape(blocks, -1, vsize + LANES), 'seq', 0, 0)  24.8 us
    ppermute x17, starting transfers between devices, around(): return lax.ppermute(x, 'val', [(i, (i + distance) % n) for i in range(n)])  23.4 us
    unnamed x42, local copies, waits for them, and re-layouts  15.2 us
    transpose x1, local copies, waits for them, and re-layouts, per_device(): wo.reshape(heads, blocks // heads, nval, part, chunk)  8.5 us
    pallas_call x1, Pallas kernels, prefixes(): pl.pallas_call(prefix_kernel, out_shape=jax.ShapeDtypeStruct(got.shape, B...  4.45 us
    all_to_all x1, waiting for transfers between devices, per_device(): prefix = lax.all_to_all(prefixes(got), 'seq', 0, 0)  4.24 us
  transfers between devices with their start and end apart: 19, of which 5 were waited for; matrix products, arithmetic and copies ran while one was open for 14% of the time, Pallas kernels for 23%

profile of v2, /device:TPU:1, one launch (start us, length us, event | category | flops | bytes accessed | tf_op | source)
XLA Modules:
  0.0 189.2 jit_solution(12534679546698551715)
XLA Ops:
  6.5 1.1 fusion
  7.7 2.2 %collective-permute-start.14 = (bf16[32,1024]{1,0:T(8,128)(2,1)S(1)}, bf16[32,1024]{1,0:T(8,128)(2,1)S(1)}, u32[]{:S(2)}, u32[]{:S(2)}) collective-permute-start(bf16[32,1024]{1,0:T(8,128)(2,1)S(1)} %get-tuple-element.29), channel_id=1, source_target_pairs={{0,1},{1,2},{2,3},{3,0},{4,5},{5,6},{6,7},{7,4},{8,9},{9,10},{10,1... | collective-permute-start | bytes 196616 | tf_op jit(solution)/shard_map/ppermute | solution.py:19
  9.9 1.5 collective-permute-start.15
  11.4 1.6 collective-permute-start.16
  13.0 1.0 bitcast_dynamic-update-slice_fusion.3
  14.1 2.0 %collective-permute-done.16 = bf16[32,1024]{1,0:T(8,128)(2,1)S(1)} collective-permute-done((bf16[32,1024]{1,0:T(8,128)(2,1)S(1)}, bf16[32,1024]{1,0:T(8,128)(2,1)S(1)}, u32[]{:S(2)}, u32[]{:S(2)}) %collective-permute-start.16) | collective-permute-done | bytes 65568 | tf_op jit(solution)/shard_map/ppermute | solution.py:19
  17.1 2.4 %collective-permute-start.2 = (bf16[384,1024]{1,0:T(8,128)(2,1)}, bf16[384,1024]{1,0:T(8,128)(2,1)S(1)}, u32[]{:S(2)}, u32[]{:S(2)}) collective-permute-start(bf16[384,1024]{1,0:T(8,128)(2,1)} %refs_0_.7), channel_id=1, source_target_pairs={{0,3},{1,0},{2,1},{3,2},{4,7},{5,4},{6,5},{7,6},{8,11},{9,8},{10,9... | collective-permute-start | bytes 2359304 | tf_op jit(solution)/shard_map/ppermute | solution.py:19
  19.8 15.4 %collective-permute-done.refs_1_ = bf16[384,1024]{1,0:T(8,128)(2,1)S(1)} collective-permute-done((bf16[384,1024]{1,0:T(8,128)(2,1)}, bf16[384,1024]{1,0:T(8,128)(2,1)S(1)}, u32[]{:S(2)}, u32[]{:S(2)}) %collective-permute-start) | collective-permute-done | bytes 786464 | tf_op jit(solution)/shard_map/ppermute | solution.py:19
  35.3 0.8 slice.16
  36.0 0.8 slice.17
  36.9 2.7 %collective-permute-start.3 = (bf16[192,1024]{1,0:T(8,128)(2,1)}, bf16[192,1024]{1,0:T(8,128)(2,1)}, u32[]{:S(2)}, u32[]{:S(2)}) collective-permute-start(bf16[192,1024]{1,0:T(8,128)(2,1)} %slice.17), channel_id=1, source_target_pairs={{0,3},{1,0},{2,1},{3,2},{4,7},{5,4},{6,5},{7,6},{8,11},{9,8},{10,9... | collective-permute-start | bytes 1179656 | tf_op jit(solution)/shard_map/ppermute | solution.py:19
  39.5 0.7 constant_dynamic-slice_fusion.4
  40.3 8.8 %copy.27 = bf16[512,8,8,128]{3,1,2,0:T(8,128)(2,1)} copy(bf16[512,8,8,128]{3,2,1,0:T(8,128)(2,1)} %bitcast.52) | data formatting | bytes 16777216
  49.1 1.4 copy.18
  50.5 1.7 pad.8.refs_3_.refs_4_.refs_5_.refs_2_
  52.3 1.1 copy-done.6
  53.5 1.3 shard_map.86.refs_3_
  54.8 3.7 %shard_map.84.refs_3_ = f32[384,512]{1,0:T(8,128)S(1)} custom-call(s32[4]{0:T(128)S(1)} %pad_add_fusion.1.scalars, bf16[384,1024]{1,0:T(8,128)(2,1)S(1)} %copy-done.6, bf16[384,1024]{1,0:T(8,128)(2,1)S(1)} %collective-permute-done.refs_1_, bf16[384,1024]{1,0:T(8,128)(2,1)S(1)} %collective-permute-done.2.refs_2_, bf16[4096,512]{1,0:T(8,128)(2,1)} %refs_2_.3, ...), custom_call_target="tpu_custom_call" | custom-call | flops 1207959552 | bytes 6291456 | tf_op jit(solution)/shard_map/pallas_call | solution.py:96
  58.5 6.1 %shard_map.89.refs_3_ = f32[384,1024]{1,0:T(8,128)S(1)} custom-call(s32[4]{0:T(128)S(1)} %pad_add_fusion.1.scalars, bf16[384,1024]{1,0:T(8,128)(2,1)S(1)} %copy-done.6, bf16[384,1024]{1,0:T(8,128)(2,1)S(1)} %collective-permute-done.refs_1_, bf16[384,1024]{1,0:T(8,128)(2,1)S(1)} %collective-permute-done.2.refs_2_, bf16[4096,1024]{1,0:T(8,128)(2,1)} %bitcast.44, ...), custom_call_target="tpu_custom_call" | custom-call | flops 2415919104 | bytes 10223616 | tf_op jit(solution)/shard_map/pallas_call | solution.py:96
  64.7 5.0 %shard_map.90 = (bf16[2,384,128]{2,1,0:T(8,128)(2,1)S(1)}, bf16[2,384,128]{2,1,0:T(8,128)(2,1)}, bf16[2,384,128]{2,1,0:T(8,128)(2,1)}, bf16[2,384,128]{2,1,0:T(8,128)(2,1)}) custom-call(s32[2]{0:T(128)S(1)} %get-tuple-element.35.scalars, bf16[192,1024]{1,0:T(8,128)(2,1)S(1)} %collective-permute-done.1.refs_0_, ...), custom_call_target="tpu_custom_call" | custom-call | flops 805306368 | bytes 4456448 | tf_op jit(solution)/shard_map/pallas_call | solution.py:96
  69.7 2.7 %collective-permute-start.5 = (bf16[2,384,128]{2,1,0:T(8,128)(2,1)}, bf16[2,384,128]{2,1,0:T(8,128)(2,1)S(1)}, u32[]{:S(2)}, u32[]{:S(2)}) collective-permute-start(bf16[2,384,128]{2,1,0:T(8,128)(2,1)} %get-tuple-element.19), channel_id=1, source_target_pairs={{0,3},{1,0},{2,1},{3,2},{4,7},{5,4},{6,5},{7,6},{8,11},{9,8},{10,9... | collective-permute-start | bytes 589832 | tf_op jit(solution)/shard_map/ppermute | solution.py:19
  72.7 4.1 %shard_map.82.refs_3_ = f32[384,512]{1,0:T(8,128)S(1)} custom-call(s32[4]{0:T(128)S(1)} %pad_add_fusion.1.scalars, bf16[384,1024]{1,0:T(8,128)(2,1)S(1)} %copy-done.7, bf16[384,1024]{1,0:T(8,128)(2,1)S(1)} %collective-permute-done.refs_1_, bf16[384,1024]{1,0:T(8,128)(2,1)S(1)} %copy-done.5, bf16[4096,512]{1,0:T(8,128)(2,1)} %refs_2_.2, ...), custom_call_target="tpu_custom_call" | custom-call | flops 1207959552 | bytes 6291456 | tf_op jit(solution)/shard_map/pallas_call | solution.py:96
  76.8 1.9 %shard_map.87.g_ref = f32[384,128]{1,0:T(8,128)S(1)} custom-call(s32[2]{0:T(128)S(1)} %get-tuple-element.34.scalars, bf16[192,1024]{1,0:T(8,128)(2,1)S(1)} %copy-done.9, bf16[192,1024]{1,0:T(8,128)(2,1)} %collective-permute-done.3.refs_1_, bf16[4096,128]{1,0:T(8,128)(2,1)S(1)} %pad.8.refs_3_.refs_4_.refs_5_.refs_2_, f32[384,128]{1,0:T(8,128)S(1)} %shard_map.86.refs_3_), custom_call_target="tpu_custom_call" | custom-call | flops 100663296 | bytes 1245184 | tf_op jit(solution)/shard_map/pallas_call | solution.py:96
  78.8 2.4 %shard_map.85.k_ref = bf16[384,512]{1,0:T(8,128)(2,1)S(1)} custom-call(s32[2]{0:T(128)S(1)} %get-tuple-element.34.scalars, bf16[192,1024]{1,0:T(8,128)(2,1)S(1)} %copy-done.9, bf16[192,1024]{1,0:T(8,128)(2,1)} %collective-permute-done.3.refs_1_, bf16[4096,512]{1,0:T(8,128)(2,1)S(1)} %copy-done.2, f32[384,512]{1,0:T(8,128)S(1)} %copy-done.11), custom_call_target="tpu_custom_call" | custom-call | flops 402653184 | bytes 2621440 | tf_op jit(solution)/shard_map/pallas_call | solution.py:96
  81.2 2.4 %shard_map.83.q_ref = bf16[384,512]{1,0:T(8,128)(2,1)S(1)} custom-call(s32[2]{0:T(128)S(1)} %get-tuple-element.34.scalars, bf16[192,1024]{1,0:T(8,128)(2,1)S(1)} %copy-done.9, bf16[192,1024]{1,0:T(8,128)(2,1)} %collective-permute-done.3.refs_1_, bf16[4096,512]{1,0:T(8,128)(2,1)S(1)} %copy-done.3, f32[384,512]{1,0:T(8,128)S(1)} %shard_map.82.refs_3_), custom_call_target="tpu_custom_call" | custom-call | flops 402653184 | bytes 2621440 | tf_op jit(solution)/shard_map/pallas_call | solution.py:96
  83.6 1.7 shard_map.88
  85.4 0.8 copy-done.12
  86.2 0.7 copy-done.16
  86.9 0.9 copy-done.17
  87.9 2.1 %shard_map.91 = (bf16[512,640]{1,0:T(8,128)(2,1)S(1)}, bf16[2,384,512]{2,1,0:T(8,128)(2,1)S(1)}) custom-call(s32[4]{0:T(128)S(1)} %get-tuple-element.25.scalars, bf16[512,384]{1,0:T(8,128)(2,1)S(1)} %get-tuple-element.15.kwt_ref, f32[8,128]{1,0:T(8,128)S(1)} %get-tuple-element.16.mark_ref, bf16[2,384,128]{2,1,0:T(8,128)(2,1)S(1)} %get-tuple-element.17.v0, ...), custom_call_target="tpu_custom_call" | custom-call | flops 201326592 | bytes 2359296 | tf_op jit(solution)/shard_map/pallas_call | solution.py:188
  89.9 24.8 %all_to_all.10.got_ref = bf16[32,16,640]{2,1,0:T(8,128)(2,1)S(1)} all-to-all(bf16[32,16,640]{2,1,0:T(8,128)(2,1)S(1)} %bitcast.42), channel_id=1, replica_groups=mesh['seq'=32,'val'=4] {'seq'}, dimensions={0} | all-to-all | bytes 1310720 | tf_op jit(solution)/shard_map/all_to_all | solution.py:344
  114.7 4.5 %shard_map.92 = bf16[32,16,640]{2,1,0:T(8,128)(2,1)} custom-call(bf16[32,16,640]{2,1,0:T(8,128)(2,1)S(1)} %all_to_all.10.got_ref), custom_call_target="tpu_custom_call" | custom-call | flops 1310720 | bytes 1310720 | tf_op jit(solution)/shard_map/pallas_call | solution.py:246
  119.2 3.7 %all-to-all-start.1 = ((bf16[32,16,640]{2,1,0:T(8,128)(2,1)}), bf16[32,16,640]{2,1,0:T(8,128)(2,1)S(1)}, u32[]{:S(2)}, u32[]{:S(2)}) async-start(bf16[32,16,640]{2,1,0:T(8,128)(2,1)} %shard_map.92), calls=%async_computation.1 | async-start | bytes 1310720 | tf_op jit(solution)/shard_map/all_to_all | solution.py:346
  123.2 2.5 %collective-permute-start.8 = (f32[2,128]{1,0:T(2,128)S(1)}, f32[2,128]{1,0:T(2,128)S(1)}, u32[]{:S(2)}, u32[]{:S(2)}) collective-permute-start(f32[2,128]{1,0:T(2,128)S(1)} %get-tuple-element.33), channel_id=1, source_target_pairs={{0,3},{1,0},{2,1},{3,2},{4,7},{5,4},{6,5},{7,6},{8,11},{9,8},{10,9... | collective-permute-start | bytes 3080 | tf_op jit(solution)/shard_map/ppermute | solution.py:19
  125.7 1.6 collective-permute-start.9
  127.4 2.5 %collective-permute-done.9 = f32[2,128]{1,0:T(2,128)S(1)} collective-permute-done((f32[2,128]{1,0:T(2,128)S(1)}, f32[2,128]{1,0:T(2,128)S(1)}, u32[]{:S(2)}, u32[]{:S(2)}) %collective-permute-start.9) | collective-permute-done | bytes 1056 | tf_op jit(solution)/shard_map/ppermute | solution.py:19
  130.0 1.1 copy-done.13
  131.6 4.2 %all-to-all-done.1 = bf16[32,16,640]{2,1,0:T(8,128)(2,1)S(1)} async-done(((bf16[32,16,640]{2,1,0:T(8,128)(2,1)}), bf16[32,16,640]{2,1,0:T(8,128)(2,1)S(1)}, u32[]{:S(2)}, u32[]{:S(2)}) %all-to-all-start.1) | async-done | bytes 655392 | tf_op jit(solution)/shard_map/all_to_all | solution.py:346
  135.9 0.9 copy-done.15
  136.8 1.5 shard_map.94.refs_0_
  138.5 2.6 %collective-permute-start.12 = (bf16[384,1024]{1,0:T(8,128)(2,1)S(1)}, bf16[384,1024]{1,0:T(8,128)(2,1)S(1)}, u32[]{:S(2)}, u32[]{:S(2)}) collective-permute-start(bf16[384,1024]{1,0:T(8,128)(2,1)S(1)} %shard_map.94.refs_0_), channel_id=1, source_target_pairs={{0,3},{1,0},{2,1},{3,2},{4,7},{5,4},{6,5},{7,6},{8,11},{9,8},{10,9... | collective-permute-start | bytes 2359304 | tf_op jit(solution)/shard_map/ppermute | solution.py:19
  141.1 17.8 %collective-permute-done.10.refs_1_ = bf16[384,1024]{1,0:T(8,128)(2,1)S(1)} collective-permute-done((bf16[384,1024]{1,0:T(8,128)(2,1)S(1)}, bf16[384,1024]{1,0:T(8,128)(2,1)S(1)}, u32[]{:S(2)}, u32[]{:S(2)}) %collective-permute-start.10) | collective-permute-done | bytes 786464 | tf_op jit(solution)/shard_map/ppermute | solution.py:19
  158.9 0.8 slice.18
  159.6 0.8 slice.19
  160.4 2.7 %collective-permute-start.13 = (bf16[192,1024]{1,0:T(8,128)(2,1)}, bf16[192,1024]{1,0:T(8,128)(2,1)S(1)}, u32[]{:S(2)}, u32[]{:S(2)}) collective-permute-start(bf16[192,1024]{1,0:T(8,128)(2,1)} %slice.19), channel_id=1, source_target_pairs={{0,3},{1,0},{2,1},{3,2},{4,7},{5,4},{6,5},{7,6},{8,11},{9,8},{10,9... | collective-permute-start | bytes 1179656 | tf_op jit(solution)/shard_map/ppermute | solution.py:19
  163.1 8.5 %copy.22 = bf16[8,4,4,32,1024]{4,3,2,1,0:T(8,128)(2,1)} copy(bf16[8,4,4,32,1024]{4,3,1,2,0:T(8,128)(2,1)} %bitcast.53) | data formatting | bytes 16777216 | tf_op jit(solution)/shard_map/transpose | solution.py:322
  171.6 5.9 %shard_map.95.refs_3_ = f32[384,1024]{1,0:T(8,128)S(1)} custom-call(s32[4]{0:T(128)S(1)} %pad_add_fusion.1.scalars, bf16[384,1024]{1,0:T(8,128)(2,1)S(1)} %shard_map.94.refs_0_, bf16[384,1024]{1,0:T(8,128)(2,1)S(1)} %collective-permute-done.10.refs_1_, bf16[384,1024]{1,0:T(8,128)(2,1)S(1)} %collective-permute-done.12.refs_2_, bf16[4096,1024]{1,0:T(8,128)(2,1)} %bitcast.48, ...), custom_call_target="tpu_custom_call" | custom-call | flops 2415919104 | bytes 10223616 | tf_op jit(solution)/shard_map/pallas_call | solution.py:96
  177.5 4.8 %shard_map.96 = bf16[384,1024]{1,0:T(8,128)(2,1)} custom-call(s32[2]{0:T(128)S(1)} %get-tuple-element.34.scalars, bf16[192,1024]{1,0:T(8,128)(2,1)S(1)} %collective-permute-done.11.refs_0_, bf16[192,1024]{1,0:T(8,128)(2,1)S(1)} %collective-permute-done.13.refs_1_, bf16[4096,1024]{1,0:T(8,128)(2,1)} %bitcast.51, f32[384,1024]{1,0:T(8,128)S(1)} %shard_map.95.refs_3_), custom_call_target="tpu_custom_call" | custom-call | flops 805306368 | bytes 4456448 | tf_op jit(solution)/shard_map/pallas_call | solution.py:96
  (76 shorter events, 3.0 us)
Async XLA Ops:
  6.5 13.2 %copy-start = (bf16[4096,2,8]{0,2,1:T(8,128)(2,1)S(1)}, bf16[4096,2,8]{0,2,1:T(8,128)(2,1)}, u32[]{:S(2)}) copy-start(bf16[4096,2,8]{0,2,1:T(8,128)(2,1)} %param.12) | copy-start | bytes 393220
  6.5 156.6 %all-gather.2.cloned.1.call-start = ((), (), s32[]{:S(2)}) async-start(), calls=%async_computation.2 | async-start | bytes 8650752 | tf_op jit(solution)/shard_map/all_gather | solution.py:321
  7.7 6.3 %collective-permute-start.14 = (bf16[32,1024]{1,0:T(8,128)(2,1)S(1)}, bf16[32,1024]{1,0:T(8,128)(2,1)S(1)}, u32[]{:S(2)}, u32[]{:S(2)}) collective-permute-start(bf16[32,1024]{1,0:T(8,128)(2,1)S(1)} %get-tuple-element.29), channel_id=1, source_target_pairs={{0,1},{1,2},{2,3},{3,0},{4,5},{5,6},{6,7},{7,4},{8,9},{9,10},{10,1... | collective-permute-start | bytes 196616 | tf_op jit(solution)/shard_map/ppermute | solution.py:19
  9.9 4.1 %collective-permute-start.15 = (bf16[32,1024]{1,0:T(8,128)(2,1)S(1)}, bf16[32,1024]{1,0:T(8,128)(2,1)S(1)}, u32[]{:S(2)}, u32[]{:S(2)}) collective-permute-start(bf16[32,1024]{1,0:T(8,128)(2,1)S(1)} %get-tuple-element.28), channel_id=1, source_target_pairs={{0,3},{1,0},{2,1},{3,2},{4,7},{5,4},{6,5},{7,6},{8,11},{9,8},{10,9... | collective-permute-start | bytes 196616 | tf_op jit(solution)/shard_map/ppermute | solution.py:19
  11.4 4.6 %collective-permute-start.16 = (bf16[32,1024]{1,0:T(8,128)(2,1)S(1)}, bf16[32,1024]{1,0:T(8,128)(2,1)S(1)}, u32[]{:S(2)}, u32[]{:S(2)}) collective-permute-start(bf16[32,1024]{1,0:T(8,128)(2,1)S(1)} %get-tuple-element.27), channel_id=1, source_target_pairs={{0,2},{1,3},{2,0},{3,1},{4,6},{5,7},{6,4},{7,5},{8,10},{9,11},{10,... | collective-permute-start | bytes 196616 | tf_op jit(solution)/shard_map/ppermute | solution.py:19
  16.0 0.7 copy-start.18
  16.8 18.5 %collective-permute-start = (bf16[384,1024]{1,0:T(8,128)(2,1)}, bf16[384,1024]{1,0:T(8,128)(2,1)S(1)}, u32[]{:S(2)}, u32[]{:S(2)}) collective-permute-start(bf16[384,1024]{1,0:T(8,128)(2,1)} %refs_0_.7), channel_id=1, source_target_pairs={{0,1},{1,2},{2,3},{3,0},{4,5},{5,6},{6,7},{7,4},{8,9},{9,10},{10,1... | collective-permute-start | bytes 2359304 | tf_op jit(solution)/shard_map/ppermute | solution.py:19
  17.1 18.9 %collective-permute-start.2 = (bf16[384,1024]{1,0:T(8,128)(2,1)}, bf16[384,1024]{1,0:T(8,128)(2,1)S(1)}, u32[]{:S(2)}, u32[]{:S(2)}) collective-permute-start(bf16[384,1024]{1,0:T(8,128)(2,1)} %refs_0_.7), channel_id=1, source_target_pairs={{0,3},{1,0},{2,1},{3,2},{4,7},{5,4},{6,5},{7,6},{8,11},{9,8},{10,9... | collective-permute-start | bytes 2359304 | tf_op jit(solution)/shard_map/ppermute | solution.py:19
  36.0 28.6 %collective-permute-start.1 = (bf16[192,1024]{1,0:T(8,128)(2,1)}, bf16[192,1024]{1,0:T(8,128)(2,1)S(1)}, u32[]{:S(2)}, u32[]{:S(2)}) collective-permute-start(bf16[192,1024]{1,0:T(8,128)(2,1)} %slice.16), channel_id=1, source_target_pairs={{0,1},{1,2},{2,3},{3,0},{4,5},{5,6},{6,7},{7,4},{8,9},{9,10},{10,1... | collective-permute-start | bytes 1179656 | tf_op jit(solution)/shard_map/ppermute | solution.py:19
  36.0 22.5 %copy-start.4 = (bf16[384,1024]{1,0:T(8,128)(2,1)}, bf16[384,1024]{1,0:T(8,128)(2,1)S(1)}, u32[]{:S(2)}) copy-start(bf16[384,1024]{1,0:T(8,128)(2,1)S(1)} %collective-permute-done.2.refs_2_) | copy-start | bytes 2359300
  36.9 27.8 %collective-permute-start.3 = (bf16[192,1024]{1,0:T(8,128)(2,1)}, bf16[192,1024]{1,0:T(8,128)(2,1)}, u32[]{:S(2)}, u32[]{:S(2)}) collective-permute-start(bf16[192,1024]{1,0:T(8,128)(2,1)} %slice.17), channel_id=1, source_target_pairs={{0,3},{1,0},{2,1},{3,2},{4,7},{5,4},{6,5},{7,6},{8,11},{9,8},{10,9... | collective-permute-start | bytes 1179656 | tf_op jit(solution)/shard_map/ppermute | solution.py:19
  52.3 1.1 copy-start.6
  58.5 6.1 %copy-start.10 = (f32[384,512]{1,0:T(8,128)}, f32[384,512]{1,0:T(8,128)S(1)}, u32[]{:S(2)}) copy-start(f32[384,512]{1,0:T(8,128)S(1)} %shard_map.84.refs_3_) | copy-start | bytes 2359300
  64.6 8.0 %copy-start.5 = (bf16[384,1024]{1,0:T(8,128)(2,1)S(1)}, bf16[384,1024]{1,0:T(8,128)(2,1)}, u32[]{:S(2)}) copy-start(bf16[384,1024]{1,0:T(8,128)(2,1)} %copy-done.4) | copy-start | bytes 2359300
  64.6 8.0 %copy-start.7 = (bf16[384,1024]{1,0:T(8,128)(2,1)S(1)}, bf16[384,1024]{1,0:T(8,128)(2,1)}, u32[]{:S(2)}) copy-start(bf16[384,1024]{1,0:T(8,128)(2,1)} %refs_0_.7) | copy-start | bytes 2359300
  64.7 7.7 %copy-start.8 = (bf16[192,1024]{1,0:T(8,128)(2,1)}, bf16[192,1024]{1,0:T(8,128)(2,1)S(1)}, u32[]{:S(2)}) copy-start(bf16[192,1024]{1,0:T(8,128)(2,1)S(1)} %collective-permute-done.1.refs_0_) | copy-start | bytes 1179652
  69.7 16.5 %collective-permute-start.4 = (bf16[2,384,128]{2,1,0:T(8,128)(2,1)}, bf16[2,384,128]{2,1,0:T(8,128)(2,1)S(1)}, u32[]{:S(2)}, u32[]{:S(2)}) collective-permute-start(bf16[2,384,128]{2,1,0:T(8,128)(2,1)} %get-tuple-element.18), channel_id=1, source_target_pairs={{0,1},{1,2},{2,3},{3,0},{4,5},{5,6},{6,7},{7,4},{8,9},{9,10},{10,1... | collective-permute-start | bytes 589832 | tf_op jit(solution)/shard_map/ppermute | solution.py:19
  69.7 16.5 %collective-permute-start.5 = (bf16[2,384,128]{2,1,0:T(8,128)(2,1)}, bf16[2,384,128]{2,1,0:T(8,128)(2,1)S(1)}, u32[]{:S(2)}, u32[]{:S(2)}) collective-permute-start(bf16[2,384,128]{2,1,0:T(8,128)(2,1)} %get-tuple-element.19), channel_id=1, source_target_pairs={{0,3},{1,0},{2,1},{3,2},{4,7},{5,4},{6,5},{7,6},{8,11},{9,8},{10,9... | collective-permute-start | bytes 589832 | tf_op jit(solution)/shard_map/ppermute | solution.py:19
  72.4 4.5 %copy-start.9 = (bf16[192,1024]{1,0:T(8,128)(2,1)S(1)}, bf16[192,1024]{1,0:T(8,128)(2,1)}, u32[]{:S(2)}) copy-start(bf16[192,1024]{1,0:T(8,128)(2,1)} %copy-done.8) | copy-start | bytes 1179652
  72.4 6.4 %copy-start.2 = (bf16[4096,512]{1,0:T(8,128)(2,1)S(1)}, bf16[4096,512]{1,0:T(8,128)(2,1)}, u32[]{:S(2)}) copy-start(bf16[4096,512]{1,0:T(8,128)(2,1)} %refs_2_.3) | copy-start | bytes 12582916
  72.4 6.4 %copy-start.11 = (f32[384,512]{1,0:T(8,128)S(1)}, f32[384,512]{1,0:T(8,128)}, u32[]{:S(2)}) copy-start(f32[384,512]{1,0:T(8,128)} %copy-done.10) | copy-start | bytes 2359300
  72.4 8.8 %copy-start.3 = (bf16[4096,512]{1,0:T(8,128)(2,1)S(1)}, bf16[4096,512]{1,0:T(8,128)(2,1)}, u32[]{:S(2)}) copy-start(bf16[4096,512]{1,0:T(8,128)(2,1)} %refs_2_.2) | copy-start | bytes 12582916
  72.4 14.6 %collective-permute-start.6 = (bf16[2,384,128]{2,1,0:T(8,128)(2,1)}, bf16[2,384,128]{2,1,0:T(8,128)(2,1)}, u32[]{:S(2)}, u32[]{:S(2)}) collective-permute-start(bf16[2,384,128]{2,1,0:T(8,128)(2,1)} %get-tuple-element.20), channel_id=1, source_target_pairs={{0,2},{1,3},{2,0},{3,1},{4,6},{5,7},{6,4},{7,5},{8,10},{9,11},{10,... | collective-permute-start | bytes 589832 | tf_op jit(solution)/shard_map/ppermute | solution.py:19
  78.8 44.2 %copy-start.19 = (f32[8,128]{1,0:T(8,128)S(1)}, f32[8,128]{1,0:T(8,128)}, u32[]{:S(2)}) copy-start(f32[8,128]{1,0:T(8,128)} %param.14) | copy-start | bytes 12292
  85.4 0.9 copy-start.12
  86.2 28.5 %copy-start.14 = (f32[384,128]{1,0:T(8,128)}, f32[384,128]{1,0:T(8,128)S(1)}, u32[]{:S(2)}) copy-start(f32[384,128]{1,0:T(8,128)S(1)} %get-tuple-element.24.stat_ref) | copy-start | bytes 589828
  86.2 0.7 copy-start.16
  86.9 0.9 copy-start.17
  119.2 16.7 %all-to-all-start.1 = ((bf16[32,16,640]{2,1,0:T(8,128)(2,1)}), bf16[32,16,640]{2,1,0:T(8,128)(2,1)S(1)}, u32[]{:S(2)}, u32[]{:S(2)}) async-start(bf16[32,16,640]{2,1,0:T(8,128)(2,1)} %shard_map.92), calls=%async_computation.1 | async-start | bytes 1310720 | tf_op jit(solution)/shard_map/all_to_all | solution.py:346
  123.0 4.4 %collective-permute-start.7 = (f32[2,128]{1,0:T(2,128)S(1)}, f32[2,128]{1,0:T(2,128)S(1)}, u32[]{:S(2)}, u32[]{:S(2)}) collective-permute-start(f32[2,128]{1,0:T(2,128)S(1)} %get-tuple-element.31), channel_id=1, source_target_pairs={{0,1},{1,2},{2,3},{3,0},{4,5},{5,6},{6,7},{7,4},{8,9},{9,10},{10,1... | collective-permute-start | bytes 3080 | tf_op jit(solution)/shard_map/ppermute | solution.py:19
  123.2 4.2 %collective-permute-start.8 = (f32[2,128]{1,0:T(2,128)S(1)}, f32[2,128]{1,0:T(2,128)S(1)}, u32[]{:S(2)}, u32[]{:S(2)}) collective-permute-start(f32[2,128]{1,0:T(2,128)S(1)} %get-tuple-element.33), channel_id=1, source_target_pairs={{0,3},{1,0},{2,1},{3,2},{4,7},{5,4},{6,5},{7,6},{8,11},{9,8},{10,9... | collective-permute-start | bytes 3080 | tf_op jit(solution)/shard_map/ppermute | solution.py:19
  125.7 4.2 %collective-permute-start.9 = (f32[2,128]{1,0:T(2,128)S(1)}, f32[2,128]{1,0:T(2,128)S(1)}, u32[]{:S(2)}, u32[]{:S(2)}) collective-permute-start(f32[2,128]{1,0:T(2,128)S(1)} %get-tuple-element.30), channel_id=1, source_target_pairs={{0,2},{1,3},{2,0},{3,1},{4,6},{5,7},{6,4},{7,5},{8,10},{9,11},{10,... | collective-permute-start | bytes 3080 | tf_op jit(solution)/shard_map/ppermute | solution.py:19
  130.0 1.1 copy-start.13
  135.9 0.9 copy-start.15
  138.3 20.6 %collective-permute-start.10 = (bf16[384,1024]{1,0:T(8,128)(2,1)S(1)}, bf16[384,1024]{1,0:T(8,128)(2,1)S(1)}, u32[]{:S(2)}, u32[]{:S(2)}) collective-permute-start(bf16[384,1024]{1,0:T(8,128)(2,1)S(1)} %shard_map.94.refs_0_), channel_id=1, source_target_pairs={{0,1},{1,2},{2,3},{3,0},{4,5},{5,6},{6,7},{7,4},{8,9},{9,10},{10,1... | collective-permute-start | bytes 2359304 | tf_op jit(solution)/shard_map/ppermute | solution.py:19
  138.5 21.1 %collective-permute-start.12 = (bf16[384,1024]{1,0:T(8,128)(2,1)S(1)}, bf16[384,1024]{1,0:T(8,128)(2,1)S(1)}, u32[]{:S(2)}, u32[]{:S(2)}) collective-permute-start(bf16[384,1024]{1,0:T(8,128)(2,1)S(1)} %shard_map.94.refs_0_), channel_id=1, source_target_pairs={{0,3},{1,0},{2,1},{3,2},{4,7},{5,4},{6,5},{7,6},{8,11},{9,8},{10,9... | collective-permute-start | bytes 2359304 | tf_op jit(solution)/shard_map/ppermute | solution.py:19
  159.6 17.9 %collective-permute-start.11 = (bf16[192,1024]{1,0:T(8,128)(2,1)}, bf16[192,1024]{1,0:T(8,128)(2,1)S(1)}, u32[]{:S(2)}, u32[]{:S(2)}) collective-permute-start(bf16[192,1024]{1,0:T(8,128)(2,1)} %slice.18), channel_id=1, source_target_pairs={{0,1},{1,2},{2,3},{3,0},{4,5},{5,6},{6,7},{7,4},{8,9},{9,10},{10,1... | collective-permute-start | bytes 1179656 | tf_op jit(solution)/shard_map/ppermute | solution.py:19
  160.4 17.1 %collective-permute-start.13 = (bf16[192,1024]{1,0:T(8,128)(2,1)}, bf16[192,1024]{1,0:T(8,128)(2,1)S(1)}, u32[]{:S(2)}, u32[]{:S(2)}) collective-permute-start(bf16[192,1024]{1,0:T(8,128)(2,1)} %slice.19), channel_id=1, source_target_pairs={{0,3},{1,0},{2,1},{3,2},{4,7},{5,4},{6,5},{7,6},{8,11},{9,8},{10,9... | collective-permute-start | bytes 1179656 | tf_op jit(solution)/shard_map/ppermute | solution.py:19
  171.6 10.7 %copy-start.1 = (bf16[4096,2,8]{0,2,1:T(8,128)(2,1)S(1)}, bf16[4096,2,8]{0,2,1:T(8,128)(2,1)}, u32[]{:S(2)}) copy-start(bf16[4096,2,8]{0,2,1:T(8,128)(2,1)} %param.12) | copy-start | bytes 393220
Sparse Core Ops, SparseCore 0:
  16.9 56.1 all-gather.1

commit v3 on v2

v3 whole, which is shorter than its diff:
```python
import functools

import jax
import jax.numpy as jnp
from jax import lax
from jax.experimental import pallas as pl
from jax.experimental.pallas import tpu as pltpu
from jax.sharding import PartitionSpec as P

F32 = jnp.float32
BF16 = jnp.bfloat16
LANES = 128
NEVER = -1e30
BLOCK = 512
AHEAD = 3


def around(x, distance):
    n = lax.axis_size("val")
    return lax.ppermute(x, "val", [(i, (i + distance) % n) for i in range(n)])


def params(mib=48):
    return pltpu.CompilerParams(vmem_limit_bytes=mib * 1024 * 1024)


def cost(flops, nbytes, exps=0):
    return pl.CostEstimate(flops=flops, bytes_accessed=nbytes, transcendentals=exps)


class Ring:
    def __init__(self, plus, minus, later, keep):
        self.plus, self.minus = around(plus, 1), around(minus, -1)
        self.later, self.keep = later, keep

    def second(self, after):
        plus, minus = moved(self.later, [[(1, 0, 0)], [(0, 0, 0)]], after)
        self.sent = plus
        self.left = (self.plus, around(plus, 1))
        self.right = (around(minus, -1), self.minus)

    def forward(self):
        half = self.later[0].shape[0]
        cuts = [(0, half), (self.plus.shape[0] - self.keep, self.keep)]
        plus, minus = moved(
            [self.plus, self.minus], [[(n, *cut) for cut in cuts if cut[1]] for n in (0, 1)], [self.sent]
        )
        self.opposite = (around(plus, 1), around(minus, -1))


def moved_kernel(n, n_after, plan, *refs):
    sources, outs = refs[:n], refs[n + n_after :]
    for out, parts in zip(outs, plan):
        at = 0
        for source, first, count in parts:
            count = count or sources[source].shape[0] - first
            out[at : at + count] = sources[source][first : first + count]
            at += count


def moved(arrays, plan, after):
    shapes = [sum(c or arrays[n].shape[0] - f for n, f, c in parts) for parts in plan]
    anywhere, vmem = (pl.BlockSpec(memory_space=m) for m in (pl.ANY, pltpu.VMEM))
    return pl.pallas_call(
        functools.partial(moved_kernel, len(arrays), len(after), plan),
        in_specs=[vmem] * len(arrays) + [anywhere] * len(after),
        out_specs=[vmem] * len(plan),
        out_shape=[
            jax.ShapeDtypeStruct((n, arrays[0].shape[1]), arrays[0].dtype) for n in shapes
        ],
        compiler_params=params(),
        cost_estimate=cost(0, 4 * sum(shapes) * arrays[0].shape[1]),
    )(*arrays, *after)


def packed_kernel(scalars, x_ref, w_ref, plus, minus, own_ref, sems):
    rows, cols = x_ref.shape
    half, part = rows // 2, own_ref.shape[0]
    copies = Copies(sems)
    me, n = scalars[1], w_ref.shape[1] // cols

    def piece(to, first, count):
        at = pl.multiple_of(scalars[0] * part + first, 16)
        columns = pl.ds(pl.multiple_of(lax.rem(me + to, n) * cols, cols), cols)
        return w_ref.at[pl.ds(at, count), columns]

    started = []
    for out, first, to, piece_first in ((plus, 0, 1, 0), (minus, half, n - 1, part // 2)):
        started += [
            copies.start(x_ref.at[pl.ds(first, half)], out.at[pl.ds(0, half)]),
            copies.start(piece(to, 0, part), out.at[pl.ds(half, part)]),
            copies.start(
                piece(2, piece_first, part // 2), out.at[pl.ds(half + part, part // 2)]
            ),
        ]
    started.append(copies.start(piece(0, 0, part), own_ref))
    for copy in started:
        copy.wait()


def packed(x, w, place, me, part):
    rows, cols = x.shape
    shapes = [(rows // 2 + part + part // 2, cols)] * 2 + [(part, cols)]
    return pl.pallas_call(
        packed_kernel,
        in_specs=[pl.BlockSpec(memory_space=pltpu.SMEM)] + [pl.BlockSpec(memory_space=pltpu.HBM)] * 2,
        out_specs=[pl.BlockSpec(memory_space=pltpu.VMEM)] * 3,
        out_shape=[jax.ShapeDtypeStruct(shape, x.dtype) for shape in shapes],
        scratch_shapes=[pltpu.SemaphoreType.DMA((7,))],
        compiler_params=params(),
        cost_estimate=cost(0, 8 * x.size),
    )(jnp.stack([place, me]), x, w)


def flat_kernel(n, w_ref, *refs):
    refs[-2][...] = w_ref[...].reshape(refs[-2].shape)
    refs[-1][...] = jnp.zeros_like(refs[-1])


def flat(w, turn, before=None):
    rows, heads, size = w.shape
    steps = 4
    block = rows // (2 * steps)
    args = [w] if before is None else [w, before]
    return pl.pallas_call(
        functools.partial(flat_kernel, len(args)),
        grid=(steps,),
        in_specs=[
            pl.BlockSpec((block, heads, size), lambda j: (j + turn * steps, 0, 0)),
            pl.BlockSpec(memory_space=pl.ANY),
        ][: len(args)],
        out_specs=[
            pl.BlockSpec((block, heads * size), lambda j: (j + turn * steps, 0)),
            pl.BlockSpec((8, LANES), lambda j: (0, 0)),
        ],
        out_shape=[
            jax.ShapeDtypeStruct((rows, heads * size), w.dtype),
            jax.ShapeDtypeStruct((8, LANES), F32),
        ],
        input_output_aliases={} if before is None else {1: 0},
        compiler_params=params(),
        cost_estimate=cost(0, 2 * w.size),
    )(*args)


class Copies:
    def __init__(self, sems):
        self.sems = sems
        self.used = 0

    def start(self, source, target):
        copy = pltpu.make_async_copy(source, target, self.sems.at[self.used])
        self.used += 1
        copy.start()
        return copy


class Loads:
    def __init__(self, ahead):
        self.ahead = ahead
        self.waiting = []
        self.started = []

    def add(self, start):
        self.waiting.append(start)

    def next(self):
        while self.waiting and len(self.started) <= self.ahead:
            self.started.append(self.waiting.pop(0)())
        for copy in self.started.pop(0):
            copy.wait()


def fetch_rows(copies, pieces, buffer):
    started, at = [], 0
    for piece in pieces:
        n = min(piece.shape[0], buffer.shape[0] // len(pieces))
        piece = piece.at[pl.ds(0, n)]
        started.append(copies.start(piece, buffer.at[pl.ds(at, n)]))
        at += n
    return started


def fetch_weight(copies, w, chunk, columns, target, sources):
    if len(w.shape) == 2:
        n = target.shape[0]
        rows = pl.ds(pl.multiple_of(chunk * n, n), n)
        return [copies.start(w.at[rows, columns], target)]
    own, nval = target.shape[:2]
    started = []
    for h in range(own):
        for n in range(nval):
            source = w.at[chunk * own + h, :, n, :, columns]
            started.append(copies.start(source, target.at[h, sources[n]]))
    return started


def product_kernel(counts, blocks, with_total, n_after, scalars, *refs):
    refs = list(refs)
    take = lambda n: [refs.pop(0) for _ in range(n)]
    ngroups, nweights = len(counts), len(blocks)
    groups = [take(n) for n in counts]
    weights = take(nweights)
    totals = take(nweights) if with_total else None
    take(n_after)
    outs = take(nweights)
    xs = take(ngroups)
    ws = take(nweights)
    ts = take(nweights) if with_total else None
    os = take(nweights)
    copies = Copies(refs[0])
    sources = [scalars[ngroups + n] for n in range(4)]
    loads = Loads(AHEAD)
    tasks = []
    for n, block in enumerate(blocks):
        for at in range(0, ws[n].shape[-1], block):
            columns = pl.ds(at, block)
            for g in range(ngroups):
                if not tasks:
                    loads.add(lambda g=g: fetch_rows(copies, groups[g], xs[g]))
                loads.add(
                    lambda n=n, g=g, columns=columns: fetch_weight(
                        copies, weights[n], scalars[g], columns, ws[n].at[g, ..., columns], sources
                    )
                )
            if with_total:
                loads.add(
                    lambda n=n, columns=columns: [
                        copies.start(totals[n].at[:, columns], ts[n].at[:, columns])
                    ]
                )
            tasks.append((n, columns))
    last = []
    for at, (n, columns) in enumerate(tasks):
        total = None
        for g in range(ngroups):
            if at == 0:
                loads.next()
            loads.next()
            w = ws[n][g, ..., columns].reshape(xs[g].shape[1], -1)
            term = jnp.dot(xs[g][...], w, preferred_element_type=F32)
            total = term if total is None else total + term
        if with_total:
            loads.next()
            total = total + ts[n][:, columns]
        os[n][:, columns] = total.astype(os[n].dtype)
        last.append(copies.start(os[n].at[:, columns], outs[n].at[:, columns]))
    for copy in last:
        copy.wait()


def product(rows, groups, index, weights, totals, dtypes, sources, after=()):
    chunk = groups[0][0].shape[1]
    widths = [w.shape[-1] for w in weights]
    blocks = [min(BLOCK, n) for n in widths]
    steps = sum(n // block for n, block in zip(widths, blocks))
    anywhere, hbm = pl.BlockSpec(memory_space=pl.ANY), pl.BlockSpec(memory_space=pltpu.HBM)
    args = [x for g in groups for x in g]
    spaces = [anywhere] * len(args) + [hbm] * len(weights)
    args += list(weights) + list(totals or []) + list(after)
    spaces += [anywhere] * (len(args) - len(spaces))
    scratch = [pltpu.VMEM((rows, chunk), BF16) for _ in groups]
    for w in weights:
        if w.ndim == 2:
            held = (chunk, w.shape[1])
        else:
            heads, parts, nval, n, cols = w.shape
            held = (chunk // (parts * nval * n), nval, parts, n, cols)
        scratch.append(pltpu.VMEM((len(groups), *held), BF16))
    if totals is not None:
        scratch += [pltpu.VMEM((rows, n), F32) for n in widths]
    scratch += [pltpu.VMEM((rows, n), d) for n, d in zip(widths, dtypes)]
    pieces = 8
    scratch.append(pltpu.SemaphoreType.DMA((8 + steps * (len(groups) * pieces + 2),)))
    cols = sum(widths)
    return pl.pallas_call(
        functools.partial(
            product_kernel, [len(g) for g in groups], blocks, totals is not None, len(after)
        ),
        in_specs=[pl.BlockSpec(memory_space=pltpu.SMEM)]
        + spaces,
        out_specs=[anywhere] * len(weights),
        out_shape=[jax.ShapeDtypeStruct((rows, n), d) for n, d in zip(widths, dtypes)],
        scratch_shapes=scratch,
        compiler_params=params(),
        cost_estimate=cost(
            2 * rows * chunk * len(groups) * cols,
            2 * chunk * len(groups) * (cols + rows) + 4 * rows * cols,
        ),
    )(jnp.stack(list(index) + list(sources)), *args)


def values_kernel(scalars, upper, lower, w_ref, acc_ref, gain_ref, *refs):
    n = (len(refs) - 5) // 2
    outs, (x, w, acc), os, (sems, out_sems) = refs[:n], refs[n : n + 3], refs[n + 3 : -2], refs[-2:]
    own, more, vlocal = outs[0].shape
    rows, block = acc.shape[1], acc.shape[2]
    copies = Copies(sems)
    loads = Loads(AHEAD)
    order = [1, n - 1, *range(2, n - 1), 0]

    def fetch(k):
        to = lax.rem(scalars[1] + k, n)
        columns = pl.ds(pl.multiple_of(to * block, block), block)
        return fetch_weight(copies, w_ref, scalars[0], columns, w.at[k], None) + [
            copies.start(acc_ref.at[:, columns], acc.at[k])
        ]

    loads.add(lambda: fetch_rows(copies, (upper, lower), x))
    for k in order:
        loads.add(lambda k=k: fetch(k))
    loads.next()
    line = lax.broadcasted_iota(jnp.int32, (more - rows, vlocal), 0)
    out_copies = Copies(out_sems)
    last = []
    for k in order:
        to = lax.rem(scalars[1] + k, n)
        loads.next()
        total = acc[k] + jnp.dot(x[...], w[k], preferred_element_type=F32)
        total = total.astype(BF16)
        for h in range(own):
            os[k][h, :rows] = total[:, h * vlocal : (h + 1) * vlocal]
            tail = jnp.zeros((more - rows, vlocal), F32)
            for m, part in enumerate(parts_of(gain_ref[pl.ds(to * own + h, 1), :])):
                tail = jnp.where(line == m, part, tail)
            os[k][h, rows:] = tail.astype(BF16)
        last.append(out_copies.start(os[k], outs[k]))
    for copy in last:
        copy.wait()


def values_by_device(halves, index, me, w, acc, gain, own):
    rows, cols = acc.shape
    chunk = halves[0].shape[1]
    vlocal = gain.shape[1]
    block = own * vlocal
    steps = cols // block
    shape = (own, rows + 16, vlocal)
    anywhere = pl.BlockSpec(memory_space=pl.ANY)
    return pl.pallas_call(
        values_kernel,
        in_specs=[pl.BlockSpec(memory_space=pltpu.SMEM)]
        + [anywhere] * 2
        + [pl.BlockSpec(memory_space=pltpu.HBM), anywhere]
        + [pl.BlockSpec(memory_space=pltpu.VMEM)],
        out_specs=[anywhere] * steps,
        out_shape=[jax.ShapeDtypeStruct(shape, BF16)] * steps,
        scratch_shapes=[
            pltpu.VMEM((rows, chunk), BF16),
            pltpu.VMEM((steps, chunk, block), BF16),
            pltpu.VMEM((steps, rows, block), F32),
        ]
        + [pltpu.VMEM(shape, BF16)] * steps
        + [pltpu.SemaphoreType.DMA((2 + 2 * steps,)), pltpu.SemaphoreType.DMA((steps,))],
        compiler_params=params(),
        cost_estimate=cost(2 * rows * chunk * cols, 2 * chunk * (cols + rows) + 6 * rows * cols),
    )(jnp.stack([index, me]), *halves, w, acc, gain)


def exchanged(pieces):
    return [pieces[0], around(pieces[1], 1), around(pieces[3], -1), around(pieces[2], 2)]


def within_kernel(q_ref, k_ref, g_ref, bias_ref, kwt_ref, p_ref, stat_ref, mark_ref):
    own, rows, _ = p_ref.shape
    qsize = q_ref.shape[1] // own
    g = g_ref[...] + bias_ref[...]
    logf = jnp.minimum(g, 0.0) - jnp.log1p(jnp.exp(-jnp.abs(g)))
    late = lax.broadcasted_iota(jnp.int32, (rows, rows), 0)
    early = lax.broadcasted_iota(jnp.int32, (rows, rows), 1)
    causal = late >= early
    cumb = jnp.dot(
        causal.astype(F32), logf, precision=lax.Precision.HIGHEST, preferred_element_type=F32
    )
    cumb = pltpu.roll(cumb, LANES - own, axis=1)
    gap = g - cumb
    gap_rows = gap.T
    most = jnp.max(gap, axis=0, keepdims=True)
    total = cumb[rows - 1 : rows]
    mark_ref[...] = jnp.concatenate([total + most, total, jnp.zeros((6, LANES), F32)], axis=0)
    lane = lax.broadcasted_iota(jnp.int32, (rows, LANES), 1)
    stat = jnp.zeros((rows, LANES), F32)
    for h in range(own):
        q = q_ref[:, h * qsize : (h + 1) * qsize]
        k = k_ref[:, h * qsize : (h + 1) * qsize]
        seen = jnp.where(causal, gap_rows[h : h + 1, :], F32(NEVER))
        high = jnp.max(seen, axis=1, keepdims=True)
        score = lax.dot_general(q, k, (((1,), (1,)), ((), ())), preferred_element_type=F32)
        wts = jnp.exp(seen - high) * (score * qsize ** (-0.5))
        wts = jnp.where(causal, wts, 0.0).astype(BF16)
        p_ref[h] = wts
        denom = jnp.sum(wts.astype(F32), axis=1, keepdims=True)
        stat = jnp.where(lane == h, high, jnp.where(lane == own + h, denom, stat))
        fall = jnp.exp(gap[:, h : h + 1] - most[:, h : h + 1])
        kw = (k.astype(F32) * fall).astype(BF16)
        kwt_ref[h * qsize : (h + 1) * qsize] = kw.astype(F32).T.astype(BF16)
    stat_ref[...] = stat


def within(q, k, g, bias, own):
    rows, width = q.shape
    return pl.pallas_call(
        within_kernel,
        out_shape=[
            jax.ShapeDtypeStruct((width, rows), BF16),
            jax.ShapeDtypeStruct((own, rows, rows), BF16),
            jax.ShapeDtypeStruct((rows, LANES), F32),
            jax.ShapeDtypeStruct((8, LANES), F32),
        ],
        compiler_params=params(),
        cost_estimate=cost(2 * rows * rows * width, 4 * rows * width, own * rows * rows),
    )(q, k, g, bias)


def parts_of(x):
    hi = x.astype(BF16).astype(F32)
    mid = (x - hi).astype(BF16).astype(F32)
    return [hi, mid, x - hi - mid]


def summary_kernel(scalars, kwt_ref, mark_ref, v0, v1, v2, v3, sent_ref, v_ref, gain_ref):
    vlocal = v0.shape[2]
    own, rows, vsize = v_ref.shape
    gain_ref[...] = jnp.zeros_like(gain_ref)
    qsize = kwt_ref.shape[0] // own
    for n, ref in enumerate((v0, v1, v2, v3)):
        at = pl.multiple_of(scalars[n] * vlocal, vlocal)
        for h in range(own):
            v_ref[h, :, pl.ds(at, vlocal)] = ref[h, :rows]
            tail = ref[h, rows:].astype(F32)
            gain_ref[h : h + 1, pl.ds(at, vlocal)] = tail[0:1] + tail[1:2] + tail[2:3]
    lane = lax.broadcasted_iota(jnp.int32, (qsize, LANES), 1)
    for h in range(own):
        kwt = kwt_ref[h * qsize : (h + 1) * qsize]
        state = jnp.dot(kwt, v_ref[h], preferred_element_type=F32)
        extra = jnp.where(lane == 0, jnp.sum(kwt.astype(F32), axis=1, keepdims=True), 0.0)
        marks = parts_of(mark_ref[0:1, h : h + 1]) + parts_of(mark_ref[1:2, h : h + 1])
        for n, x in enumerate(marks):
            extra = jnp.where(lane == 1 + n, x, extra)
        sent_ref[h * qsize : (h + 1) * qsize, :vsize] = state.astype(BF16)
        sent_ref[h * qsize : (h + 1) * qsize, vsize:] = extra.astype(BF16)


def summary(index, kwt, mark, pieces):
    own, _, vlocal = pieces[0].shape
    rows = kwt.shape[1]
    vsize = vlocal * len(pieces)
    whole = lambda shape: pl.BlockSpec(shape, lambda j, s: (0,) * len(shape))
    return pl.pallas_call(
        summary_kernel,
        grid_spec=pltpu.PrefetchScalarGridSpec(
            num_scalar_prefetch=1,
            grid=(1,),
            in_specs=[whole(kwt.shape), whole(mark.shape)] + [whole(x.shape) for x in pieces],
            out_specs=[whole((kwt.shape[0], vsize + LANES)), whole((own, rows, vsize)), whole((8, vsize))],
        ),
        out_shape=[
            jax.ShapeDtypeStruct((kwt.shape[0], vsize + LANES), BF16),
            jax.ShapeDtypeStruct((own, rows, vsize), BF16),
            jax.ShapeDtypeStruct((8, vsize), F32),
        ],
        compiler_params=params(),
        cost_estimate=cost(2 * kwt.size * vsize, 3 * own * rows * vsize * 2),
    )(jnp.stack(index), kwt, mark, *pieces)


def inside_kernel(p_ref, v_ref, out_ref):
    for h in range(p_ref.shape[0]):
        out_ref[h] = jnp.dot(p_ref[h], v_ref[h], preferred_element_type=F32)


def inside(p, v):
    return pl.pallas_call(
        inside_kernel,
        out_shape=jax.ShapeDtypeStruct(v.shape, F32),
        compiler_params=params(),
        cost_estimate=cost(2 * p.size * v.shape[2], 6 * v.size),
    )(p, v)


def prefix_kernel(got_ref, out_ref):
    blocks, cut, width = got_ref.shape
    body = width - LANES
    lane = lax.broadcasted_iota(jnp.int32, (cut, LANES), 1)
    source = lax.broadcasted_iota(jnp.int32, (LANES, 2 * LANES), 0)
    target = lax.broadcasted_iota(jnp.int32, (LANES, 2 * LANES), 1)
    first = jnp.where(target < LANES, 1, 4)
    spread = ((source >= first) & (source < first + 3)).astype(F32).astype(BF16)
    marks = jnp.dot(
        got_ref[:, :, body:].reshape(blocks * cut, LANES), spread, preferred_element_type=F32
    )
    state = [jnp.zeros((cut, LANES), F32) for _ in range(width // LANES)]
    ptop = jnp.full((cut, LANES), NEVER, F32)
    for b in range(blocks):
        held = state[-1]
        for n, x in enumerate(parts_of(ptop)):
            held = jnp.where(lane == 1 + n, x, held)
        for n, x in enumerate(state[:-1] + [held]):
            out_ref[b, :, n * LANES : (n + 1) * LANES] = x.astype(BF16)
        if b == blocks - 1:
            break
        top = marks[b * cut : (b + 1) * cut, :LANES]
        total = marks[b * cut : (b + 1) * cut, LANES:]
        new = jnp.maximum(ptop + total, top)
        keep = jnp.exp(ptop + total - new)
        add = jnp.exp(top - new)
        state = [
            keep * x + add * got_ref[b, :, n * LANES : (n + 1) * LANES].astype(F32)
            for n, x in enumerate(state)
        ]
        ptop = new


def prefixes(got):
    return pl.pallas_call(
        prefix_kernel,
        out_shape=jax.ShapeDtypeStruct(got.shape, BF16),
        compiler_params=params(),
        cost_estimate=cost(4 * got.size, 4 * got.size),
    )(got)


def finish_kernel(q_ref, prefix_ref, numer_ref, stat_ref, gain_ref, upper, lower):
    own, rows, vsize = numer_ref.shape
    qsize = q_ref.shape[1] // own
    for h in range(own):
        inter = jnp.dot(
            q_ref[:, h * qsize : (h + 1) * qsize], prefix_ref[h], preferred_element_type=F32
        )
        ext = prefix_ref[h, 0:16, vsize:].astype(F32)[0:1]
        ptop = ext[:, 1:2] + ext[:, 2:3] + ext[:, 3:4]
        high = stat_ref[:, h : h + 1]
        top = jnp.maximum(high, ptop)
        fade = jnp.exp(high - top)
        decay = jnp.exp(ptop - top) * qsize ** (-0.5)
        denom = stat_ref[:, own + h : own + h + 1] * fade + inter[:, vsize : vsize + 1] * decay
        share = 1.0 / jnp.maximum(jnp.abs(denom), 1.0)
        hidden = numer_ref[h] * (fade * share) + inter[:, :vsize] * (decay * share)
        mean = jnp.mean(hidden, axis=1, keepdims=True)
        msq = jnp.mean(hidden * hidden, axis=1, keepdims=True)
        normed = (hidden - mean) * lax.rsqrt(msq - mean * mean + 1e-06) * gain_ref[h : h + 1]
        normed = normed.astype(BF16)
        upper[:, h * vsize : (h + 1) * vsize] = normed[: rows // 2]
        lower[:, h * vsize : (h + 1) * vsize] = normed[rows // 2 :]


def finish(q, prefix, numer, stat, gain):
    own, rows, vsize = numer.shape
    return pl.pallas_call(
        finish_kernel,
        out_shape=[jax.ShapeDtypeStruct((rows // 2, own * vsize), BF16)] * 2,
        compiler_params=params(),
        cost_estimate=cost(2 * q.size * vsize, 8 * numer.size),
    )(q, prefix, numer, stat, gain)


def per_device(tokens, w_query, w_key, w_value, w_gate, gate_bias, norm_gain, w_out):
    me = lax.axis_index("val")
    nval = lax.axis_size("val")
    place = lax.axis_index("seq")
    blocks = lax.axis_size("seq")
    rows, chunk = tokens.shape
    width = w_query.shape[0]
    heads, vlocal = w_value.shape[1:]
    own = heads // nval
    qsize = w_query.shape[1] // own
    vsize = vlocal * nval
    index = [(me + d) % nval for d in (0, nval - 1, 1, 2)]

    part = heads * vlocal // blocks
    half = rows // 2
    plus, minus, kept = packed(tokens, w_out.reshape(heads * vlocal, -1), place, me, part)
    ring = Ring(plus, minus, [tokens[:half], tokens[half:]], part // 2)
    wv, mark = flat(w_value, 0)
    ring.second([mark])
    ring.forward()
    wv, _ = flat(w_value, 1, wv)
    wg = lax.dynamic_slice_in_dim(w_gate, me * own, own, axis=2).reshape(width, 2 * own)
    wg = jnp.pad(wg, ((0, 0), (0, LANES - 2 * own)))
    bias = lax.dynamic_slice_in_dim(gate_bias, me * own, own, axis=1).reshape(1, 2 * own)
    bias = jnp.pad(bias, ((0, 0), (0, LANES - 2 * own)))
    groups = [(tokens,), ring.left, ring.right]
    acc = product(rows, groups, index[:3], [wv], None, [F32], index, [wg])[0]
    values = values_by_device(ring.opposite, index[3], me, wv, acc, norm_gain, own)
    first = values[0]
    q, k, g = product(
        rows,
        groups + [ring.opposite],
        index,
        [w_query, w_key, wg],
        None,
        [BF16, BF16, F32],
        index,
        [first],
    )
    arrived = [kept, ring.plus, ring.minus, *ring.opposite]
    cuts = [(0, 0, 0), (1, half, part), (2, half, part), (3, half, 0), (4, half, 0)]
    wo = moved(arrived, [cuts], [acc])[0]
    wo = lax.all_gather(wo, "seq", axis=0)
    wo = wo.reshape(heads, blocks // heads, nval, part, chunk)

    values = exchanged(values)
    kwt, p, stat, mark = within(q, k, g, bias, own)
    sent, v, gain = summary(index, kwt, mark, values)
    got = lax.all_to_all(sent.reshape(blocks, -1, vsize + LANES), "seq", 0, 0)
    numer = inside(p, v)
    prefix = lax.all_to_all(prefixes(got), "seq", 0, 0)
    upper, lower = finish(q, prefix.reshape(own, qsize, vsize + LANES), numer, stat, gain)

    ring = Ring(upper, lower, [upper, lower], 0)
    accs = product(rows, [(upper, lower)], index[:1], [wo], None, [F32], index)
    ring.second(accs)
    ring.forward()
    accs = product(rows, [ring.left, ring.right], index[1:3], [wo], accs, [F32], index)
    return product(rows, [ring.opposite], index[3:], [wo], accs, [BF16], index)[0]


def solution(mesh):
    placed = (
        P("seq", "val"),
        P(None, "val"),
        P(None, "val"),
        P(None, None, "val"),
        P(),
        P(),
        P(None, "val"),
        P(None, "val", None),
    )
    return jax.shard_map(
        per_device, mesh=mesh, in_specs=placed, out_specs=P("seq", "val"), check_vma=False
    )
```

time: 190 us -> 166 us (0.87)
  local copies, waits for them, and re-layouts: 33.2 us -> 13.1 us
  waiting for transfers between devices: 42 us -> 26.2 us
  Pallas kernels: 48 us -> 58.7 us
  blocking collectives: 24.8 us -> 30.7 us
  starting transfers between devices: 27.1 us -> 22.5 us
    ppermute x17 -> x15, waiting for transfers between devices: 37.8 us -> 14.9 us  [around(): return lax.ppermute(x, 'val', [(i, (i + distance) % n) for i in range(n)])]
    pallas_call x1 -> x10, Pallas kernels: 1.52 us -> 23.2 us  [the longest x2 9.73 us: flat(): pl.pallas_call(functools.partial(flat_kernel, len(args)), grid=(steps,),...]
    transpose x1 -> x0, local copies, waits for them, and re-layouts: 8.5 us -> none  [per_device(): wo.reshape(heads, blocks // heads, nval, part, chunk)]
    all_to_all x1, waiting for transfers between devices: 4.24 us -> 11.3 us  [per_device(): prefix = lax.all_to_all(prefixes(got), 'seq', 0, 0)]
    pallas_call x10 -> x5, Pallas kernels: 37.7 us -> 30.8 us  [product(): pl.pallas_call(functools.partial(product_kernel, [len(g) for g in groups]...]
    unnamed x42, local copies, waits for them, and re-layouts: 15.2 us -> 8.58 us
    all_to_all x1, blocking collectives: 24.8 us -> 30.7 us  [per_device(): got = lax.all_to_all(sent.reshape(blocks, -1, vsize + LANES), 'seq', 0, 0)]
    ppermute x17 -> x15, starting transfers between devices: 23.4 us -> 17.6 us  [around(): return lax.ppermute(x, 'val', [(i, (i + distance) % n) for i in range(n)])]
  transfers between devices with their start and end apart: 19 -> 17, of which waited for: 5 -> 6; matrix products, arithmetic and copies ran while one was open for 14% -> 3% of each run, Pallas kernels for 23% -> 30%
where the time goes in v3:
time: 166 us; the launch traced here: 165 us
  Pallas kernels  58.7 us (35%)
  blocking collectives  30.7 us (18%)
  waiting for transfers between devices  26.2 us (16%)
  starting transfers between devices  22.5 us (14%)
  between operations  13.7 us (8%)
  local copies, waits for them, and re-layouts  13.1 us (8%)
    pallas_call x5, Pallas kernels, product(): pl.pallas_call(functools.partial(product_kernel, [len(g) for g in groups]...  30.8 us
    all_to_all x1, blocking collectives, per_device(): got = lax.all_to_all(sent.reshape(blocks, -1, vsize + LANES), 'seq', 0, 0)  30.7 us
    ppermute x15, starting transfers between devices, around(): return lax.ppermute(x, 'val', [(i, (i + distance) % n) for i in range(n)])  17.6 us
    ppermute x15, waiting for transfers between devices, around(): return lax.ppermute(x, 'val', [(i, (i + distance) % n) for i in range(n)])  14.9 us
    all_to_all x1, waiting for transfers between devices, per_device(): prefix = lax.all_to_all(prefixes(got), 'seq', 0, 0)  11.3 us
    pallas_call x2, Pallas kernels, flat(): pl.pallas_call(functools.partial(flat_kernel, len(args)), grid=(steps,),...  9.73 us
    unnamed x42, local copies, waits for them, and re-layouts  8.58 us
    pallas_call x1, Pallas kernels, values_by_device(): pl.pallas_call(values_kernel, in_specs=[pl.BlockSpec(memory_space=pltpu.S...  5.24 us
  transfers between devices with their start and end apart: 17, of which 6 were waited for; matrix products, arithmetic and copies ran while one was open for 3% of the time, Pallas kernels for 30%

profile of v3, /device:TPU:1, one launch (start us, length us, event | category | flops | bytes accessed | tf_op | source)
XLA Modules:
  0.0 165.3 jit_solution(15434201604081582652)
XLA Ops:
  6.6 1.1 copy-done.2
  7.7 2.7 %shard_map.82 = (bf16[240,1024]{1,0:T(8,128)(2,1)}, bf16[240,1024]{1,0:T(8,128)(2,1)S(1)}, bf16[32,1024]{1,0:T(8,128)(2,1)S(1)}) custom-call(s32[2]{0:T(128)S(1)} %pad_add_fusion.scalars, bf16[384,1024]{1,0:T(8,128)(2,1)S(1)} %copy-done.2, bf16[1024,4096]{1,0:T(8,128)(2,1)} %bitcast.17), custom_call_target="tpu_custom_call" | custom-call | bytes 3145728 | tf_op jit(solution)/shard_map/pallas_call | solution.py:104
  10.4 2.2 %collective-permute-start = (bf16[240,1024]{1,0:T(8,128)(2,1)}, bf16[240,1024]{1,0:T(8,128)(2,1)S(1)}, u32[]{:S(2)}, u32[]{:S(2)}) collective-permute-start(bf16[240,1024]{1,0:T(8,128)(2,1)} %get-tuple-element.35), channel_id=1, source_target_pairs={{0,1},{1,2},{2,3},{3,0},{4,5},{5,6},{6,7},{7,4},{8,9},{9,10},{10,1... | collective-permute-start | bytes 1474568 | tf_op jit(solution)/shard_map/ppermute | solution.py:20
  12.6 1.5 collective-permute-start.3
  14.1 4.9 %shard_map.83 = (bf16[4096,1024]{1,0:T(8,128)(2,1)}, f32[8,128]{1,0:T(8,128)S(1)}) custom-call(bf16[4096,8,128]{2,1,0:T(8,128)(2,1)} %w_ref.3), custom_call_target="tpu_custom_call" | custom-call | bytes 8388608 | tf_op jit(solution)/shard_map/pallas_call | solution.py:125
  19.1 1.5 collective-permute-start.2
  20.7 4.4 %collective-permute-done.refs_0_.refs_1_ = bf16[240,1024]{1,0:T(8,128)(2,1)S(1)} collective-permute-done((bf16[240,1024]{1,0:T(8,128)(2,1)}, bf16[240,1024]{1,0:T(8,128)(2,1)S(1)}, u32[]{:S(2)}, u32[]{:S(2)}) %collective-permute-start) | collective-permute-done | bytes 491552 | tf_op jit(solution)/shard_map/ppermute | solution.py:20
  25.1 1.0 shard_map.85
  26.0 0.6 collective-permute-start.4
  26.7 2.1 %collective-permute-start.5 = (bf16[208,1024]{1,0:T(8,128)(2,1)}, bf16[208,1024]{1,0:T(8,128)(2,1)}, u32[]{:S(2)}, u32[]{:S(2)}) collective-permute-start(bf16[208,1024]{1,0:T(8,128)(2,1)} %get-tuple-element.41), channel_id=1, source_target_pairs={{0,3},{1,0},{2,1},{3,2},{4,7},{5,4},{6,5},{7,6},{8,11},{9,8},{10,9... | collective-permute-start | bytes 1277960 | tf_op jit(solution)/shard_map/ppermute | solution.py:20
  28.8 1.4 copy.11
  30.2 4.8 %shard_map.86 = (bf16[4096,1024]{1,0:T(8,128)(2,1)}, f32[8,128]{1,0:T(8,128)}) custom-call(bf16[4096,8,128]{2,1,0:T(8,128)(2,1)} %w_ref.3, bf16[4096,1024]{1,0:T(8,128)(2,1)} %get-tuple-element.42.refs_0_), custom_call_target="tpu_custom_call", output_to_operand_aliasing={{0}: (1, {})} | custom-call | bytes 8388608 | tf_op jit(solution)/shard_map/pallas_call | solution.py:125
  35.1 2.4 %pad.8.refs_6_.refs_9_ = bf16[4096,128]{1,0:T(8,128)(2,1)} pad(bf16[4096,4]{1,0:T(8,128)(2,1)} %copy.11, bf16[]{:T(256)} %constant.44.clone.1), padding=0_0x0_124 | pad | bytes 1081346 | tf_op jit(solution)/shard_map/jit(_pad)/pad | solution.py:579
  37.6 0.7 copy-done.11
  38.4 0.8 copy-done.14
  39.1 1.2 copy-done.4
  40.4 1.0 copy-done.12
  41.3 1.0 copy-done.15
  42.3 6.1 %shard_map.87.acc_ref.refs_5_ = f32[384,1024]{1,0:T(8,128)S(1)} custom-call(s32[7]{0:T(128)S(1)} %stack.38.scalars, bf16[384,1024]{1,0:T(8,128)(2,1)S(1)} %copy-done.3, bf16[240,1024]{1,0:T(8,128)(2,1)S(1)} %collective-permute-done.refs_0_.refs_1_, bf16[192,1024]{1,0:T(8,128)(2,1)S(1)} %copy-done.15, bf16[192,1024]{1,0:T(8,128)(2,1)S(1)} %copy-done.12, ...), custom_call_target="tpu_custom_call" | custom-call | flops 2415919104 | bytes 10223616 | tf_op jit(solution)/shard_map/pallas_call | solution.py:276
  48.4 1.2 shard_map.95
  49.6 0.7 copy-done.8
  50.7 5.2 %shard_map.88 = (bf16[2,400,128]{2,1,0:T(8,128)(2,1)S(1)}, bf16[2,400,128]{2,1,0:T(8,128)(2,1)S(1)}, bf16[2,400,128]{2,1,0:T(8,128)(2,1)S(1)}, bf16[2,400,128]{2,1,0:T(8,128)(2,1)S(1)}) custom-call(s32[2]{0:T(128)S(1)} %pad_add_fusion.1.scalars, bf16[208,1024]{1,0:T(8,128)(2,1)} %collective-permute-done.4.upper.refs_5_.refs_3_, ...), custom_call_target="tpu_custom_call" | custom-call | flops 805306368 | bytes 5242880 | tf_op jit(solution)/shard_map/pallas_call | solution.py:340
  56.1 2.7 %collective-permute-start.7 = (bf16[2,400,128]{2,1,0:T(8,128)(2,1)S(1)}, bf16[2,400,128]{2,1,0:T(8,128)(2,1)S(1)}, u32[]{:S(2)}, u32[]{:S(2)}) collective-permute-start(bf16[2,400,128]{2,1,0:T(8,128)(2,1)S(1)} %get-tuple-element.51), channel_id=1, source_target_pairs={{0,3},{1,0},{2,1},{3,2},{4,7},{5,4},{6,5},{7,6},{8,11},{9,8},{10,9... | collective-permute-start | bytes 614408 | tf_op jit(solution)/shard_map/ppermute | solution.py:20
  58.8 10.9 %shard_map.89 = (bf16[384,512]{1,0:T(8,128)(2,1)S(1)}, bf16[384,512]{1,0:T(8,128)(2,1)S(1)}, f32[384,128]{1,0:T(8,128)S(1)}) custom-call(s32[8]{0:T(128)S(1)} %stack.33.scalars, bf16[384,1024]{1,0:T(8,128)(2,1)S(1)} %copy-done.3, bf16[240,1024]{1,0:T(8,128)(2,1)S(1)} %collective-permute-done.refs_0_.refs_1_, bf16[192,1024]{1,0:T(8,128)(2,1)S(1)} %copy-done.16, ...), custom_call_target="tpu_custom_call" | custom-call | flops 3623878656 | bytes 14352384 | tf_op jit(solution)/shard_map/pallas_call | solution.py:276
  69.7 1.7 %shard_map.90 = (bf16[512,384]{1,0:T(8,128)(2,1)S(1)}, bf16[2,384,384]{2,1,0:T(8,128)(2,1)S(1)}, f32[384,128]{1,0:T(8,128)S(1)}, f32[8,128]{1,0:T(8,128)S(1)}) custom-call(bf16[384,512]{1,0:T(8,128)(2,1)S(1)} %get-tuple-element.45.q_ref, bf16[384,512]{1,0:T(8,128)(2,1)S(1)} %get-tuple-element.46.k_ref, f32[384,128]{1,0:T(8,128)S(1)} %get-tuple-element.47.g_ref, ...), custom_call_target="tpu_custom_call" | custom-call | flops 150994944 | bytes 786432 | tf_op jit(solution)/shard_map/pallas_call | solution.py:402
  71.4 1.1 shard_map.91
  72.6 30.7 %all_to_all.10.got_ref = bf16[32,16,640]{2,1,0:T(8,128)(2,1)S(1)} all-to-all(bf16[32,16,640]{2,1,0:T(8,128)(2,1)S(1)} %bitcast.13), channel_id=1, replica_groups=mesh['seq'=32,'val'=4] {'seq'}, dimensions={0} | all-to-all | bytes 1310720 | tf_op jit(solution)/shard_map/all_to_all | solution.py:605
  103.4 1.3 shard_map.92
  104.7 5.0 %all-to-all-start.1 = ((bf16[32,16,640]{2,1,0:T(8,128)(2,1)}), bf16[32,16,640]{2,1,0:T(8,128)(2,1)S(1)}, u32[]{:S(2)}, u32[]{:S(2)}) async-start(bf16[32,16,640]{2,1,0:T(8,128)(2,1)} %shard_map.92), calls=%async_computation.1 | async-start | bytes 1310720 | tf_op jit(solution)/shard_map/all_to_all | solution.py:607
  109.6 1.1 copy-done.10
  110.7 0.6 shard_map.93.numer_ref
  111.3 11.3 %all-to-all-done.1 = bf16[32,16,640]{2,1,0:T(8,128)(2,1)S(1)} async-done(((bf16[32,16,640]{2,1,0:T(8,128)(2,1)}), bf16[32,16,640]{2,1,0:T(8,128)(2,1)S(1)}, u32[]{:S(2)}, u32[]{:S(2)}) %all-to-all-start.1) | async-done | bytes 655392 | tf_op jit(solution)/shard_map/all_to_all | solution.py:607
  122.6 0.9 copy-done.18
  123.5 1.5 shard_map.94
  125.0 0.6 collective-permute-start.9
  125.6 2.1 %collective-permute-start.10 = (bf16[192,1024]{1,0:T(8,128)(2,1)S(1)}, bf16[192,1024]{1,0:T(8,128)(2,1)S(1)}, u32[]{:S(2)}, u32[]{:S(2)}) collective-permute-start(bf16[192,1024]{1,0:T(8,128)(2,1)S(1)} %get-tuple-element.59.refs_1_), channel_id=1, source_target_pairs={{0,3},{1,0},{2,1},{3,2},{4,7},{5,4},{6,5},{7,6},{8,11},{9,8},{10,9... | collective-permute-start | bytes 1179656 | tf_op jit(solution)/shard_map/ppermute | solution.py:20
  127.9 3.7 %shard_map.96.refs_2_.refs_5_ = f32[384,1024]{1,0:T(8,128)S(1)} custom-call(s32[5]{0:T(128)S(1)} %stack.40.scalars, bf16[192,1024]{1,0:T(8,128)(2,1)S(1)} %get-tuple-element.58.refs_0_, bf16[192,1024]{1,0:T(8,128)(2,1)S(1)} %get-tuple-element.59.refs_1_, bf16[8,4,4,32,1024]{4,3,2,1,0:T(8,128)(2,1)} %bitcast.14), custom_call_target="tpu_custom_call" | custom-call | flops 805306368 | bytes 4456448 | tf_op jit(solution)/shard_map/pallas_call | solution.py:276
  131.6 1.0 shard_map.97
  132.6 0.5 collective-permute-start.14
  133.0 1.0 collective-permute-start.13
  134.0 3.1 %collective-permute-done.9.refs_0_ = bf16[192,1024]{1,0:T(8,128)(2,1)S(1)} collective-permute-done((bf16[192,1024]{1,0:T(8,128)(2,1)S(1)}, bf16[192,1024]{1,0:T(8,128)(2,1)S(1)}, u32[]{:S(2)}, u32[]{:S(2)}) %collective-permute-start.9) | collective-permute-done | bytes 393248 | tf_op jit(solution)/shard_map/ppermute | solution.py:20
  137.1 0.9 shard_map.98
  138.1 1.2 collective-permute-start.11
  139.3 1.5 collective-permute-start.12
  140.9 4.5 %collective-permute-done.14.refs_2_ = bf16[192,1024]{1,0:T(8,128)(2,1)} collective-permute-done((bf16[192,1024]{1,0:T(8,128)(2,1)}, bf16[192,1024]{1,0:T(8,128)(2,1)}, u32[]{:S(2)}, u32[]{:S(2)}) %collective-permute-start.14) | collective-permute-done | bytes 393248 | tf_op jit(solution)/shard_map/ppermute | solution.py:20
  145.5 5.5 %shard_map.99.refs_3_ = f32[384,1024]{1,0:T(8,128)S(1)} custom-call(s32[6]{0:T(128)S(1)} %stack.41.scalars, bf16[192,1024]{1,0:T(8,128)(2,1)S(1)} %collective-permute-done.9.refs_0_, bf16[192,1024]{1,0:T(8,128)(2,1)} %collective-permute-done.13.refs_1_, bf16[192,1024]{1,0:T(8,128)(2,1)} %collective-permute-done.14.refs_2_, ...), custom_call_target="tpu_custom_call" | custom-call | flops 1610612736 | bytes 7340032 | tf_op jit(solution)/shard_map/pallas_call | solution.py:276
  150.9 2.8 %collective-permute-done.11.refs_0_ = bf16[192,1024]{1,0:T(8,128)(2,1)S(1)} collective-permute-done((bf16[192,1024]{1,0:T(8,128)(2,1)}, bf16[192,1024]{1,0:T(8,128)(2,1)S(1)}, u32[]{:S(2)}, u32[]{:S(2)}) %collective-permute-start.11) | collective-permute-done | bytes 393248 | tf_op jit(solution)/shard_map/ppermute | solution.py:20
  153.8 4.6 %shard_map.100 = bf16[384,1024]{1,0:T(8,128)(2,1)} custom-call(s32[5]{0:T(128)S(1)} %stack.32.scalars, bf16[192,1024]{1,0:T(8,128)(2,1)S(1)} %collective-permute-done.11.refs_0_, bf16[192,1024]{1,0:T(8,128)(2,1)S(1)} %collective-permute-done.12.refs_1_, bf16[8,4,4,32,1024]{4,3,2,1,0:T(8,128)(2,1)} %bitcast.16, f32[384,1024]{1,0:T(8,128)S(1)} %shard_map.99.refs_3_), custom_call_target="tpu_custom_call" | custom-call | flops 805306368 | bytes 4456448 | tf_op jit(solution)/shard_map/pallas_call | solution.py:276
  (65 shorter events, 1.3 us)
Async XLA Ops:
  6.5 22.2 %copy-start = (bf16[4096,2,8]{0,2,1:T(8,128)(2,1)S(1)}, bf16[4096,2,8]{0,2,1:T(8,128)(2,1)}, u32[]{:S(2)}) copy-start(bf16[4096,2,8]{0,2,1:T(8,128)(2,1)} %param.12) | copy-start | bytes 393220
  6.5 121.3 %all-gather.3.cloned.1.call-start = ((), (), s32[]{:S(2)}) async-start(), calls=%async_computation.2 | async-start | bytes 8650752 | tf_op jit(solution)/shard_map/all_gather | solution.py:599
  6.6 1.1 copy-start.2
  10.4 14.6 %collective-permute-start = (bf16[240,1024]{1,0:T(8,128)(2,1)}, bf16[240,1024]{1,0:T(8,128)(2,1)S(1)}, u32[]{:S(2)}, u32[]{:S(2)}) collective-permute-start(bf16[240,1024]{1,0:T(8,128)(2,1)} %get-tuple-element.35), channel_id=1, source_target_pairs={{0,1},{1,2},{2,3},{3,0},{4,5},{5,6},{6,7},{7,4},{8,9},{9,10},{10,1... | collective-permute-start | bytes 1474568 | tf_op jit(solution)/shard_map/ppermute | solution.py:20
  12.6 12.4 %collective-permute-start.3 = (bf16[240,1024]{1,0:T(8,128)(2,1)S(1)}, bf16[240,1024]{1,0:T(8,128)(2,1)S(1)}, u32[]{:S(2)}, u32[]{:S(2)}) collective-permute-start(bf16[240,1024]{1,0:T(8,128)(2,1)S(1)} %get-tuple-element.39), channel_id=1, source_target_pairs={{0,3},{1,0},{2,1},{3,2},{4,7},{5,4},{6,5},{7,6},{8,11},{9,8},{10,9... | collective-permute-start | bytes 1474568 | tf_op jit(solution)/shard_map/ppermute | solution.py:20
  19.1 18.5 %collective-permute-start.2 = (bf16[192,1024]{1,0:T(8,128)(2,1)S(1)}, bf16[192,1024]{1,0:T(8,128)(2,1)S(1)}, u32[]{:S(2)}, u32[]{:S(2)}) collective-permute-start(bf16[192,1024]{1,0:T(8,128)(2,1)S(1)} %get-tuple-element.38), channel_id=1, source_target_pairs={{0,3},{1,0},{2,1},{3,2},{4,7},{5,4},{6,5},{7,6},{8,11},{9,8},{10,9... | collective-permute-start | bytes 1179656 | tf_op jit(solution)/shard_map/ppermute | solution.py:20
  20.6 17.8 %collective-permute-start.1 = (bf16[192,1024]{1,0:T(8,128)(2,1)S(1)}, bf16[192,1024]{1,0:T(8,128)(2,1)S(1)}, u32[]{:S(2)}, u32[]{:S(2)}) collective-permute-start(bf16[192,1024]{1,0:T(8,128)(2,1)S(1)} %get-tuple-element.37.refs_2_), channel_id=1, source_target_pairs={{0,1},{1,2},{2,3},{3,0},{4,5},{5,6},{6,7},{7,4},{8,9},{9,10},{10,1... | collective-permute-start | bytes 1179656 | tf_op jit(solution)/shard_map/ppermute | solution.py:20
  26.0 22.4 %collective-permute-start.4 = (bf16[208,1024]{1,0:T(8,128)(2,1)}, bf16[208,1024]{1,0:T(8,128)(2,1)}, u32[]{:S(2)}, u32[]{:S(2)}) collective-permute-start(bf16[208,1024]{1,0:T(8,128)(2,1)} %get-tuple-element.40), channel_id=1, source_target_pairs={{0,1},{1,2},{2,3},{3,0},{4,5},{5,6},{6,7},{7,4},{8,9},{9,10},{10,1... | collective-permute-start | bytes 1277960 | tf_op jit(solution)/shard_map/ppermute | solution.py:20
  26.7 21.8 %collective-permute-start.5 = (bf16[208,1024]{1,0:T(8,128)(2,1)}, bf16[208,1024]{1,0:T(8,128)(2,1)}, u32[]{:S(2)}, u32[]{:S(2)}) collective-permute-start(bf16[208,1024]{1,0:T(8,128)(2,1)} %get-tuple-element.41), channel_id=1, source_target_pairs={{0,3},{1,0},{2,1},{3,2},{4,7},{5,4},{6,5},{7,6},{8,11},{9,8},{10,9... | collective-permute-start | bytes 1277960 | tf_op jit(solution)/shard_map/ppermute | solution.py:20
  30.2 8.9 %copy-start.3 = (bf16[384,1024]{1,0:T(8,128)(2,1)S(1)}, bf16[384,1024]{1,0:T(8,128)(2,1)}, u32[]{:S(2)}) copy-start(bf16[384,1024]{1,0:T(8,128)(2,1)} %refs_0_.3) | copy-start | bytes 2359300
  37.6 0.7 copy-start.11
  38.4 0.8 copy-start.14
  39.1 1.2 copy-start.4
  40.4 1.0 copy-start.12
  41.3 1.0 copy-start.15
  42.3 8.1 %copy-start.20 = (f32[2,8]{1,0:T(2,128)S(1)}, f32[2,8]{1,0:T(2,128)}, u32[]{:S(2)}) copy-start(f32[2,8]{1,0:T(2,128)} %param.13) | copy-start | bytes 196
  42.3 8.4 %copy-start.19 = (f32[8,128]{1,0:T(8,128)S(1)}, f32[8,128]{1,0:T(8,128)}, u32[]{:S(2)}) copy-start(f32[8,128]{1,0:T(8,128)} %gain_ref.1) | copy-start | bytes 12292
  49.6 0.7 copy-start.8
  50.7 8.0 %copy-start.5 = (bf16[4096,128]{1,0:T(8,128)(2,1)S(1)}, bf16[4096,128]{1,0:T(8,128)(2,1)}, u32[]{:S(2)}) copy-start(bf16[4096,128]{1,0:T(8,128)(2,1)} %pad.8.refs_6_.refs_9_) | copy-start | bytes 3145732
  50.7 8.0 %copy-start.13 = (bf16[192,1024]{1,0:T(8,128)(2,1)S(1)}, bf16[192,1024]{1,0:T(8,128)(2,1)}, u32[]{:S(2)}) copy-start(bf16[192,1024]{1,0:T(8,128)(2,1)} %copy-done.11) | copy-start | bytes 1179652
  50.7 8.0 %copy-start.16 = (bf16[192,1024]{1,0:T(8,128)(2,1)S(1)}, bf16[192,1024]{1,0:T(8,128)(2,1)}, u32[]{:S(2)}) copy-start(bf16[192,1024]{1,0:T(8,128)(2,1)} %copy-done.14) | copy-start | bytes 1179652
  56.0 15.4 %collective-permute-start.6 = (bf16[2,400,128]{2,1,0:T(8,128)(2,1)S(1)}, bf16[2,400,128]{2,1,0:T(8,128)(2,1)S(1)}, u32[]{:S(2)}, u32[]{:S(2)}) collective-permute-start(bf16[2,400,128]{2,1,0:T(8,128)(2,1)S(1)} %get-tuple-element.50), channel_id=1, source_target_pairs={{0,1},{1,2},{2,3},{3,0},{4,5},{5,6},{6,7},{7,4},{8,9},{9,10},{10,1... | collective-permute-start | bytes 614408 | tf_op jit(solution)/shard_map/ppermute | solution.py:20
  56.1 15.4 %collective-permute-start.7 = (bf16[2,400,128]{2,1,0:T(8,128)(2,1)S(1)}, bf16[2,400,128]{2,1,0:T(8,128)(2,1)S(1)}, u32[]{:S(2)}, u32[]{:S(2)}) collective-permute-start(bf16[2,400,128]{2,1,0:T(8,128)(2,1)S(1)} %get-tuple-element.51), channel_id=1, source_target_pairs={{0,3},{1,0},{2,1},{3,2},{4,7},{5,4},{6,5},{7,6},{8,11},{9,8},{10,9... | collective-permute-start | bytes 614408 | tf_op jit(solution)/shard_map/ppermute | solution.py:20
  58.7 12.7 %collective-permute-start.8 = (bf16[2,400,128]{2,1,0:T(8,128)(2,1)S(1)}, bf16[2,400,128]{2,1,0:T(8,128)(2,1)S(1)}, u32[]{:S(2)}, u32[]{:S(2)}) collective-permute-start(bf16[2,400,128]{2,1,0:T(8,128)(2,1)S(1)} %get-tuple-element.52), channel_id=1, source_target_pairs={{0,2},{1,3},{2,0},{3,1},{4,6},{5,7},{6,4},{7,5},{8,10},{9,11},{10,... | collective-permute-start | bytes 614408 | tf_op jit(solution)/shard_map/ppermute | solution.py:20
  69.7 2.9 %copy-start.6 = (bf16[384,512]{1,0:T(8,128)(2,1)}, bf16[384,512]{1,0:T(8,128)(2,1)S(1)}, u32[]{:S(2)}) copy-start(bf16[384,512]{1,0:T(8,128)(2,1)S(1)} %get-tuple-element.45.q_ref) | copy-start | bytes 1179652
  71.4 1.2 copy-start.9
  71.4 1.2 copy-start.17
  72.6 49.9 %copy-start.7 = (bf16[384,512]{1,0:T(8,128)(2,1)S(1)}, bf16[384,512]{1,0:T(8,128)(2,1)}, u32[]{:S(2)}) copy-start(bf16[384,512]{1,0:T(8,128)(2,1)} %copy-done.6) | copy-start | bytes 1179652
  104.7 17.9 %all-to-all-start.1 = ((bf16[32,16,640]{2,1,0:T(8,128)(2,1)}), bf16[32,16,640]{2,1,0:T(8,128)(2,1)S(1)}, u32[]{:S(2)}, u32[]{:S(2)}) async-start(bf16[32,16,640]{2,1,0:T(8,128)(2,1)} %shard_map.92), calls=%async_computation.1 | async-start | bytes 1310720 | tf_op jit(solution)/shard_map/all_to_all | solution.py:607
  109.6 1.1 copy-start.10
  122.6 0.9 copy-start.18
  125.0 12.1 %collective-permute-start.9 = (bf16[192,1024]{1,0:T(8,128)(2,1)S(1)}, bf16[192,1024]{1,0:T(8,128)(2,1)S(1)}, u32[]{:S(2)}, u32[]{:S(2)}) collective-permute-start(bf16[192,1024]{1,0:T(8,128)(2,1)S(1)} %get-tuple-element.58.refs_0_), channel_id=1, source_target_pairs={{0,1},{1,2},{2,3},{3,0},{4,5},{5,6},{6,7},{7,4},{8,9},{9,10},{10,1... | collective-permute-start | bytes 1179656 | tf_op jit(solution)/shard_map/ppermute | solution.py:20
  125.6 11.5 %collective-permute-start.10 = (bf16[192,1024]{1,0:T(8,128)(2,1)S(1)}, bf16[192,1024]{1,0:T(8,128)(2,1)S(1)}, u32[]{:S(2)}, u32[]{:S(2)}) collective-permute-start(bf16[192,1024]{1,0:T(8,128)(2,1)S(1)} %get-tuple-element.59.refs_1_), channel_id=1, source_target_pairs={{0,3},{1,0},{2,1},{3,2},{4,7},{5,4},{6,5},{7,6},{8,11},{9,8},{10,9... | collective-permute-start | bytes 1179656 | tf_op jit(solution)/shard_map/ppermute | solution.py:20
  132.6 12.9 %collective-permute-start.14 = (bf16[192,1024]{1,0:T(8,128)(2,1)}, bf16[192,1024]{1,0:T(8,128)(2,1)}, u32[]{:S(2)}, u32[]{:S(2)}) collective-permute-start(bf16[192,1024]{1,0:T(8,128)(2,1)} %get-tuple-element.64), channel_id=1, source_target_pairs={{0,3},{1,0},{2,1},{3,2},{4,7},{5,4},{6,5},{7,6},{8,11},{9,8},{10,9... | collective-permute-start | bytes 1179656 | tf_op jit(solution)/shard_map/ppermute | solution.py:20
  133.0 12.4 %collective-permute-start.13 = (bf16[192,1024]{1,0:T(8,128)(2,1)}, bf16[192,1024]{1,0:T(8,128)(2,1)}, u32[]{:S(2)}, u32[]{:S(2)}) collective-permute-start(bf16[192,1024]{1,0:T(8,128)(2,1)} %get-tuple-element.61.refs_2_), channel_id=1, source_target_pairs={{0,1},{1,2},{2,3},{3,0},{4,5},{5,6},{6,7},{7,4},{8,9},{9,10},{10,1... | collective-permute-start | bytes 1179656 | tf_op jit(solution)/shard_map/ppermute | solution.py:20
  138.1 15.6 %collective-permute-start.11 = (bf16[192,1024]{1,0:T(8,128)(2,1)}, bf16[192,1024]{1,0:T(8,128)(2,1)S(1)}, u32[]{:S(2)}, u32[]{:S(2)}) collective-permute-start(bf16[192,1024]{1,0:T(8,128)(2,1)} %get-tuple-element.62), channel_id=1, source_target_pairs={{0,1},{1,2},{2,3},{3,0},{4,5},{5,6},{6,7},{7,4},{8,9},{9,10},{10,1... | collective-permute-start | bytes 1179656 | tf_op jit(solution)/shard_map/ppermute | solution.py:20
  139.3 14.5 %collective-permute-start.12 = (bf16[192,1024]{1,0:T(8,128)(2,1)}, bf16[192,1024]{1,0:T(8,128)(2,1)S(1)}, u32[]{:S(2)}, u32[]{:S(2)}) collective-permute-start(bf16[192,1024]{1,0:T(8,128)(2,1)} %get-tuple-element.63), channel_id=1, source_target_pairs={{0,3},{1,0},{2,1},{3,2},{4,7},{5,4},{6,5},{7,6},{8,11},{9,8},{10,9... | collective-permute-start | bytes 1179656 | tf_op jit(solution)/shard_map/ppermute | solution.py:20
  145.5 13.0 %copy-start.1 = (bf16[4096,2,8]{0,2,1:T(8,128)(2,1)S(1)}, bf16[4096,2,8]{0,2,1:T(8,128)(2,1)}, u32[]{:S(2)}) copy-start(bf16[4096,2,8]{0,2,1:T(8,128)(2,1)} %param.12) | copy-start | bytes 393220
Sparse Core Ops, SparseCore 0:
  50.4 63.8 all-gather.2

commit v4 on v3

v4 whole, which is shorter than its diff:
```python
import functools

import jax
import jax.numpy as jnp
from jax import lax
from jax.experimental import pallas as pl
from jax.experimental.pallas import tpu as pltpu
from jax.sharding import PartitionSpec as P

F32 = jnp.float32
BF16 = jnp.bfloat16
LANES = 128
NEVER = -1e30
BLOCK = 512
AHEAD = 4


def around(x, distance):
    n = lax.axis_size("val")
    return lax.ppermute(x, "val", [(i, (i + distance) % n) for i in range(n)])


def params(mib=48):
    return pltpu.CompilerParams(vmem_limit_bytes=mib * 1024 * 1024)


def cost(flops, nbytes, exps=0):
    return pl.CostEstimate(flops=flops, bytes_accessed=nbytes, transcendentals=exps)


class Ring:
    def __init__(self, plus, minus, later):
        self.plus, self.minus = around(plus, 1), around(minus, -1)
        self.later = later

    def second(self, after):
        plus, minus = moved(self.later, [[(1, 0, 0)], [(0, 0, 0)]], after)
        self.sent = plus
        self.left = (self.plus, around(plus, 1))
        self.right = (around(minus, -1), self.minus)

    def forward(self, after=()):
        half = self.later[0].shape[0]
        plus, minus = moved(
            [self.plus, self.minus], [[(0, 0, half)], [(1, 0, half)]], [self.sent, *after]
        )
        self.opposite = (around(plus, 1), around(minus, -1))


def moved_kernel(n, n_after, plan, *refs):
    sources, outs = refs[:n], refs[n + n_after :]
    for out, parts in zip(outs, plan):
        at = 0
        for source, first, count in parts:
            count = count or sources[source].shape[0] - first
            out[at : at + count] = sources[source][first : first + count]
            at += count


def moved(arrays, plan, after):
    shapes = [sum(c or arrays[n].shape[0] - f for n, f, c in parts) for parts in plan]
    anywhere, vmem = (pl.BlockSpec(memory_space=m) for m in (pl.ANY, pltpu.VMEM))
    return pl.pallas_call(
        functools.partial(moved_kernel, len(arrays), len(after), plan),
        in_specs=[vmem] * len(arrays) + [anywhere] * len(after),
        out_specs=[vmem] * len(plan),
        out_shape=[
            jax.ShapeDtypeStruct((n, arrays[0].shape[1]), arrays[0].dtype) for n in shapes
        ],
        compiler_params=params(),
        cost_estimate=cost(0, 4 * sum(shapes) * arrays[0].shape[1]),
    )(*arrays, *after)


def packed_kernel(scalars, x_ref, w_ref, plus, minus, across, kept, sems):
    rows, cols = x_ref.shape
    half, part = rows // 2, kept.shape[0]
    copies = Copies(sems)
    me, n = scalars[1], w_ref.shape[1] // cols

    def piece(to):
        at = pl.multiple_of(scalars[0] * part, part)
        columns = pl.ds(pl.multiple_of(lax.rem(me + to, n) * cols, cols), cols)
        return w_ref.at[pl.ds(at, part), columns]

    started = [
        copies.start(piece(1), plus.at[pl.ds(half, part)]),
        copies.start(piece(n - 1), minus.at[pl.ds(half, part)]),
        copies.start(piece(2), across),
        copies.start(piece(0), kept),
    ]
    plus[:half] = x_ref[:half]
    minus[:half] = x_ref[half:]
    for copy in started:
        copy.wait()


def packed(x, w, place, me, part):
    rows, cols = x.shape
    shapes = [(rows // 2 + part, cols)] * 2 + [(part, cols)] * 2
    return pl.pallas_call(
        packed_kernel,
        in_specs=[pl.BlockSpec(memory_space=m) for m in (pltpu.SMEM, pltpu.VMEM, pl.ANY)],
        out_specs=[pl.BlockSpec(memory_space=pltpu.VMEM)] * 4,
        out_shape=[jax.ShapeDtypeStruct(shape, x.dtype) for shape in shapes],
        scratch_shapes=[pltpu.SemaphoreType.DMA((4,))],
        compiler_params=params(),
        cost_estimate=cost(0, 8 * x.size),
    )(jnp.stack([place, me]), x, w)


def flat_kernel(n, w_ref, *refs):
    refs[-2][...] = w_ref[...].reshape(refs[-2].shape)
    refs[-1][...] = jnp.zeros_like(refs[-1])


def flat(w, turn, before=None):
    rows, heads, size = w.shape
    steps = 4
    block = rows // (2 * steps)
    args = [w] if before is None else [w, before]
    return pl.pallas_call(
        functools.partial(flat_kernel, len(args)),
        grid=(steps,),
        in_specs=[
            pl.BlockSpec((block, heads, size), lambda j: (j + turn * steps, 0, 0)),
            pl.BlockSpec(memory_space=pl.ANY),
        ][: len(args)],
        out_specs=[
            pl.BlockSpec((block, heads * size), lambda j: (j + turn * steps, 0)),
            pl.BlockSpec((8, LANES), lambda j: (0, 0)),
        ],
        out_shape=[
            jax.ShapeDtypeStruct((rows, heads * size), w.dtype),
            jax.ShapeDtypeStruct((8, LANES), F32),
        ],
        input_output_aliases={} if before is None else {1: 0},
        compiler_params=params(),
        cost_estimate=cost(0, 2 * w.size),
    )(*args)


class Copies:
    def __init__(self, sems):
        self.sems = sems
        self.used = 0

    def start(self, source, target):
        copy = pltpu.make_async_copy(source, target, self.sems.at[self.used])
        self.used += 1
        copy.start()
        return copy


class Loads:
    def __init__(self, ahead):
        self.ahead = ahead
        self.waiting = []
        self.started = []

    def add(self, start):
        self.waiting.append(start)

    def begin(self):
        while self.waiting and len(self.started) <= self.ahead:
            self.started.append(self.waiting.pop(0)())

    def next(self):
        self.begin()
        for copy in self.started.pop(0):
            copy.wait()


def put_rows(pieces, buffer):
    n = buffer.shape[0] // len(pieces)
    for at, piece in enumerate(pieces):
        buffer[at * n : (at + 1) * n] = piece[:n]


def fetch_weight(copies, w, chunk, columns, target, sources):
    if len(w.shape) == 2:
        n = target.shape[0]
        rows = pl.ds(pl.multiple_of(chunk * n, n), n)
        return [copies.start(w.at[rows, columns], target)]
    own, nval = target.shape[:2]
    started = []
    for h in range(own):
        for n in range(nval):
            source = w.at[chunk * own + h, :, n, :, columns]
            started.append(copies.start(source, target.at[h, sources[n]]))
    return started


def product_kernel(counts, tasks, with_total, n_after, staged, scalars, *refs):
    refs = list(refs)
    take = lambda n: [refs.pop(0) for _ in range(n)]
    ngroups, nweights = len(counts), 1 + max(n for _, segments in tasks for n, _ in segments)
    groups = [take(n) for n in counts]
    weights = take(nweights)
    totals = take(nweights) if with_total else None
    take(n_after)
    outs = take(nweights)
    x, ws = take(2)
    os = take(nweights) if staged else outs
    copies = Copies(refs[0])
    chunk = x.shape[1] // ngroups
    sources = [scalars[ngroups + n] for n in range(4)]
    part = lambda g: x.at[:, pl.ds(g * chunk, chunk)]

    def load(g, at, segments):
        started = []
        for n, columns in segments:
            target = ws.at[g, ..., pl.ds(at, columns.size)]
            started += fetch_weight(copies, weights[n], scalars[g], columns, target, sources)
            at += columns.size
        return started

    loads = Loads(AHEAD)
    for at, segments in tasks:
        for g in range(ngroups):
            loads.add(functools.partial(load, g, at, segments))
    loads.begin()
    for g in range(ngroups):
        put_rows(groups[g], part(g))
    last = []
    for at, segments in tasks:
        width = sum(columns.size for _, columns in segments)
        total = None
        for g in range(ngroups):
            loads.next()
            w = ws[g, ..., at : at + width].reshape(chunk, -1)
            term = jnp.dot(part(g)[...], w, preferred_element_type=F32)
            total = term if total is None else total + term
        at = 0
        for n, columns in segments:
            out = total[:, at : at + columns.size]
            if with_total:
                out = out + totals[n][:, columns]
            os[n][:, columns] = out.astype(os[n].dtype)
            if staged:
                last.append(copies.start(os[n].at[:, columns], outs[n].at[:, columns]))
            at += columns.size
    for copy in last:
        copy.wait()


def product(rows, groups, index, weights, totals, dtypes, sources, after=(), staged=False):
    chunk = groups[0][0].shape[1]
    widths = [w.shape[-1] for w in weights]
    tasks, held = [], 0
    for n, width in enumerate(widths):
        for at in range(0, width, BLOCK):
            tasks.append((held, [(n, pl.ds(at, min(BLOCK, width)))]))
            held += min(BLOCK, width)
    anywhere, vmem = (pl.BlockSpec(memory_space=m) for m in (pl.ANY, pltpu.VMEM))
    pieces = [x for g in groups for x in g]
    specs = [vmem] * len(pieces) + [anywhere] * len(weights)
    specs += [vmem] * len(totals or []) + [anywhere] * len(after)
    args = pieces + list(weights) + list(totals or []) + list(after)
    shape = (chunk, held)
    if weights[0].ndim > 2:
        heads, parts, nval, n, cols = weights[0].shape
        shape = (chunk // (parts * nval * n), nval, parts, n, cols)
    scratch = [pltpu.VMEM((rows, len(groups) * chunk), BF16)]
    scratch.append(pltpu.VMEM((len(groups), *shape), BF16))
    if staged:
        scratch += [pltpu.VMEM((rows, n), d) for n, d in zip(widths, dtypes)]
    copies = len(tasks) * (len(groups) * 8 + 2)
    scratch.append(pltpu.SemaphoreType.DMA((copies,)))
    cols = sum(widths)
    return pl.pallas_call(
        functools.partial(
            product_kernel,
            [len(g) for g in groups],
            tasks,
            totals is not None,
            len(after),
            staged,
        ),
        in_specs=[pl.BlockSpec(memory_space=pltpu.SMEM)] + specs,
        out_specs=[anywhere if staged else vmem] * len(weights),
        out_shape=[jax.ShapeDtypeStruct((rows, n), d) for n, d in zip(widths, dtypes)],
        scratch_shapes=scratch,
        compiler_params=params(),
        cost_estimate=cost(
            2 * rows * chunk * len(groups) * cols,
            2 * chunk * len(groups) * (cols + rows) + 4 * rows * cols,
        ),
    )(jnp.stack(list(index) + list(sources)), *args)


def values_kernel(scalars, upper, lower, w_ref, acc_ref, gain_ref, *refs):
    n = len(refs) - 3
    outs, (x, w, sems) = refs[:n], refs[n:]
    own, more, vlocal = outs[0].shape
    rows, block = acc_ref.shape[0], own * vlocal
    copies = Copies(sems)
    loads = Loads(AHEAD)
    order = [1, n - 1, *range(2, n - 1), 0]

    def spot(k):
        to = lax.rem(scalars[1] + k, n)
        return to, pl.ds(pl.multiple_of(to * block, block), block)

    for k in order:
        loads.add(lambda k=k: fetch_weight(copies, w_ref, scalars[0], spot(k)[1], w.at[k], None))
    loads.begin()
    put_rows((upper, lower), x)
    line = lax.broadcasted_iota(jnp.int32, (more - rows, vlocal), 0)
    for k in order:
        to, columns = spot(k)
        loads.next()
        total = acc_ref[:, columns] + jnp.dot(x[...], w[k], preferred_element_type=F32)
        total = total.astype(BF16)
        for h in range(own):
            outs[k][h, :rows] = total[:, h * vlocal : (h + 1) * vlocal]
            tail = jnp.zeros((more - rows, vlocal), F32)
            for m, part in enumerate(parts_of(gain_ref[pl.ds(to * own + h, 1), :])):
                tail = jnp.where(line == m, part, tail)
            outs[k][h, rows:] = tail.astype(BF16)


def values_by_device(halves, index, me, w, acc, gain, own):
    rows, cols = acc.shape
    chunk = halves[0].shape[1]
    vlocal = gain.shape[1]
    block = own * vlocal
    steps = cols // block
    shape = (own, rows + 16, vlocal)
    vmem = pl.BlockSpec(memory_space=pltpu.VMEM)
    return pl.pallas_call(
        values_kernel,
        in_specs=[
            pl.BlockSpec(memory_space=pltpu.SMEM),
            vmem,
            vmem,
            pl.BlockSpec(memory_space=pl.ANY),
            vmem,
            vmem,
        ],
        out_specs=[vmem] * steps,
        out_shape=[jax.ShapeDtypeStruct(shape, BF16)] * steps,
        scratch_shapes=[
            pltpu.VMEM((rows, chunk), BF16),
            pltpu.VMEM((steps, chunk, block), BF16),
            pltpu.SemaphoreType.DMA((steps,)),
        ],
        compiler_params=params(),
        cost_estimate=cost(2 * rows * chunk * cols, 2 * chunk * (cols + rows) + 6 * rows * cols),
    )(jnp.stack([index, me]), *halves, w, acc, gain)


def exchanged(pieces):
    return [pieces[0], around(pieces[1], 1), around(pieces[3], -1), around(pieces[2], 2)]


def within_kernel(counts, scalars, *refs):
    pieces = iter(refs[: sum(counts)])
    wg_ref, bias_ref, q_ref, k_ref, kwt_ref, p_ref, stat_ref, mark_ref = refs[sum(counts) :]
    own, rows, _ = p_ref.shape
    qsize = q_ref.shape[1] // own
    chunk = refs[0].shape[1]
    g = bias_ref[...]
    for n, count in enumerate(counts):
        w = wg_ref[pl.ds(pl.multiple_of(scalars[n] * chunk, chunk), chunk), :]
        terms = []
        for _ in range(count):
            x = next(pieces)[: rows // count]
            terms.append(jnp.dot(x, w, preferred_element_type=F32))
        g = g + (terms[0] if count == 1 else jnp.concatenate(terms, axis=0))
    logf = jnp.minimum(g, 0.0) - jnp.log1p(jnp.exp(-jnp.abs(g)))
    late = lax.broadcasted_iota(jnp.int32, (rows, rows), 0)
    early = lax.broadcasted_iota(jnp.int32, (rows, rows), 1)
    causal = late >= early
    cumb = jnp.dot(
        causal.astype(F32), logf, precision=lax.Precision.HIGHEST, preferred_element_type=F32
    )
    cumb = pltpu.roll(cumb, LANES - own, axis=1)
    gap = g - cumb
    gap_rows = gap.T
    most = jnp.max(gap, axis=0, keepdims=True)
    total = cumb[rows - 1 : rows]
    mark_ref[...] = jnp.concatenate([total + most, total, jnp.zeros((6, LANES), F32)], axis=0)
    lane = lax.broadcasted_iota(jnp.int32, (rows, LANES), 1)
    stat = jnp.zeros((rows, LANES), F32)
    for h in range(own):
        q = q_ref[:, h * qsize : (h + 1) * qsize]
        k = k_ref[:, h * qsize : (h + 1) * qsize]
        seen = jnp.where(causal, gap_rows[h : h + 1, :], F32(NEVER))
        high = jnp.max(seen, axis=1, keepdims=True)
        score = lax.dot_general(q, k, (((1,), (1,)), ((), ())), preferred_element_type=F32)
        wts = jnp.exp(seen - high) * (score * qsize ** (-0.5))
        wts = jnp.where(causal, wts, 0.0).astype(BF16)
        p_ref[h] = wts
        denom = jnp.sum(wts.astype(F32), axis=1, keepdims=True)
        stat = jnp.where(lane == h, high, jnp.where(lane == own + h, denom, stat))
        fall = jnp.exp(gap[:, h : h + 1] - most[:, h : h + 1])
        kw = (k.astype(F32) * fall).astype(BF16)
        kwt_ref[h * qsize : (h + 1) * qsize] = kw.astype(F32).T.astype(BF16)
    stat_ref[...] = stat


def within(groups, index, wg, bias, q, k, own):
    rows, width = q.shape
    pieces = [x for g in groups for x in g]
    vmem = pl.BlockSpec(memory_space=pltpu.VMEM)
    return pl.pallas_call(
        functools.partial(within_kernel, [len(g) for g in groups]),
        in_specs=[pl.BlockSpec(memory_space=pltpu.SMEM)] + [vmem] * (len(pieces) + 4),
        out_specs=[vmem] * 4,
        out_shape=[
            jax.ShapeDtypeStruct((width, rows), BF16),
            jax.ShapeDtypeStruct((own, rows, rows), BF16),
            jax.ShapeDtypeStruct((rows, LANES), F32),
            jax.ShapeDtypeStruct((8, LANES), F32),
        ],
        compiler_params=params(),
        cost_estimate=cost(4 * rows * rows * width, 8 * rows * width, own * rows * rows),
    )(jnp.stack(list(index)), *pieces, wg, bias, q, k)


def parts_of(x):
    hi = x.astype(BF16).astype(F32)
    mid = (x - hi).astype(BF16).astype(F32)
    return [hi, mid, x - hi - mid]


def of_head(head, rows):
    return jnp.where(head == 0, rows[:, 0:1], rows[:, 1:2])


def marked(extra, top, total):
    lane = lax.broadcasted_iota(jnp.int32, extra.shape, 1)
    for n, x in enumerate(parts_of(top) + ([] if total is None else parts_of(total))):
        extra = jnp.where(lane == 1 + n, x, extra)
    return extra


def marks_of(extra):
    top = extra[:, 1:2] + extra[:, 2:3] + extra[:, 3:4]
    total = extra[:, 4:5] + extra[:, 5:6] + extra[:, 6:7]
    return top, total


def summary_kernel(scalars, kwt_ref, mark_ref, v0, v1, v2, v3, mine, other, v_ref, gain_ref):
    vlocal = v0.shape[2]
    own, rows, vsize = v_ref.shape
    gain_ref[...] = jnp.zeros_like(gain_ref)
    qsize = kwt_ref.shape[0] // own
    for n, ref in enumerate((v0, v1, v2, v3)):
        at = pl.multiple_of(scalars[n] * vlocal, vlocal)
        for h in range(own):
            v_ref[h, :, pl.ds(at, vlocal)] = ref[h, :rows]
            tail = ref[h, rows:].astype(F32)
            gain_ref[h : h + 1, pl.ds(at, vlocal)] = tail[0:1] + tail[1:2] + tail[2:3]
    lane = lax.broadcasted_iota(jnp.int32, (qsize, LANES), 1)
    core = scalars[4]
    for h, out in ((core, mine), (1 - core, other)):
        kwt = kwt_ref[pl.ds(pl.multiple_of(h * qsize, qsize), qsize), :]
        out[:, :vsize] = jnp.dot(kwt, v_ref[h], preferred_element_type=F32).astype(BF16)
        extra = jnp.where(lane == 0, jnp.sum(kwt.astype(F32), axis=1, keepdims=True), 0.0)
        top, total = of_head(h, mark_ref[0:1, :]), of_head(h, mark_ref[1:2, :])
        out[:, vsize:] = marked(extra, top, total).astype(BF16)


def summary(index, core, kwt, mark, pieces):
    own, _, vlocal = pieces[0].shape
    rows = kwt.shape[1]
    vsize = vlocal * len(pieces)
    whole = lambda shape: pl.BlockSpec(shape, lambda j, s: (0,) * len(shape))
    shapes = [((kwt.shape[0] // own, vsize + LANES), BF16)] * 2
    shapes += [((own, rows, vsize), BF16), ((8, vsize), F32)]
    return pl.pallas_call(
        summary_kernel,
        grid_spec=pltpu.PrefetchScalarGridSpec(
            num_scalar_prefetch=1,
            grid=(1,),
            in_specs=[whole(kwt.shape), whole(mark.shape)] + [whole(x.shape) for x in pieces],
            out_specs=[whole(shape) for shape, _ in shapes],
        ),
        out_shape=[jax.ShapeDtypeStruct(shape, dtype) for shape, dtype in shapes],
        compiler_params=params(),
        cost_estimate=cost(2 * kwt.size * vsize, 3 * own * rows * vsize * 2),
    )(jnp.stack(list(index) + [core]), kwt, mark, *pieces)


def pair_kernel(scalars, mine, got, out):
    first = scalars[0] == 0
    body = mine.shape[1] - LANES
    a, b = mine[:, body:].astype(F32), got[:, body:].astype(F32)
    early, late = jnp.where(first, a, b), jnp.where(first, b, a)
    (etop, etotal), (ltop, ltotal) = marks_of(early), marks_of(late)
    top = jnp.maximum(etop + ltotal, ltop)
    fe, fl = jnp.exp(etop + ltotal - top), jnp.exp(ltop - top)
    fa, fb = jnp.where(first, fe, fl), jnp.where(first, fl, fe)
    state = fa * mine[:, :body].astype(F32) + fb * got[:, :body].astype(F32)
    out[:, :body] = state.astype(BF16)
    out[:, body:] = marked(fa * a + fb * b, top, etotal + ltotal).astype(BF16)


def pair(core, mine, got):
    vmem = pl.BlockSpec(memory_space=pltpu.VMEM)
    return pl.pallas_call(
        pair_kernel,
        in_specs=[pl.BlockSpec(memory_space=pltpu.SMEM), vmem, vmem],
        out_specs=vmem,
        out_shape=jax.ShapeDtypeStruct(mine.shape, BF16),
        compiler_params=params(),
        cost_estimate=cost(4 * mine.size, 6 * mine.size),
    )(jnp.stack([core]), mine, got)


def unpair_kernel(scalars, prefix, mine, got, keep, send):
    first = scalars[0] == 0
    body = mine.shape[1] - LANES
    p = prefix[:, body:].astype(F32)
    s = jnp.where(first, mine[:, body:].astype(F32), got[:, body:].astype(F32))
    ptop, _ = marks_of(p)
    stop, stotal = marks_of(s)
    top = jnp.maximum(ptop + stotal, stop)
    fp, fs = jnp.exp(ptop + stotal - top), jnp.exp(stop - top)
    state = jnp.where(first, mine[:, :body], got[:, :body]).astype(F32)
    state = (fp * prefix[:, :body].astype(F32) + fs * state).astype(BF16)
    extra = marked(fp * p + fs * s, top, None).astype(BF16)
    keep[:, :body] = jnp.where(first, prefix[:, :body], state)
    send[:, :body] = jnp.where(first, state, prefix[:, :body])
    keep[:, body:] = jnp.where(first, prefix[:, body:], extra)
    send[:, body:] = jnp.where(first, extra, prefix[:, body:])


def unpair(core, prefix, mine, got):
    vmem = pl.BlockSpec(memory_space=pltpu.VMEM)
    return pl.pallas_call(
        unpair_kernel,
        in_specs=[pl.BlockSpec(memory_space=pltpu.SMEM)] + [vmem] * 3,
        out_specs=[vmem] * 2,
        out_shape=[jax.ShapeDtypeStruct(mine.shape, BF16)] * 2,
        compiler_params=params(),
        cost_estimate=cost(4 * mine.size, 10 * mine.size),
    )(jnp.stack([core]), prefix, mine, got)


def inside_kernel(p_ref, v_ref, out_ref):
    for h in range(p_ref.shape[0]):
        out_ref[h] = jnp.dot(p_ref[h], v_ref[h], preferred_element_type=F32)


def inside(p, v):
    return pl.pallas_call(
        inside_kernel,
        out_shape=jax.ShapeDtypeStruct(v.shape, F32),
        compiler_params=params(),
        cost_estimate=cost(2 * p.size * v.shape[2], 6 * v.size),
    )(p, v)


def prefix_kernel(got_ref, out_ref):
    blocks, cut, width = got_ref.shape
    body = width - LANES
    lane = lax.broadcasted_iota(jnp.int32, (cut, LANES), 1)
    source = lax.broadcasted_iota(jnp.int32, (LANES, 2 * LANES), 0)
    target = lax.broadcasted_iota(jnp.int32, (LANES, 2 * LANES), 1)
    first = jnp.where(target < LANES, 1, 4)
    spread = ((source >= first) & (source < first + 3)).astype(F32).astype(BF16)
    marks = jnp.dot(
        got_ref[:, :, body:].reshape(blocks * cut, LANES), spread, preferred_element_type=F32
    )
    state = [jnp.zeros((cut, LANES), F32) for _ in range(width // LANES)]
    ptop = jnp.full((cut, LANES), NEVER, F32)
    for b in range(blocks):
        held = state[-1]
        for n, x in enumerate(parts_of(ptop)):
            held = jnp.where(lane == 1 + n, x, held)
        for n, x in enumerate(state[:-1] + [held]):
            out_ref[b, :, n * LANES : (n + 1) * LANES] = x.astype(BF16)
        if b == blocks - 1:
            break
        top = marks[b * cut : (b + 1) * cut, :LANES]
        total = marks[b * cut : (b + 1) * cut, LANES:]
        new = jnp.maximum(ptop + total, top)
        keep = jnp.exp(ptop + total - new)
        add = jnp.exp(top - new)
        state = [
            keep * x + add * got_ref[b, :, n * LANES : (n + 1) * LANES].astype(F32)
            for n, x in enumerate(state)
        ]
        ptop = new


def prefixes(got):
    return pl.pallas_call(
        prefix_kernel,
        out_shape=jax.ShapeDtypeStruct(got.shape, BF16),
        compiler_params=params(),
        cost_estimate=cost(4 * got.size, 4 * got.size),
    )(got)


def finish_kernel(scalars, q_ref, mine, got, numer_ref, stat_ref, gain_ref, upper, lower):
    own, rows, vsize = numer_ref.shape
    qsize = q_ref.shape[1] // own
    core = scalars[0]
    for h, prefix_ref in ((core, mine), (1 - core, got)):
        q = q_ref[:, pl.ds(pl.multiple_of(h * qsize, qsize), qsize)]
        inter = jnp.dot(q, prefix_ref[...], preferred_element_type=F32)
        ptop, _ = marks_of(prefix_ref[0:16, vsize:].astype(F32)[0:1])
        high = of_head(h, stat_ref[...])
        top = jnp.maximum(high, ptop)
        fade = jnp.exp(high - top)
        decay = jnp.exp(ptop - top) * qsize ** (-0.5)
        denom = of_head(h, stat_ref[:, own : 2 * own])
        denom = denom * fade + inter[:, vsize : vsize + 1] * decay
        share = 1.0 / jnp.maximum(jnp.abs(denom), 1.0)
        hidden = numer_ref[h] * (fade * share) + inter[:, :vsize] * (decay * share)
        mean = jnp.mean(hidden, axis=1, keepdims=True)
        msq = jnp.mean(hidden * hidden, axis=1, keepdims=True)
        gain = gain_ref[pl.ds(h, 1), :]
        normed = (hidden - mean) * lax.rsqrt(msq - mean * mean + 1e-06) * gain
        normed = normed.astype(BF16)
        columns = pl.ds(pl.multiple_of(h * vsize, vsize), vsize)
        upper[:, columns] = normed[: rows // 2]
        lower[:, columns] = normed[rows // 2 :]


def finish(core, q, mine, got, numer, stat, gain):
    own, rows, vsize = numer.shape
    vmem = pl.BlockSpec(memory_space=pltpu.VMEM)
    return pl.pallas_call(
        finish_kernel,
        in_specs=[pl.BlockSpec(memory_space=pltpu.SMEM)] + [vmem] * 6,
        out_specs=[vmem] * 2,
        out_shape=[jax.ShapeDtypeStruct((rows // 2, own * vsize), BF16)] * 2,
        compiler_params=params(),
        cost_estimate=cost(2 * q.size * vsize, 8 * numer.size),
    )(jnp.stack([core]), q, mine, got, numer, stat, gain)


def per_device(tokens, w_query, w_key, w_value, w_gate, gate_bias, norm_gain, w_out):
    me = lax.axis_index("val")
    nval = lax.axis_size("val")
    place = lax.axis_index("seq")
    blocks = lax.axis_size("seq")
    rows, chunk = tokens.shape
    width = w_query.shape[0]
    heads, vlocal = w_value.shape[1:]
    own = heads // nval
    qsize = w_query.shape[1] // own
    vsize = vlocal * nval
    index = [(me + d) % nval for d in (0, nval - 1, 1, 2)]

    part = heads * vlocal // blocks
    half = rows // 2
    plus, minus, across, kept = packed(
        tokens, w_out.reshape(heads * vlocal, -1), place, me, part
    )
    ring = Ring(plus, minus, [tokens[:half], tokens[half:]])
    across = around(across, 2)
    wg = lax.dynamic_slice_in_dim(w_gate, me * own, own, axis=2).reshape(width, 2 * own)
    wg = jnp.pad(wg, ((0, 0), (0, LANES - 2 * own)))
    bias = lax.dynamic_slice_in_dim(gate_bias, me * own, own, axis=1).reshape(1, 2 * own)
    bias = jnp.pad(bias, ((0, 0), (0, LANES - 2 * own)))
    wv, early = flat(w_value, 0)
    ring.second([early, wg])
    wv, late = flat(w_value, 1, wv)
    ring.forward([late])
    groups = [(tokens,), ring.left, ring.right]
    acc = product(rows, groups, index[:3], [wv], None, [F32], index)[0]
    values = values_by_device(ring.opposite, index[3], me, wv, acc, norm_gain, own)
    groups.append(ring.opposite)
    q, k = product(
        rows, groups, index, [w_query, w_key], None, [BF16] * 2, index, values[:1]
    )
    cuts = [(0, 0, 0), (1, half, part), (2, half, part), (3, 0, 0)]
    wo = moved([kept, ring.plus, ring.minus, across], [cuts], [early])[0]
    wo = lax.all_gather(wo, "seq", axis=0)
    wo = wo.reshape(heads, blocks // heads, nval, part, chunk)

    values = exchanged(values)
    kwt, p, stat, mark = within(groups, index, wg, bias, q, k, own)
    core = place % 2
    mine, other, v, gain = summary(index, core, kwt, mark, values)
    cores = [(i, i ^ 1) for i in range(blocks)]
    got = lax.ppermute(other, "seq", cores)
    chips = [list(range(n, blocks, 2)) for n in range(2)]
    sliced = (blocks // 2, -1, vsize + LANES)
    both = pair(core, mine, got).reshape(sliced)
    both = lax.all_to_all(both, "seq", 0, 0, axis_index_groups=chips)
    numer = inside(p, v)
    prefix = lax.all_to_all(prefixes(both), "seq", 0, 0, axis_index_groups=chips)
    keep, send = unpair(core, prefix.reshape(mine.shape), mine, got)
    came = lax.ppermute(send, "seq", cores)
    upper, lower = finish(core, q, keep, came, numer, stat, gain)

    ring = Ring(upper, lower, [upper, lower])
    accs = product(rows, [(upper, lower)], index[:1], [wo], None, [F32], index)
    ring.second(accs)
    ring.forward()
    accs = product(rows, [ring.left, ring.right], index[1:3], [wo], accs, [F32], index)
    return product(rows, [ring.opposite], index[3:], [wo], accs, [BF16], index, staged=True)[0]


def solution(mesh):
    placed = (
        P("seq", "val"),
        P(None, "val"),
        P(None, "val"),
        P(None, None, "val"),
        P(),
        P(),
        P(None, "val"),
        P(None, "val", None),
    )
    return jax.shard_map(
        per_device, mesh=mesh, in_specs=placed, out_specs=P("seq", "val"), check_vma=False
    )
```

time: 166 us -> 148 us (0.89)
  local copies, waits for them, and re-layouts: 13.1 us -> 4.76 us
  waiting for transfers between devices: 26.2 us -> 18 us
  starting transfers between devices: 22.5 us -> 29.7 us
  Pallas kernels: 58.7 us -> 53.9 us
  blocking collectives: 30.7 us -> 26.7 us
    all_to_all x1 -> x0, waiting for transfers between devices: 11.3 us -> none  [per_device(): prefix = lax.all_to_all(prefixes(got), 'seq', 0, 0)]
    unnamed x42 -> x14, local copies, waits for them, and re-layouts: 8.58 us -> 1.16 us
    ppermute x0 -> x2, starting transfers between devices: none -> 7.3 us  [the longest x1 4.27 us: per_device(): got = lax.ppermute(other, 'seq', cores)]
    pallas_call x5, Pallas kernels: 30.8 us -> 25.4 us  [product(): pl.pallas_call(functools.partial(product_kernel, [len(g) for g in groups]...]
    all_to_all x1 -> x0, starting transfers between devices: 4.96 us -> none  [per_device(): prefix = lax.all_to_all(prefixes(got), 'seq', 0, 0)]
    ppermute x15 -> x16, starting transfers between devices: 17.6 us -> 22.4 us  [around(): return lax.ppermute(x, 'val', [(i, (i + distance) % n) for i in range(n)])]
    all_to_all x1 -> x2, blocking collectives: 30.7 us -> 26.7 us  [the longest x1 15.2 us: per_device(): both = lax.all_to_all(both, 'seq', 0, 0, axis_index_groups=chips)]
    pallas_call x3 -> x5, Pallas kernels: 5.85 us -> 8.32 us  [the longest x1 4 us: within(): pl.pallas_call(functools.partial(within_kernel, [len(g) for g in groups])...]
  transfers between devices with their start and end apart: 17 -> 19, of which waited for: 6 -> 7; matrix products, arithmetic and copies ran while one was open for 3% -> 3% of each run, Pallas kernels for 30% -> 32%
where the time goes in v4:
time: 148 us; the launch traced here: 147 us
  Pallas kernels  53.9 us (36%)
  starting transfers between devices  29.7 us (20%)
  blocking collectives  26.7 us (18%)
  waiting for transfers between devices  18 us (12%)
  between operations  13.6 us (9%)
  local copies, waits for them, and re-layouts  4.76 us (3%)
    pallas_call x5, Pallas kernels, product(): pl.pallas_call(functools.partial(product_kernel, [len(g) for g in groups]...  25.4 us
    ppermute x16, starting transfers between devices, around(): return lax.ppermute(x, 'val', [(i, (i + distance) % n) for i in range(n)])  22.4 us
    ppermute x16, waiting for transfers between devices, around(): return lax.ppermute(x, 'val', [(i, (i + distance) % n) for i in range(n)])  16 us
    all_to_all x1, blocking collectives, per_device(): both = lax.all_to_all(both, 'seq', 0, 0, axis_index_groups=chips)  15.2 us
    all_to_all x1, blocking collectives, per_device(): lax.all_to_all(prefixes(both), 'seq', 0, 0, axis_index_groups=chips)  11.5 us
    pallas_call x2, Pallas kernels, flat(): pl.pallas_call(functools.partial(flat_kernel, len(args)), grid=(steps,),...  9.63 us
    pallas_call x5, Pallas kernels, moved(): pl.pallas_call(functools.partial(moved_kernel, len(arrays), len(after), p...  4.64 us
    ppermute x1, starting transfers between devices, per_device(): got = lax.ppermute(other, 'seq', cores)  4.27 us
  transfers between devices with their start and end apart: 19, of which 7 were waited for; matrix products, arithmetic and copies ran while one was open for 3% of the time, Pallas kernels for 32%

profile of v4, /device:TPU:1, one launch (start us, length us, event | category | flops | bytes accessed | tf_op | source)
XLA Modules:
  0.0 146.9 jit_solution(8901352006860383084)
XLA Ops:
  6.6 1.1 copy-done.2
  7.7 1.5 %shard_map.82 = (bf16[224,1024]{1,0:T(8,128)(2,1)S(1)}, bf16[224,1024]{1,0:T(8,128)(2,1)S(1)}, bf16[32,1024]{1,0:T(8,128)(2,1)S(1)}, bf16[32,1024]{1,0:T(8,128)(2,1)S(1)}) custom-call(s32[2]{0:T(128)S(1)} %pad_add_fusion.scalars, bf16[384,1024]{1,0:T(8,128)(2,1)S(1)} %copy-done.2, bf16[1024,4096]{1,0:T(8,128)(2,1)} %bitcast.18), custom_call_target="tpu_custom_call" | custom-call | bytes 3145728 | tf_op jit(solution)/shard_map/pallas_call | solution.py:101
  9.3 2.2 %collective-permute-start = (bf16[224,1024]{1,0:T(8,128)(2,1)S(1)}, bf16[224,1024]{1,0:T(8,128)(2,1)S(1)}, u32[]{:S(2)}, u32[]{:S(2)}) collective-permute-start(bf16[224,1024]{1,0:T(8,128)(2,1)S(1)} %get-tuple-element.39), channel_id=1, source_target_pairs={{0,1},{1,2},{2,3},{3,0},{4,5},{5,6},{6,7},{7,4},{8,9},{9,10},{10,1... | collective-permute-start | bytes 1376264 | tf_op jit(solution)/shard_map/ppermute | solution.py:20
  11.5 1.5 %collective-permute-start.3 = (bf16[224,1024]{1,0:T(8,128)(2,1)S(1)}, bf16[224,1024]{1,0:T(8,128)(2,1)S(1)}, u32[]{:S(2)}, u32[]{:S(2)}) collective-permute-start(bf16[224,1024]{1,0:T(8,128)(2,1)S(1)} %get-tuple-element.43), channel_id=1, source_target_pairs={{0,3},{1,0},{2,1},{3,2},{4,7},{5,4},{6,5},{7,6},{8,11},{9,8},{10,9... | collective-permute-start | bytes 1376264 | tf_op jit(solution)/shard_map/ppermute | solution.py:20
  13.0 1.6 %collective-permute-start.13 = (bf16[32,1024]{1,0:T(8,128)(2,1)S(1)}, bf16[32,1024]{1,0:T(8,128)(2,1)S(1)}, u32[]{:S(2)}, u32[]{:S(2)}) collective-permute-start(bf16[32,1024]{1,0:T(8,128)(2,1)S(1)} %get-tuple-element.68), channel_id=1, source_target_pairs={{0,2},{1,3},{2,0},{3,1},{4,6},{5,7},{6,4},{7,5},{8,10},{9,11},{10,... | collective-permute-start | bytes 196616 | tf_op jit(solution)/shard_map/ppermute | solution.py:20
  14.6 4.8 %shard_map.83 = (bf16[4096,1024]{1,0:T(8,128)(2,1)}, f32[8,128]{1,0:T(8,128)S(1)}) custom-call(bf16[4096,8,128]{2,1,0:T(8,128)(2,1)} %w_ref.3), custom_call_target="tpu_custom_call" | custom-call | bytes 8388608 | tf_op jit(solution)/shard_map/pallas_call | solution.py:122
  19.4 5.7 %collective-permute-done.13.refs_3_ = bf16[32,1024]{1,0:T(8,128)(2,1)S(1)} collective-permute-done((bf16[32,1024]{1,0:T(8,128)(2,1)S(1)}, bf16[32,1024]{1,0:T(8,128)(2,1)S(1)}, u32[]{:S(2)}, u32[]{:S(2)}) %collective-permute-start.13) | collective-permute-done | bytes 65568 | tf_op jit(solution)/shard_map/ppermute | solution.py:20
  25.1 0.7 shard_map.97
  26.0 1.4 copy.11
  27.4 1.4 pad.8.refs_3_.refs_7_
  28.9 1.1 shard_map.84
  30.0 0.5 collective-permute-start.1
  30.5 2.1 %collective-permute-start.2 = (bf16[192,1024]{1,0:T(8,128)(2,1)}, bf16[192,1024]{1,0:T(8,128)(2,1)}, u32[]{:S(2)}, u32[]{:S(2)}) collective-permute-start(bf16[192,1024]{1,0:T(8,128)(2,1)} %get-tuple-element.42), channel_id=1, source_target_pairs={{0,3},{1,0},{2,1},{3,2},{4,7},{5,4},{6,5},{7,6},{8,11},{9,8},{10,9... | collective-permute-start | bytes 1179656 | tf_op jit(solution)/shard_map/ppermute | solution.py:20
  32.6 4.8 %shard_map.85 = (bf16[4096,1024]{1,0:T(8,128)(2,1)}, f32[8,128]{1,0:T(8,128)S(1)}) custom-call(bf16[4096,8,128]{2,1,0:T(8,128)(2,1)} %w_ref.3, bf16[4096,1024]{1,0:T(8,128)(2,1)} %get-tuple-element.44.refs_0_), custom_call_target="tpu_custom_call", output_to_operand_aliasing={{0}: (1, {})} | custom-call | bytes 8388608 | tf_op jit(solution)/shard_map/pallas_call | solution.py:122
  37.5 0.9 shard_map.86
  38.5 2.7 %collective-permute-start.5 = (bf16[192,1024]{1,0:T(8,128)(2,1)}, bf16[192,1024]{1,0:T(8,128)(2,1)S(1)}, u32[]{:S(2)}, u32[]{:S(2)}) collective-permute-start(bf16[192,1024]{1,0:T(8,128)(2,1)} %get-tuple-element.47), channel_id=1, source_target_pairs={{0,3},{1,0},{2,1},{3,2},{4,7},{5,4},{6,5},{7,6},{8,11},{9,8},{10,9... | collective-permute-start | bytes 1179656 | tf_op jit(solution)/shard_map/ppermute | solution.py:20
  41.6 6.0 %shard_map.87.acc_ref = f32[384,1024]{1,0:T(8,128)S(1)} custom-call(s32[7]{0:T(128)S(1)} %stack.43.scalars, bf16[384,1024]{1,0:T(8,128)(2,1)S(1)} %copy-done.3, bf16[224,1024]{1,0:T(8,128)(2,1)S(1)} %collective-permute-done.refs_0_.refs_1_, bf16[192,1024]{1,0:T(8,128)(2,1)S(1)} %collective-permute-done.1.refs_2_, ...), custom_call_target="tpu_custom_call" | custom-call | flops 2415919104 | bytes 10223616 | tf_op jit(solution)/shard_map/pallas_call | solution.py:271
  47.7 0.5 collective-permute-done.4.upper.refs_5_
  48.2 3.9 %shard_map.88 = (bf16[2,400,128]{2,1,0:T(8,128)(2,1)S(1)}, bf16[2,400,128]{2,1,0:T(8,128)(2,1)S(1)}, bf16[2,400,128]{2,1,0:T(8,128)(2,1)S(1)}, bf16[2,400,128]{2,1,0:T(8,128)(2,1)S(1)}) custom-call(s32[2]{0:T(128)S(1)} %pad_add_fusion.1.scalars, bf16[192,1024]{1,0:T(8,128)(2,1)S(1)} %collective-permute-done.4.upper.refs_5_, ...), custom_call_target="tpu_custom_call" | custom-call | flops 805306368 | bytes 5242880 | tf_op jit(solution)/shard_map/pallas_call | solution.py:331
  52.1 2.7 %collective-permute-start.7 = (bf16[2,400,128]{2,1,0:T(8,128)(2,1)S(1)}, bf16[2,400,128]{2,1,0:T(8,128)(2,1)S(1)}, u32[]{:S(2)}, u32[]{:S(2)}) collective-permute-start(bf16[2,400,128]{2,1,0:T(8,128)(2,1)S(1)} %get-tuple-element.55), channel_id=1, source_target_pairs={{0,3},{1,0},{2,1},{3,2},{4,7},{5,4},{6,5},{7,6},{8,11},{9,8},{10,9... | collective-permute-start | bytes 614408 | tf_op jit(solution)/shard_map/ppermute | solution.py:20
  54.8 0.9 collective-permute-start.8
  55.7 7.1 %shard_map.89 = (bf16[384,512]{1,0:T(8,128)(2,1)S(1)}, bf16[384,512]{1,0:T(8,128)(2,1)S(1)}) custom-call(s32[8]{0:T(128)S(1)} %stack.38.scalars, bf16[384,1024]{1,0:T(8,128)(2,1)S(1)} %copy-done.3, bf16[224,1024]{1,0:T(8,128)(2,1)S(1)} %collective-permute-done.refs_0_.refs_1_, bf16[192,1024]{1,0:T(8,128)(2,1)S(1)} %collective-permute-done.1.refs_2_, ...), custom_call_target="tpu_custom_call" | custom-call | flops 3221225472 | bytes 13107200 | tf_op jit(solution)/shard_map/pallas_call | solution.py:271
  62.8 4.0 %shard_map.90 = (bf16[512,384]{1,0:T(8,128)(2,1)S(1)}, bf16[2,384,384]{2,1,0:T(8,128)(2,1)S(1)}, f32[384,128]{1,0:T(8,128)S(1)}, f32[8,128]{1,0:T(8,128)S(1)}) custom-call(s32[4]{0:T(128)S(1)} %pad_add_fusion.2.scalars, bf16[384,1024]{1,0:T(8,128)(2,1)S(1)} %copy-done.3, bf16[224,1024]{1,0:T(8,128)(2,1)S(1)} %collective-permute-done.refs_0_.refs_1_, ...), custom_call_target="tpu_custom_call" | custom-call | flops 301989888 | bytes 1572864 | tf_op jit(solution)/shard_map/pallas_call | solution.py:407
  66.8 1.1 shard_map.91
  68.0 4.3 %collective-permute-start.9 = (bf16[256,640]{1,0:T(8,128)(2,1)S(1)}, bf16[256,640]{1,0:T(8,128)(2,1)S(1)}, u32[]{:S(2)}, u32[]{:S(2)}) collective-permute-start(bf16[256,640]{1,0:T(8,128)(2,1)S(1)} %get-tuple-element.58), channel_id=1, source_target_pairs={{0,4},{4,0},{8,12},{12,8},{16,20},{20,16},{24,28},{28,24},{32,36},... | collective-permute-start | bytes 983048 | tf_op jit(solution)/shard_map/ppermute | solution.py:683
  72.3 1.3 collective-permute-done.9.got
  73.5 0.5 shard_map.92
  74.0 15.2 %all_to_all.10.got_ref = bf16[16,16,640]{2,1,0:T(8,128)(2,1)S(1)} all-to-all(bf16[16,16,640]{2,1,0:T(8,128)(2,1)S(1)} %bitcast.14), channel_id=1, replica_groups={{0,8,16,24,32,40,48,56,64,72,80,88,96,104,112,120},{4,12,20,28,36,44,52..., dimensions={0} | all-to-all | bytes 655360 | tf_op jit(solution)/shard_map/all_to_all | solution.py:687
  89.3 0.3 shard_map.93
  89.6 11.5 %all_to_all.11 = bf16[16,16,640]{2,1,0:T(8,128)(2,1)S(1)} all-to-all(bf16[16,16,640]{2,1,0:T(8,128)(2,1)S(1)} %shard_map.93), channel_id=1, replica_groups={{0,8,16,24,32,40,48,56,64,72,80,88,96,104,112,120},{4,12,20,28,36,44,52..., dimensions={0} | all-to-all | bytes 655360 | tf_op jit(solution)/shard_map/all_to_all | solution.py:689
  101.1 0.5 shard_map.94
  101.6 3.0 %collective-permute-start.10 = (bf16[256,640]{1,0:T(8,128)(2,1)S(1)}, bf16[256,640]{1,0:T(8,128)(2,1)S(1)}, u32[]{:S(2)}, u32[]{:S(2)}) collective-permute-start(bf16[256,640]{1,0:T(8,128)(2,1)S(1)} %get-tuple-element.60), channel_id=1, source_target_pairs={{0,4},{4,0},{8,12},{12,8},{16,20},{20,16},{24,28},{28,24},{32,36},... | collective-permute-start | bytes 983048 | tf_op jit(solution)/shard_map/ppermute | solution.py:691
  104.6 0.6 shard_map.95.numer_ref
  105.2 0.7 collective-permute-done.10.got
  105.9 1.8 %shard_map.96 = (bf16[192,1024]{1,0:T(8,128)(2,1)S(1)}, bf16[192,1024]{1,0:T(8,128)(2,1)S(1)}) custom-call(s32[1]{0:T(128)} %bitcast.4.scalars, bf16[384,512]{1,0:T(8,128)(2,1)S(1)} %get-tuple-element.50.refs_9_.q_ref, bf16[256,640]{1,0:T(8,128)(2,1)S(1)} %get-tuple-element.59.mine, bf16[256,640]{1,0:T(8,128)(2,1)S(1)} %collective-permute-done.10.got, ...), custom_call_target="tpu_custom_call" | custom-call | flops 201326592 | bytes 3145728 | tf_op jit(solution)/shard_map/pallas_call | solution.py:628
  107.7 1.2 collective-permute-start.11
  108.9 1.5 %collective-permute-start.12 = (bf16[192,1024]{1,0:T(8,128)(2,1)S(1)}, bf16[192,1024]{1,0:T(8,128)(2,1)S(1)}, u32[]{:S(2)}, u32[]{:S(2)}) collective-permute-start(bf16[192,1024]{1,0:T(8,128)(2,1)S(1)} %get-tuple-element.66.refs_1_), channel_id=1, source_target_pairs={{0,3},{1,0},{2,1},{3,2},{4,7},{5,4},{6,5},{7,6},{8,11},{9,8},{10,9... | collective-permute-start | bytes 1179656 | tf_op jit(solution)/shard_map/ppermute | solution.py:20
  110.5 3.2 %shard_map.98.refs_2_.refs_5_ = f32[384,1024]{1,0:T(8,128)S(1)} custom-call(s32[5]{0:T(128)S(1)} %stack.46.scalars, bf16[192,1024]{1,0:T(8,128)(2,1)S(1)} %get-tuple-element.65.refs_0_, bf16[192,1024]{1,0:T(8,128)(2,1)S(1)} %get-tuple-element.66.refs_1_, bf16[8,4,4,32,1024]{4,3,2,1,0:T(8,128)(2,1)} %bitcast.15), custom_call_target="tpu_custom_call" | custom-call | flops 805306368 | bytes 4456448 | tf_op jit(solution)/shard_map/pallas_call | solution.py:271
  113.7 1.0 shard_map.99
  114.6 2.7 %collective-permute-start.17 = (bf16[192,1024]{1,0:T(8,128)(2,1)}, bf16[192,1024]{1,0:T(8,128)(2,1)}, u32[]{:S(2)}, u32[]{:S(2)}) collective-permute-start(bf16[192,1024]{1,0:T(8,128)(2,1)} %get-tuple-element.72), channel_id=1, source_target_pairs={{0,3},{1,0},{2,1},{3,2},{4,7},{5,4},{6,5},{7,6},{8,11},{9,8},{10,9... | collective-permute-start | bytes 1179656 | tf_op jit(solution)/shard_map/ppermute | solution.py:20
  117.3 1.9 %collective-permute-done.11.refs_0_ = bf16[192,1024]{1,0:T(8,128)(2,1)S(1)} collective-permute-done((bf16[192,1024]{1,0:T(8,128)(2,1)S(1)}, bf16[192,1024]{1,0:T(8,128)(2,1)S(1)}, u32[]{:S(2)}, u32[]{:S(2)}) %collective-permute-start.11) | collective-permute-done | bytes 393248 | tf_op jit(solution)/shard_map/ppermute | solution.py:20
  119.2 0.9 shard_map.100
  120.2 0.3 collective-permute-start.14
  120.5 2.4 %collective-permute-start.15 = (bf16[192,1024]{1,0:T(8,128)(2,1)}, bf16[192,1024]{1,0:T(8,128)(2,1)S(1)}, u32[]{:S(2)}, u32[]{:S(2)}) collective-permute-start(bf16[192,1024]{1,0:T(8,128)(2,1)} %get-tuple-element.71), channel_id=1, source_target_pairs={{0,3},{1,0},{2,1},{3,2},{4,7},{5,4},{6,5},{7,6},{8,11},{9,8},{10,9... | collective-permute-start | bytes 1179656 | tf_op jit(solution)/shard_map/ppermute | solution.py:20
  123.0 4.7 %collective-permute-done.16.refs_1_ = bf16[192,1024]{1,0:T(8,128)(2,1)} collective-permute-done((bf16[192,1024]{1,0:T(8,128)(2,1)}, bf16[192,1024]{1,0:T(8,128)(2,1)}, u32[]{:S(2)}, u32[]{:S(2)}) %collective-permute-start.16) | collective-permute-done | bytes 393248 | tf_op jit(solution)/shard_map/ppermute | solution.py:20
  127.8 5.2 %shard_map.101.refs_3_ = f32[384,1024]{1,0:T(8,128)S(1)} custom-call(s32[6]{0:T(128)S(1)} %stack.47.scalars, bf16[192,1024]{1,0:T(8,128)(2,1)S(1)} %collective-permute-done.11.refs_0_, bf16[192,1024]{1,0:T(8,128)(2,1)} %collective-permute-done.16.refs_1_, bf16[192,1024]{1,0:T(8,128)(2,1)} %collective-permute-done.17.refs_2_, ...), custom_call_target="tpu_custom_call" | custom-call | flops 1610612736 | bytes 7340032 | tf_op jit(solution)/shard_map/pallas_call | solution.py:271
  133.0 3.1 %collective-permute-done.14.refs_0_ = bf16[192,1024]{1,0:T(8,128)(2,1)S(1)} collective-permute-done((bf16[192,1024]{1,0:T(8,128)(2,1)}, bf16[192,1024]{1,0:T(8,128)(2,1)S(1)}, u32[]{:S(2)}, u32[]{:S(2)}) %collective-permute-start.14) | collective-permute-done | bytes 393248 | tf_op jit(solution)/shard_map/ppermute | solution.py:20
  136.1 3.9 %shard_map.102 = bf16[384,1024]{1,0:T(8,128)(2,1)} custom-call(s32[5]{0:T(128)S(1)} %stack.36.scalars, bf16[192,1024]{1,0:T(8,128)(2,1)S(1)} %collective-permute-done.14.refs_0_, bf16[192,1024]{1,0:T(8,128)(2,1)S(1)} %collective-permute-done.15.refs_1_, bf16[8,4,4,32,1024]{4,3,2,1,0:T(8,128)(2,1)} %bitcast.17, f32[384,1024]{1,0:T(8,128)S(1)} %shard_map.101.refs_3_), custom_call_target="tpu_custom_call" | custom-call | flops 805306368 | bytes 4456448 | tf_op jit(solution)/shard_map/pallas_call | solution.py:271
  (45 shorter events, 1.2 us)
Async XLA Ops:
  6.5 19.3 %copy-start = (bf16[4096,2,8]{0,2,1:T(8,128)(2,1)S(1)}, bf16[4096,2,8]{0,2,1:T(8,128)(2,1)}, u32[]{:S(2)}) copy-start(bf16[4096,2,8]{0,2,1:T(8,128)(2,1)} %param.12) | copy-start | bytes 393220
  6.5 103.9 %all-gather.3.cloned.1.call-start = ((), (), s32[]{:S(2)}) async-start(), calls=%async_computation.2 | async-start | bytes 8650752 | tf_op jit(solution)/shard_map/all_gather | solution.py:675
  6.6 1.1 copy-start.2
  9.3 15.8 %collective-permute-start = (bf16[224,1024]{1,0:T(8,128)(2,1)S(1)}, bf16[224,1024]{1,0:T(8,128)(2,1)S(1)}, u32[]{:S(2)}, u32[]{:S(2)}) collective-permute-start(bf16[224,1024]{1,0:T(8,128)(2,1)S(1)} %get-tuple-element.39), channel_id=1, source_target_pairs={{0,1},{1,2},{2,3},{3,0},{4,5},{5,6},{6,7},{7,4},{8,9},{9,10},{10,1... | collective-permute-start | bytes 1376264 | tf_op jit(solution)/shard_map/ppermute | solution.py:20
  11.5 13.7 %collective-permute-start.3 = (bf16[224,1024]{1,0:T(8,128)(2,1)S(1)}, bf16[224,1024]{1,0:T(8,128)(2,1)S(1)}, u32[]{:S(2)}, u32[]{:S(2)}) collective-permute-start(bf16[224,1024]{1,0:T(8,128)(2,1)S(1)} %get-tuple-element.43), channel_id=1, source_target_pairs={{0,3},{1,0},{2,1},{3,2},{4,7},{5,4},{6,5},{7,6},{8,11},{9,8},{10,9... | collective-permute-start | bytes 1376264 | tf_op jit(solution)/shard_map/ppermute | solution.py:20
  13.0 12.1 %collective-permute-start.13 = (bf16[32,1024]{1,0:T(8,128)(2,1)S(1)}, bf16[32,1024]{1,0:T(8,128)(2,1)S(1)}, u32[]{:S(2)}, u32[]{:S(2)}) collective-permute-start(bf16[32,1024]{1,0:T(8,128)(2,1)S(1)} %get-tuple-element.68), channel_id=1, source_target_pairs={{0,2},{1,3},{2,0},{3,1},{4,6},{5,7},{6,4},{7,5},{8,10},{9,11},{10,... | collective-permute-start | bytes 196616 | tf_op jit(solution)/shard_map/ppermute | solution.py:20
  19.4 9.4 %copy-start.3 = (bf16[384,1024]{1,0:T(8,128)(2,1)S(1)}, bf16[384,1024]{1,0:T(8,128)(2,1)}, u32[]{:S(2)}) copy-start(bf16[384,1024]{1,0:T(8,128)(2,1)} %refs_0_.5) | copy-start | bytes 2359300
  28.8 8.6 %copy-start.4 = (bf16[4096,128]{1,0:T(8,128)(2,1)}, bf16[4096,128]{1,0:T(8,128)(2,1)S(1)}, u32[]{:S(2)}) copy-start(bf16[4096,128]{1,0:T(8,128)(2,1)S(1)} %pad.8.refs_3_.refs_7_) | copy-start | bytes 3145732
  30.0 11.7 %collective-permute-start.1 = (bf16[192,1024]{1,0:T(8,128)(2,1)}, bf16[192,1024]{1,0:T(8,128)(2,1)S(1)}, u32[]{:S(2)}, u32[]{:S(2)}) collective-permute-start(bf16[192,1024]{1,0:T(8,128)(2,1)} %get-tuple-element.41.refs_2_), channel_id=1, source_target_pairs={{0,1},{1,2},{2,3},{3,0},{4,5},{5,6},{6,7},{7,4},{8,9},{9,10},{10,1... | collective-permute-start | bytes 1179656 | tf_op jit(solution)/shard_map/ppermute | solution.py:20
  30.5 11.1 %collective-permute-start.2 = (bf16[192,1024]{1,0:T(8,128)(2,1)}, bf16[192,1024]{1,0:T(8,128)(2,1)}, u32[]{:S(2)}, u32[]{:S(2)}) collective-permute-start(bf16[192,1024]{1,0:T(8,128)(2,1)} %get-tuple-element.42), channel_id=1, source_target_pairs={{0,3},{1,0},{2,1},{3,2},{4,7},{5,4},{6,5},{7,6},{8,11},{9,8},{10,9... | collective-permute-start | bytes 1179656 | tf_op jit(solution)/shard_map/ppermute | solution.py:20
  32.6 4.8 %copy-start.6 = (f32[2,8]{1,0:T(2,128)S(1)}, f32[2,8]{1,0:T(2,128)}, u32[]{:S(2)}) copy-start(f32[2,8]{1,0:T(2,128)} %param.13) | copy-start | bytes 196
  38.5 9.7 %collective-permute-start.4 = (bf16[192,1024]{1,0:T(8,128)(2,1)}, bf16[192,1024]{1,0:T(8,128)(2,1)S(1)}, u32[]{:S(2)}, u32[]{:S(2)}) collective-permute-start(bf16[192,1024]{1,0:T(8,128)(2,1)} %get-tuple-element.46), channel_id=1, source_target_pairs={{0,1},{1,2},{2,3},{3,0},{4,5},{5,6},{6,7},{7,4},{8,9},{9,10},{10,1... | collective-permute-start | bytes 1179656 | tf_op jit(solution)/shard_map/ppermute | solution.py:20
  38.5 9.7 %collective-permute-start.5 = (bf16[192,1024]{1,0:T(8,128)(2,1)}, bf16[192,1024]{1,0:T(8,128)(2,1)S(1)}, u32[]{:S(2)}, u32[]{:S(2)}) collective-permute-start(bf16[192,1024]{1,0:T(8,128)(2,1)} %get-tuple-element.47), channel_id=1, source_target_pairs={{0,3},{1,0},{2,1},{3,2},{4,7},{5,4},{6,5},{7,6},{8,11},{9,8},{10,9... | collective-permute-start | bytes 1179656 | tf_op jit(solution)/shard_map/ppermute | solution.py:20
  41.6 6.6 %copy-start.5 = (f32[8,128]{1,0:T(8,128)S(1)}, f32[8,128]{1,0:T(8,128)}, u32[]{:S(2)}) copy-start(f32[8,128]{1,0:T(8,128)} %gain_ref.1) | copy-start | bytes 12292
  52.0 14.8 %collective-permute-start.6 = (bf16[2,400,128]{2,1,0:T(8,128)(2,1)S(1)}, bf16[2,400,128]{2,1,0:T(8,128)(2,1)S(1)}, u32[]{:S(2)}, u32[]{:S(2)}) collective-permute-start(bf16[2,400,128]{2,1,0:T(8,128)(2,1)S(1)} %get-tuple-element.54), channel_id=1, source_target_pairs={{0,1},{1,2},{2,3},{3,0},{4,5},{5,6},{6,7},{7,4},{8,9},{9,10},{10,1... | collective-permute-start | bytes 614408 | tf_op jit(solution)/shard_map/ppermute | solution.py:20
  52.1 14.7 %collective-permute-start.7 = (bf16[2,400,128]{2,1,0:T(8,128)(2,1)S(1)}, bf16[2,400,128]{2,1,0:T(8,128)(2,1)S(1)}, u32[]{:S(2)}, u32[]{:S(2)}) collective-permute-start(bf16[2,400,128]{2,1,0:T(8,128)(2,1)S(1)} %get-tuple-element.55), channel_id=1, source_target_pairs={{0,3},{1,0},{2,1},{3,2},{4,7},{5,4},{6,5},{7,6},{8,11},{9,8},{10,9... | collective-permute-start | bytes 614408 | tf_op jit(solution)/shard_map/ppermute | solution.py:20
  54.8 12.0 %collective-permute-start.8 = (bf16[2,400,128]{2,1,0:T(8,128)(2,1)S(1)}, bf16[2,400,128]{2,1,0:T(8,128)(2,1)S(1)}, u32[]{:S(2)}, u32[]{:S(2)}) collective-permute-start(bf16[2,400,128]{2,1,0:T(8,128)(2,1)S(1)} %get-tuple-element.56), channel_id=1, source_target_pairs={{0,2},{1,3},{2,0},{3,1},{4,6},{5,7},{6,4},{7,5},{8,10},{9,11},{10,... | collective-permute-start | bytes 614408 | tf_op jit(solution)/shard_map/ppermute | solution.py:20
  68.0 5.5 %collective-permute-start.9 = (bf16[256,640]{1,0:T(8,128)(2,1)S(1)}, bf16[256,640]{1,0:T(8,128)(2,1)S(1)}, u32[]{:S(2)}, u32[]{:S(2)}) collective-permute-start(bf16[256,640]{1,0:T(8,128)(2,1)S(1)} %get-tuple-element.58), channel_id=1, source_target_pairs={{0,4},{4,0},{8,12},{12,8},{16,20},{20,16},{24,28},{28,24},{32,36},... | collective-permute-start | bytes 983048 | tf_op jit(solution)/shard_map/ppermute | solution.py:683
  101.6 4.3 %collective-permute-start.10 = (bf16[256,640]{1,0:T(8,128)(2,1)S(1)}, bf16[256,640]{1,0:T(8,128)(2,1)S(1)}, u32[]{:S(2)}, u32[]{:S(2)}) collective-permute-start(bf16[256,640]{1,0:T(8,128)(2,1)S(1)} %get-tuple-element.60), channel_id=1, source_target_pairs={{0,4},{4,0},{8,12},{12,8},{16,20},{20,16},{24,28},{28,24},{32,36},... | collective-permute-start | bytes 983048 | tf_op jit(solution)/shard_map/ppermute | solution.py:691
  107.7 11.6 %collective-permute-start.11 = (bf16[192,1024]{1,0:T(8,128)(2,1)S(1)}, bf16[192,1024]{1,0:T(8,128)(2,1)S(1)}, u32[]{:S(2)}, u32[]{:S(2)}) collective-permute-start(bf16[192,1024]{1,0:T(8,128)(2,1)S(1)} %get-tuple-element.65.refs_0_), channel_id=1, source_target_pairs={{0,1},{1,2},{2,3},{3,0},{4,5},{5,6},{6,7},{7,4},{8,9},{9,10},{10,1... | collective-permute-start | bytes 1179656 | tf_op jit(solution)/shard_map/ppermute | solution.py:20
  108.9 10.4 %collective-permute-start.12 = (bf16[192,1024]{1,0:T(8,128)(2,1)S(1)}, bf16[192,1024]{1,0:T(8,128)(2,1)S(1)}, u32[]{:S(2)}, u32[]{:S(2)}) collective-permute-start(bf16[192,1024]{1,0:T(8,128)(2,1)S(1)} %get-tuple-element.66.refs_1_), channel_id=1, source_target_pairs={{0,3},{1,0},{2,1},{3,2},{4,7},{5,4},{6,5},{7,6},{8,11},{9,8},{10,9... | collective-permute-start | bytes 1179656 | tf_op jit(solution)/shard_map/ppermute | solution.py:20
  114.6 13.1 %collective-permute-start.16 = (bf16[192,1024]{1,0:T(8,128)(2,1)}, bf16[192,1024]{1,0:T(8,128)(2,1)}, u32[]{:S(2)}, u32[]{:S(2)}) collective-permute-start(bf16[192,1024]{1,0:T(8,128)(2,1)} %get-tuple-element.69.refs_2_), channel_id=1, source_target_pairs={{0,1},{1,2},{2,3},{3,0},{4,5},{5,6},{6,7},{7,4},{8,9},{9,10},{10,1... | collective-permute-start | bytes 1179656 | tf_op jit(solution)/shard_map/ppermute | solution.py:20
  114.6 13.1 %collective-permute-start.17 = (bf16[192,1024]{1,0:T(8,128)(2,1)}, bf16[192,1024]{1,0:T(8,128)(2,1)}, u32[]{:S(2)}, u32[]{:S(2)}) collective-permute-start(bf16[192,1024]{1,0:T(8,128)(2,1)} %get-tuple-element.72), channel_id=1, source_target_pairs={{0,3},{1,0},{2,1},{3,2},{4,7},{5,4},{6,5},{7,6},{8,11},{9,8},{10,9... | collective-permute-start | bytes 1179656 | tf_op jit(solution)/shard_map/ppermute | solution.py:20
  120.2 15.9 %collective-permute-start.14 = (bf16[192,1024]{1,0:T(8,128)(2,1)}, bf16[192,1024]{1,0:T(8,128)(2,1)S(1)}, u32[]{:S(2)}, u32[]{:S(2)}) collective-permute-start(bf16[192,1024]{1,0:T(8,128)(2,1)} %get-tuple-element.70), channel_id=1, source_target_pairs={{0,1},{1,2},{2,3},{3,0},{4,5},{5,6},{6,7},{7,4},{8,9},{9,10},{10,1... | collective-permute-start | bytes 1179656 | tf_op jit(solution)/shard_map/ppermute | solution.py:20
  120.5 15.6 %collective-permute-start.15 = (bf16[192,1024]{1,0:T(8,128)(2,1)}, bf16[192,1024]{1,0:T(8,128)(2,1)S(1)}, u32[]{:S(2)}, u32[]{:S(2)}) collective-permute-start(bf16[192,1024]{1,0:T(8,128)(2,1)} %get-tuple-element.71), channel_id=1, source_target_pairs={{0,3},{1,0},{2,1},{3,2},{4,7},{5,4},{6,5},{7,6},{8,11},{9,8},{10,9... | collective-permute-start | bytes 1179656 | tf_op jit(solution)/shard_map/ppermute | solution.py:20
  127.8 12.3 %copy-start.1 = (bf16[4096,2,8]{0,2,1:T(8,128)(2,1)S(1)}, bf16[4096,2,8]{0,2,1:T(8,128)(2,1)}, u32[]{:S(2)}) copy-start(bf16[4096,2,8]{0,2,1:T(8,128)(2,1)} %param.12) | copy-start | bytes 393220
Sparse Core Ops, SparseCore 0:
  26.0 55.6 all-gather.2

commit v5 on v4

--- a/solution.py
+++ b/solution.py
@@ -30,6 +30,7 @@
 
 class Ring:
     def __init__(self, plus, minus, later):
+        self.own = (plus, minus)
         self.plus, self.minus = around(plus, 1), around(minus, -1)
         self.later = later
 
@@ -40,11 +41,26 @@
         self.right = (around(minus, -1), self.minus)
 
     def forward(self, after=()):
-        half = self.later[0].shape[0]
-        plus, minus = moved(
-            [self.plus, self.minus], [[(0, 0, half)], [(1, 0, half)]], [self.sent, *after]
-        )
-        self.opposite = (around(plus, 1), around(minus, -1))
+        self.plus, self.minus = tied([self.plus, self.minus], [self.sent, *after])
+        self.left = (self.plus, self.left[1])
+        self.right = (self.right[0], self.minus)
+        self.opposite = (around(self.plus, 1), around(self.minus, -1))
+
+
+def nothing(*refs):
+    pass
+
+
+def tied(arrays, after):
+    anywhere = pl.BlockSpec(memory_space=pl.ANY)
+    return pl.pallas_call(
+        nothing,
+        in_specs=[anywhere] * (len(arrays) + len(after)),
+        out_specs=[anywhere] * len(arrays),
+        out_shape=[jax.ShapeDtypeStruct(x.shape, x.dtype) for x in arrays],
+        input_output_aliases={n: n for n in range(len(arrays))},
+        compiler_params=params(),
+    )(*arrays, *after)
 
 
 def moved_kernel(n, n_after, plan, *refs):
@@ -67,46 +83,9 @@
         out_shape=[
             jax.ShapeDtypeStruct((n, arrays[0].shape[1]), arrays[0].dtype) for n in shapes
         ],
-        compiler_params=params(),
+        compiler_params=params(32),
         cost_estimate=cost(0, 4 * sum(shapes) * arrays[0].shape[1]),
     )(*arrays, *after)
-
-
-def packed_kernel(scalars, x_ref, w_ref, plus, minus, across, kept, sems):
-    rows, cols = x_ref.shape
-    half, part = rows // 2, kept.shape[0]
-    copies = Copies(sems)
-    me, n = scalars[1], w_ref.shape[1] // cols
-
-    def piece(to):
-        at = pl.multiple_of(scalars[0] * part, part)
-        columns = pl.ds(pl.multiple_of(lax.rem(me + to, n) * cols, cols), cols)
-        return w_ref.at[pl.ds(at, part), columns]
-
-    started = [
-        copies.start(piece(1), plus.at[pl.ds(half, part)]),
-        copies.start(piece(n - 1), minus.at[pl.ds(half, part)]),
-        copies.start(piece(2), across),
-        copies.start(piece(0), kept),
-    ]
-    plus[:half] = x_ref[:half]
-    minus[:half] = x_ref[half:]
-    for copy in started:
-        copy.wait()
-
-
-def packed(x, w, place, me, part):
-    rows, cols = x.shape
-    shapes = [(rows // 2 + part, cols)] * 2 + [(part, cols)] * 2
-    return pl.pallas_call(
-        packed_kernel,
-        in_specs=[pl.BlockSpec(memory_space=m) for m in (pltpu.SMEM, pltpu.VMEM, pl.ANY)],
-        out_specs=[pl.BlockSpec(memory_space=pltpu.VMEM)] * 4,
-        out_shape=[jax.ShapeDtypeStruct(shape, x.dtype) for shape in shapes],
-        scratch_shapes=[pltpu.SemaphoreType.DMA((4,))],
-        compiler_params=params(),
-        cost_estimate=cost(0, 8 * x.size),
-    )(jnp.stack([place, me]), x, w)
 
 
 def flat_kernel(n, w_ref, *refs):
@@ -177,119 +156,177 @@
         buffer[at * n : (at + 1) * n] = piece[:n]
 
 
-def fetch_weight(copies, w, chunk, columns, target, sources):
-    if len(w.shape) == 2:
-        n = target.shape[0]
-        rows = pl.ds(pl.multiple_of(chunk * n, n), n)
-        return [copies.start(w.at[rows, columns], target)]
-    own, nval = target.shape[:2]
-    started = []
-    for h in range(own):
-        for n in range(nval):
-            source = w.at[chunk * own + h, :, n, :, columns]
-            started.append(copies.start(source, target.at[h, sources[n]]))
-    return started
-
-
-def product_kernel(counts, tasks, with_total, n_after, staged, scalars, *refs):
+def fetch_weight(copies, w, chunk, columns, target):
+    n = target.shape[0]
+    return [copies.start(w.at[pl.ds(pl.multiple_of(chunk * n, n), n), columns], target)]
+
+
+def product_kernel(counts, tasks, n_after, scalars, *refs):
     refs = list(refs)
     take = lambda n: [refs.pop(0) for _ in range(n)]
-    ngroups, nweights = len(counts), 1 + max(n for _, segments in tasks for n, _ in segments)
+    ngroups, nweights = len(counts), 1 + max(n for n, *_ in tasks)
     groups = [take(n) for n in counts]
     weights = take(nweights)
-    totals = take(nweights) if with_total else None
     take(n_after)
     outs = take(nweights)
-    x, ws = take(2)
-    os = take(nweights) if staged else outs
-    copies = Copies(refs[0])
+    x, ws, sems = refs
+    copies = Copies(sems)
     chunk = x.shape[1] // ngroups
-    sources = [scalars[ngroups + n] for n in range(4)]
     part = lambda g: x.at[:, pl.ds(g * chunk, chunk)]
 
-    def load(g, at, segments):
-        started = []
-        for n, columns in segments:
-            target = ws.at[g, ..., pl.ds(at, columns.size)]
-            started += fetch_weight(copies, weights[n], scalars[g], columns, target, sources)
-            at += columns.size
-        return started
+    def load(g, n, at, columns):
+        target = ws.at[g, :, pl.ds(at, columns.size)]
+        return fetch_weight(copies, weights[n], scalars[g], columns, target)
 
     loads = Loads(AHEAD)
-    for at, segments in tasks:
+    for task in tasks:
         for g in range(ngroups):
-            loads.add(functools.partial(load, g, at, segments))
+            loads.add(functools.partial(load, g, *task))
     loads.begin()
     for g in range(ngroups):
         put_rows(groups[g], part(g))
-    last = []
-    for at, segments in tasks:
-        width = sum(columns.size for _, columns in segments)
+    for n, at, columns in tasks:
         total = None
         for g in range(ngroups):
             loads.next()
-            w = ws[g, ..., at : at + width].reshape(chunk, -1)
+            w = ws[g, :, at : at + columns.size]
             term = jnp.dot(part(g)[...], w, preferred_element_type=F32)
             total = term if total is None else total + term
-        at = 0
-        for n, columns in segments:
-            out = total[:, at : at + columns.size]
-            if with_total:
-                out = out + totals[n][:, columns]
-            os[n][:, columns] = out.astype(os[n].dtype)
-            if staged:
-                last.append(copies.start(os[n].at[:, columns], outs[n].at[:, columns]))
-            at += columns.size
-    for copy in last:
-        copy.wait()
-
-
-def product(rows, groups, index, weights, totals, dtypes, sources, after=(), staged=False):
+        outs[n][:, columns] = total.astype(outs[n].dtype)
+
+
+def product(rows, groups, index, weights, dtypes, after=()):
     chunk = groups[0][0].shape[1]
-    widths = [w.shape[-1] for w in weights]
+    widths = [w.shape[1] for w in weights]
     tasks, held = [], 0
     for n, width in enumerate(widths):
         for at in range(0, width, BLOCK):
-            tasks.append((held, [(n, pl.ds(at, min(BLOCK, width)))]))
-            held += min(BLOCK, width)
+            tasks.append((n, held, pl.ds(at, BLOCK)))
+            held += BLOCK
     anywhere, vmem = (pl.BlockSpec(memory_space=m) for m in (pl.ANY, pltpu.VMEM))
     pieces = [x for g in groups for x in g]
-    specs = [vmem] * len(pieces) + [anywhere] * len(weights)
-    specs += [vmem] * len(totals or []) + [anywhere] * len(after)
-    args = pieces + list(weights) + list(totals or []) + list(after)
-    shape = (chunk, held)
-    if weights[0].ndim > 2:
-        heads, parts, nval, n, cols = weights[0].shape
-        shape = (chunk // (parts * nval * n), nval, parts, n, cols)
-    scratch = [pltpu.VMEM((rows, len(groups) * chunk), BF16)]
-    scratch.append(pltpu.VMEM((len(groups), *shape), BF16))
-    if staged:
-        scratch += [pltpu.VMEM((rows, n), d) for n, d in zip(widths, dtypes)]
-    copies = len(tasks) * (len(groups) * 8 + 2)
-    scratch.append(pltpu.SemaphoreType.DMA((copies,)))
     cols = sum(widths)
     return pl.pallas_call(
-        functools.partial(
-            product_kernel,
-            [len(g) for g in groups],
-            tasks,
-            totals is not None,
-            len(after),
-            staged,
-        ),
-        in_specs=[pl.BlockSpec(memory_space=pltpu.SMEM)] + specs,
-        out_specs=[anywhere if staged else vmem] * len(weights),
+        functools.partial(product_kernel, [len(g) for g in groups], tasks, len(after)),
+        in_specs=[pl.BlockSpec(memory_space=pltpu.SMEM)]
+        + [vmem] * len(pieces)
+        + [anywhere] * (len(weights) + len(after)),
+        out_specs=[vmem] * len(weights),
         out_shape=[jax.ShapeDtypeStruct((rows, n), d) for n, d in zip(widths, dtypes)],
-        scratch_shapes=scratch,
+        scratch_shapes=[
+            pltpu.VMEM((rows, len(groups) * chunk), BF16),
+            pltpu.VMEM((len(groups), chunk, held), BF16),
+            pltpu.SemaphoreType.DMA((len(tasks) * len(groups),)),
+        ],
         compiler_params=params(),
         cost_estimate=cost(
             2 * rows * chunk * len(groups) * cols,
             2 * chunk * len(groups) * (cols + rows) + 4 * rows * cols,
         ),
-    )(jnp.stack(list(index) + list(sources)), *args)
-
-
-def values_kernel(scalars, upper, lower, w_ref, acc_ref, gain_ref, *refs):
+    )(jnp.stack(list(index)), *pieces, *weights, *after)
+
+
+def cut_kernel(n_after, scalars, w_ref, *refs):
+    outs, sems = refs[n_after:-1], refs[-1]
+    copies = Copies(sems)
+    cols = outs[0].shape[1]
+    n = w_ref.shape[1] // (2 * cols)
+    spots = [2 * scalars[0] + scalars[1], 2 * scalars[0] + 1 - scalars[1]]
+    spots += [2 * lax.rem(scalars[0] + to, n) + scalars[1] for to in range(1, n)]
+    started = []
+    for at, out in zip(spots, outs):
+        started.append(
+            copies.start(w_ref.at[:, pl.ds(pl.multiple_of(at * cols, cols), cols)], out)
+        )
+    for copy in started:
+        copy.wait()
+
+
+def cut_by_device(w, me, core, nval, after):
+    rows, cols = w.shape[0], w.shape[1] // (2 * nval)
+    anywhere, vmem = (pl.BlockSpec(memory_space=m) for m in (pl.ANY, pltpu.VMEM))
+    return pl.pallas_call(
+        functools.partial(cut_kernel, len(after)),
+        in_specs=[pl.BlockSpec(memory_space=pltpu.SMEM)] + [anywhere] * (1 + len(after)),
+        out_specs=[vmem] * (nval + 1),
+        out_shape=[jax.ShapeDtypeStruct((rows, cols), w.dtype)] * (nval + 1),
+        scratch_shapes=[pltpu.SemaphoreType.DMA((nval + 1,))],
+        compiler_params=params(),
+        cost_estimate=cost(0, 4 * rows * cols * (nval + 1)),
+    )(jnp.stack([me, core]), w, *after)
+
+
+def out_kernel(counts, with_total, scalars, *refs):
+    refs = list(refs)
+    take = lambda n: [refs.pop(0) for _ in range(n)]
+    ngroups = len(counts)
+    groups = [take(n) for n in counts]
+    halves = [take(4), take(4)]
+    total_ref = take(1)[0] if with_total else None
+    out, x, ws, held, sems, out_sems = refs
+    copies, out_copies = Copies(sems), Copies(out_sems)
+    sources = [scalars[ngroups + n] for n in range(4)]
+    core = scalars[ngroups + 4]
+    chunk = x.shape[1] // ngroups
+    cols, vlocal = ws.shape[2], chunk // 8
+    row = lambda n: pl.ds(pl.multiple_of(n * vlocal, vlocal), vlocal)
+
+    def load(t):
+        started = []
+        for g in range(ngroups):
+            for n, w in enumerate(halves[t]):
+                for h in range(2):
+                    to = row(g * 8 + h * 4 + sources[n])
+                    source = w.at[row(scalars[g] * 2 + h), :]
+                    started.append(copies.start(source, ws.at[t, to, :]))
+        return started
+
+    started = [load(t) for t in range(2)]
+    for g in range(ngroups):
+        put_rows(groups[g], x.at[:, pl.ds(g * chunk, chunk)])
+    last = []
+    for t, side in enumerate((core, 1 - core)):
+        columns = pl.ds(pl.multiple_of(side * cols, cols), cols)
+        for copy in started[t]:
+            copy.wait()
+        total = jnp.dot(x[...], ws[t], preferred_element_type=F32)
+        if with_total:
+            total = total + total_ref[:, columns]
+        held[t] = total.astype(held.dtype)
+        last.append(out_copies.start(held.at[t], out.at[:, columns]))
+    for copy in last:
+        copy.wait()
+
+
+def out_product(rows, groups, index, sources, core, mine, others, total, dtype):
+    chunk = groups[0][0].shape[1]
+    cols = mine[0].shape[1]
+    anywhere, vmem = (pl.BlockSpec(memory_space=m) for m in (pl.ANY, pltpu.VMEM))
+    pieces = [x for g in groups for x in g]
+    totals = [] if total is None else [total]
+    args = [*pieces, *mine, *others, *totals]
+    n = len(groups)
+    return pl.pallas_call(
+        functools.partial(out_kernel, [len(g) for g in groups], total is not None),
+        in_specs=[pl.BlockSpec(memory_space=pltpu.SMEM)]
+        + [vmem] * len(pieces)
+        + [anywhere] * 8
+        + [vmem] * len(totals),
+        out_specs=anywhere,
+        out_shape=jax.ShapeDtypeStruct((rows, 2 * cols), dtype),
+        scratch_shapes=[
+            pltpu.VMEM((rows, n * chunk), BF16),
+            pltpu.VMEM((2, n * chunk, cols), BF16),
+            pltpu.VMEM((2, rows, cols), dtype),
+            pltpu.SemaphoreType.DMA((16 * n,)),
+            pltpu.SemaphoreType.DMA((2,)),
+        ],
+        compiler_params=params(56),
+        cost_estimate=cost(4 * rows * chunk * n * cols, 4 * chunk * n * cols + 8 * rows * cols),
+    )(jnp.stack(list(index) + list(sources) + [core]), *args)
+
+
+def values_kernel(scalars, upper, lower, w_ref, acc_ref, gain_ref, after, *refs):
     n = len(refs) - 3
     outs, (x, w, sems) = refs[:n], refs[n:]
     own, more, vlocal = outs[0].shape
@@ -303,7 +340,7 @@
         return to, pl.ds(pl.multiple_of(to * block, block), block)
 
     for k in order:
-        loads.add(lambda k=k: fetch_weight(copies, w_ref, scalars[0], spot(k)[1], w.at[k], None))
+        loads.add(lambda k=k: fetch_weight(copies, w_ref, scalars[0], spot(k)[1], w.at[k]))
     loads.begin()
     put_rows((upper, lower), x)
     line = lax.broadcasted_iota(jnp.int32, (more - rows, vlocal), 0)
@@ -320,7 +357,7 @@
             outs[k][h, rows:] = tail.astype(BF16)
 
 
-def values_by_device(halves, index, me, w, acc, gain, own):
+def values_by_device(halves, index, me, w, acc, gain, own, after):
     rows, cols = acc.shape
     chunk = halves[0].shape[1]
     vlocal = gain.shape[1]
@@ -337,6 +374,7 @@
             pl.BlockSpec(memory_space=pl.ANY),
             vmem,
             vmem,
+            pl.BlockSpec(memory_space=pl.ANY),
         ],
         out_specs=[vmem] * steps,
         out_shape=[jax.ShapeDtypeStruct(shape, BF16)] * steps,
@@ -347,7 +385,7 @@
         ],
         compiler_params=params(),
         cost_estimate=cost(2 * rows * chunk * cols, 2 * chunk * (cols + rows) + 6 * rows * cols),
-    )(jnp.stack([index, me]), *halves, w, acc, gain)
+    )(jnp.stack([index, me]), *halves, w, acc, gain, after)
 
 
 def exchanged(pieces):
@@ -479,7 +517,7 @@
             out_specs=[whole(shape) for shape, _ in shapes],
         ),
         out_shape=[jax.ShapeDtypeStruct(shape, dtype) for shape, dtype in shapes],
-        compiler_params=params(),
+        compiler_params=params(32),
         cost_estimate=cost(2 * kwt.size * vsize, 3 * own * rows * vsize * 2),
     )(jnp.stack(list(index) + [core]), kwt, mark, *pieces)
 
@@ -505,7 +543,7 @@
         in_specs=[pl.BlockSpec(memory_space=pltpu.SMEM), vmem, vmem],
         out_specs=vmem,
         out_shape=jax.ShapeDtypeStruct(mine.shape, BF16),
-        compiler_params=params(),
+        compiler_params=params(32),
         cost_estimate=cost(4 * mine.size, 6 * mine.size),
     )(jnp.stack([core]), mine, got)
 
@@ -535,7 +573,7 @@
         in_specs=[pl.BlockSpec(memory_space=pltpu.SMEM)] + [vmem] * 3,
         out_specs=[vmem] * 2,
         out_shape=[jax.ShapeDtypeStruct(mine.shape, BF16)] * 2,
-        compiler_params=params(),
+        compiler_params=params(32),
         cost_estimate=cost(4 * mine.size, 10 * mine.size),
     )(jnp.stack([core]), prefix, mine, got)
 
@@ -549,7 +587,7 @@
     return pl.pallas_call(
         inside_kernel,
         out_shape=jax.ShapeDtypeStruct(v.shape, F32),
-        compiler_params=params(),
+        compiler_params=params(32),
         cost_estimate=cost(2 * p.size * v.shape[2], 6 * v.size),
     )(p, v)
 
@@ -591,7 +629,7 @@
     return pl.pallas_call(
         prefix_kernel,
         out_shape=jax.ShapeDtypeStruct(got.shape, BF16),
-        compiler_params=params(),
+        compiler_params=params(32),
         cost_estimate=cost(4 * got.size, 4 * got.size),
     )(got)
 
@@ -630,7 +668,7 @@
         in_specs=[pl.BlockSpec(memory_space=pltpu.SMEM)] + [vmem] * 6,
         out_specs=[vmem] * 2,
         out_shape=[jax.ShapeDtypeStruct((rows // 2, own * vsize), BF16)] * 2,
-        compiler_params=params(),
+        compiler_params=params(32),
         cost_estimate=cost(2 * q.size * vsize, 8 * numer.size),
     )(jnp.stack([core]), q, mine, got, numer, stat, gain)
 
@@ -648,13 +686,9 @@
     vsize = vlocal * nval
     index = [(me + d) % nval for d in (0, nval - 1, 1, 2)]
 
-    part = heads * vlocal // blocks
     half = rows // 2
-    plus, minus, across, kept = packed(
-        tokens, w_out.reshape(heads * vlocal, -1), place, me, part
-    )
-    ring = Ring(plus, minus, [tokens[:half], tokens[half:]])
-    across = around(across, 2)
+    upper, lower = moved([tokens], [[(0, 0, half)], [(0, half, half)]], [])
+    ring = Ring(upper, lower, [upper, lower])
     wg = lax.dynamic_slice_in_dim(w_gate, me * own, own, axis=2).reshape(width, 2 * own)
     wg = jnp.pad(wg, ((0, 0), (0, LANES - 2 * own)))
     bias = lax.dynamic_slice_in_dim(gate_bias, me * own, own, axis=1).reshape(1, 2 * own)
@@ -664,22 +698,20 @@
     wv, late = flat(w_value, 1, wv)
     ring.forward([late])
     groups = [(tokens,), ring.left, ring.right]
-    acc = product(rows, groups, index[:3], [wv], None, [F32], index)[0]
-    values = values_by_device(ring.opposite, index[3], me, wv, acc, norm_gain, own)
+    acc = product(rows, groups, index[:3], [wv], [F32])[0]
+    core = place % 2
+    cores = [(i, i ^ 1) for i in range(blocks)]
+    kept, away, *pieces = cut_by_device(
+        w_out.reshape(heads * vlocal, -1), me, core, nval, [acc]
+    )
+    values = values_by_device(ring.opposite, index[3], me, wv, acc, norm_gain, own, kept)
+    halves = exchanged([None, *tied(pieces, values[:1])])[1:]
     groups.append(ring.opposite)
-    q, k = product(
-        rows, groups, index, [w_query, w_key], None, [BF16] * 2, index, values[:1]
-    )
-    cuts = [(0, 0, 0), (1, half, part), (2, half, part), (3, 0, 0)]
-    wo = moved([kept, ring.plus, ring.minus, across], [cuts], [early])[0]
-    wo = lax.all_gather(wo, "seq", axis=0)
-    wo = wo.reshape(heads, blocks // heads, nval, part, chunk)
+    q, k = product(rows, groups, index, [w_query, w_key], [BF16] * 2, values[:1])
 
     values = exchanged(values)
     kwt, p, stat, mark = within(groups, index, wg, bias, q, k, own)
-    core = place % 2
     mine, other, v, gain = summary(index, core, kwt, mark, values)
-    cores = [(i, i ^ 1) for i in range(blocks)]
     got = lax.ppermute(other, "seq", cores)
     chips = [list(range(n, blocks, 2)) for n in range(2)]
     sliced = (blocks // 2, -1, vsize + LANES)
@@ -692,11 +724,15 @@
     upper, lower = finish(core, q, keep, came, numer, stat, gain)
 
     ring = Ring(upper, lower, [upper, lower])
-    accs = product(rows, [(upper, lower)], index[:1], [wo], None, [F32], index)
-    ring.second(accs)
+    halves = tied(halves, [upper])
+    others = [lax.ppermute(x, "seq", cores) for x in halves]
+    ring.second(others)
     ring.forward()
-    accs = product(rows, [ring.left, ring.right], index[1:3], [wo], accs, [F32], index)
-    return product(rows, [ring.opposite], index[3:], [wo], accs, [BF16], index, staged=True)[0]
+    halves, others = [kept, *halves], [away, *others]
+    groups = [ring.own, ring.left, ring.right]
+    weights = (index, core, halves, others)
+    acc = out_product(rows, groups, index[:3], *weights, None, F32)
+    return out_product(rows, [ring.opposite], index[3:], *weights, acc, BF16)
 
 
 def solution(mesh):

time: 148 us -> 144 us (0.973)
  between operations: 13.6 us -> 0.5 us
  local copies, waits for them, and re-layouts: 4.76 us -> 8.71 us
  starting transfers between devices: 29.7 us -> 33 us
    pallas_call x1 -> x7, Pallas kernels: 1.52 us -> 15.9 us  [the longest x2 12.8 us: out_product(): pl.pallas_call(functools.partial(out_kernel, [len(g) for g in groups], to...]
    pallas_call x5 -> x2, Pallas kernels: 25.4 us -> 11.8 us  [product(): pl.pallas_call(functools.partial(product_kernel, [len(g) for g in groups]...]
    unnamed x14 -> x38, local copies, waits for them, and re-layouts: 1.16 us -> 5.5 us
    ppermute x0 -> x3, waiting for transfers between devices: none -> 2.08 us  [per_device(): others = [lax.ppermute(x, 'seq', cores) for x in halves]]
    ppermute x16 -> x18, starting transfers between devices: 22.4 us -> 24.2 us  [around(): return lax.ppermute(x, 'val', [(i, (i + distance) % n) for i in range(n)])]
    pallas_call x5 -> x3, Pallas kernels: 4.64 us -> 3.94 us  [moved(): pl.pallas_call(functools.partial(moved_kernel, len(arrays), len(after), p...]
    ppermute x16 -> x18, waiting for transfers between devices: 16 us -> 16.6 us  [around(): return lax.ppermute(x, 'val', [(i, (i + distance) % n) for i in range(n)])]
  transfers between devices with their start and end apart: 19 -> 23, of which waited for: 7 -> 8; matrix products, arithmetic and copies ran while one was open for 3% -> 2% of each run, Pallas kernels for 32% -> 30%
where the time goes in v5:
time: 144 us; the launch traced here: 143 us
  Pallas kernels  55.1 us (38%)
  starting transfers between devices  33 us (23%)
  blocking collectives  26.3 us (18%)
  waiting for transfers between devices  19.3 us (13%)
  local copies, waits for them, and re-layouts  8.71 us (6%)
    ppermute x18, starting transfers between devices, around(): return lax.ppermute(x, 'val', [(i, (i + distance) % n) for i in range(n)])  24.2 us
    ppermute x18, waiting for transfers between devices, around(): return lax.ppermute(x, 'val', [(i, (i + distance) % n) for i in range(n)])  16.6 us
    all_to_all x1, blocking collectives, per_device(): both = lax.all_to_all(both, 'seq', 0, 0, axis_index_groups=chips)  15.2 us
    pallas_call x2, Pallas kernels, out_product(): pl.pallas_call(functools.partial(out_kernel, [len(g) for g in groups], to...  12.8 us
    pallas_call x2, Pallas kernels, product(): pl.pallas_call(functools.partial(product_kernel, [len(g) for g in groups]...  11.8 us
    all_to_all x1, blocking collectives, per_device(): lax.all_to_all(prefixes(both), 'seq', 0, 0, axis_index_groups=chips)  11.1 us
    pallas_call x2, Pallas kernels, flat(): pl.pallas_call(functools.partial(flat_kernel, len(args)), grid=(steps,),...  9.77 us
    unnamed x38, local copies, waits for them, and re-layouts  5.5 us
  transfers between devices with their start and end apart: 23, of which 8 were waited for; matrix products, arithmetic and copies ran while one was open for 2% of the time, Pallas kernels for 30%

profile of v5, /device:TPU:1, one launch (start us, length us, event | category | flops | bytes accessed | tf_op | source)
XLA Modules:
  0.0 143.1 jit_solution(17840687632657169005)
XLA Ops:
  0.0 1.2 copy-done.11
  1.2 0.9 shard_map.82
  2.1 2.1 %collective-permute-start = (bf16[192,1024]{1,0:T(8,128)(2,1)}, bf16[192,1024]{1,0:T(8,128)(2,1)S(1)}, u32[]{:S(2)}, u32[]{:S(2)}) collective-permute-start(bf16[192,1024]{1,0:T(8,128)(2,1)} %get-tuple-element.48.refs_0_), channel_id=1, source_target_pairs={{0,1},{1,2},{2,3},{3,0},{4,5},{5,6},{6,7},{7,4},{8,9},{9,10},{10,1... | collective-permute-start | bytes 1179656 | tf_op jit(solution)/shard_map/ppermute | solution.py:20
  4.2 1.4 %collective-permute-start.1 = (bf16[192,1024]{1,0:T(8,128)(2,1)}, bf16[192,1024]{1,0:T(8,128)(2,1)S(1)}, u32[]{:S(2)}, u32[]{:S(2)}) collective-permute-start(bf16[192,1024]{1,0:T(8,128)(2,1)} %get-tuple-element.49.refs_1_), channel_id=1, source_target_pairs={{0,3},{1,0},{2,1},{3,2},{4,7},{5,4},{6,5},{7,6},{8,11},{9,8},{10,9... | collective-permute-start | bytes 1179656 | tf_op jit(solution)/shard_map/ppermute | solution.py:20
  5.8 1.4 copy.21
  7.2 4.9 %shard_map.83 = (bf16[4096,1024]{1,0:T(8,128)(2,1)}, f32[8,128]{1,0:T(8,128)S(1)}) custom-call(bf16[4096,8,128]{2,1,0:T(8,128)(2,1)} %w_ref.3), custom_call_target="tpu_custom_call" | custom-call | bytes 8388608 | tf_op jit(solution)/shard_map/pallas_call | solution.py:101
  12.3 2.1 %shard_map.84 = (bf16[192,1024]{1,0:T(8,128)(2,1)}, bf16[192,1024]{1,0:T(8,128)(2,1)}) custom-call(bf16[192,1024]{1,0:T(8,128)(2,1)} %get-tuple-element.48.refs_0_, bf16[192,1024]{1,0:T(8,128)(2,1)} %get-tuple-element.49.refs_1_, f32[8,128]{1,0:T(8,128)S(1)} %get-tuple-element.50.refs_2_, bf16[4096,128]{1,0:T(8,128)(2,1)S(1)} %pad.8.refs_3_.refs_7_), custom_call_target="tpu_custom_call" | custom-call | bytes 1572864 | tf_op jit(solution)/shard_map/pallas_call | solution.py:79
  14.4 2.7 %collective-permute-start.3 = (bf16[192,1024]{1,0:T(8,128)(2,1)}, bf16[192,1024]{1,0:T(8,128)(2,1)S(1)}, u32[]{:S(2)}, u32[]{:S(2)}) collective-permute-start(bf16[192,1024]{1,0:T(8,128)(2,1)} %get-tuple-element.55), channel_id=1, source_target_pairs={{0,3},{1,0},{2,1},{3,2},{4,7},{5,4},{6,5},{7,6},{8,11},{9,8},{10,9... | collective-permute-start | bytes 1179656 | tf_op jit(solution)/shard_map/ppermute | solution.py:20
  17.0 4.9 %shard_map.85 = (bf16[4096,1024]{1,0:T(8,128)(2,1)}, f32[8,128]{1,0:T(8,128)S(1)}) custom-call(bf16[4096,8,128]{2,1,0:T(8,128)(2,1)} %w_ref.3, bf16[4096,1024]{1,0:T(8,128)(2,1)} %get-tuple-element.52.refs_0_), custom_call_target="tpu_custom_call", output_to_operand_aliasing={{0}: (1, {})} | custom-call | bytes 8388608 | tf_op jit(solution)/shard_map/pallas_call | solution.py:101
  22.2 2.7 %collective-permute-start.5 = (bf16[192,1024]{1,0:T(8,128)(2,1)S(1)}, bf16[192,1024]{1,0:T(8,128)(2,1)}, u32[]{:S(2)}, u32[]{:S(2)}) collective-permute-start(bf16[192,1024]{1,0:T(8,128)(2,1)S(1)} %get-tuple-element.56.refs_4_), channel_id=1, source_target_pairs={{0,3},{1,0},{2,1},{3,2},{4,7},{5,4},{6,5},{7,6},{8,11},{9,8},{10,9... | collective-permute-start | bytes 1179656 | tf_op jit(solution)/shard_map/ppermute | solution.py:20
  25.3 5.2 %shard_map.87.refs_0_.acc_ref = f32[384,1024]{1,0:T(8,128)S(1)} custom-call(s32[3]{0:T(128)S(1)} %pad_add_fusion.2.scalars, bf16[384,1024]{1,0:T(8,128)(2,1)S(1)} %copy-done.12, bf16[192,1024]{1,0:T(8,128)(2,1)S(1)} %get-tuple-element.54.refs_1_, bf16[192,1024]{1,0:T(8,128)(2,1)S(1)} %collective-permute-done.2.refs_2_, ...), custom_call_target="tpu_custom_call" | custom-call | flops 2415919104 | bytes 10223616 | tf_op jit(solution)/shard_map/pallas_call | solution.py:209
  30.5 1.2 copy-done.2
  31.7 3.1 %shard_map.88 = (bf16[1024,512]{1,0:T(8,128)(2,1)S(1)}, bf16[1024,512]{1,0:T(8,128)(2,1)S(1)}, bf16[1024,512]{1,0:T(8,128)(2,1)S(1)}, bf16[1024,512]{1,0:T(8,128)(2,1)S(1)}, bf16[1024,512]{1,0:T(8,128)(2,1)S(1)}) custom-call(s32[2]{0:T(128)S(1)} %pad_add_fusion.3.scalars, bf16[1024,4096]{1,0:T(8,128)(2,1)} %bitcast.13, f32[384,1024]{1,0:T(8,128)} %copy-done.2), custom_call_target="tpu_custom_call" | custom-call | bytes 10485760 | tf_op jit(solution)/shard_map/pallas_call | solution.py:248
  34.9 5.0 %shard_map.89 = (bf16[2,400,128]{2,1,0:T(8,128)(2,1)S(1)}, bf16[2,400,128]{2,1,0:T(8,128)(2,1)S(1)}, bf16[2,400,128]{2,1,0:T(8,128)(2,1)S(1)}, bf16[2,400,128]{2,1,0:T(8,128)(2,1)S(1)}) custom-call(s32[2]{0:T(128)S(1)} %pad_add_fusion.1.scalars, bf16[192,1024]{1,0:T(8,128)(2,1)} %collective-permute-done.4.upper.refs_5_, ...), custom_call_target="tpu_custom_call" | custom-call | flops 805306368 | bytes 5242880 | tf_op jit(solution)/shard_map/pallas_call | solution.py:368
  40.0 2.7 %collective-permute-start.7 = (bf16[2,400,128]{2,1,0:T(8,128)(2,1)S(1)}, bf16[2,400,128]{2,1,0:T(8,128)(2,1)S(1)}, u32[]{:S(2)}, u32[]{:S(2)}) collective-permute-start(bf16[2,400,128]{2,1,0:T(8,128)(2,1)S(1)} %get-tuple-element.65), channel_id=1, source_target_pairs={{0,3},{1,0},{2,1},{3,2},{4,7},{5,4},{6,5},{7,6},{8,11},{9,8},{10,9... | collective-permute-start | bytes 614408 | tf_op jit(solution)/shard_map/ppermute | solution.py:20
  42.7 0.9 collective-permute-start.8
  43.6 6.7 %shard_map.90 = (bf16[384,512]{1,0:T(8,128)(2,1)S(1)}, bf16[384,512]{1,0:T(8,128)(2,1)S(1)}) custom-call(s32[4]{0:T(128)S(1)} %pad_add_fusion.scalars, bf16[384,1024]{1,0:T(8,128)(2,1)S(1)} %copy-done.12, bf16[192,1024]{1,0:T(8,128)(2,1)S(1)} %get-tuple-element.54.refs_1_, bf16[192,1024]{1,0:T(8,128)(2,1)S(1)} %collective-permute-done.2.refs_2_, ...), custom_call_target="tpu_custom_call" | custom-call | flops 3221225472 | bytes 13107200 | tf_op jit(solution)/shard_map/pallas_call | solution.py:209
  50.3 3.8 %shard_map.91 = (bf16[512,384]{1,0:T(8,128)(2,1)S(1)}, bf16[2,384,384]{2,1,0:T(8,128)(2,1)S(1)}, f32[384,128]{1,0:T(8,128)S(1)}, f32[8,128]{1,0:T(8,128)S(1)}) custom-call(s32[4]{0:T(128)S(1)} %pad_add_fusion.scalars, bf16[384,1024]{1,0:T(8,128)(2,1)S(1)} %copy-done.12, bf16[192,1024]{1,0:T(8,128)(2,1)S(1)} %get-tuple-element.54.refs_1_, ...), custom_call_target="tpu_custom_call" | custom-call | flops 301989888 | bytes 1572864 | tf_op jit(solution)/shard_map/pallas_call | solution.py:445
  54.1 1.1 shard_map.92
  55.2 3.7 %collective-permute-start.9 = (bf16[256,640]{1,0:T(8,128)(2,1)S(1)}, bf16[256,640]{1,0:T(8,128)(2,1)S(1)}, u32[]{:S(2)}, u32[]{:S(2)}) collective-permute-start(bf16[256,640]{1,0:T(8,128)(2,1)S(1)} %get-tuple-element.68), channel_id=1, source_target_pairs={{0,4},{4,0},{8,12},{12,8},{16,20},{20,16},{24,28},{28,24},{32,36},... | collective-permute-start | bytes 983048 | tf_op jit(solution)/shard_map/ppermute | solution.py:715
  58.9 1.2 collective-permute-start.13
  60.1 1.5 %collective-permute-start.14 = (bf16[1024,512]{1,0:T(8,128)(2,1)S(1)}, bf16[1024,512]{1,0:T(8,128)(2,1)S(1)}, u32[]{:S(2)}, u32[]{:S(2)}) collective-permute-start(bf16[1024,512]{1,0:T(8,128)(2,1)S(1)} %get-tuple-element.81), channel_id=1, source_target_pairs={{0,3},{1,0},{2,1},{3,2},{4,7},{5,4},{6,5},{7,6},{8,11},{9,8},{10,9... | collective-permute-start | bytes 3145736 | tf_op jit(solution)/shard_map/ppermute | solution.py:20
  61.6 0.9 collective-permute-start.15
  63.0 15.2 %all_to_all.10.got_ref = bf16[16,16,640]{2,1,0:T(8,128)(2,1)S(1)} all-to-all(bf16[16,16,640]{2,1,0:T(8,128)(2,1)S(1)} %bitcast.12), channel_id=1, replica_groups={{0,8,16,24,32,40,48,56,64,72,80,88,96,104,112,120},{4,12,20,28,36,44,52..., dimensions={0} | all-to-all | bytes 655360 | tf_op jit(solution)/shard_map/all_to_all | solution.py:719
  78.5 11.1 %all_to_all.11 = bf16[16,16,640]{2,1,0:T(8,128)(2,1)S(1)} all-to-all(bf16[16,16,640]{2,1,0:T(8,128)(2,1)S(1)} %shard_map.94), channel_id=1, replica_groups={{0,8,16,24,32,40,48,56,64,72,80,88,96,104,112,120},{4,12,20,28,36,44,52..., dimensions={0} | all-to-all | bytes 655360 | tf_op jit(solution)/shard_map/all_to_all | solution.py:721
  90.1 3.6 %collective-permute-start.10 = (bf16[256,640]{1,0:T(8,128)(2,1)S(1)}, bf16[256,640]{1,0:T(8,128)(2,1)S(1)}, u32[]{:S(2)}, u32[]{:S(2)}) collective-permute-start(bf16[256,640]{1,0:T(8,128)(2,1)S(1)} %get-tuple-element.70), channel_id=1, source_target_pairs={{0,4},{4,0},{8,12},{12,8},{16,20},{20,16},{24,28},{28,24},{32,36},... | collective-permute-start | bytes 983048 | tf_op jit(solution)/shard_map/ppermute | solution.py:723
  94.3 0.7 collective-permute-done.10.got
  95.0 1.8 %shard_map.97 = (bf16[192,1024]{1,0:T(8,128)(2,1)S(1)}, bf16[192,1024]{1,0:T(8,128)(2,1)S(1)}) custom-call(s32[1]{0:T(128)} %bitcast.4.scalars, bf16[384,512]{1,0:T(8,128)(2,1)S(1)} %get-tuple-element.60.refs_9_.q_ref, bf16[256,640]{1,0:T(8,128)(2,1)S(1)} %get-tuple-element.69.mine, bf16[256,640]{1,0:T(8,128)(2,1)S(1)} %collective-permute-done.10.got, ...), custom_call_target="tpu_custom_call" | custom-call | flops 201326592 | bytes 3145728 | tf_op jit(solution)/shard_map/pallas_call | solution.py:666
  96.8 10.6 %collective-permute-done.15.refs_2_ = bf16[1024,512]{1,0:T(8,128)(2,1)S(1)} collective-permute-done((bf16[1024,512]{1,0:T(8,128)(2,1)S(1)}, bf16[1024,512]{1,0:T(8,128)(2,1)S(1)}, u32[]{:S(2)}, u32[]{:S(2)}) %collective-permute-start.15) | collective-permute-done | bytes 1048608 | tf_op jit(solution)/shard_map/ppermute | solution.py:20
  107.4 0.9 collective-permute-start.16
  108.9 0.9 collective-permute-start.11
  109.8 1.8 %collective-permute-start.12 = (bf16[192,1024]{1,0:T(8,128)(2,1)S(1)}, bf16[192,1024]{1,0:T(8,128)(2,1)}, u32[]{:S(2)}, u32[]{:S(2)}) collective-permute-start(bf16[192,1024]{1,0:T(8,128)(2,1)S(1)} %get-tuple-element.76.refs_1_), channel_id=1, source_target_pairs={{0,3},{1,0},{2,1},{3,2},{4,7},{5,4},{6,5},{7,6},{8,11},{9,8},{10,9... | collective-permute-start | bytes 1179656 | tf_op jit(solution)/shard_map/ppermute | solution.py:20
  111.6 0.6 collective-permute-done.17.refs_3_.refs_12_.refs_8_
  112.2 1.5 %collective-permute-done.18.refs_4_.refs_13_.refs_9_ = bf16[1024,512]{1,0:T(8,128)(2,1)S(1)} collective-permute-done((bf16[1024,512]{1,0:T(8,128)(2,1)S(1)}, bf16[1024,512]{1,0:T(8,128)(2,1)S(1)}, u32[]{:S(2)}, u32[]{:S(2)}) %collective-permute-start.18) | collective-permute-done | bytes 1048608 | tf_op jit(solution)/shard_map/ppermute | solution.py:728
  113.7 0.9 shard_map.100
  114.6 1.0 copy-done.7
  115.6 1.0 copy-done.8
  116.6 1.1 copy-done.9
  117.6 0.9 collective-permute-start.21
  118.5 1.8 %collective-permute-start.22 = (bf16[192,1024]{1,0:T(8,128)(2,1)}, bf16[192,1024]{1,0:T(8,128)(2,1)}, u32[]{:S(2)}, u32[]{:S(2)}) collective-permute-start(bf16[192,1024]{1,0:T(8,128)(2,1)} %get-tuple-element.90), channel_id=1, source_target_pairs={{0,3},{1,0},{2,1},{3,2},{4,7},{5,4},{6,5},{7,6},{8,11},{9,8},{10,9... | collective-permute-start | bytes 1179656 | tf_op jit(solution)/shard_map/ppermute | solution.py:20
  120.9 0.8 collective-permute-start.19
  121.7 1.9 %collective-permute-start.20 = (bf16[192,1024]{1,0:T(8,128)(2,1)}, bf16[192,1024]{1,0:T(8,128)(2,1)}, u32[]{:S(2)}, u32[]{:S(2)}) collective-permute-start(bf16[192,1024]{1,0:T(8,128)(2,1)} %get-tuple-element.88.refs_5_), channel_id=1, source_target_pairs={{0,3},{1,0},{2,1},{3,2},{4,7},{5,4},{6,5},{7,6},{8,11},{9,8},{10,9... | collective-permute-start | bytes 1179656 | tf_op jit(solution)/shard_map/ppermute | solution.py:20
  123.6 0.6 stack.38.scalars
  124.2 0.7 stack.31.scalars
  124.9 4.6 %collective-permute-done.21.refs_3_ = bf16[192,1024]{1,0:T(8,128)(2,1)} collective-permute-done((bf16[192,1024]{1,0:T(8,128)(2,1)}, bf16[192,1024]{1,0:T(8,128)(2,1)}, u32[]{:S(2)}, u32[]{:S(2)}) %collective-permute-start.21) | collective-permute-done | bytes 393248 | tf_op jit(solution)/shard_map/ppermute | solution.py:20
  129.5 7.7 %shard_map.102.refs_10_ = f32[384,1024]{1,0:T(8,128)} custom-call(s32[8]{0:T(128)} %stack.38.scalars, bf16[192,1024]{1,0:T(8,128)(2,1)} %copy-done.14, bf16[192,1024]{1,0:T(8,128)(2,1)} %copy-done.15, bf16[192,1024]{1,0:T(8,128)(2,1)} %get-tuple-element.87.refs_2_, bf16[192,1024]{1,0:T(8,128)(2,1)} %collective-permute-done.21.refs_3_, ...), custom_call_target="tpu_custom_call" | custom-call | flops 2415919104 | bytes 7864320 | tf_op jit(solution)/shard_map/pallas_call | solution.py:309
  137.3 0.6 collective-permute-done.19.refs_0_
  137.9 5.0 %shard_map.103 = bf16[384,1024]{1,0:T(8,128)(2,1)} custom-call(s32[6]{0:T(128)} %stack.31.scalars, bf16[192,1024]{1,0:T(8,128)(2,1)} %collective-permute-done.19.refs_0_, bf16[192,1024]{1,0:T(8,128)(2,1)} %collective-permute-done.20.refs_1_, bf16[1024,512]{1,0:T(8,128)(2,1)} %copy-done.10, bf16[1024,512]{1,0:T(8,128)(2,1)} %copy-done.4, ...), custom_call_target="tpu_custom_call" | custom-call | flops 805306368 | bytes 3670016 | tf_op jit(solution)/shard_map/pallas_call | solution.py:309
  (74 shorter events, 4.2 us)
Async XLA Ops:
  0.0 5.7 %copy-start = (bf16[4096,2,8]{0,2,1:T(8,128)(2,1)S(1)}, bf16[4096,2,8]{0,2,1:T(8,128)(2,1)}, u32[]{:S(2)}) copy-start(bf16[4096,2,8]{0,2,1:T(8,128)(2,1)} %param.12) | copy-start | bytes 393220
  0.0 1.2 copy-start.11
  2.1 20.0 %collective-permute-start = (bf16[192,1024]{1,0:T(8,128)(2,1)}, bf16[192,1024]{1,0:T(8,128)(2,1)S(1)}, u32[]{:S(2)}, u32[]{:S(2)}) collective-permute-start(bf16[192,1024]{1,0:T(8,128)(2,1)} %get-tuple-element.48.refs_0_), channel_id=1, source_target_pairs={{0,1},{1,2},{2,3},{3,0},{4,5},{5,6},{6,7},{7,4},{8,9},{9,10},{10,1... | collective-permute-start | bytes 1179656 | tf_op jit(solution)/shard_map/ppermute | solution.py:20
  4.2 17.9 %collective-permute-start.1 = (bf16[192,1024]{1,0:T(8,128)(2,1)}, bf16[192,1024]{1,0:T(8,128)(2,1)S(1)}, u32[]{:S(2)}, u32[]{:S(2)}) collective-permute-start(bf16[192,1024]{1,0:T(8,128)(2,1)} %get-tuple-element.49.refs_1_), channel_id=1, source_target_pairs={{0,3},{1,0},{2,1},{3,2},{4,7},{5,4},{6,5},{7,6},{8,11},{9,8},{10,9... | collective-permute-start | bytes 1179656 | tf_op jit(solution)/shard_map/ppermute | solution.py:20
  7.1 4.9 %copy-start.17 = (bf16[4096,4]{1,0:T(8,128)(2,1)S(1)}, bf16[4096,4]{1,0:T(8,128)(2,1)}, u32[]{:S(2)}) copy-start(bf16[4096,4]{1,0:T(8,128)(2,1)} %copy.21) | copy-start | bytes 98308
  14.3 10.9 %collective-permute-start.2 = (bf16[192,1024]{1,0:T(8,128)(2,1)}, bf16[192,1024]{1,0:T(8,128)(2,1)S(1)}, u32[]{:S(2)}, u32[]{:S(2)}) collective-permute-start(bf16[192,1024]{1,0:T(8,128)(2,1)} %get-tuple-element.51.refs_2_), channel_id=1, source_target_pairs={{0,1},{1,2},{2,3},{3,0},{4,5},{5,6},{6,7},{7,4},{8,9},{9,10},{10,1... | collective-permute-start | bytes 1179656 | tf_op jit(solution)/shard_map/ppermute | solution.py:20
  14.4 10.9 %collective-permute-start.3 = (bf16[192,1024]{1,0:T(8,128)(2,1)}, bf16[192,1024]{1,0:T(8,128)(2,1)S(1)}, u32[]{:S(2)}, u32[]{:S(2)}) collective-permute-start(bf16[192,1024]{1,0:T(8,128)(2,1)} %get-tuple-element.55), channel_id=1, source_target_pairs={{0,3},{1,0},{2,1},{3,2},{4,7},{5,4},{6,5},{7,6},{8,11},{9,8},{10,9... | collective-permute-start | bytes 1179656 | tf_op jit(solution)/shard_map/ppermute | solution.py:20
  17.0 5.0 %copy-start.18 = (f32[2,8]{1,0:T(2,128)S(1)}, f32[2,8]{1,0:T(2,128)}, u32[]{:S(2)}) copy-start(f32[2,8]{1,0:T(2,128)} %param.13) | copy-start | bytes 196
  17.0 8.3 %copy-start.12 = (bf16[384,1024]{1,0:T(8,128)(2,1)S(1)}, bf16[384,1024]{1,0:T(8,128)(2,1)}, u32[]{:S(2)}) copy-start(bf16[384,1024]{1,0:T(8,128)(2,1)} %refs_0_.7) | copy-start | bytes 2359300
  22.1 12.7 %collective-permute-start.4 = (bf16[192,1024]{1,0:T(8,128)(2,1)S(1)}, bf16[192,1024]{1,0:T(8,128)(2,1)}, u32[]{:S(2)}, u32[]{:S(2)}) collective-permute-start(bf16[192,1024]{1,0:T(8,128)(2,1)S(1)} %get-tuple-element.54.refs_1_), channel_id=1, source_target_pairs={{0,1},{1,2},{2,3},{3,0},{4,5},{5,6},{6,7},{7,4},{8,9},{9,10},{10,1... | collective-permute-start | bytes 1179656 | tf_op jit(solution)/shard_map/ppermute | solution.py:20
  22.2 12.7 %collective-permute-start.5 = (bf16[192,1024]{1,0:T(8,128)(2,1)S(1)}, bf16[192,1024]{1,0:T(8,128)(2,1)}, u32[]{:S(2)}, u32[]{:S(2)}) collective-permute-start(bf16[192,1024]{1,0:T(8,128)(2,1)S(1)} %get-tuple-element.56.refs_4_), channel_id=1, source_target_pairs={{0,3},{1,0},{2,1},{3,2},{4,7},{5,4},{6,5},{7,6},{8,11},{9,8},{10,9... | collective-permute-start | bytes 1179656 | tf_op jit(solution)/shard_map/ppermute | solution.py:20
  30.5 1.2 copy-start.2
  31.7 3.2 %copy-start.3 = (f32[384,1024]{1,0:T(8,128)S(1)}, f32[384,1024]{1,0:T(8,128)}, u32[]{:S(2)}) copy-start(f32[384,1024]{1,0:T(8,128)} %copy-done.2) | copy-start | bytes 4718596
  31.7 3.2 %copy-start.16 = (f32[8,128]{1,0:T(8,128)S(1)}, f32[8,128]{1,0:T(8,128)}, u32[]{:S(2)}) copy-start(f32[8,128]{1,0:T(8,128)} %gain_ref.1) | copy-start | bytes 12292
  34.8 5.1 %copy-start.10 = (bf16[1024,512]{1,0:T(8,128)(2,1)}, bf16[1024,512]{1,0:T(8,128)(2,1)S(1)}, u32[]{:S(2)}) copy-start(bf16[1024,512]{1,0:T(8,128)(2,1)S(1)} %get-tuple-element.58.after.refs_6_.refs_2_) | copy-start | bytes 3145732
  34.8 5.1 %copy-start.13 = (bf16[1024,512]{1,0:T(8,128)(2,1)}, bf16[1024,512]{1,0:T(8,128)(2,1)S(1)}, u32[]{:S(2)}) copy-start(bf16[1024,512]{1,0:T(8,128)(2,1)S(1)} %get-tuple-element.89.refs_10_.refs_6_) | copy-start | bytes 3145732
  39.9 14.1 %collective-permute-start.6 = (bf16[2,400,128]{2,1,0:T(8,128)(2,1)S(1)}, bf16[2,400,128]{2,1,0:T(8,128)(2,1)S(1)}, u32[]{:S(2)}, u32[]{:S(2)}) collective-permute-start(bf16[2,400,128]{2,1,0:T(8,128)(2,1)S(1)} %get-tuple-element.64), channel_id=1, source_target_pairs={{0,1},{1,2},{2,3},{3,0},{4,5},{5,6},{6,7},{7,4},{8,9},{9,10},{10,1... | collective-permute-start | bytes 614408 | tf_op jit(solution)/shard_map/ppermute | solution.py:20
  40.0 14.0 %collective-permute-start.7 = (bf16[2,400,128]{2,1,0:T(8,128)(2,1)S(1)}, bf16[2,400,128]{2,1,0:T(8,128)(2,1)S(1)}, u32[]{:S(2)}, u32[]{:S(2)}) collective-permute-start(bf16[2,400,128]{2,1,0:T(8,128)(2,1)S(1)} %get-tuple-element.65), channel_id=1, source_target_pairs={{0,3},{1,0},{2,1},{3,2},{4,7},{5,4},{6,5},{7,6},{8,11},{9,8},{10,9... | collective-permute-start | bytes 614408 | tf_op jit(solution)/shard_map/ppermute | solution.py:20
  42.7 11.4 %collective-permute-start.8 = (bf16[2,400,128]{2,1,0:T(8,128)(2,1)S(1)}, bf16[2,400,128]{2,1,0:T(8,128)(2,1)S(1)}, u32[]{:S(2)}, u32[]{:S(2)}) collective-permute-start(bf16[2,400,128]{2,1,0:T(8,128)(2,1)S(1)} %get-tuple-element.66), channel_id=1, source_target_pairs={{0,2},{1,3},{2,0},{3,1},{4,6},{5,7},{6,4},{7,5},{8,10},{9,11},{10,... | collective-permute-start | bytes 614408 | tf_op jit(solution)/shard_map/ppermute | solution.py:20
  55.2 7.2 %collective-permute-start.9 = (bf16[256,640]{1,0:T(8,128)(2,1)S(1)}, bf16[256,640]{1,0:T(8,128)(2,1)S(1)}, u32[]{:S(2)}, u32[]{:S(2)}) collective-permute-start(bf16[256,640]{1,0:T(8,128)(2,1)S(1)} %get-tuple-element.68), channel_id=1, source_target_pairs={{0,4},{4,0},{8,12},{12,8},{16,20},{20,16},{24,28},{28,24},{32,36},... | collective-permute-start | bytes 983048 | tf_op jit(solution)/shard_map/ppermute | solution.py:715
  58.9 37.9 %collective-permute-start.13 = (bf16[1024,512]{1,0:T(8,128)(2,1)S(1)}, bf16[1024,512]{1,0:T(8,128)(2,1)S(1)}, u32[]{:S(2)}, u32[]{:S(2)}) collective-permute-start(bf16[1024,512]{1,0:T(8,128)(2,1)S(1)} %get-tuple-element.80), channel_id=1, source_target_pairs={{0,1},{1,2},{2,3},{3,0},{4,5},{5,6},{6,7},{7,4},{8,9},{9,10},{10,1... | collective-permute-start | bytes 3145736 | tf_op jit(solution)/shard_map/ppermute | solution.py:20
  60.1 36.8 %collective-permute-start.14 = (bf16[1024,512]{1,0:T(8,128)(2,1)S(1)}, bf16[1024,512]{1,0:T(8,128)(2,1)S(1)}, u32[]{:S(2)}, u32[]{:S(2)}) collective-permute-start(bf16[1024,512]{1,0:T(8,128)(2,1)S(1)} %get-tuple-element.81), channel_id=1, source_target_pairs={{0,3},{1,0},{2,1},{3,2},{4,7},{5,4},{6,5},{7,6},{8,11},{9,8},{10,9... | collective-permute-start | bytes 3145736 | tf_op jit(solution)/shard_map/ppermute | solution.py:20
  61.6 45.8 %collective-permute-start.15 = (bf16[1024,512]{1,0:T(8,128)(2,1)S(1)}, bf16[1024,512]{1,0:T(8,128)(2,1)S(1)}, u32[]{:S(2)}, u32[]{:S(2)}) collective-permute-start(bf16[1024,512]{1,0:T(8,128)(2,1)S(1)} %get-tuple-element.82), channel_id=1, source_target_pairs={{0,2},{1,3},{2,0},{3,1},{4,6},{5,7},{6,4},{7,5},{8,10},{9,11},{10,... | collective-permute-start | bytes 3145736 | tf_op jit(solution)/shard_map/ppermute | solution.py:20
  90.1 4.9 %collective-permute-start.10 = (bf16[256,640]{1,0:T(8,128)(2,1)S(1)}, bf16[256,640]{1,0:T(8,128)(2,1)S(1)}, u32[]{:S(2)}, u32[]{:S(2)}) collective-permute-start(bf16[256,640]{1,0:T(8,128)(2,1)S(1)} %get-tuple-element.70), channel_id=1, source_target_pairs={{0,4},{4,0},{8,12},{12,8},{16,20},{20,16},{24,28},{28,24},{32,36},... | collective-permute-start | bytes 983048 | tf_op jit(solution)/shard_map/ppermute | solution.py:723
  96.8 17.8 %copy-start.14 = (bf16[192,1024]{1,0:T(8,128)(2,1)}, bf16[192,1024]{1,0:T(8,128)(2,1)S(1)}, u32[]{:S(2)}) copy-start(bf16[192,1024]{1,0:T(8,128)(2,1)S(1)} %get-tuple-element.75.refs_3_.refs_0_) | copy-start | bytes 1179652
  96.8 24.1 %copy-start.15 = (bf16[192,1024]{1,0:T(8,128)(2,1)}, bf16[192,1024]{1,0:T(8,128)(2,1)S(1)}, u32[]{:S(2)}) copy-start(bf16[192,1024]{1,0:T(8,128)(2,1)S(1)} %get-tuple-element.76.refs_1_) | copy-start | bytes 1179652
  107.4 22.1 %copy-start.4 = (bf16[1024,512]{1,0:T(8,128)(2,1)}, bf16[1024,512]{1,0:T(8,128)(2,1)S(1)}, u32[]{:S(2)}) copy-start(bf16[1024,512]{1,0:T(8,128)(2,1)S(1)} %get-tuple-element.83.refs_7_.refs_3_) | copy-start | bytes 3145732
  107.4 22.1 %copy-start.5 = (bf16[1024,512]{1,0:T(8,128)(2,1)}, bf16[1024,512]{1,0:T(8,128)(2,1)S(1)}, u32[]{:S(2)}) copy-start(bf16[1024,512]{1,0:T(8,128)(2,1)S(1)} %get-tuple-element.84.refs_8_.refs_4_) | copy-start | bytes 3145732
  107.4 22.1 %copy-start.6 = (bf16[1024,512]{1,0:T(8,128)(2,1)}, bf16[1024,512]{1,0:T(8,128)(2,1)S(1)}, u32[]{:S(2)}) copy-start(bf16[1024,512]{1,0:T(8,128)(2,1)S(1)} %get-tuple-element.85.refs_9_.refs_5_) | copy-start | bytes 3145732
  107.4 4.2 %collective-permute-start.16 = (bf16[1024,512]{1,0:T(8,128)(2,1)S(1)}, bf16[1024,512]{1,0:T(8,128)(2,1)S(1)}, u32[]{:S(2)}, u32[]{:S(2)}) collective-permute-start(bf16[1024,512]{1,0:T(8,128)(2,1)S(1)} %get-tuple-element.83.refs_7_.refs_3_), channel_id=1, source_target_pairs={{0,4},{4,0},{8,12},{12,8},{16,20},{20,16},{24,28},{28,24},{32,36},... | collective-permute-start | bytes 3145736 | tf_op jit(solution)/shard_map/ppermute | solution.py:728
  108.4 3.8 %collective-permute-start.17 = (bf16[1024,512]{1,0:T(8,128)(2,1)S(1)}, bf16[1024,512]{1,0:T(8,128)(2,1)S(1)}, u32[]{:S(2)}, u32[]{:S(2)}) collective-permute-start(bf16[1024,512]{1,0:T(8,128)(2,1)S(1)} %get-tuple-element.84.refs_8_.refs_4_), channel_id=1, source_target_pairs={{0,4},{4,0},{8,12},{12,8},{16,20},{20,16},{24,28},{28,24},{32,36},... | collective-permute-start | bytes 3145736 | tf_op jit(solution)/shard_map/ppermute | solution.py:728
  108.5 5.2 %collective-permute-start.18 = (bf16[1024,512]{1,0:T(8,128)(2,1)S(1)}, bf16[1024,512]{1,0:T(8,128)(2,1)S(1)}, u32[]{:S(2)}, u32[]{:S(2)}) collective-permute-start(bf16[1024,512]{1,0:T(8,128)(2,1)S(1)} %get-tuple-element.85.refs_9_.refs_5_), channel_id=1, source_target_pairs={{0,4},{4,0},{8,12},{12,8},{16,20},{20,16},{24,28},{28,24},{32,36},... | collective-permute-start | bytes 3145736 | tf_op jit(solution)/shard_map/ppermute | solution.py:728
  108.9 12.0 %collective-permute-start.11 = (bf16[192,1024]{1,0:T(8,128)(2,1)S(1)}, bf16[192,1024]{1,0:T(8,128)(2,1)}, u32[]{:S(2)}, u32[]{:S(2)}) collective-permute-start(bf16[192,1024]{1,0:T(8,128)(2,1)S(1)} %get-tuple-element.75.refs_3_.refs_0_), channel_id=1, source_target_pairs={{0,1},{1,2},{2,3},{3,0},{4,5},{5,6},{6,7},{7,4},{8,9},{9,10},{10,1... | collective-permute-start | bytes 1179656 | tf_op jit(solution)/shard_map/ppermute | solution.py:20
  109.8 11.1 %collective-permute-start.12 = (bf16[192,1024]{1,0:T(8,128)(2,1)S(1)}, bf16[192,1024]{1,0:T(8,128)(2,1)}, u32[]{:S(2)}, u32[]{:S(2)}) collective-permute-start(bf16[192,1024]{1,0:T(8,128)(2,1)S(1)} %get-tuple-element.76.refs_1_), channel_id=1, source_target_pairs={{0,3},{1,0},{2,1},{3,2},{4,7},{5,4},{6,5},{7,6},{8,11},{9,8},{10,9... | collective-permute-start | bytes 1179656 | tf_op jit(solution)/shard_map/ppermute | solution.py:20
  114.6 1.0 copy-start.7
  115.6 1.0 copy-start.8
  116.6 1.1 copy-start.9
  117.6 11.9 %collective-permute-start.21 = (bf16[192,1024]{1,0:T(8,128)(2,1)}, bf16[192,1024]{1,0:T(8,128)(2,1)}, u32[]{:S(2)}, u32[]{:S(2)}) collective-permute-start(bf16[192,1024]{1,0:T(8,128)(2,1)} %get-tuple-element.86.refs_2_), channel_id=1, source_target_pairs={{0,1},{1,2},{2,3},{3,0},{4,5},{5,6},{6,7},{7,4},{8,9},{9,10},{10,1... | collective-permute-start | bytes 1179656 | tf_op jit(solution)/shard_map/ppermute | solution.py:20
  118.5 11.0 %collective-permute-start.22 = (bf16[192,1024]{1,0:T(8,128)(2,1)}, bf16[192,1024]{1,0:T(8,128)(2,1)}, u32[]{:S(2)}, u32[]{:S(2)}) collective-permute-start(bf16[192,1024]{1,0:T(8,128)(2,1)} %get-tuple-element.90), channel_id=1, source_target_pairs={{0,3},{1,0},{2,1},{3,2},{4,7},{5,4},{6,5},{7,6},{8,11},{9,8},{10,9... | collective-permute-start | bytes 1179656 | tf_op jit(solution)/shard_map/ppermute | solution.py:20
  120.9 17.0 %collective-permute-start.19 = (bf16[192,1024]{1,0:T(8,128)(2,1)}, bf16[192,1024]{1,0:T(8,128)(2,1)}, u32[]{:S(2)}, u32[]{:S(2)}) collective-permute-start(bf16[192,1024]{1,0:T(8,128)(2,1)} %get-tuple-element.87.refs_2_), channel_id=1, source_target_pairs={{0,1},{1,2},{2,3},{3,0},{4,5},{5,6},{6,7},{7,4},{8,9},{9,10},{10,1... | collective-permute-start | bytes 1179656 | tf_op jit(solution)/shard_map/ppermute | solution.py:20
  121.7 16.3 %collective-permute-start.20 = (bf16[192,1024]{1,0:T(8,128)(2,1)}, bf16[192,1024]{1,0:T(8,128)(2,1)}, u32[]{:S(2)}, u32[]{:S(2)}) collective-permute-start(bf16[192,1024]{1,0:T(8,128)(2,1)} %get-tuple-element.88.refs_5_), channel_id=1, source_target_pairs={{0,3},{1,0},{2,1},{3,2},{4,7},{5,4},{6,5},{7,6},{8,11},{9,8},{10,9... | collective-permute-start | bytes 1179656 | tf_op jit(solution)/shard_map/ppermute | solution.py:20
  129.5 13.4 %copy-start.1 = (bf16[4096,2,8]{0,2,1:T(8,128)(2,1)S(1)}, bf16[4096,2,8]{0,2,1:T(8,128)(2,1)}, u32[]{:S(2)}) copy-start(bf16[4096,2,8]{0,2,1:T(8,128)(2,1)} %param.12) | copy-start | bytes 393220

commit v6 on v5

--- a/solution.py
+++ b/solution.py
@@ -47,17 +47,20 @@
         self.opposite = (around(self.plus, 1), around(self.minus, -1))
 
 
-def nothing(*refs):
-    pass
-
-
-def tied(arrays, after):
+def tied_kernel(with_mark, *refs):
+    if with_mark:
+        refs[-1][...] = jnp.zeros_like(refs[-1])
+
+
+def tied(arrays, after, with_mark=False):
     anywhere = pl.BlockSpec(memory_space=pl.ANY)
-    return pl.pallas_call(
-        nothing,
+    marks = int(with_mark)
+    return pl.pallas_call(
+        functools.partial(tied_kernel, with_mark),
         in_specs=[anywhere] * (len(arrays) + len(after)),
-        out_specs=[anywhere] * len(arrays),
-        out_shape=[jax.ShapeDtypeStruct(x.shape, x.dtype) for x in arrays],
+        out_specs=[anywhere] * len(arrays) + [pl.BlockSpec(memory_space=pltpu.VMEM)] * marks,
+        out_shape=[jax.ShapeDtypeStruct(x.shape, x.dtype) for x in arrays]
+        + [jax.ShapeDtypeStruct((8, LANES), F32)] * marks,
         input_output_aliases={n: n for n in range(len(arrays))},
         compiler_params=params(),
     )(*arrays, *after)
@@ -93,20 +96,19 @@
     refs[-1][...] = jnp.zeros_like(refs[-1])
 
 
-def flat(w, turn, before=None):
+def flat(w, first, steps, before=None):
     rows, heads, size = w.shape
-    steps = 4
-    block = rows // (2 * steps)
+    block = rows // 8
     args = [w] if before is None else [w, before]
     return pl.pallas_call(
         functools.partial(flat_kernel, len(args)),
         grid=(steps,),
         in_specs=[
-            pl.BlockSpec((block, heads, size), lambda j: (j + turn * steps, 0, 0)),
+            pl.BlockSpec((block, heads, size), lambda j: (j + first, 0, 0)),
             pl.BlockSpec(memory_space=pl.ANY),
         ][: len(args)],
         out_specs=[
-            pl.BlockSpec((block, heads * size), lambda j: (j + turn * steps, 0)),
+            pl.BlockSpec((block, heads * size), lambda j: (j + first, 0)),
             pl.BlockSpec((8, LANES), lambda j: (0, 0)),
         ],
         out_shape=[
@@ -115,7 +117,7 @@
         ],
         input_output_aliases={} if before is None else {1: 0},
         compiler_params=params(),
-        cost_estimate=cost(0, 2 * w.size),
+        cost_estimate=cost(0, 2 * w.size * steps // 8),
     )(*args)
 
 
@@ -227,17 +229,17 @@
 
 
 def cut_kernel(n_after, scalars, w_ref, *refs):
-    outs, sems = refs[n_after:-1], refs[-1]
+    outs, mark, sems = refs[n_after:-2], refs[-2], refs[-1]
     copies = Copies(sems)
     cols = outs[0].shape[1]
     n = w_ref.shape[1] // (2 * cols)
-    spots = [2 * scalars[0] + scalars[1], 2 * scalars[0] + 1 - scalars[1]]
-    spots += [2 * lax.rem(scalars[0] + to, n) + scalars[1] for to in range(1, n)]
     started = []
-    for at, out in zip(spots, outs):
+    for to, out in enumerate(outs):
+        at = 2 * lax.rem(scalars[0] + 1 + to, n) + scalars[1]
         started.append(
             copies.start(w_ref.at[:, pl.ds(pl.multiple_of(at * cols, cols), cols)], out)
         )
+    mark[...] = jnp.zeros_like(mark)
     for copy in started:
         copy.wait()
 
@@ -248,11 +250,12 @@
     return pl.pallas_call(
         functools.partial(cut_kernel, len(after)),
         in_specs=[pl.BlockSpec(memory_space=pltpu.SMEM)] + [anywhere] * (1 + len(after)),
-        out_specs=[vmem] * (nval + 1),
-        out_shape=[jax.ShapeDtypeStruct((rows, cols), w.dtype)] * (nval + 1),
-        scratch_shapes=[pltpu.SemaphoreType.DMA((nval + 1,))],
+        out_specs=[vmem] * nval,
+        out_shape=[jax.ShapeDtypeStruct((rows, cols), w.dtype)] * (nval - 1)
+        + [jax.ShapeDtypeStruct((8, LANES), F32)],
+        scratch_shapes=[pltpu.SemaphoreType.DMA((nval - 1,))],
         compiler_params=params(),
-        cost_estimate=cost(0, 4 * rows * cols * (nval + 1)),
+        cost_estimate=cost(0, 4 * rows * cols * (nval - 1)),
     )(jnp.stack([me, core]), w, *after)
 
 
@@ -261,7 +264,8 @@
     take = lambda n: [refs.pop(0) for _ in range(n)]
     ngroups = len(counts)
     groups = [take(n) for n in counts]
-    halves = [take(4), take(4)]
+    (local,) = take(1)
+    halves = [take(3), take(3)]
     total_ref = take(1)[0] if with_total else None
     out, x, ws, held, sems, out_sems = refs
     copies, out_copies = Copies(sems), Copies(out_sems)
@@ -271,10 +275,14 @@
     cols, vlocal = ws.shape[2], chunk // 8
     row = lambda n: pl.ds(pl.multiple_of(n * vlocal, vlocal), vlocal)
 
+    sides = (core, 1 - core)
+
     def load(t):
+        at = (2 * sources[0] + sides[t]) * cols
+        mine = local.at[:, pl.ds(pl.multiple_of(at, cols), cols)]
         started = []
         for g in range(ngroups):
-            for n, w in enumerate(halves[t]):
+            for n, w in enumerate([mine, *halves[t]]):
                 for h in range(2):
                     to = row(g * 8 + h * 4 + sources[n])
                     source = w.at[row(scalars[g] * 2 + h), :]
@@ -285,7 +293,7 @@
     for g in range(ngroups):
         put_rows(groups[g], x.at[:, pl.ds(g * chunk, chunk)])
     last = []
-    for t, side in enumerate((core, 1 - core)):
+    for t, side in enumerate(sides):
         columns = pl.ds(pl.multiple_of(side * cols, cols), cols)
         for copy in started[t]:
             copy.wait()
@@ -298,19 +306,19 @@
         copy.wait()
 
 
-def out_product(rows, groups, index, sources, core, mine, others, total, dtype):
+def out_product(rows, groups, index, sources, core, local, mine, others, total, dtype):
     chunk = groups[0][0].shape[1]
     cols = mine[0].shape[1]
     anywhere, vmem = (pl.BlockSpec(memory_space=m) for m in (pl.ANY, pltpu.VMEM))
     pieces = [x for g in groups for x in g]
     totals = [] if total is None else [total]
-    args = [*pieces, *mine, *others, *totals]
+    args = [*pieces, local, *mine, *others, *totals]
     n = len(groups)
     return pl.pallas_call(
         functools.partial(out_kernel, [len(g) for g in groups], total is not None),
         in_specs=[pl.BlockSpec(memory_space=pltpu.SMEM)]
         + [vmem] * len(pieces)
-        + [anywhere] * 8
+        + [anywhere] * 7
         + [vmem] * len(totals),
         out_specs=anywhere,
         out_shape=jax.ShapeDtypeStruct((rows, 2 * cols), dtype),
@@ -392,32 +400,43 @@
     return [pieces[0], around(pieces[1], 1), around(pieces[3], -1), around(pieces[2], 2)]
 
 
-def within_kernel(counts, scalars, *refs):
+def within_kernel(counts, scalars, bias_ref, *refs):
     pieces = iter(refs[: sum(counts)])
-    wg_ref, bias_ref, q_ref, k_ref, kwt_ref, p_ref, stat_ref, mark_ref = refs[sum(counts) :]
+    wg_ref, q_ref, k_ref, kwt_ref, p_ref, stat_ref, mark_ref, g_ref = refs[sum(counts) :]
     own, rows, _ = p_ref.shape
     qsize = q_ref.shape[1] // own
     chunk = refs[0].shape[1]
-    g = bias_ref[...]
+    heads = bias_ref.shape[1]
+    gates = None
     for n, count in enumerate(counts):
-        w = wg_ref[pl.ds(pl.multiple_of(scalars[n] * chunk, chunk), chunk), :]
-        terms = []
-        for _ in range(count):
-            x = next(pieces)[: rows // count]
-            terms.append(jnp.dot(x, w, preferred_element_type=F32))
-        g = g + (terms[0] if count == 1 else jnp.concatenate(terms, axis=0))
-    logf = jnp.minimum(g, 0.0) - jnp.log1p(jnp.exp(-jnp.abs(g)))
+        w = wg_ref[:, pl.ds(pl.multiple_of(scalars[n] * chunk, chunk), chunk)]
+        x = [next(pieces)[: rows // count] for _ in range(count)]
+        x = x[0] if count == 1 else jnp.concatenate(x, axis=0)
+        term = lax.dot_general(w, x, (((1,), (1,)), ((), ())), preferred_element_type=F32)
+        gates = term if gates is None else gates + term
+    g_ref[...] = gates
     late = lax.broadcasted_iota(jnp.int32, (rows, rows), 0)
     early = lax.broadcasted_iota(jnp.int32, (rows, rows), 1)
     causal = late >= early
+    line = lax.broadcasted_iota(jnp.int32, (8, rows), 0)
+    igate, forget = jnp.zeros((8, rows), F32), jnp.zeros((8, rows), F32)
+    for h in range(own):
+        head = scalars[0] * own + h
+        igate = jnp.where(line == h, g_ref[pl.ds(head, 1), :] + bias_ref[0, head], igate)
+        row = g_ref[pl.ds(heads + head, 1), :] + bias_ref[1, head]
+        forget = jnp.where(line == h, row, forget)
+    logf = jnp.minimum(forget, 0.0) - jnp.log1p(jnp.exp(-jnp.abs(forget)))
     cumb = jnp.dot(
-        causal.astype(F32), logf, precision=lax.Precision.HIGHEST, preferred_element_type=F32
+        logf,
+        (early >= late).astype(F32),
+        precision=lax.Precision.HIGHEST,
+        preferred_element_type=F32,
     )
-    cumb = pltpu.roll(cumb, LANES - own, axis=1)
-    gap = g - cumb
-    gap_rows = gap.T
+    gap_rows = igate - cumb
+    both = jnp.concatenate([gap_rows, cumb, jnp.zeros((LANES - 16, rows), F32)], axis=0).T
+    gap = both
     most = jnp.max(gap, axis=0, keepdims=True)
-    total = cumb[rows - 1 : rows]
+    total = pltpu.roll(both[rows - 8 : rows], LANES - 8, axis=1)[7:8]
     mark_ref[...] = jnp.concatenate([total + most, total, jnp.zeros((6, LANES), F32)], axis=0)
     lane = lax.broadcasted_iota(jnp.int32, (rows, LANES), 1)
     stat = jnp.zeros((rows, LANES), F32)
@@ -444,7 +463,7 @@
     vmem = pl.BlockSpec(memory_space=pltpu.VMEM)
     return pl.pallas_call(
         functools.partial(within_kernel, [len(g) for g in groups]),
-        in_specs=[pl.BlockSpec(memory_space=pltpu.SMEM)] + [vmem] * (len(pieces) + 4),
+        in_specs=[pl.BlockSpec(memory_space=pltpu.SMEM)] * 2 + [vmem] * (len(pieces) + 3),
         out_specs=[vmem] * 4,
         out_shape=[
             jax.ShapeDtypeStruct((width, rows), BF16),
@@ -452,9 +471,10 @@
             jax.ShapeDtypeStruct((rows, LANES), F32),
             jax.ShapeDtypeStruct((8, LANES), F32),
         ],
+        scratch_shapes=[pltpu.VMEM((wg.shape[0], rows), F32)],
         compiler_params=params(),
         cost_estimate=cost(4 * rows * rows * width, 8 * rows * width, own * rows * rows),
-    )(jnp.stack(list(index)), *pieces, wg, bias, q, k)
+    )(jnp.stack(list(index)), bias, *pieces, wg, q, k)
 
 
 def parts_of(x):
@@ -689,28 +709,26 @@
     half = rows // 2
     upper, lower = moved([tokens], [[(0, 0, half)], [(0, half, half)]], [])
     ring = Ring(upper, lower, [upper, lower])
-    wg = lax.dynamic_slice_in_dim(w_gate, me * own, own, axis=2).reshape(width, 2 * own)
-    wg = jnp.pad(wg, ((0, 0), (0, LANES - 2 * own)))
-    bias = lax.dynamic_slice_in_dim(gate_bias, me * own, own, axis=1).reshape(1, 2 * own)
-    bias = jnp.pad(bias, ((0, 0), (0, LANES - 2 * own)))
-    wv, early = flat(w_value, 0)
-    ring.second([early, wg])
-    wv, late = flat(w_value, 1, wv)
+    wg = w_gate.transpose(1, 2, 0).reshape(2 * heads, width)
+    wv, early = flat(w_value, 0, 2)
+    ring.second([early])
+    wv, late = flat(w_value, 2, 2, wv)
     ring.forward([late])
+    wv, _ = flat(w_value, 4, 4, wv)
     groups = [(tokens,), ring.left, ring.right]
     acc = product(rows, groups, index[:3], [wv], [F32])[0]
     core = place % 2
     cores = [(i, i ^ 1) for i in range(blocks)]
-    kept, away, *pieces = cut_by_device(
-        w_out.reshape(heads * vlocal, -1), me, core, nval, [acc]
-    )
-    values = values_by_device(ring.opposite, index[3], me, wv, acc, norm_gain, own, kept)
-    halves = exchanged([None, *tied(pieces, values[:1])])[1:]
+    local = w_out.reshape(heads * vlocal, -1)
+    *pieces, mark = cut_by_device(local, me, core, nval, [acc])
+    values = values_by_device(ring.opposite, index[3], me, wv, acc, norm_gain, own, mark)
+    pieces = tied(pieces, values[:1])
+    halves = exchanged([None, *pieces])[1:]
     groups.append(ring.opposite)
     q, k = product(rows, groups, index, [w_query, w_key], [BF16] * 2, values[:1])
 
     values = exchanged(values)
-    kwt, p, stat, mark = within(groups, index, wg, bias, q, k, own)
+    kwt, p, stat, mark = within(groups, index, wg, gate_bias, q, k, own)
     mine, other, v, gain = summary(index, core, kwt, mark, values)
     got = lax.ppermute(other, "seq", cores)
     chips = [list(range(n, blocks, 2)) for n in range(2)]
@@ -726,11 +744,11 @@
     ring = Ring(upper, lower, [upper, lower])
     halves = tied(halves, [upper])
     others = [lax.ppermute(x, "seq", cores) for x in halves]
-    ring.second(others)
+    *others, there = tied(others, [], with_mark=True)
+    ring.second([there])
     ring.forward()
-    halves, others = [kept, *halves], [away, *others]
     groups = [ring.own, ring.left, ring.right]
-    weights = (index, core, halves, others)
+    weights = (index, core, local, halves, others)
     acc = out_product(rows, groups, index[:3], *weights, None, F32)
     return out_product(rows, [ring.opposite], index[3:], *weights, acc, BF16)
 

time: 144 us -> 136 us (0.944)
  Pallas kernels: 55.1 us -> 49.3 us
  local copies, waits for them, and re-layouts: 8.71 us -> 5.51 us
  waiting for transfers between devices: 19.3 us -> 21.1 us
    pallas_call x3, Pallas kernels: 3.94 us -> 1.03 us  [moved(): pl.pallas_call(functools.partial(moved_kernel, len(arrays), len(after), p...]
    ppermute x18, waiting for transfers between devices: 16.6 us -> 18.3 us  [around(): return lax.ppermute(x, 'val', [(i, (i + distance) % n) for i in range(n)])]
    reshape x3 -> x0, local copies, waits for them, and re-layouts: 1.49 us -> none  [the longest x2 1.41 us: per_device(): lax.dynamic_slice_in_dim(w_gate, me * own, own, axis=2)]
    unnamed x38 -> x26, local copies, waits for them, and re-layouts: 5.5 us -> 4.19 us
    pallas_call x2 -> x3, Pallas kernels: 9.77 us -> 10.2 us  [flat(): pl.pallas_call(functools.partial(flat_kernel, len(args)), grid=(steps,),...]
  transfers between devices with their start and end apart: 23 -> 23, of which waited for: 8 -> 10; matrix products, arithmetic and copies ran while one was open for 2% -> 1% of each run, Pallas kernels for 30% -> 29%
where the time goes in v6:
time: 136 us
  Pallas kernels  49.3 us (36%)
  starting transfers between devices  32.9 us (24%)
  blocking collectives  26.2 us (19%)
  waiting for transfers between devices  21.1 us (16%)
  local copies, waits for them, and re-layouts  5.51 us (4%)
    ppermute x18, starting transfers between devices, around(): return lax.ppermute(x, 'val', [(i, (i + distance) % n) for i in range(n)])  24 us
    ppermute x18, waiting for transfers between devices, around(): return lax.ppermute(x, 'val', [(i, (i + distance) % n) for i in range(n)])  18.3 us
    all_to_all x1, blocking collectives, per_device(): both = lax.all_to_all(both, 'seq', 0, 0, axis_index_groups=chips)  15.2 us
    pallas_call x2, Pallas kernels, out_product(): pl.pallas_call(functools.partial(out_kernel, [len(g) for g in groups], to...  12.7 us
    pallas_call x2, Pallas kernels, product(): pl.pallas_call(functools.partial(product_kernel, [len(g) for g in groups]...  11.3 us
    all_to_all x1, blocking collectives, per_device(): lax.all_to_all(prefixes(both), 'seq', 0, 0, axis_index_groups=chips)  11.1 us
    pallas_call x3, Pallas kernels, flat(): pl.pallas_call(functools.partial(flat_kernel, len(args)), grid=(steps,),...  10.2 us
    unnamed x26, local copies, waits for them, and re-layouts  4.19 us
  transfers between devices with their start and end apart: 23, of which 10 were waited for; matrix products, arithmetic and copies ran while one was open for 1% of the time, Pallas kernels for 29%

profile of v6, /device:TPU:1, one launch (start us, length us, event | category | flops | bytes accessed | tf_op | source)
XLA Modules:
  0.0 135.8 jit_solution(17848839499660187802)
XLA Ops:
  0.0 1.1 copy-done.6
  1.2 2.2 %collective-permute-start = (bf16[192,1024]{1,0:T(8,128)(2,1)S(1)}, bf16[192,1024]{1,0:T(8,128)(2,1)S(1)}, u32[]{:S(2)}, u32[]{:S(2)}) collective-permute-start(bf16[192,1024]{1,0:T(8,128)(2,1)S(1)} %get-tuple-element.52.refs_0_), channel_id=1, source_target_pairs={{0,1},{1,2},{2,3},{3,0},{4,5},{5,6},{6,7},{7,4},{8,9},{9,10},{10,1... | collective-permute-start | bytes 1179656 | tf_op jit(solution)/shard_map/ppermute | solution.py:20
  3.4 1.5 %collective-permute-start.1 = (bf16[192,1024]{1,0:T(8,128)(2,1)S(1)}, bf16[192,1024]{1,0:T(8,128)(2,1)S(1)}, u32[]{:S(2)}, u32[]{:S(2)}) collective-permute-start(bf16[192,1024]{1,0:T(8,128)(2,1)S(1)} %get-tuple-element.53.refs_1_), channel_id=1, source_target_pairs={{0,3},{1,0},{2,1},{3,2},{4,7},{5,4},{6,5},{7,6},{8,11},{9,8},{10,9... | collective-permute-start | bytes 1179656 | tf_op jit(solution)/shard_map/ppermute | solution.py:20
  4.9 2.7 %shard_map.83 = (bf16[4096,1024]{1,0:T(8,128)(2,1)}, f32[8,128]{1,0:T(8,128)S(1)}) custom-call(bf16[4096,8,128]{2,1,0:T(8,128)(2,1)} %w_ref.5), custom_call_target="tpu_custom_call" | custom-call | bytes 2097152 | tf_op jit(solution)/shard_map/pallas_call | solution.py:103
  7.7 2.7 %collective-permute-start.3 = (bf16[192,1024]{1,0:T(8,128)(2,1)S(1)}, bf16[192,1024]{1,0:T(8,128)(2,1)S(1)}, u32[]{:S(2)}, u32[]{:S(2)}) collective-permute-start(bf16[192,1024]{1,0:T(8,128)(2,1)S(1)} %get-tuple-element.59), channel_id=1, source_target_pairs={{0,3},{1,0},{2,1},{3,2},{4,7},{5,4},{6,5},{7,6},{8,11},{9,8},{10,9... | collective-permute-start | bytes 1179656 | tf_op jit(solution)/shard_map/ppermute | solution.py:20
  10.4 2.7 %shard_map.85 = (bf16[4096,1024]{1,0:T(8,128)(2,1)}, f32[8,128]{1,0:T(8,128)S(1)}) custom-call(bf16[4096,8,128]{2,1,0:T(8,128)(2,1)} %w_ref.5, bf16[4096,1024]{1,0:T(8,128)(2,1)} %get-tuple-element.56.refs_0_), custom_call_target="tpu_custom_call", output_to_operand_aliasing={{0}: (1, {})} | custom-call | bytes 2097152 | tf_op jit(solution)/shard_map/pallas_call | solution.py:103
  13.5 0.8 collective-permute-start.4
  14.3 1.8 %collective-permute-start.5 = (bf16[192,1024]{1,0:T(8,128)(2,1)S(1)}, bf16[192,1024]{1,0:T(8,128)(2,1)S(1)}, u32[]{:S(2)}, u32[]{:S(2)}) collective-permute-start(bf16[192,1024]{1,0:T(8,128)(2,1)S(1)} %get-tuple-element.60.refs_4_), channel_id=1, source_target_pairs={{0,3},{1,0},{2,1},{3,2},{4,7},{5,4},{6,5},{7,6},{8,11},{9,8},{10,9... | collective-permute-start | bytes 1179656 | tf_op jit(solution)/shard_map/ppermute | solution.py:20
  16.4 4.9 %shard_map.87 = (bf16[4096,1024]{1,0:T(8,128)(2,1)}, f32[8,128]{1,0:T(8,128)}) custom-call(bf16[4096,8,128]{2,1,0:T(8,128)(2,1)} %w_ref.5, bf16[4096,1024]{1,0:T(8,128)(2,1)} %get-tuple-element.61.refs_0_), custom_call_target="tpu_custom_call", output_to_operand_aliasing={{0}: (1, {})} | custom-call | bytes 4194304 | tf_op jit(solution)/shard_map/pallas_call | solution.py:103
  21.3 0.6 collective-permute-done.2.refs_2_
  21.9 5.2 %shard_map.88.refs_0_.acc_ref = f32[384,1024]{1,0:T(8,128)S(1)} custom-call(s32[3]{0:T(128)S(1)} %pad_add_fusion.2.scalars, bf16[384,1024]{1,0:T(8,128)(2,1)S(1)} %copy-done.7, bf16[192,1024]{1,0:T(8,128)(2,1)S(1)} %get-tuple-element.58.refs_1_, bf16[192,1024]{1,0:T(8,128)(2,1)S(1)} %collective-permute-done.2.refs_2_, ...), custom_call_target="tpu_custom_call" | custom-call | flops 2415919104 | bytes 10223616 | tf_op jit(solution)/shard_map/pallas_call | solution.py:211
  27.1 2.5 %shard_map.89 = (bf16[1024,512]{1,0:T(8,128)(2,1)S(1)}, bf16[1024,512]{1,0:T(8,128)(2,1)S(1)}, bf16[1024,512]{1,0:T(8,128)(2,1)S(1)}, f32[8,128]{1,0:T(8,128)S(1)}) custom-call(s32[2]{0:T(128)S(1)} %pad_add_fusion.3.scalars, bf16[1024,4096]{1,0:T(8,128)(2,1)} %bitcast.15, f32[384,1024]{1,0:T(8,128)S(1)} %shard_map.88.refs_0_.acc_ref), custom_call_target="tpu_custom_call" | custom-call | bytes 6291456 | tf_op jit(solution)/shard_map/pallas_call | solution.py:250
  29.6 0.8 collective-permute-done.4.upper.refs_5_
  30.4 3.9 %shard_map.90 = (bf16[2,400,128]{2,1,0:T(8,128)(2,1)S(1)}, bf16[2,400,128]{2,1,0:T(8,128)(2,1)S(1)}, bf16[2,400,128]{2,1,0:T(8,128)(2,1)S(1)}, bf16[2,400,128]{2,1,0:T(8,128)(2,1)S(1)}) custom-call(s32[2]{0:T(128)S(1)} %pad_add_fusion.1.scalars, bf16[192,1024]{1,0:T(8,128)(2,1)S(1)} %collective-permute-done.4.upper.refs_5_, ...), custom_call_target="tpu_custom_call" | custom-call | flops 805306368 | bytes 5242880 | tf_op jit(solution)/shard_map/pallas_call | solution.py:376
  34.3 0.9 collective-permute-start.6
  35.2 1.8 %collective-permute-start.7 = (bf16[2,400,128]{2,1,0:T(8,128)(2,1)S(1)}, bf16[2,400,128]{2,1,0:T(8,128)(2,1)S(1)}, u32[]{:S(2)}, u32[]{:S(2)}) collective-permute-start(bf16[2,400,128]{2,1,0:T(8,128)(2,1)S(1)} %get-tuple-element.70), channel_id=1, source_target_pairs={{0,3},{1,0},{2,1},{3,2},{4,7},{5,4},{6,5},{7,6},{8,11},{9,8},{10,9... | collective-permute-start | bytes 614408 | tf_op jit(solution)/shard_map/ppermute | solution.py:20
  37.0 1.0 collective-permute-start.8
  38.0 6.1 %shard_map.91 = (bf16[384,512]{1,0:T(8,128)(2,1)S(1)}, bf16[384,512]{1,0:T(8,128)(2,1)S(1)}) custom-call(s32[4]{0:T(128)S(1)} %pad_add_fusion.scalars, bf16[384,1024]{1,0:T(8,128)(2,1)S(1)} %copy-done.7, bf16[192,1024]{1,0:T(8,128)(2,1)S(1)} %get-tuple-element.58.refs_1_, bf16[192,1024]{1,0:T(8,128)(2,1)S(1)} %collective-permute-done.2.refs_2_, ...), custom_call_target="tpu_custom_call" | custom-call | flops 3221225472 | bytes 13107200 | tf_op jit(solution)/shard_map/pallas_call | solution.py:211
  44.2 2.9 %shard_map.92 = (bf16[512,384]{1,0:T(8,128)(2,1)S(1)}, bf16[2,384,384]{2,1,0:T(8,128)(2,1)S(1)}, f32[384,128]{1,0:T(8,128)S(1)}, f32[8,128]{1,0:T(8,128)S(1)}) custom-call(s32[4]{0:T(128)S(1)} %pad_add_fusion.scalars, f32[2,8]{1,0:T(2,128)S(1)} %copy-done.12, bf16[384,1024]{1,0:T(8,128)(2,1)S(1)} %copy-done.7, ...), custom_call_target="tpu_custom_call" | custom-call | flops 301989888 | bytes 1572864 | tf_op jit(solution)/shard_map/pallas_call | solution.py:464
  47.1 1.1 shard_map.93
  48.3 3.4 %collective-permute-start.9 = (bf16[256,640]{1,0:T(8,128)(2,1)S(1)}, bf16[256,640]{1,0:T(8,128)(2,1)S(1)}, u32[]{:S(2)}, u32[]{:S(2)}) collective-permute-start(bf16[256,640]{1,0:T(8,128)(2,1)S(1)} %get-tuple-element.73), channel_id=1, source_target_pairs={{0,4},{4,0},{8,12},{12,8},{16,20},{20,16},{24,28},{28,24},{32,36},... | collective-permute-start | bytes 983048 | tf_op jit(solution)/shard_map/ppermute | solution.py:733
  52.1 2.2 %collective-permute-start.14 = (bf16[1024,512]{1,0:T(8,128)(2,1)S(1)}, bf16[1024,512]{1,0:T(8,128)(2,1)S(1)}, u32[]{:S(2)}, u32[]{:S(2)}) collective-permute-start(bf16[1024,512]{1,0:T(8,128)(2,1)S(1)} %get-tuple-element.86), channel_id=1, source_target_pairs={{0,3},{1,0},{2,1},{3,2},{4,7},{5,4},{6,5},{7,6},{8,11},{9,8},{10,9... | collective-permute-start | bytes 3145736 | tf_op jit(solution)/shard_map/ppermute | solution.py:20
  55.3 15.2 %all_to_all.10.got_ref = bf16[16,16,640]{2,1,0:T(8,128)(2,1)S(1)} all-to-all(bf16[16,16,640]{2,1,0:T(8,128)(2,1)S(1)} %bitcast.13), channel_id=1, replica_groups={{0,8,16,24,32,40,48,56,64,72,80,88,96,104,112,120},{4,12,20,28,36,44,52..., dimensions={0} | all-to-all | bytes 655360 | tf_op jit(solution)/shard_map/all_to_all | solution.py:737
  70.8 11.1 %all_to_all.11 = bf16[16,16,640]{2,1,0:T(8,128)(2,1)S(1)} all-to-all(bf16[16,16,640]{2,1,0:T(8,128)(2,1)S(1)} %shard_map.95), channel_id=1, replica_groups={{0,8,16,24,32,40,48,56,64,72,80,88,96,104,112,120},{4,12,20,28,36,44,52..., dimensions={0} | all-to-all | bytes 655360 | tf_op jit(solution)/shard_map/all_to_all | solution.py:739
  82.3 3.6 %collective-permute-start.10 = (bf16[256,640]{1,0:T(8,128)(2,1)S(1)}, bf16[256,640]{1,0:T(8,128)(2,1)S(1)}, u32[]{:S(2)}, u32[]{:S(2)}) collective-permute-start(bf16[256,640]{1,0:T(8,128)(2,1)S(1)} %get-tuple-element.75), channel_id=1, source_target_pairs={{0,4},{4,0},{8,12},{12,8},{16,20},{20,16},{24,28},{28,24},{32,36},... | collective-permute-start | bytes 983048 | tf_op jit(solution)/shard_map/ppermute | solution.py:741
  86.0 0.6 shard_map.97.numer_ref
  86.5 0.7 collective-permute-done.10.got
  87.2 1.8 %shard_map.98 = (bf16[192,1024]{1,0:T(8,128)(2,1)S(1)}, bf16[192,1024]{1,0:T(8,128)(2,1)S(1)}) custom-call(s32[1]{0:T(128)} %bitcast.4.scalars, bf16[384,512]{1,0:T(8,128)(2,1)S(1)} %get-tuple-element.65.refs_8_.q_ref, bf16[256,640]{1,0:T(8,128)(2,1)S(1)} %get-tuple-element.74.mine, bf16[256,640]{1,0:T(8,128)(2,1)S(1)} %collective-permute-done.10.got, ...), custom_call_target="tpu_custom_call" | custom-call | flops 201326592 | bytes 3145728 | tf_op jit(solution)/shard_map/pallas_call | solution.py:686
  89.1 10.6 %collective-permute-done.15.refs_2_ = bf16[1024,512]{1,0:T(8,128)(2,1)S(1)} collective-permute-done((bf16[1024,512]{1,0:T(8,128)(2,1)S(1)}, bf16[1024,512]{1,0:T(8,128)(2,1)S(1)}, u32[]{:S(2)}, u32[]{:S(2)}) %collective-permute-start.15) | collective-permute-done | bytes 1048608 | tf_op jit(solution)/shard_map/ppermute | solution.py:20
  99.7 1.4 collective-permute-start.16
  101.6 0.6 collective-permute-start.11
  102.1 2.1 %collective-permute-start.12 = (bf16[192,1024]{1,0:T(8,128)(2,1)S(1)}, bf16[192,1024]{1,0:T(8,128)(2,1)}, u32[]{:S(2)}, u32[]{:S(2)}) collective-permute-start(bf16[192,1024]{1,0:T(8,128)(2,1)S(1)} %get-tuple-element.81.refs_1_), channel_id=1, source_target_pairs={{0,3},{1,0},{2,1},{3,2},{4,7},{5,4},{6,5},{7,6},{8,11},{9,8},{10,9... | collective-permute-start | bytes 1179656 | tf_op jit(solution)/shard_map/ppermute | solution.py:20
  104.3 0.6 collective-permute-done.17.refs_1_
  104.8 1.5 %collective-permute-done.18.refs_2_ = bf16[1024,512]{1,0:T(8,128)(2,1)S(1)} collective-permute-done((bf16[1024,512]{1,0:T(8,128)(2,1)S(1)}, bf16[1024,512]{1,0:T(8,128)(2,1)S(1)}, u32[]{:S(2)}, u32[]{:S(2)}) %collective-permute-start.18) | collective-permute-done | bytes 1048608 | tf_op jit(solution)/shard_map/ppermute | solution.py:746
  106.4 1.0 copy-done.3
  107.3 1.0 copy-done.4
  108.3 1.1 copy-done.5
  109.4 0.9 shard_map.102
  110.9 2.1 %collective-permute-start.22 = (bf16[192,1024]{1,0:T(8,128)(2,1)}, bf16[192,1024]{1,0:T(8,128)(2,1)}, u32[]{:S(2)}, u32[]{:S(2)}) collective-permute-start(bf16[192,1024]{1,0:T(8,128)(2,1)} %get-tuple-element.98), channel_id=1, source_target_pairs={{0,3},{1,0},{2,1},{3,2},{4,7},{5,4},{6,5},{7,6},{8,11},{9,8},{10,9... | collective-permute-start | bytes 1179656 | tf_op jit(solution)/shard_map/ppermute | solution.py:20
  113.0 0.6 collective-permute-done.11.refs_0_
  113.6 0.8 collective-permute-start.19
  114.4 1.8 %collective-permute-start.20 = (bf16[192,1024]{1,0:T(8,128)(2,1)}, bf16[192,1024]{1,0:T(8,128)(2,1)}, u32[]{:S(2)}, u32[]{:S(2)}) collective-permute-start(bf16[192,1024]{1,0:T(8,128)(2,1)} %get-tuple-element.94.refs_5_), channel_id=1, source_target_pairs={{0,3},{1,0},{2,1},{3,2},{4,7},{5,4},{6,5},{7,6},{8,11},{9,8},{10,9... | collective-permute-start | bytes 1179656 | tf_op jit(solution)/shard_map/ppermute | solution.py:20
  116.2 0.6 stack.38.scalars
  116.8 0.7 stack.31.scalars
  117.5 4.7 %collective-permute-done.21.refs_3_ = bf16[192,1024]{1,0:T(8,128)(2,1)} collective-permute-done((bf16[192,1024]{1,0:T(8,128)(2,1)}, bf16[192,1024]{1,0:T(8,128)(2,1)}, u32[]{:S(2)}, u32[]{:S(2)}) %collective-permute-start.21) | collective-permute-done | bytes 393248 | tf_op jit(solution)/shard_map/ppermute | solution.py:20
  122.2 7.7 %shard_map.104.refs_9_ = f32[384,1024]{1,0:T(8,128)} custom-call(s32[8]{0:T(128)} %stack.38.scalars, bf16[192,1024]{1,0:T(8,128)(2,1)} %copy-done.8, bf16[192,1024]{1,0:T(8,128)(2,1)} %copy-done.9, bf16[192,1024]{1,0:T(8,128)(2,1)} %get-tuple-element.93.refs_2_, bf16[192,1024]{1,0:T(8,128)(2,1)} %collective-permute-done.21.refs_3_, ...), custom_call_target="tpu_custom_call" | custom-call | flops 2415919104 | bytes 7864320 | tf_op jit(solution)/shard_map/pallas_call | solution.py:317
  129.9 0.7 collective-permute-done.19.refs_0_
  130.6 5.0 %shard_map.105 = bf16[384,1024]{1,0:T(8,128)(2,1)} custom-call(s32[6]{0:T(128)} %stack.31.scalars, bf16[192,1024]{1,0:T(8,128)(2,1)} %collective-permute-done.19.refs_0_, bf16[192,1024]{1,0:T(8,128)(2,1)} %collective-permute-done.20.refs_1_, bf16[1024,4096]{1,0:T(8,128)(2,1)} %bitcast.17, bf16[1024,512]{1,0:T(8,128)(2,1)} %copy-done, ...), custom_call_target="tpu_custom_call" | custom-call | flops 805306368 | bytes 3670016 | tf_op jit(solution)/shard_map/pallas_call | solution.py:317
  (57 shorter events, 4.2 us)
Async XLA Ops:
  0.0 1.1 copy-start.6
  1.2 12.3 %collective-permute-start = (bf16[192,1024]{1,0:T(8,128)(2,1)S(1)}, bf16[192,1024]{1,0:T(8,128)(2,1)S(1)}, u32[]{:S(2)}, u32[]{:S(2)}) collective-permute-start(bf16[192,1024]{1,0:T(8,128)(2,1)S(1)} %get-tuple-element.52.refs_0_), channel_id=1, source_target_pairs={{0,1},{1,2},{2,3},{3,0},{4,5},{5,6},{6,7},{7,4},{8,9},{9,10},{10,1... | collective-permute-start | bytes 1179656 | tf_op jit(solution)/shard_map/ppermute | solution.py:20
  3.4 10.1 %collective-permute-start.1 = (bf16[192,1024]{1,0:T(8,128)(2,1)S(1)}, bf16[192,1024]{1,0:T(8,128)(2,1)S(1)}, u32[]{:S(2)}, u32[]{:S(2)}) collective-permute-start(bf16[192,1024]{1,0:T(8,128)(2,1)S(1)} %get-tuple-element.53.refs_1_), channel_id=1, source_target_pairs={{0,3},{1,0},{2,1},{3,2},{4,7},{5,4},{6,5},{7,6},{8,11},{9,8},{10,9... | collective-permute-start | bytes 1179656 | tf_op jit(solution)/shard_map/ppermute | solution.py:20
  7.6 14.3 %collective-permute-start.2 = (bf16[192,1024]{1,0:T(8,128)(2,1)S(1)}, bf16[192,1024]{1,0:T(8,128)(2,1)S(1)}, u32[]{:S(2)}, u32[]{:S(2)}) collective-permute-start(bf16[192,1024]{1,0:T(8,128)(2,1)S(1)} %get-tuple-element.55.refs_2_), channel_id=1, source_target_pairs={{0,1},{1,2},{2,3},{3,0},{4,5},{5,6},{6,7},{7,4},{8,9},{9,10},{10,1... | collective-permute-start | bytes 1179656 | tf_op jit(solution)/shard_map/ppermute | solution.py:20
  7.7 14.2 %collective-permute-start.3 = (bf16[192,1024]{1,0:T(8,128)(2,1)S(1)}, bf16[192,1024]{1,0:T(8,128)(2,1)S(1)}, u32[]{:S(2)}, u32[]{:S(2)}) collective-permute-start(bf16[192,1024]{1,0:T(8,128)(2,1)S(1)} %get-tuple-element.59), channel_id=1, source_target_pairs={{0,3},{1,0},{2,1},{3,2},{4,7},{5,4},{6,5},{7,6},{8,11},{9,8},{10,9... | collective-permute-start | bytes 1179656 | tf_op jit(solution)/shard_map/ppermute | solution.py:20
  13.5 16.8 %collective-permute-start.4 = (bf16[192,1024]{1,0:T(8,128)(2,1)S(1)}, bf16[192,1024]{1,0:T(8,128)(2,1)S(1)}, u32[]{:S(2)}, u32[]{:S(2)}) collective-permute-start(bf16[192,1024]{1,0:T(8,128)(2,1)S(1)} %get-tuple-element.58.refs_1_), channel_id=1, source_target_pairs={{0,1},{1,2},{2,3},{3,0},{4,5},{5,6},{6,7},{7,4},{8,9},{9,10},{10,1... | collective-permute-start | bytes 1179656 | tf_op jit(solution)/shard_map/ppermute | solution.py:20
  14.3 16.0 %collective-permute-start.5 = (bf16[192,1024]{1,0:T(8,128)(2,1)S(1)}, bf16[192,1024]{1,0:T(8,128)(2,1)S(1)}, u32[]{:S(2)}, u32[]{:S(2)}) collective-permute-start(bf16[192,1024]{1,0:T(8,128)(2,1)S(1)} %get-tuple-element.60.refs_4_), channel_id=1, source_target_pairs={{0,3},{1,0},{2,1},{3,2},{4,7},{5,4},{6,5},{7,6},{8,11},{9,8},{10,9... | collective-permute-start | bytes 1179656 | tf_op jit(solution)/shard_map/ppermute | solution.py:20
  16.4 5.6 %copy-start.7 = (bf16[384,1024]{1,0:T(8,128)(2,1)S(1)}, bf16[384,1024]{1,0:T(8,128)(2,1)}, u32[]{:S(2)}) copy-start(bf16[384,1024]{1,0:T(8,128)(2,1)} %refs_0_.7) | copy-start | bytes 2359300
  21.9 8.4 %copy-start.11 = (f32[8,128]{1,0:T(8,128)S(1)}, f32[8,128]{1,0:T(8,128)}, u32[]{:S(2)}) copy-start(f32[8,128]{1,0:T(8,128)} %gain_ref.1) | copy-start | bytes 12292
  34.2 9.9 %copy-start.10 = (bf16[4096,2,8]{0,2,1:T(8,128)(2,1)S(1)}, bf16[4096,2,8]{0,2,1:T(8,128)(2,1)}, u32[]{:S(2)}) copy-start(bf16[4096,2,8]{0,2,1:T(8,128)(2,1)} %param.12) | copy-start | bytes 393220
  34.2 9.9 %copy-start.12 = (f32[2,8]{1,0:T(2,128)S(1)}, f32[2,8]{1,0:T(2,128)}, u32[]{:S(2)}) copy-start(f32[2,8]{1,0:T(2,128)} %bias_ref.1) | copy-start | bytes 196
  34.3 12.9 %collective-permute-start.6 = (bf16[2,400,128]{2,1,0:T(8,128)(2,1)S(1)}, bf16[2,400,128]{2,1,0:T(8,128)(2,1)S(1)}, u32[]{:S(2)}, u32[]{:S(2)}) collective-permute-start(bf16[2,400,128]{2,1,0:T(8,128)(2,1)S(1)} %get-tuple-element.69), channel_id=1, source_target_pairs={{0,1},{1,2},{2,3},{3,0},{4,5},{5,6},{6,7},{7,4},{8,9},{9,10},{10,1... | collective-permute-start | bytes 614408 | tf_op jit(solution)/shard_map/ppermute | solution.py:20
  35.2 12.0 %collective-permute-start.7 = (bf16[2,400,128]{2,1,0:T(8,128)(2,1)S(1)}, bf16[2,400,128]{2,1,0:T(8,128)(2,1)S(1)}, u32[]{:S(2)}, u32[]{:S(2)}) collective-permute-start(bf16[2,400,128]{2,1,0:T(8,128)(2,1)S(1)} %get-tuple-element.70), channel_id=1, source_target_pairs={{0,3},{1,0},{2,1},{3,2},{4,7},{5,4},{6,5},{7,6},{8,11},{9,8},{10,9... | collective-permute-start | bytes 614408 | tf_op jit(solution)/shard_map/ppermute | solution.py:20
  37.0 10.1 %collective-permute-start.8 = (bf16[2,400,128]{2,1,0:T(8,128)(2,1)S(1)}, bf16[2,400,128]{2,1,0:T(8,128)(2,1)S(1)}, u32[]{:S(2)}, u32[]{:S(2)}) collective-permute-start(bf16[2,400,128]{2,1,0:T(8,128)(2,1)S(1)} %get-tuple-element.71), channel_id=1, source_target_pairs={{0,2},{1,3},{2,0},{3,1},{4,6},{5,7},{6,4},{7,5},{8,10},{9,11},{10,... | collective-permute-start | bytes 614408 | tf_op jit(solution)/shard_map/ppermute | solution.py:20
  48.3 6.4 %collective-permute-start.9 = (bf16[256,640]{1,0:T(8,128)(2,1)S(1)}, bf16[256,640]{1,0:T(8,128)(2,1)S(1)}, u32[]{:S(2)}, u32[]{:S(2)}) collective-permute-start(bf16[256,640]{1,0:T(8,128)(2,1)S(1)} %get-tuple-element.73), channel_id=1, source_target_pairs={{0,4},{4,0},{8,12},{12,8},{16,20},{20,16},{24,28},{28,24},{32,36},... | collective-permute-start | bytes 983048 | tf_op jit(solution)/shard_map/ppermute | solution.py:733
  51.7 37.4 %collective-permute-start.13 = (bf16[1024,512]{1,0:T(8,128)(2,1)S(1)}, bf16[1024,512]{1,0:T(8,128)(2,1)S(1)}, u32[]{:S(2)}, u32[]{:S(2)}) collective-permute-start(bf16[1024,512]{1,0:T(8,128)(2,1)S(1)} %get-tuple-element.85), channel_id=1, source_target_pairs={{0,1},{1,2},{2,3},{3,0},{4,5},{5,6},{6,7},{7,4},{8,9},{9,10},{10,1... | collective-permute-start | bytes 3145736 | tf_op jit(solution)/shard_map/ppermute | solution.py:20
  52.1 36.9 %collective-permute-start.14 = (bf16[1024,512]{1,0:T(8,128)(2,1)S(1)}, bf16[1024,512]{1,0:T(8,128)(2,1)S(1)}, u32[]{:S(2)}, u32[]{:S(2)}) collective-permute-start(bf16[1024,512]{1,0:T(8,128)(2,1)S(1)} %get-tuple-element.86), channel_id=1, source_target_pairs={{0,3},{1,0},{2,1},{3,2},{4,7},{5,4},{6,5},{7,6},{8,11},{9,8},{10,9... | collective-permute-start | bytes 3145736 | tf_op jit(solution)/shard_map/ppermute | solution.py:20
  54.4 45.3 %collective-permute-start.15 = (bf16[1024,512]{1,0:T(8,128)(2,1)S(1)}, bf16[1024,512]{1,0:T(8,128)(2,1)S(1)}, u32[]{:S(2)}, u32[]{:S(2)}) collective-permute-start(bf16[1024,512]{1,0:T(8,128)(2,1)S(1)} %get-tuple-element.87), channel_id=1, source_target_pairs={{0,2},{1,3},{2,0},{3,1},{4,6},{5,7},{6,4},{7,5},{8,10},{9,11},{10,... | collective-permute-start | bytes 3145736 | tf_op jit(solution)/shard_map/ppermute | solution.py:20
  82.3 4.9 %collective-permute-start.10 = (bf16[256,640]{1,0:T(8,128)(2,1)S(1)}, bf16[256,640]{1,0:T(8,128)(2,1)S(1)}, u32[]{:S(2)}, u32[]{:S(2)}) collective-permute-start(bf16[256,640]{1,0:T(8,128)(2,1)S(1)} %get-tuple-element.75), channel_id=1, source_target_pairs={{0,4},{4,0},{8,12},{12,8},{16,20},{20,16},{24,28},{28,24},{32,36},... | collective-permute-start | bytes 983048 | tf_op jit(solution)/shard_map/ppermute | solution.py:741
  89.0 24.5 %copy-start.9 = (bf16[192,1024]{1,0:T(8,128)(2,1)}, bf16[192,1024]{1,0:T(8,128)(2,1)S(1)}, u32[]{:S(2)}) copy-start(bf16[192,1024]{1,0:T(8,128)(2,1)S(1)} %get-tuple-element.81.refs_1_) | copy-start | bytes 1179652
  89.0 33.1 %copy-start.8 = (bf16[192,1024]{1,0:T(8,128)(2,1)}, bf16[192,1024]{1,0:T(8,128)(2,1)S(1)}, u32[]{:S(2)}) copy-start(bf16[192,1024]{1,0:T(8,128)(2,1)S(1)} %get-tuple-element.80.refs_3_.refs_0_) | copy-start | bytes 1179652
  99.7 22.5 %copy-start = (bf16[1024,512]{1,0:T(8,128)(2,1)}, bf16[1024,512]{1,0:T(8,128)(2,1)S(1)}, u32[]{:S(2)}) copy-start(bf16[1024,512]{1,0:T(8,128)(2,1)S(1)} %get-tuple-element.88.refs_7_.refs_3_) | copy-start | bytes 3145732
  99.7 22.5 %copy-start.1 = (bf16[1024,512]{1,0:T(8,128)(2,1)}, bf16[1024,512]{1,0:T(8,128)(2,1)S(1)}, u32[]{:S(2)}) copy-start(bf16[1024,512]{1,0:T(8,128)(2,1)S(1)} %get-tuple-element.89.refs_8_.refs_4_) | copy-start | bytes 3145732
  99.7 22.5 %copy-start.2 = (bf16[1024,512]{1,0:T(8,128)(2,1)}, bf16[1024,512]{1,0:T(8,128)(2,1)S(1)}, u32[]{:S(2)}) copy-start(bf16[1024,512]{1,0:T(8,128)(2,1)S(1)} %get-tuple-element.90.refs_9_.refs_5_) | copy-start | bytes 3145732
  99.7 4.6 %collective-permute-start.16 = (bf16[1024,512]{1,0:T(8,128)(2,1)S(1)}, bf16[1024,512]{1,0:T(8,128)(2,1)S(1)}, u32[]{:S(2)}, u32[]{:S(2)}) collective-permute-start(bf16[1024,512]{1,0:T(8,128)(2,1)S(1)} %get-tuple-element.88.refs_7_.refs_3_), channel_id=1, source_target_pairs={{0,4},{4,0},{8,12},{12,8},{16,20},{20,16},{24,28},{28,24},{32,36},... | collective-permute-start | bytes 3145736 | tf_op jit(solution)/shard_map/ppermute | solution.py:746
  101.1 3.8 %collective-permute-start.17 = (bf16[1024,512]{1,0:T(8,128)(2,1)S(1)}, bf16[1024,512]{1,0:T(8,128)(2,1)S(1)}, u32[]{:S(2)}, u32[]{:S(2)}) collective-permute-start(bf16[1024,512]{1,0:T(8,128)(2,1)S(1)} %get-tuple-element.89.refs_8_.refs_4_), channel_id=1, source_target_pairs={{0,4},{4,0},{8,12},{12,8},{16,20},{20,16},{24,28},{28,24},{32,36},... | collective-permute-start | bytes 3145736 | tf_op jit(solution)/shard_map/ppermute | solution.py:746
  101.2 5.2 %collective-permute-start.18 = (bf16[1024,512]{1,0:T(8,128)(2,1)S(1)}, bf16[1024,512]{1,0:T(8,128)(2,1)S(1)}, u32[]{:S(2)}, u32[]{:S(2)}) collective-permute-start(bf16[1024,512]{1,0:T(8,128)(2,1)S(1)} %get-tuple-element.90.refs_9_.refs_5_), channel_id=1, source_target_pairs={{0,4},{4,0},{8,12},{12,8},{16,20},{20,16},{24,28},{28,24},{32,36},... | collective-permute-start | bytes 3145736 | tf_op jit(solution)/shard_map/ppermute | solution.py:746
  101.6 12.0 %collective-permute-start.11 = (bf16[192,1024]{1,0:T(8,128)(2,1)S(1)}, bf16[192,1024]{1,0:T(8,128)(2,1)}, u32[]{:S(2)}, u32[]{:S(2)}) collective-permute-start(bf16[192,1024]{1,0:T(8,128)(2,1)S(1)} %get-tuple-element.80.refs_3_.refs_0_), channel_id=1, source_target_pairs={{0,1},{1,2},{2,3},{3,0},{4,5},{5,6},{6,7},{7,4},{8,9},{9,10},{10,1... | collective-permute-start | bytes 1179656 | tf_op jit(solution)/shard_map/ppermute | solution.py:20
  102.1 11.4 %collective-permute-start.12 = (bf16[192,1024]{1,0:T(8,128)(2,1)S(1)}, bf16[192,1024]{1,0:T(8,128)(2,1)}, u32[]{:S(2)}, u32[]{:S(2)}) collective-permute-start(bf16[192,1024]{1,0:T(8,128)(2,1)S(1)} %get-tuple-element.81.refs_1_), channel_id=1, source_target_pairs={{0,3},{1,0},{2,1},{3,2},{4,7},{5,4},{6,5},{7,6},{8,11},{9,8},{10,9... | collective-permute-start | bytes 1179656 | tf_op jit(solution)/shard_map/ppermute | solution.py:20
  106.4 1.0 copy-start.3
  107.3 1.0 copy-start.4
  108.3 1.1 copy-start.5
  110.3 11.9 %collective-permute-start.21 = (bf16[192,1024]{1,0:T(8,128)(2,1)}, bf16[192,1024]{1,0:T(8,128)(2,1)}, u32[]{:S(2)}, u32[]{:S(2)}) collective-permute-start(bf16[192,1024]{1,0:T(8,128)(2,1)} %get-tuple-element.92.refs_2_), channel_id=1, source_target_pairs={{0,1},{1,2},{2,3},{3,0},{4,5},{5,6},{6,7},{7,4},{8,9},{9,10},{10,1... | collective-permute-start | bytes 1179656 | tf_op jit(solution)/shard_map/ppermute | solution.py:20
  110.9 11.3 %collective-permute-start.22 = (bf16[192,1024]{1,0:T(8,128)(2,1)}, bf16[192,1024]{1,0:T(8,128)(2,1)}, u32[]{:S(2)}, u32[]{:S(2)}) collective-permute-start(bf16[192,1024]{1,0:T(8,128)(2,1)} %get-tuple-element.98), channel_id=1, source_target_pairs={{0,3},{1,0},{2,1},{3,2},{4,7},{5,4},{6,5},{7,6},{8,11},{9,8},{10,9... | collective-permute-start | bytes 1179656 | tf_op jit(solution)/shard_map/ppermute | solution.py:20
  113.6 17.0 %collective-permute-start.19 = (bf16[192,1024]{1,0:T(8,128)(2,1)}, bf16[192,1024]{1,0:T(8,128)(2,1)}, u32[]{:S(2)}, u32[]{:S(2)}) collective-permute-start(bf16[192,1024]{1,0:T(8,128)(2,1)} %get-tuple-element.93.refs_2_), channel_id=1, source_target_pairs={{0,1},{1,2},{2,3},{3,0},{4,5},{5,6},{6,7},{7,4},{8,9},{9,10},{10,1... | collective-permute-start | bytes 1179656 | tf_op jit(solution)/shard_map/ppermute | solution.py:20
  114.4 16.2 %collective-permute-start.20 = (bf16[192,1024]{1,0:T(8,128)(2,1)}, bf16[192,1024]{1,0:T(8,128)(2,1)}, u32[]{:S(2)}, u32[]{:S(2)}) collective-permute-start(bf16[192,1024]{1,0:T(8,128)(2,1)} %get-tuple-element.94.refs_5_), channel_id=1, source_target_pairs={{0,3},{1,0},{2,1},{3,2},{4,7},{5,4},{6,5},{7,6},{8,11},{9,8},{10,9... | collective-permute-start | bytes 1179656 | tf_op jit(solution)/shard_map/ppermute | solution.py:20

commit v7 on v6

--- a/solution.py
+++ b/solution.py
@@ -289,7 +289,7 @@
                     started.append(copies.start(source, ws.at[t, to, :]))
         return started
 
-    started = [load(t) for t in range(2)]
+    started = [load(0)]
     for g in range(ngroups):
         put_rows(groups[g], x.at[:, pl.ds(g * chunk, chunk)])
     last = []
@@ -297,6 +297,8 @@
         columns = pl.ds(pl.multiple_of(side * cols, cols), cols)
         for copy in started[t]:
             copy.wait()
+        if t == 0:
+            started.append(load(1))
         total = jnp.dot(x[...], ws[t], preferred_element_type=F32)
         if with_total:
             total = total + total_ref[:, columns]

time: 136 us -> 138 us (1.015)
  no operation moved by 1% of the time
where the time goes in v7:
time: 138 us; the launch traced here: 136 us
  Pallas kernels  50.5 us (37%)
  starting transfers between devices  32.9 us (24%)
  blocking collectives  26.2 us (19%)
  waiting for transfers between devices  20.6 us (15%)
  local copies, waits for them, and re-layouts  5.51 us (4%)
    ppermute x18, starting transfers between devices, around(): return lax.ppermute(x, 'val', [(i, (i + distance) % n) for i in range(n)])  24 us
    ppermute x18, waiting for transfers between devices, around(): return lax.ppermute(x, 'val', [(i, (i + distance) % n) for i in range(n)])  17.8 us
    all_to_all x1, blocking collectives, per_device(): both = lax.all_to_all(both, 'seq', 0, 0, axis_index_groups=chips)  15.2 us
    pallas_call x2, Pallas kernels, out_product(): pl.pallas_call(functools.partial(out_kernel, [len(g) for g in groups], to...  13.9 us
    pallas_call x2, Pallas kernels, product(): pl.pallas_call(functools.partial(product_kernel, [len(g) for g in groups]...  11.3 us
    all_to_all x1, blocking collectives, per_device(): lax.all_to_all(prefixes(both), 'seq', 0, 0, axis_index_groups=chips)  11.1 us
    pallas_call x3, Pallas kernels, flat(): pl.pallas_call(functools.partial(flat_kernel, len(args)), grid=(steps,),...  10.2 us
    unnamed x26, local copies, waits for them, and re-layouts  4.19 us
  transfers between devices with their start and end apart: 23, of which 10 were waited for; matrix products, arithmetic and copies ran while one was open for 1% of the time, Pallas kernels for 29%

profile of v7, /device:TPU:1, one launch (start us, length us, event | category | flops | bytes accessed | tf_op | source)
XLA Modules:
  0.0 136.5 jit_solution(5896014100431264277)
XLA Ops:
  0.0 1.1 copy-done.6
  1.2 2.2 %collective-permute-start = (bf16[192,1024]{1,0:T(8,128)(2,1)S(1)}, bf16[192,1024]{1,0:T(8,128)(2,1)S(1)}, u32[]{:S(2)}, u32[]{:S(2)}) collective-permute-start(bf16[192,1024]{1,0:T(8,128)(2,1)S(1)} %get-tuple-element.52.refs_0_), channel_id=1, source_target_pairs={{0,1},{1,2},{2,3},{3,0},{4,5},{5,6},{6,7},{7,4},{8,9},{9,10},{10,1... | collective-permute-start | bytes 1179656 | tf_op jit(solution)/shard_map/ppermute | solution.py:20
  3.4 1.5 %collective-permute-start.1 = (bf16[192,1024]{1,0:T(8,128)(2,1)S(1)}, bf16[192,1024]{1,0:T(8,128)(2,1)S(1)}, u32[]{:S(2)}, u32[]{:S(2)}) collective-permute-start(bf16[192,1024]{1,0:T(8,128)(2,1)S(1)} %get-tuple-element.53.refs_1_), channel_id=1, source_target_pairs={{0,3},{1,0},{2,1},{3,2},{4,7},{5,4},{6,5},{7,6},{8,11},{9,8},{10,9... | collective-permute-start | bytes 1179656 | tf_op jit(solution)/shard_map/ppermute | solution.py:20
  4.9 2.7 %shard_map.83 = (bf16[4096,1024]{1,0:T(8,128)(2,1)}, f32[8,128]{1,0:T(8,128)S(1)}) custom-call(bf16[4096,8,128]{2,1,0:T(8,128)(2,1)} %w_ref.5), custom_call_target="tpu_custom_call" | custom-call | bytes 2097152 | tf_op jit(solution)/shard_map/pallas_call | solution.py:103
  7.7 2.7 %collective-permute-start.3 = (bf16[192,1024]{1,0:T(8,128)(2,1)S(1)}, bf16[192,1024]{1,0:T(8,128)(2,1)S(1)}, u32[]{:S(2)}, u32[]{:S(2)}) collective-permute-start(bf16[192,1024]{1,0:T(8,128)(2,1)S(1)} %get-tuple-element.59), channel_id=1, source_target_pairs={{0,3},{1,0},{2,1},{3,2},{4,7},{5,4},{6,5},{7,6},{8,11},{9,8},{10,9... | collective-permute-start | bytes 1179656 | tf_op jit(solution)/shard_map/ppermute | solution.py:20
  10.4 2.7 %shard_map.85 = (bf16[4096,1024]{1,0:T(8,128)(2,1)}, f32[8,128]{1,0:T(8,128)S(1)}) custom-call(bf16[4096,8,128]{2,1,0:T(8,128)(2,1)} %w_ref.5, bf16[4096,1024]{1,0:T(8,128)(2,1)} %get-tuple-element.56.refs_0_), custom_call_target="tpu_custom_call", output_to_operand_aliasing={{0}: (1, {})} | custom-call | bytes 2097152 | tf_op jit(solution)/shard_map/pallas_call | solution.py:103
  13.5 0.8 collective-permute-start.4
  14.3 1.8 %collective-permute-start.5 = (bf16[192,1024]{1,0:T(8,128)(2,1)S(1)}, bf16[192,1024]{1,0:T(8,128)(2,1)S(1)}, u32[]{:S(2)}, u32[]{:S(2)}) collective-permute-start(bf16[192,1024]{1,0:T(8,128)(2,1)S(1)} %get-tuple-element.60.refs_4_), channel_id=1, source_target_pairs={{0,3},{1,0},{2,1},{3,2},{4,7},{5,4},{6,5},{7,6},{8,11},{9,8},{10,9... | collective-permute-start | bytes 1179656 | tf_op jit(solution)/shard_map/ppermute | solution.py:20
  16.4 4.9 %shard_map.87 = (bf16[4096,1024]{1,0:T(8,128)(2,1)}, f32[8,128]{1,0:T(8,128)}) custom-call(bf16[4096,8,128]{2,1,0:T(8,128)(2,1)} %w_ref.5, bf16[4096,1024]{1,0:T(8,128)(2,1)} %get-tuple-element.61.refs_0_), custom_call_target="tpu_custom_call", output_to_operand_aliasing={{0}: (1, {})} | custom-call | bytes 4194304 | tf_op jit(solution)/shard_map/pallas_call | solution.py:103
  21.3 0.6 collective-permute-done.2.refs_2_
  21.9 5.2 %shard_map.88.refs_0_.acc_ref = f32[384,1024]{1,0:T(8,128)S(1)} custom-call(s32[3]{0:T(128)S(1)} %pad_add_fusion.2.scalars, bf16[384,1024]{1,0:T(8,128)(2,1)S(1)} %copy-done.7, bf16[192,1024]{1,0:T(8,128)(2,1)S(1)} %get-tuple-element.58.refs_1_, bf16[192,1024]{1,0:T(8,128)(2,1)S(1)} %collective-permute-done.2.refs_2_, ...), custom_call_target="tpu_custom_call" | custom-call | flops 2415919104 | bytes 10223616 | tf_op jit(solution)/shard_map/pallas_call | solution.py:211
  27.1 2.5 %shard_map.89 = (bf16[1024,512]{1,0:T(8,128)(2,1)S(1)}, bf16[1024,512]{1,0:T(8,128)(2,1)S(1)}, bf16[1024,512]{1,0:T(8,128)(2,1)S(1)}, f32[8,128]{1,0:T(8,128)S(1)}) custom-call(s32[2]{0:T(128)S(1)} %pad_add_fusion.3.scalars, bf16[1024,4096]{1,0:T(8,128)(2,1)} %bitcast.15, f32[384,1024]{1,0:T(8,128)S(1)} %shard_map.88.refs_0_.acc_ref), custom_call_target="tpu_custom_call" | custom-call | bytes 6291456 | tf_op jit(solution)/shard_map/pallas_call | solution.py:250
  29.6 0.8 collective-permute-done.4.upper.refs_5_
  30.4 3.9 %shard_map.90 = (bf16[2,400,128]{2,1,0:T(8,128)(2,1)S(1)}, bf16[2,400,128]{2,1,0:T(8,128)(2,1)S(1)}, bf16[2,400,128]{2,1,0:T(8,128)(2,1)S(1)}, bf16[2,400,128]{2,1,0:T(8,128)(2,1)S(1)}) custom-call(s32[2]{0:T(128)S(1)} %pad_add_fusion.1.scalars, bf16[192,1024]{1,0:T(8,128)(2,1)S(1)} %collective-permute-done.4.upper.refs_5_, ...), custom_call_target="tpu_custom_call" | custom-call | flops 805306368 | bytes 5242880 | tf_op jit(solution)/shard_map/pallas_call | solution.py:378
  34.3 0.9 collective-permute-start.6
  35.2 1.8 %collective-permute-start.7 = (bf16[2,400,128]{2,1,0:T(8,128)(2,1)S(1)}, bf16[2,400,128]{2,1,0:T(8,128)(2,1)S(1)}, u32[]{:S(2)}, u32[]{:S(2)}) collective-permute-start(bf16[2,400,128]{2,1,0:T(8,128)(2,1)S(1)} %get-tuple-element.70), channel_id=1, source_target_pairs={{0,3},{1,0},{2,1},{3,2},{4,7},{5,4},{6,5},{7,6},{8,11},{9,8},{10,9... | collective-permute-start | bytes 614408 | tf_op jit(solution)/shard_map/ppermute | solution.py:20
  37.0 1.0 collective-permute-start.8
  38.0 6.1 %shard_map.91 = (bf16[384,512]{1,0:T(8,128)(2,1)S(1)}, bf16[384,512]{1,0:T(8,128)(2,1)S(1)}) custom-call(s32[4]{0:T(128)S(1)} %pad_add_fusion.scalars, bf16[384,1024]{1,0:T(8,128)(2,1)S(1)} %copy-done.7, bf16[192,1024]{1,0:T(8,128)(2,1)S(1)} %get-tuple-element.58.refs_1_, bf16[192,1024]{1,0:T(8,128)(2,1)S(1)} %collective-permute-done.2.refs_2_, ...), custom_call_target="tpu_custom_call" | custom-call | flops 3221225472 | bytes 13107200 | tf_op jit(solution)/shard_map/pallas_call | solution.py:211
  44.2 2.9 %shard_map.92 = (bf16[512,384]{1,0:T(8,128)(2,1)S(1)}, bf16[2,384,384]{2,1,0:T(8,128)(2,1)S(1)}, f32[384,128]{1,0:T(8,128)S(1)}, f32[8,128]{1,0:T(8,128)S(1)}) custom-call(s32[4]{0:T(128)S(1)} %pad_add_fusion.scalars, f32[2,8]{1,0:T(2,128)S(1)} %copy-done.12, bf16[384,1024]{1,0:T(8,128)(2,1)S(1)} %copy-done.7, ...), custom_call_target="tpu_custom_call" | custom-call | flops 301989888 | bytes 1572864 | tf_op jit(solution)/shard_map/pallas_call | solution.py:466
  47.1 1.1 shard_map.93
  48.3 3.4 %collective-permute-start.9 = (bf16[256,640]{1,0:T(8,128)(2,1)S(1)}, bf16[256,640]{1,0:T(8,128)(2,1)S(1)}, u32[]{:S(2)}, u32[]{:S(2)}) collective-permute-start(bf16[256,640]{1,0:T(8,128)(2,1)S(1)} %get-tuple-element.73), channel_id=1, source_target_pairs={{0,4},{4,0},{8,12},{12,8},{16,20},{20,16},{24,28},{28,24},{32,36},... | collective-permute-start | bytes 983048 | tf_op jit(solution)/shard_map/ppermute | solution.py:735
  52.1 2.2 %collective-permute-start.14 = (bf16[1024,512]{1,0:T(8,128)(2,1)S(1)}, bf16[1024,512]{1,0:T(8,128)(2,1)S(1)}, u32[]{:S(2)}, u32[]{:S(2)}) collective-permute-start(bf16[1024,512]{1,0:T(8,128)(2,1)S(1)} %get-tuple-element.86), channel_id=1, source_target_pairs={{0,3},{1,0},{2,1},{3,2},{4,7},{5,4},{6,5},{7,6},{8,11},{9,8},{10,9... | collective-permute-start | bytes 3145736 | tf_op jit(solution)/shard_map/ppermute | solution.py:20
  55.3 15.2 %all_to_all.10.got_ref = bf16[16,16,640]{2,1,0:T(8,128)(2,1)S(1)} all-to-all(bf16[16,16,640]{2,1,0:T(8,128)(2,1)S(1)} %bitcast.13), channel_id=1, replica_groups={{0,8,16,24,32,40,48,56,64,72,80,88,96,104,112,120},{4,12,20,28,36,44,52..., dimensions={0} | all-to-all | bytes 655360 | tf_op jit(solution)/shard_map/all_to_all | solution.py:739
  70.8 11.1 %all_to_all.11 = bf16[16,16,640]{2,1,0:T(8,128)(2,1)S(1)} all-to-all(bf16[16,16,640]{2,1,0:T(8,128)(2,1)S(1)} %shard_map.95), channel_id=1, replica_groups={{0,8,16,24,32,40,48,56,64,72,80,88,96,104,112,120},{4,12,20,28,36,44,52..., dimensions={0} | all-to-all | bytes 655360 | tf_op jit(solution)/shard_map/all_to_all | solution.py:741
  82.3 3.6 %collective-permute-start.10 = (bf16[256,640]{1,0:T(8,128)(2,1)S(1)}, bf16[256,640]{1,0:T(8,128)(2,1)S(1)}, u32[]{:S(2)}, u32[]{:S(2)}) collective-permute-start(bf16[256,640]{1,0:T(8,128)(2,1)S(1)} %get-tuple-element.75), channel_id=1, source_target_pairs={{0,4},{4,0},{8,12},{12,8},{16,20},{20,16},{24,28},{28,24},{32,36},... | collective-permute-start | bytes 983048 | tf_op jit(solution)/shard_map/ppermute | solution.py:743
  86.0 0.6 shard_map.97.numer_ref
  86.5 0.7 collective-permute-done.10.got
  87.2 1.8 %shard_map.98 = (bf16[192,1024]{1,0:T(8,128)(2,1)S(1)}, bf16[192,1024]{1,0:T(8,128)(2,1)S(1)}) custom-call(s32[1]{0:T(128)} %bitcast.4.scalars, bf16[384,512]{1,0:T(8,128)(2,1)S(1)} %get-tuple-element.65.refs_8_.q_ref, bf16[256,640]{1,0:T(8,128)(2,1)S(1)} %get-tuple-element.74.mine, bf16[256,640]{1,0:T(8,128)(2,1)S(1)} %collective-permute-done.10.got, ...), custom_call_target="tpu_custom_call" | custom-call | flops 201326592 | bytes 3145728 | tf_op jit(solution)/shard_map/pallas_call | solution.py:688
  89.1 10.6 %collective-permute-done.15.refs_2_ = bf16[1024,512]{1,0:T(8,128)(2,1)S(1)} collective-permute-done((bf16[1024,512]{1,0:T(8,128)(2,1)S(1)}, bf16[1024,512]{1,0:T(8,128)(2,1)S(1)}, u32[]{:S(2)}, u32[]{:S(2)}) %collective-permute-start.15) | collective-permute-done | bytes 1048608 | tf_op jit(solution)/shard_map/ppermute | solution.py:20
  99.7 1.4 collective-permute-start.16
  101.6 0.6 collective-permute-start.11
  102.1 2.1 %collective-permute-start.12 = (bf16[192,1024]{1,0:T(8,128)(2,1)S(1)}, bf16[192,1024]{1,0:T(8,128)(2,1)}, u32[]{:S(2)}, u32[]{:S(2)}) collective-permute-start(bf16[192,1024]{1,0:T(8,128)(2,1)S(1)} %get-tuple-element.81.refs_1_), channel_id=1, source_target_pairs={{0,3},{1,0},{2,1},{3,2},{4,7},{5,4},{6,5},{7,6},{8,11},{9,8},{10,9... | collective-permute-start | bytes 1179656 | tf_op jit(solution)/shard_map/ppermute | solution.py:20
  104.3 0.6 collective-permute-done.17.refs_1_
  104.8 1.5 %collective-permute-done.18.refs_2_ = bf16[1024,512]{1,0:T(8,128)(2,1)S(1)} collective-permute-done((bf16[1024,512]{1,0:T(8,128)(2,1)S(1)}, bf16[1024,512]{1,0:T(8,128)(2,1)S(1)}, u32[]{:S(2)}, u32[]{:S(2)}) %collective-permute-start.18) | collective-permute-done | bytes 1048608 | tf_op jit(solution)/shard_map/ppermute | solution.py:748
  106.4 1.0 copy-done.3
  107.3 1.0 copy-done.4
  108.3 1.1 copy-done.5
  109.4 0.9 shard_map.102
  110.3 0.6 collective-permute-start.21
  110.9 2.1 %collective-permute-start.22 = (bf16[192,1024]{1,0:T(8,128)(2,1)}, bf16[192,1024]{1,0:T(8,128)(2,1)}, u32[]{:S(2)}, u32[]{:S(2)}) collective-permute-start(bf16[192,1024]{1,0:T(8,128)(2,1)} %get-tuple-element.98), channel_id=1, source_target_pairs={{0,3},{1,0},{2,1},{3,2},{4,7},{5,4},{6,5},{7,6},{8,11},{9,8},{10,9... | collective-permute-start | bytes 1179656 | tf_op jit(solution)/shard_map/ppermute | solution.py:20
  113.0 0.6 collective-permute-done.11.refs_0_
  113.6 0.8 collective-permute-start.19
  114.4 1.8 %collective-permute-start.20 = (bf16[192,1024]{1,0:T(8,128)(2,1)}, bf16[192,1024]{1,0:T(8,128)(2,1)}, u32[]{:S(2)}, u32[]{:S(2)}) collective-permute-start(bf16[192,1024]{1,0:T(8,128)(2,1)} %get-tuple-element.94.refs_5_), channel_id=1, source_target_pairs={{0,3},{1,0},{2,1},{3,2},{4,7},{5,4},{6,5},{7,6},{8,11},{9,8},{10,9... | collective-permute-start | bytes 1179656 | tf_op jit(solution)/shard_map/ppermute | solution.py:20
  116.2 0.6 stack.38.scalars
  116.8 0.7 stack.31.scalars
  117.5 4.7 %collective-permute-done.21.refs_3_ = bf16[192,1024]{1,0:T(8,128)(2,1)} collective-permute-done((bf16[192,1024]{1,0:T(8,128)(2,1)}, bf16[192,1024]{1,0:T(8,128)(2,1)}, u32[]{:S(2)}, u32[]{:S(2)}) %collective-permute-start.21) | collective-permute-done | bytes 393248 | tf_op jit(solution)/shard_map/ppermute | solution.py:20
  122.2 8.1 %shard_map.104.refs_9_ = f32[384,1024]{1,0:T(8,128)} custom-call(s32[8]{0:T(128)} %stack.38.scalars, bf16[192,1024]{1,0:T(8,128)(2,1)} %copy-done.8, bf16[192,1024]{1,0:T(8,128)(2,1)} %copy-done.9, bf16[192,1024]{1,0:T(8,128)(2,1)} %get-tuple-element.93.refs_2_, bf16[192,1024]{1,0:T(8,128)(2,1)} %collective-permute-done.21.refs_3_, ...), custom_call_target="tpu_custom_call" | custom-call | flops 2415919104 | bytes 7864320 | tf_op jit(solution)/shard_map/pallas_call | solution.py:319
  130.6 5.7 %shard_map.105 = bf16[384,1024]{1,0:T(8,128)(2,1)} custom-call(s32[6]{0:T(128)} %stack.31.scalars, bf16[192,1024]{1,0:T(8,128)(2,1)} %collective-permute-done.19.refs_0_, bf16[192,1024]{1,0:T(8,128)(2,1)} %collective-permute-done.20.refs_1_, bf16[1024,4096]{1,0:T(8,128)(2,1)} %bitcast.17, bf16[1024,512]{1,0:T(8,128)(2,1)} %copy-done, ...), custom_call_target="tpu_custom_call" | custom-call | flops 805306368 | bytes 3670016 | tf_op jit(solution)/shard_map/pallas_call | solution.py:319
  (57 shorter events, 3.9 us)
Async XLA Ops:
  0.0 1.1 copy-start.6
  1.2 12.3 %collective-permute-start = (bf16[192,1024]{1,0:T(8,128)(2,1)S(1)}, bf16[192,1024]{1,0:T(8,128)(2,1)S(1)}, u32[]{:S(2)}, u32[]{:S(2)}) collective-permute-start(bf16[192,1024]{1,0:T(8,128)(2,1)S(1)} %get-tuple-element.52.refs_0_), channel_id=1, source_target_pairs={{0,1},{1,2},{2,3},{3,0},{4,5},{5,6},{6,7},{7,4},{8,9},{9,10},{10,1... | collective-permute-start | bytes 1179656 | tf_op jit(solution)/shard_map/ppermute | solution.py:20
  3.4 10.1 %collective-permute-start.1 = (bf16[192,1024]{1,0:T(8,128)(2,1)S(1)}, bf16[192,1024]{1,0:T(8,128)(2,1)S(1)}, u32[]{:S(2)}, u32[]{:S(2)}) collective-permute-start(bf16[192,1024]{1,0:T(8,128)(2,1)S(1)} %get-tuple-element.53.refs_1_), channel_id=1, source_target_pairs={{0,3},{1,0},{2,1},{3,2},{4,7},{5,4},{6,5},{7,6},{8,11},{9,8},{10,9... | collective-permute-start | bytes 1179656 | tf_op jit(solution)/shard_map/ppermute | solution.py:20
  7.6 14.3 %collective-permute-start.2 = (bf16[192,1024]{1,0:T(8,128)(2,1)S(1)}, bf16[192,1024]{1,0:T(8,128)(2,1)S(1)}, u32[]{:S(2)}, u32[]{:S(2)}) collective-permute-start(bf16[192,1024]{1,0:T(8,128)(2,1)S(1)} %get-tuple-element.55.refs_2_), channel_id=1, source_target_pairs={{0,1},{1,2},{2,3},{3,0},{4,5},{5,6},{6,7},{7,4},{8,9},{9,10},{10,1... | collective-permute-start | bytes 1179656 | tf_op jit(solution)/shard_map/ppermute | solution.py:20
  7.7 14.2 %collective-permute-start.3 = (bf16[192,1024]{1,0:T(8,128)(2,1)S(1)}, bf16[192,1024]{1,0:T(8,128)(2,1)S(1)}, u32[]{:S(2)}, u32[]{:S(2)}) collective-permute-start(bf16[192,1024]{1,0:T(8,128)(2,1)S(1)} %get-tuple-element.59), channel_id=1, source_target_pairs={{0,3},{1,0},{2,1},{3,2},{4,7},{5,4},{6,5},{7,6},{8,11},{9,8},{10,9... | collective-permute-start | bytes 1179656 | tf_op jit(solution)/shard_map/ppermute | solution.py:20
  13.5 16.8 %collective-permute-start.4 = (bf16[192,1024]{1,0:T(8,128)(2,1)S(1)}, bf16[192,1024]{1,0:T(8,128)(2,1)S(1)}, u32[]{:S(2)}, u32[]{:S(2)}) collective-permute-start(bf16[192,1024]{1,0:T(8,128)(2,1)S(1)} %get-tuple-element.58.refs_1_), channel_id=1, source_target_pairs={{0,1},{1,2},{2,3},{3,0},{4,5},{5,6},{6,7},{7,4},{8,9},{9,10},{10,1... | collective-permute-start | bytes 1179656 | tf_op jit(solution)/shard_map/ppermute | solution.py:20
  14.3 16.0 %collective-permute-start.5 = (bf16[192,1024]{1,0:T(8,128)(2,1)S(1)}, bf16[192,1024]{1,0:T(8,128)(2,1)S(1)}, u32[]{:S(2)}, u32[]{:S(2)}) collective-permute-start(bf16[192,1024]{1,0:T(8,128)(2,1)S(1)} %get-tuple-element.60.refs_4_), channel_id=1, source_target_pairs={{0,3},{1,0},{2,1},{3,2},{4,7},{5,4},{6,5},{7,6},{8,11},{9,8},{10,9... | collective-permute-start | bytes 1179656 | tf_op jit(solution)/shard_map/ppermute | solution.py:20
  16.4 5.6 %copy-start.7 = (bf16[384,1024]{1,0:T(8,128)(2,1)S(1)}, bf16[384,1024]{1,0:T(8,128)(2,1)}, u32[]{:S(2)}) copy-start(bf16[384,1024]{1,0:T(8,128)(2,1)} %refs_0_.7) | copy-start | bytes 2359300
  21.9 8.4 %copy-start.11 = (f32[8,128]{1,0:T(8,128)S(1)}, f32[8,128]{1,0:T(8,128)}, u32[]{:S(2)}) copy-start(f32[8,128]{1,0:T(8,128)} %gain_ref.1) | copy-start | bytes 12292
  34.2 9.9 %copy-start.10 = (bf16[4096,2,8]{0,2,1:T(8,128)(2,1)S(1)}, bf16[4096,2,8]{0,2,1:T(8,128)(2,1)}, u32[]{:S(2)}) copy-start(bf16[4096,2,8]{0,2,1:T(8,128)(2,1)} %param.12) | copy-start | bytes 393220
  34.2 9.9 %copy-start.12 = (f32[2,8]{1,0:T(2,128)S(1)}, f32[2,8]{1,0:T(2,128)}, u32[]{:S(2)}) copy-start(f32[2,8]{1,0:T(2,128)} %bias_ref.1) | copy-start | bytes 196
  34.3 12.9 %collective-permute-start.6 = (bf16[2,400,128]{2,1,0:T(8,128)(2,1)S(1)}, bf16[2,400,128]{2,1,0:T(8,128)(2,1)S(1)}, u32[]{:S(2)}, u32[]{:S(2)}) collective-permute-start(bf16[2,400,128]{2,1,0:T(8,128)(2,1)S(1)} %get-tuple-element.69), channel_id=1, source_target_pairs={{0,1},{1,2},{2,3},{3,0},{4,5},{5,6},{6,7},{7,4},{8,9},{9,10},{10,1... | collective-permute-start | bytes 614408 | tf_op jit(solution)/shard_map/ppermute | solution.py:20
  35.2 12.0 %collective-permute-start.7 = (bf16[2,400,128]{2,1,0:T(8,128)(2,1)S(1)}, bf16[2,400,128]{2,1,0:T(8,128)(2,1)S(1)}, u32[]{:S(2)}, u32[]{:S(2)}) collective-permute-start(bf16[2,400,128]{2,1,0:T(8,128)(2,1)S(1)} %get-tuple-element.70), channel_id=1, source_target_pairs={{0,3},{1,0},{2,1},{3,2},{4,7},{5,4},{6,5},{7,6},{8,11},{9,8},{10,9... | collective-permute-start | bytes 614408 | tf_op jit(solution)/shard_map/ppermute | solution.py:20
  37.0 10.1 %collective-permute-start.8 = (bf16[2,400,128]{2,1,0:T(8,128)(2,1)S(1)}, bf16[2,400,128]{2,1,0:T(8,128)(2,1)S(1)}, u32[]{:S(2)}, u32[]{:S(2)}) collective-permute-start(bf16[2,400,128]{2,1,0:T(8,128)(2,1)S(1)} %get-tuple-element.71), channel_id=1, source_target_pairs={{0,2},{1,3},{2,0},{3,1},{4,6},{5,7},{6,4},{7,5},{8,10},{9,11},{10,... | collective-permute-start | bytes 614408 | tf_op jit(solution)/shard_map/ppermute | solution.py:20
  48.3 6.4 %collective-permute-start.9 = (bf16[256,640]{1,0:T(8,128)(2,1)S(1)}, bf16[256,640]{1,0:T(8,128)(2,1)S(1)}, u32[]{:S(2)}, u32[]{:S(2)}) collective-permute-start(bf16[256,640]{1,0:T(8,128)(2,1)S(1)} %get-tuple-element.73), channel_id=1, source_target_pairs={{0,4},{4,0},{8,12},{12,8},{16,20},{20,16},{24,28},{28,24},{32,36},... | collective-permute-start | bytes 983048 | tf_op jit(solution)/shard_map/ppermute | solution.py:735
  51.7 37.4 %collective-permute-start.13 = (bf16[1024,512]{1,0:T(8,128)(2,1)S(1)}, bf16[1024,512]{1,0:T(8,128)(2,1)S(1)}, u32[]{:S(2)}, u32[]{:S(2)}) collective-permute-start(bf16[1024,512]{1,0:T(8,128)(2,1)S(1)} %get-tuple-element.85), channel_id=1, source_target_pairs={{0,1},{1,2},{2,3},{3,0},{4,5},{5,6},{6,7},{7,4},{8,9},{9,10},{10,1... | collective-permute-start | bytes 3145736 | tf_op jit(solution)/shard_map/ppermute | solution.py:20
  52.1 36.9 %collective-permute-start.14 = (bf16[1024,512]{1,0:T(8,128)(2,1)S(1)}, bf16[1024,512]{1,0:T(8,128)(2,1)S(1)}, u32[]{:S(2)}, u32[]{:S(2)}) collective-permute-start(bf16[1024,512]{1,0:T(8,128)(2,1)S(1)} %get-tuple-element.86), channel_id=1, source_target_pairs={{0,3},{1,0},{2,1},{3,2},{4,7},{5,4},{6,5},{7,6},{8,11},{9,8},{10,9... | collective-permute-start | bytes 3145736 | tf_op jit(solution)/shard_map/ppermute | solution.py:20
  54.4 45.3 %collective-permute-start.15 = (bf16[1024,512]{1,0:T(8,128)(2,1)S(1)}, bf16[1024,512]{1,0:T(8,128)(2,1)S(1)}, u32[]{:S(2)}, u32[]{:S(2)}) collective-permute-start(bf16[1024,512]{1,0:T(8,128)(2,1)S(1)} %get-tuple-element.87), channel_id=1, source_target_pairs={{0,2},{1,3},{2,0},{3,1},{4,6},{5,7},{6,4},{7,5},{8,10},{9,11},{10,... | collective-permute-start | bytes 3145736 | tf_op jit(solution)/shard_map/ppermute | solution.py:20
  82.3 4.9 %collective-permute-start.10 = (bf16[256,640]{1,0:T(8,128)(2,1)S(1)}, bf16[256,640]{1,0:T(8,128)(2,1)S(1)}, u32[]{:S(2)}, u32[]{:S(2)}) collective-permute-start(bf16[256,640]{1,0:T(8,128)(2,1)S(1)} %get-tuple-element.75), channel_id=1, source_target_pairs={{0,4},{4,0},{8,12},{12,8},{16,20},{20,16},{24,28},{28,24},{32,36},... | collective-permute-start | bytes 983048 | tf_op jit(solution)/shard_map/ppermute | solution.py:743
  89.0 24.5 %copy-start.9 = (bf16[192,1024]{1,0:T(8,128)(2,1)}, bf16[192,1024]{1,0:T(8,128)(2,1)S(1)}, u32[]{:S(2)}) copy-start(bf16[192,1024]{1,0:T(8,128)(2,1)S(1)} %get-tuple-element.81.refs_1_) | copy-start | bytes 1179652
  89.0 33.1 %copy-start.8 = (bf16[192,1024]{1,0:T(8,128)(2,1)}, bf16[192,1024]{1,0:T(8,128)(2,1)S(1)}, u32[]{:S(2)}) copy-start(bf16[192,1024]{1,0:T(8,128)(2,1)S(1)} %get-tuple-element.80.refs_3_.refs_0_) | copy-start | bytes 1179652
  99.7 22.5 %copy-start = (bf16[1024,512]{1,0:T(8,128)(2,1)}, bf16[1024,512]{1,0:T(8,128)(2,1)S(1)}, u32[]{:S(2)}) copy-start(bf16[1024,512]{1,0:T(8,128)(2,1)S(1)} %get-tuple-element.88.refs_7_.refs_3_) | copy-start | bytes 3145732
  99.7 22.5 %copy-start.1 = (bf16[1024,512]{1,0:T(8,128)(2,1)}, bf16[1024,512]{1,0:T(8,128)(2,1)S(1)}, u32[]{:S(2)}) copy-start(bf16[1024,512]{1,0:T(8,128)(2,1)S(1)} %get-tuple-element.89.refs_8_.refs_4_) | copy-start | bytes 3145732
  99.7 22.5 %copy-start.2 = (bf16[1024,512]{1,0:T(8,128)(2,1)}, bf16[1024,512]{1,0:T(8,128)(2,1)S(1)}, u32[]{:S(2)}) copy-start(bf16[1024,512]{1,0:T(8,128)(2,1)S(1)} %get-tuple-element.90.refs_9_.refs_5_) | copy-start | bytes 3145732
  99.7 4.6 %collective-permute-start.16 = (bf16[1024,512]{1,0:T(8,128)(2,1)S(1)}, bf16[1024,512]{1,0:T(8,128)(2,1)S(1)}, u32[]{:S(2)}, u32[]{:S(2)}) collective-permute-start(bf16[1024,512]{1,0:T(8,128)(2,1)S(1)} %get-tuple-element.88.refs_7_.refs_3_), channel_id=1, source_target_pairs={{0,4},{4,0},{8,12},{12,8},{16,20},{20,16},{24,28},{28,24},{32,36},... | collective-permute-start | bytes 3145736 | tf_op jit(solution)/shard_map/ppermute | solution.py:748
  101.1 3.8 %collective-permute-start.17 = (bf16[1024,512]{1,0:T(8,128)(2,1)S(1)}, bf16[1024,512]{1,0:T(8,128)(2,1)S(1)}, u32[]{:S(2)}, u32[]{:S(2)}) collective-permute-start(bf16[1024,512]{1,0:T(8,128)(2,1)S(1)} %get-tuple-element.89.refs_8_.refs_4_), channel_id=1, source_target_pairs={{0,4},{4,0},{8,12},{12,8},{16,20},{20,16},{24,28},{28,24},{32,36},... | collective-permute-start | bytes 3145736 | tf_op jit(solution)/shard_map/ppermute | solution.py:748
  101.2 5.2 %collective-permute-start.18 = (bf16[1024,512]{1,0:T(8,128)(2,1)S(1)}, bf16[1024,512]{1,0:T(8,128)(2,1)S(1)}, u32[]{:S(2)}, u32[]{:S(2)}) collective-permute-start(bf16[1024,512]{1,0:T(8,128)(2,1)S(1)} %get-tuple-element.90.refs_9_.refs_5_), channel_id=1, source_target_pairs={{0,4},{4,0},{8,12},{12,8},{16,20},{20,16},{24,28},{28,24},{32,36},... | collective-permute-start | bytes 3145736 | tf_op jit(solution)/shard_map/ppermute | solution.py:748
  101.6 12.0 %collective-permute-start.11 = (bf16[192,1024]{1,0:T(8,128)(2,1)S(1)}, bf16[192,1024]{1,0:T(8,128)(2,1)}, u32[]{:S(2)}, u32[]{:S(2)}) collective-permute-start(bf16[192,1024]{1,0:T(8,128)(2,1)S(1)} %get-tuple-element.80.refs_3_.refs_0_), channel_id=1, source_target_pairs={{0,1},{1,2},{2,3},{3,0},{4,5},{5,6},{6,7},{7,4},{8,9},{9,10},{10,1... | collective-permute-start | bytes 1179656 | tf_op jit(solution)/shard_map/ppermute | solution.py:20
  102.1 11.4 %collective-permute-start.12 = (bf16[192,1024]{1,0:T(8,128)(2,1)S(1)}, bf16[192,1024]{1,0:T(8,128)(2,1)}, u32[]{:S(2)}, u32[]{:S(2)}) collective-permute-start(bf16[192,1024]{1,0:T(8,128)(2,1)S(1)} %get-tuple-element.81.refs_1_), channel_id=1, source_target_pairs={{0,3},{1,0},{2,1},{3,2},{4,7},{5,4},{6,5},{7,6},{8,11},{9,8},{10,9... | collective-permute-start | bytes 1179656 | tf_op jit(solution)/shard_map/ppermute | solution.py:20
  106.4 1.0 copy-start.3
  107.3 1.0 copy-start.4
  108.3 1.1 copy-start.5
  110.3 11.9 %collective-permute-start.21 = (bf16[192,1024]{1,0:T(8,128)(2,1)}, bf16[192,1024]{1,0:T(8,128)(2,1)}, u32[]{:S(2)}, u32[]{:S(2)}) collective-permute-start(bf16[192,1024]{1,0:T(8,128)(2,1)} %get-tuple-element.92.refs_2_), channel_id=1, source_target_pairs={{0,1},{1,2},{2,3},{3,0},{4,5},{5,6},{6,7},{7,4},{8,9},{9,10},{10,1... | collective-permute-start | bytes 1179656 | tf_op jit(solution)/shard_map/ppermute | solution.py:20
  110.9 11.3 %collective-permute-start.22 = (bf16[192,1024]{1,0:T(8,128)(2,1)}, bf16[192,1024]{1,0:T(8,128)(2,1)}, u32[]{:S(2)}, u32[]{:S(2)}) collective-permute-start(bf16[192,1024]{1,0:T(8,128)(2,1)} %get-tuple-element.98), channel_id=1, source_target_pairs={{0,3},{1,0},{2,1},{3,2},{4,7},{5,4},{6,5},{7,6},{8,11},{9,8},{10,9... | collective-permute-start | bytes 1179656 | tf_op jit(solution)/shard_map/ppermute | solution.py:20
  113.6 17.0 %collective-permute-start.19 = (bf16[192,1024]{1,0:T(8,128)(2,1)}, bf16[192,1024]{1,0:T(8,128)(2,1)}, u32[]{:S(2)}, u32[]{:S(2)}) collective-permute-start(bf16[192,1024]{1,0:T(8,128)(2,1)} %get-tuple-element.93.refs_2_), channel_id=1, source_target_pairs={{0,1},{1,2},{2,3},{3,0},{4,5},{5,6},{6,7},{7,4},{8,9},{9,10},{10,1... | collective-permute-start | bytes 1179656 | tf_op jit(solution)/shard_map/ppermute | solution.py:20
  114.4 16.2 %collective-permute-start.20 = (bf16[192,1024]{1,0:T(8,128)(2,1)}, bf16[192,1024]{1,0:T(8,128)(2,1)}, u32[]{:S(2)}, u32[]{:S(2)}) collective-permute-start(bf16[192,1024]{1,0:T(8,128)(2,1)} %get-tuple-element.94.refs_5_), channel_id=1, source_target_pairs={{0,3},{1,0},{2,1},{3,2},{4,7},{5,4},{6,5},{7,6},{8,11},{9,8},{10,9... | collective-permute-start | bytes 1179656 | tf_op jit(solution)/shard_map/ppermute | solution.py:20

commit v8 on v6

--- a/solution.py
+++ b/solution.py
@@ -12,7 +12,7 @@
 LANES = 128
 NEVER = -1e30
 BLOCK = 512
-AHEAD = 4
+AHEAD = 8
 
 
 def around(x, distance):

time: 136 us -> 136 us (level)
  no operation moved by 1% of the time
where the time goes in v8:
time: 136 us
  Pallas kernels  49.3 us (36%)
  starting transfers between devices  32.9 us (24%)
  blocking collectives  26.3 us (19%)
  waiting for transfers between devices  21.1 us (16%)
  local copies, waits for them, and re-layouts  5.51 us (4%)
    ppermute x18, starting transfers between devices, around(): return lax.ppermute(x, 'val', [(i, (i + distance) % n) for i in range(n)])  24 us
    ppermute x18, waiting for transfers between devices, around(): return lax.ppermute(x, 'val', [(i, (i + distance) % n) for i in range(n)])  18.3 us
    all_to_all x1, blocking collectives, per_device(): both = lax.all_to_all(both, 'seq', 0, 0, axis_index_groups=chips)  15.2 us
    pallas_call x2, Pallas kernels, out_product(): pl.pallas_call(functools.partial(out_kernel, [len(g) for g in groups], to...  12.7 us
    pallas_call x2, Pallas kernels, product(): pl.pallas_call(functools.partial(product_kernel, [len(g) for g in groups]...  11.3 us
    all_to_all x1, blocking collectives, per_device(): lax.all_to_all(prefixes(both), 'seq', 0, 0, axis_index_groups=chips)  11.1 us
    pallas_call x3, Pallas kernels, flat(): pl.pallas_call(functools.partial(flat_kernel, len(args)), grid=(steps,),...  10.2 us
    unnamed x26, local copies, waits for them, and re-layouts  4.19 us
  transfers between devices with their start and end apart: 23, of which 10 were waited for; matrix products, arithmetic and copies ran while one was open for 1% of the time, Pallas kernels for 29%

profile of v8, /device:TPU:1, one launch (start us, length us, event | category | flops | bytes accessed | tf_op | source)
XLA Modules:
  0.0 135.8 jit_solution(10580819280818914291)
XLA Ops:
  0.0 1.1 copy-done.6
  1.2 2.2 %collective-permute-start = (bf16[192,1024]{1,0:T(8,128)(2,1)S(1)}, bf16[192,1024]{1,0:T(8,128)(2,1)S(1)}, u32[]{:S(2)}, u32[]{:S(2)}) collective-permute-start(bf16[192,1024]{1,0:T(8,128)(2,1)S(1)} %get-tuple-element.52.refs_0_), channel_id=1, source_target_pairs={{0,1},{1,2},{2,3},{3,0},{4,5},{5,6},{6,7},{7,4},{8,9},{9,10},{10,1... | collective-permute-start | bytes 1179656 | tf_op jit(solution)/shard_map/ppermute | solution.py:20
  3.4 1.5 %collective-permute-start.1 = (bf16[192,1024]{1,0:T(8,128)(2,1)S(1)}, bf16[192,1024]{1,0:T(8,128)(2,1)S(1)}, u32[]{:S(2)}, u32[]{:S(2)}) collective-permute-start(bf16[192,1024]{1,0:T(8,128)(2,1)S(1)} %get-tuple-element.53.refs_1_), channel_id=1, source_target_pairs={{0,3},{1,0},{2,1},{3,2},{4,7},{5,4},{6,5},{7,6},{8,11},{9,8},{10,9... | collective-permute-start | bytes 1179656 | tf_op jit(solution)/shard_map/ppermute | solution.py:20
  4.9 2.7 %shard_map.83 = (bf16[4096,1024]{1,0:T(8,128)(2,1)}, f32[8,128]{1,0:T(8,128)S(1)}) custom-call(bf16[4096,8,128]{2,1,0:T(8,128)(2,1)} %w_ref.5), custom_call_target="tpu_custom_call" | custom-call | bytes 2097152 | tf_op jit(solution)/shard_map/pallas_call | solution.py:103
  7.7 2.7 %collective-permute-start.3 = (bf16[192,1024]{1,0:T(8,128)(2,1)S(1)}, bf16[192,1024]{1,0:T(8,128)(2,1)S(1)}, u32[]{:S(2)}, u32[]{:S(2)}) collective-permute-start(bf16[192,1024]{1,0:T(8,128)(2,1)S(1)} %get-tuple-element.59), channel_id=1, source_target_pairs={{0,3},{1,0},{2,1},{3,2},{4,7},{5,4},{6,5},{7,6},{8,11},{9,8},{10,9... | collective-permute-start | bytes 1179656 | tf_op jit(solution)/shard_map/ppermute | solution.py:20
  10.4 2.7 %shard_map.85 = (bf16[4096,1024]{1,0:T(8,128)(2,1)}, f32[8,128]{1,0:T(8,128)S(1)}) custom-call(bf16[4096,8,128]{2,1,0:T(8,128)(2,1)} %w_ref.5, bf16[4096,1024]{1,0:T(8,128)(2,1)} %get-tuple-element.56.refs_0_), custom_call_target="tpu_custom_call", output_to_operand_aliasing={{0}: (1, {})} | custom-call | bytes 2097152 | tf_op jit(solution)/shard_map/pallas_call | solution.py:103
  13.5 0.8 collective-permute-start.4
  14.3 1.8 %collective-permute-start.5 = (bf16[192,1024]{1,0:T(8,128)(2,1)S(1)}, bf16[192,1024]{1,0:T(8,128)(2,1)S(1)}, u32[]{:S(2)}, u32[]{:S(2)}) collective-permute-start(bf16[192,1024]{1,0:T(8,128)(2,1)S(1)} %get-tuple-element.60.refs_4_), channel_id=1, source_target_pairs={{0,3},{1,0},{2,1},{3,2},{4,7},{5,4},{6,5},{7,6},{8,11},{9,8},{10,9... | collective-permute-start | bytes 1179656 | tf_op jit(solution)/shard_map/ppermute | solution.py:20
  16.4 4.9 %shard_map.87 = (bf16[4096,1024]{1,0:T(8,128)(2,1)}, f32[8,128]{1,0:T(8,128)}) custom-call(bf16[4096,8,128]{2,1,0:T(8,128)(2,1)} %w_ref.5, bf16[4096,1024]{1,0:T(8,128)(2,1)} %get-tuple-element.61.refs_0_), custom_call_target="tpu_custom_call", output_to_operand_aliasing={{0}: (1, {})} | custom-call | bytes 4194304 | tf_op jit(solution)/shard_map/pallas_call | solution.py:103
  21.3 0.6 collective-permute-done.2.refs_2_
  21.9 5.2 %shard_map.88.refs_0_.acc_ref = f32[384,1024]{1,0:T(8,128)S(1)} custom-call(s32[3]{0:T(128)S(1)} %pad_add_fusion.2.scalars, bf16[384,1024]{1,0:T(8,128)(2,1)S(1)} %copy-done.7, bf16[192,1024]{1,0:T(8,128)(2,1)S(1)} %get-tuple-element.58.refs_1_, bf16[192,1024]{1,0:T(8,128)(2,1)S(1)} %collective-permute-done.2.refs_2_, ...), custom_call_target="tpu_custom_call" | custom-call | flops 2415919104 | bytes 10223616 | tf_op jit(solution)/shard_map/pallas_call | solution.py:211
  27.1 2.5 %shard_map.89 = (bf16[1024,512]{1,0:T(8,128)(2,1)S(1)}, bf16[1024,512]{1,0:T(8,128)(2,1)S(1)}, bf16[1024,512]{1,0:T(8,128)(2,1)S(1)}, f32[8,128]{1,0:T(8,128)S(1)}) custom-call(s32[2]{0:T(128)S(1)} %pad_add_fusion.3.scalars, bf16[1024,4096]{1,0:T(8,128)(2,1)} %bitcast.15, f32[384,1024]{1,0:T(8,128)S(1)} %shard_map.88.refs_0_.acc_ref), custom_call_target="tpu_custom_call" | custom-call | bytes 6291456 | tf_op jit(solution)/shard_map/pallas_call | solution.py:250
  29.6 0.8 collective-permute-done.4.upper.refs_5_
  30.4 3.9 %shard_map.90 = (bf16[2,400,128]{2,1,0:T(8,128)(2,1)S(1)}, bf16[2,400,128]{2,1,0:T(8,128)(2,1)S(1)}, bf16[2,400,128]{2,1,0:T(8,128)(2,1)S(1)}, bf16[2,400,128]{2,1,0:T(8,128)(2,1)S(1)}) custom-call(s32[2]{0:T(128)S(1)} %pad_add_fusion.1.scalars, bf16[192,1024]{1,0:T(8,128)(2,1)S(1)} %collective-permute-done.4.upper.refs_5_, ...), custom_call_target="tpu_custom_call" | custom-call | flops 805306368 | bytes 5242880 | tf_op jit(solution)/shard_map/pallas_call | solution.py:376
  34.3 0.9 collective-permute-start.6
  35.2 1.8 %collective-permute-start.7 = (bf16[2,400,128]{2,1,0:T(8,128)(2,1)S(1)}, bf16[2,400,128]{2,1,0:T(8,128)(2,1)S(1)}, u32[]{:S(2)}, u32[]{:S(2)}) collective-permute-start(bf16[2,400,128]{2,1,0:T(8,128)(2,1)S(1)} %get-tuple-element.70), channel_id=1, source_target_pairs={{0,3},{1,0},{2,1},{3,2},{4,7},{5,4},{6,5},{7,6},{8,11},{9,8},{10,9... | collective-permute-start | bytes 614408 | tf_op jit(solution)/shard_map/ppermute | solution.py:20
  37.0 1.0 collective-permute-start.8
  38.0 6.1 %shard_map.91 = (bf16[384,512]{1,0:T(8,128)(2,1)S(1)}, bf16[384,512]{1,0:T(8,128)(2,1)S(1)}) custom-call(s32[4]{0:T(128)S(1)} %pad_add_fusion.scalars, bf16[384,1024]{1,0:T(8,128)(2,1)S(1)} %copy-done.7, bf16[192,1024]{1,0:T(8,128)(2,1)S(1)} %get-tuple-element.58.refs_1_, bf16[192,1024]{1,0:T(8,128)(2,1)S(1)} %collective-permute-done.2.refs_2_, ...), custom_call_target="tpu_custom_call" | custom-call | flops 3221225472 | bytes 13107200 | tf_op jit(solution)/shard_map/pallas_call | solution.py:211
  44.2 2.9 %shard_map.92 = (bf16[512,384]{1,0:T(8,128)(2,1)S(1)}, bf16[2,384,384]{2,1,0:T(8,128)(2,1)S(1)}, f32[384,128]{1,0:T(8,128)S(1)}, f32[8,128]{1,0:T(8,128)S(1)}) custom-call(s32[4]{0:T(128)S(1)} %pad_add_fusion.scalars, f32[2,8]{1,0:T(2,128)S(1)} %copy-done.12, bf16[384,1024]{1,0:T(8,128)(2,1)S(1)} %copy-done.7, ...), custom_call_target="tpu_custom_call" | custom-call | flops 301989888 | bytes 1572864 | tf_op jit(solution)/shard_map/pallas_call | solution.py:464
  47.1 1.1 shard_map.93
  48.3 3.4 %collective-permute-start.9 = (bf16[256,640]{1,0:T(8,128)(2,1)S(1)}, bf16[256,640]{1,0:T(8,128)(2,1)S(1)}, u32[]{:S(2)}, u32[]{:S(2)}) collective-permute-start(bf16[256,640]{1,0:T(8,128)(2,1)S(1)} %get-tuple-element.73), channel_id=1, source_target_pairs={{0,4},{4,0},{8,12},{12,8},{16,20},{20,16},{24,28},{28,24},{32,36},... | collective-permute-start | bytes 983048 | tf_op jit(solution)/shard_map/ppermute | solution.py:733
  52.1 2.2 %collective-permute-start.14 = (bf16[1024,512]{1,0:T(8,128)(2,1)S(1)}, bf16[1024,512]{1,0:T(8,128)(2,1)S(1)}, u32[]{:S(2)}, u32[]{:S(2)}) collective-permute-start(bf16[1024,512]{1,0:T(8,128)(2,1)S(1)} %get-tuple-element.86), channel_id=1, source_target_pairs={{0,3},{1,0},{2,1},{3,2},{4,7},{5,4},{6,5},{7,6},{8,11},{9,8},{10,9... | collective-permute-start | bytes 3145736 | tf_op jit(solution)/shard_map/ppermute | solution.py:20
  55.3 15.2 %all_to_all.10.got_ref = bf16[16,16,640]{2,1,0:T(8,128)(2,1)S(1)} all-to-all(bf16[16,16,640]{2,1,0:T(8,128)(2,1)S(1)} %bitcast.13), channel_id=1, replica_groups={{0,8,16,24,32,40,48,56,64,72,80,88,96,104,112,120},{4,12,20,28,36,44,52..., dimensions={0} | all-to-all | bytes 655360 | tf_op jit(solution)/shard_map/all_to_all | solution.py:737
  70.8 11.1 %all_to_all.11 = bf16[16,16,640]{2,1,0:T(8,128)(2,1)S(1)} all-to-all(bf16[16,16,640]{2,1,0:T(8,128)(2,1)S(1)} %shard_map.95), channel_id=1, replica_groups={{0,8,16,24,32,40,48,56,64,72,80,88,96,104,112,120},{4,12,20,28,36,44,52..., dimensions={0} | all-to-all | bytes 655360 | tf_op jit(solution)/shard_map/all_to_all | solution.py:739
  82.3 3.6 %collective-permute-start.10 = (bf16[256,640]{1,0:T(8,128)(2,1)S(1)}, bf16[256,640]{1,0:T(8,128)(2,1)S(1)}, u32[]{:S(2)}, u32[]{:S(2)}) collective-permute-start(bf16[256,640]{1,0:T(8,128)(2,1)S(1)} %get-tuple-element.75), channel_id=1, source_target_pairs={{0,4},{4,0},{8,12},{12,8},{16,20},{20,16},{24,28},{28,24},{32,36},... | collective-permute-start | bytes 983048 | tf_op jit(solution)/shard_map/ppermute | solution.py:741
  86.0 0.6 shard_map.97.numer_ref
  86.5 0.7 collective-permute-done.10.got
  87.2 1.8 %shard_map.98 = (bf16[192,1024]{1,0:T(8,128)(2,1)S(1)}, bf16[192,1024]{1,0:T(8,128)(2,1)S(1)}) custom-call(s32[1]{0:T(128)} %bitcast.4.scalars, bf16[384,512]{1,0:T(8,128)(2,1)S(1)} %get-tuple-element.65.refs_8_.q_ref, bf16[256,640]{1,0:T(8,128)(2,1)S(1)} %get-tuple-element.74.mine, bf16[256,640]{1,0:T(8,128)(2,1)S(1)} %collective-permute-done.10.got, ...), custom_call_target="tpu_custom_call" | custom-call | flops 201326592 | bytes 3145728 | tf_op jit(solution)/shard_map/pallas_call | solution.py:686
  89.1 10.6 %collective-permute-done.15.refs_2_ = bf16[1024,512]{1,0:T(8,128)(2,1)S(1)} collective-permute-done((bf16[1024,512]{1,0:T(8,128)(2,1)S(1)}, bf16[1024,512]{1,0:T(8,128)(2,1)S(1)}, u32[]{:S(2)}, u32[]{:S(2)}) %collective-permute-start.15) | collective-permute-done | bytes 1048608 | tf_op jit(solution)/shard_map/ppermute | solution.py:20
  99.7 1.4 %collective-permute-start.16 = (bf16[1024,512]{1,0:T(8,128)(2,1)S(1)}, bf16[1024,512]{1,0:T(8,128)(2,1)S(1)}, u32[]{:S(2)}, u32[]{:S(2)}) collective-permute-start(bf16[1024,512]{1,0:T(8,128)(2,1)S(1)} %get-tuple-element.88.refs_7_.refs_3_), channel_id=1, source_target_pairs={{0,4},{4,0},{8,12},{12,8},{16,20},{20,16},{24,28},{28,24},{32,36},... | collective-permute-start | bytes 3145736 | tf_op jit(solution)/shard_map/ppermute | solution.py:746
  101.6 0.6 collective-permute-start.11
  102.1 2.1 %collective-permute-start.12 = (bf16[192,1024]{1,0:T(8,128)(2,1)S(1)}, bf16[192,1024]{1,0:T(8,128)(2,1)}, u32[]{:S(2)}, u32[]{:S(2)}) collective-permute-start(bf16[192,1024]{1,0:T(8,128)(2,1)S(1)} %get-tuple-element.81.refs_1_), channel_id=1, source_target_pairs={{0,3},{1,0},{2,1},{3,2},{4,7},{5,4},{6,5},{7,6},{8,11},{9,8},{10,9... | collective-permute-start | bytes 1179656 | tf_op jit(solution)/shard_map/ppermute | solution.py:20
  104.3 0.6 collective-permute-done.17.refs_1_
  104.8 1.5 %collective-permute-done.18.refs_2_ = bf16[1024,512]{1,0:T(8,128)(2,1)S(1)} collective-permute-done((bf16[1024,512]{1,0:T(8,128)(2,1)S(1)}, bf16[1024,512]{1,0:T(8,128)(2,1)S(1)}, u32[]{:S(2)}, u32[]{:S(2)}) %collective-permute-start.18) | collective-permute-done | bytes 1048608 | tf_op jit(solution)/shard_map/ppermute | solution.py:746
  106.4 1.0 copy-done.3
  107.3 1.0 copy-done.4
  108.3 1.1 copy-done.5
  109.4 0.9 shard_map.102
  110.9 2.1 %collective-permute-start.22 = (bf16[192,1024]{1,0:T(8,128)(2,1)}, bf16[192,1024]{1,0:T(8,128)(2,1)}, u32[]{:S(2)}, u32[]{:S(2)}) collective-permute-start(bf16[192,1024]{1,0:T(8,128)(2,1)} %get-tuple-element.98), channel_id=1, source_target_pairs={{0,3},{1,0},{2,1},{3,2},{4,7},{5,4},{6,5},{7,6},{8,11},{9,8},{10,9... | collective-permute-start | bytes 1179656 | tf_op jit(solution)/shard_map/ppermute | solution.py:20
  113.0 0.6 collective-permute-done.11.refs_0_
  113.6 0.8 collective-permute-start.19
  114.4 1.8 %collective-permute-start.20 = (bf16[192,1024]{1,0:T(8,128)(2,1)}, bf16[192,1024]{1,0:T(8,128)(2,1)}, u32[]{:S(2)}, u32[]{:S(2)}) collective-permute-start(bf16[192,1024]{1,0:T(8,128)(2,1)} %get-tuple-element.94.refs_5_), channel_id=1, source_target_pairs={{0,3},{1,0},{2,1},{3,2},{4,7},{5,4},{6,5},{7,6},{8,11},{9,8},{10,9... | collective-permute-start | bytes 1179656 | tf_op jit(solution)/shard_map/ppermute | solution.py:20
  116.2 0.6 stack.38.scalars
  116.8 0.7 stack.31.scalars
  117.5 4.7 %collective-permute-done.21.refs_3_ = bf16[192,1024]{1,0:T(8,128)(2,1)} collective-permute-done((bf16[192,1024]{1,0:T(8,128)(2,1)}, bf16[192,1024]{1,0:T(8,128)(2,1)}, u32[]{:S(2)}, u32[]{:S(2)}) %collective-permute-start.21) | collective-permute-done | bytes 393248 | tf_op jit(solution)/shard_map/ppermute | solution.py:20
  122.2 7.7 %shard_map.104.refs_9_ = f32[384,1024]{1,0:T(8,128)} custom-call(s32[8]{0:T(128)} %stack.38.scalars, bf16[192,1024]{1,0:T(8,128)(2,1)} %copy-done.8, bf16[192,1024]{1,0:T(8,128)(2,1)} %copy-done.9, bf16[192,1024]{1,0:T(8,128)(2,1)} %get-tuple-element.93.refs_2_, bf16[192,1024]{1,0:T(8,128)(2,1)} %collective-permute-done.21.refs_3_, ...), custom_call_target="tpu_custom_call" | custom-call | flops 2415919104 | bytes 7864320 | tf_op jit(solution)/shard_map/pallas_call | solution.py:317
  129.9 0.7 collective-permute-done.19.refs_0_
  130.6 5.0 %shard_map.105 = bf16[384,1024]{1,0:T(8,128)(2,1)} custom-call(s32[6]{0:T(128)} %stack.31.scalars, bf16[192,1024]{1,0:T(8,128)(2,1)} %collective-permute-done.19.refs_0_, bf16[192,1024]{1,0:T(8,128)(2,1)} %collective-permute-done.20.refs_1_, bf16[1024,4096]{1,0:T(8,128)(2,1)} %bitcast.17, bf16[1024,512]{1,0:T(8,128)(2,1)} %copy-done, ...), custom_call_target="tpu_custom_call" | custom-call | flops 805306368 | bytes 3670016 | tf_op jit(solution)/shard_map/pallas_call | solution.py:317
  (57 shorter events, 4.2 us)
Async XLA Ops:
  0.0 1.1 copy-start.6
  1.2 12.3 %collective-permute-start = (bf16[192,1024]{1,0:T(8,128)(2,1)S(1)}, bf16[192,1024]{1,0:T(8,128)(2,1)S(1)}, u32[]{:S(2)}, u32[]{:S(2)}) collective-permute-start(bf16[192,1024]{1,0:T(8,128)(2,1)S(1)} %get-tuple-element.52.refs_0_), channel_id=1, source_target_pairs={{0,1},{1,2},{2,3},{3,0},{4,5},{5,6},{6,7},{7,4},{8,9},{9,10},{10,1... | collective-permute-start | bytes 1179656 | tf_op jit(solution)/shard_map/ppermute | solution.py:20
  3.4 10.1 %collective-permute-start.1 = (bf16[192,1024]{1,0:T(8,128)(2,1)S(1)}, bf16[192,1024]{1,0:T(8,128)(2,1)S(1)}, u32[]{:S(2)}, u32[]{:S(2)}) collective-permute-start(bf16[192,1024]{1,0:T(8,128)(2,1)S(1)} %get-tuple-element.53.refs_1_), channel_id=1, source_target_pairs={{0,3},{1,0},{2,1},{3,2},{4,7},{5,4},{6,5},{7,6},{8,11},{9,8},{10,9... | collective-permute-start | bytes 1179656 | tf_op jit(solution)/shard_map/ppermute | solution.py:20
  7.6 14.3 %collective-permute-start.2 = (bf16[192,1024]{1,0:T(8,128)(2,1)S(1)}, bf16[192,1024]{1,0:T(8,128)(2,1)S(1)}, u32[]{:S(2)}, u32[]{:S(2)}) collective-permute-start(bf16[192,1024]{1,0:T(8,128)(2,1)S(1)} %get-tuple-element.55.refs_2_), channel_id=1, source_target_pairs={{0,1},{1,2},{2,3},{3,0},{4,5},{5,6},{6,7},{7,4},{8,9},{9,10},{10,1... | collective-permute-start | bytes 1179656 | tf_op jit(solution)/shard_map/ppermute | solution.py:20
  7.7 14.2 %collective-permute-start.3 = (bf16[192,1024]{1,0:T(8,128)(2,1)S(1)}, bf16[192,1024]{1,0:T(8,128)(2,1)S(1)}, u32[]{:S(2)}, u32[]{:S(2)}) collective-permute-start(bf16[192,1024]{1,0:T(8,128)(2,1)S(1)} %get-tuple-element.59), channel_id=1, source_target_pairs={{0,3},{1,0},{2,1},{3,2},{4,7},{5,4},{6,5},{7,6},{8,11},{9,8},{10,9... | collective-permute-start | bytes 1179656 | tf_op jit(solution)/shard_map/ppermute | solution.py:20
  13.5 16.8 %collective-permute-start.4 = (bf16[192,1024]{1,0:T(8,128)(2,1)S(1)}, bf16[192,1024]{1,0:T(8,128)(2,1)S(1)}, u32[]{:S(2)}, u32[]{:S(2)}) collective-permute-start(bf16[192,1024]{1,0:T(8,128)(2,1)S(1)} %get-tuple-element.58.refs_1_), channel_id=1, source_target_pairs={{0,1},{1,2},{2,3},{3,0},{4,5},{5,6},{6,7},{7,4},{8,9},{9,10},{10,1... | collective-permute-start | bytes 1179656 | tf_op jit(solution)/shard_map/ppermute | solution.py:20
  14.3 16.0 %collective-permute-start.5 = (bf16[192,1024]{1,0:T(8,128)(2,1)S(1)}, bf16[192,1024]{1,0:T(8,128)(2,1)S(1)}, u32[]{:S(2)}, u32[]{:S(2)}) collective-permute-start(bf16[192,1024]{1,0:T(8,128)(2,1)S(1)} %get-tuple-element.60.refs_4_), channel_id=1, source_target_pairs={{0,3},{1,0},{2,1},{3,2},{4,7},{5,4},{6,5},{7,6},{8,11},{9,8},{10,9... | collective-permute-start | bytes 1179656 | tf_op jit(solution)/shard_map/ppermute | solution.py:20
  16.4 5.6 %copy-start.7 = (bf16[384,1024]{1,0:T(8,128)(2,1)S(1)}, bf16[384,1024]{1,0:T(8,128)(2,1)}, u32[]{:S(2)}) copy-start(bf16[384,1024]{1,0:T(8,128)(2,1)} %refs_0_.7) | copy-start | bytes 2359300
  21.9 8.4 %copy-start.11 = (f32[8,128]{1,0:T(8,128)S(1)}, f32[8,128]{1,0:T(8,128)}, u32[]{:S(2)}) copy-start(f32[8,128]{1,0:T(8,128)} %gain_ref.1) | copy-start | bytes 12292
  34.2 9.9 %copy-start.10 = (bf16[4096,2,8]{0,2,1:T(8,128)(2,1)S(1)}, bf16[4096,2,8]{0,2,1:T(8,128)(2,1)}, u32[]{:S(2)}) copy-start(bf16[4096,2,8]{0,2,1:T(8,128)(2,1)} %param.12) | copy-start | bytes 393220
  34.2 9.9 %copy-start.12 = (f32[2,8]{1,0:T(2,128)S(1)}, f32[2,8]{1,0:T(2,128)}, u32[]{:S(2)}) copy-start(f32[2,8]{1,0:T(2,128)} %bias_ref.1) | copy-start | bytes 196
  34.3 12.9 %collective-permute-start.6 = (bf16[2,400,128]{2,1,0:T(8,128)(2,1)S(1)}, bf16[2,400,128]{2,1,0:T(8,128)(2,1)S(1)}, u32[]{:S(2)}, u32[]{:S(2)}) collective-permute-start(bf16[2,400,128]{2,1,0:T(8,128)(2,1)S(1)} %get-tuple-element.69), channel_id=1, source_target_pairs={{0,1},{1,2},{2,3},{3,0},{4,5},{5,6},{6,7},{7,4},{8,9},{9,10},{10,1... | collective-permute-start | bytes 614408 | tf_op jit(solution)/shard_map/ppermute | solution.py:20
  35.2 12.0 %collective-permute-start.7 = (bf16[2,400,128]{2,1,0:T(8,128)(2,1)S(1)}, bf16[2,400,128]{2,1,0:T(8,128)(2,1)S(1)}, u32[]{:S(2)}, u32[]{:S(2)}) collective-permute-start(bf16[2,400,128]{2,1,0:T(8,128)(2,1)S(1)} %get-tuple-element.70), channel_id=1, source_target_pairs={{0,3},{1,0},{2,1},{3,2},{4,7},{5,4},{6,5},{7,6},{8,11},{9,8},{10,9... | collective-permute-start | bytes 614408 | tf_op jit(solution)/shard_map/ppermute | solution.py:20
  37.0 10.1 %collective-permute-start.8 = (bf16[2,400,128]{2,1,0:T(8,128)(2,1)S(1)}, bf16[2,400,128]{2,1,0:T(8,128)(2,1)S(1)}, u32[]{:S(2)}, u32[]{:S(2)}) collective-permute-start(bf16[2,400,128]{2,1,0:T(8,128)(2,1)S(1)} %get-tuple-element.71), channel_id=1, source_target_pairs={{0,2},{1,3},{2,0},{3,1},{4,6},{5,7},{6,4},{7,5},{8,10},{9,11},{10,... | collective-permute-start | bytes 614408 | tf_op jit(solution)/shard_map/ppermute | solution.py:20
  48.3 6.4 %collective-permute-start.9 = (bf16[256,640]{1,0:T(8,128)(2,1)S(1)}, bf16[256,640]{1,0:T(8,128)(2,1)S(1)}, u32[]{:S(2)}, u32[]{:S(2)}) collective-permute-start(bf16[256,640]{1,0:T(8,128)(2,1)S(1)} %get-tuple-element.73), channel_id=1, source_target_pairs={{0,4},{4,0},{8,12},{12,8},{16,20},{20,16},{24,28},{28,24},{32,36},... | collective-permute-start | bytes 983048 | tf_op jit(solution)/shard_map/ppermute | solution.py:733
  51.7 37.4 %collective-permute-start.13 = (bf16[1024,512]{1,0:T(8,128)(2,1)S(1)}, bf16[1024,512]{1,0:T(8,128)(2,1)S(1)}, u32[]{:S(2)}, u32[]{:S(2)}) collective-permute-start(bf16[1024,512]{1,0:T(8,128)(2,1)S(1)} %get-tuple-element.85), channel_id=1, source_target_pairs={{0,1},{1,2},{2,3},{3,0},{4,5},{5,6},{6,7},{7,4},{8,9},{9,10},{10,1... | collective-permute-start | bytes 3145736 | tf_op jit(solution)/shard_map/ppermute | solution.py:20
  52.1 36.9 %collective-permute-start.14 = (bf16[1024,512]{1,0:T(8,128)(2,1)S(1)}, bf16[1024,512]{1,0:T(8,128)(2,1)S(1)}, u32[]{:S(2)}, u32[]{:S(2)}) collective-permute-start(bf16[1024,512]{1,0:T(8,128)(2,1)S(1)} %get-tuple-element.86), channel_id=1, source_target_pairs={{0,3},{1,0},{2,1},{3,2},{4,7},{5,4},{6,5},{7,6},{8,11},{9,8},{10,9... | collective-permute-start | bytes 3145736 | tf_op jit(solution)/shard_map/ppermute | solution.py:20
  54.4 45.3 %collective-permute-start.15 = (bf16[1024,512]{1,0:T(8,128)(2,1)S(1)}, bf16[1024,512]{1,0:T(8,128)(2,1)S(1)}, u32[]{:S(2)}, u32[]{:S(2)}) collective-permute-start(bf16[1024,512]{1,0:T(8,128)(2,1)S(1)} %get-tuple-element.87), channel_id=1, source_target_pairs={{0,2},{1,3},{2,0},{3,1},{4,6},{5,7},{6,4},{7,5},{8,10},{9,11},{10,... | collective-permute-start | bytes 3145736 | tf_op jit(solution)/shard_map/ppermute | solution.py:20
  82.3 4.9 %collective-permute-start.10 = (bf16[256,640]{1,0:T(8,128)(2,1)S(1)}, bf16[256,640]{1,0:T(8,128)(2,1)S(1)}, u32[]{:S(2)}, u32[]{:S(2)}) collective-permute-start(bf16[256,640]{1,0:T(8,128)(2,1)S(1)} %get-tuple-element.75), channel_id=1, source_target_pairs={{0,4},{4,0},{8,12},{12,8},{16,20},{20,16},{24,28},{28,24},{32,36},... | collective-permute-start | bytes 983048 | tf_op jit(solution)/shard_map/ppermute | solution.py:741
  89.0 24.5 %copy-start.9 = (bf16[192,1024]{1,0:T(8,128)(2,1)}, bf16[192,1024]{1,0:T(8,128)(2,1)S(1)}, u32[]{:S(2)}) copy-start(bf16[192,1024]{1,0:T(8,128)(2,1)S(1)} %get-tuple-element.81.refs_1_) | copy-start | bytes 1179652
  89.0 33.1 %copy-start.8 = (bf16[192,1024]{1,0:T(8,128)(2,1)}, bf16[192,1024]{1,0:T(8,128)(2,1)S(1)}, u32[]{:S(2)}) copy-start(bf16[192,1024]{1,0:T(8,128)(2,1)S(1)} %get-tuple-element.80.refs_3_.refs_0_) | copy-start | bytes 1179652
  99.7 22.5 %copy-start = (bf16[1024,512]{1,0:T(8,128)(2,1)}, bf16[1024,512]{1,0:T(8,128)(2,1)S(1)}, u32[]{:S(2)}) copy-start(bf16[1024,512]{1,0:T(8,128)(2,1)S(1)} %get-tuple-element.88.refs_7_.refs_3_) | copy-start | bytes 3145732
  99.7 22.5 %copy-start.1 = (bf16[1024,512]{1,0:T(8,128)(2,1)}, bf16[1024,512]{1,0:T(8,128)(2,1)S(1)}, u32[]{:S(2)}) copy-start(bf16[1024,512]{1,0:T(8,128)(2,1)S(1)} %get-tuple-element.89.refs_8_.refs_4_) | copy-start | bytes 3145732
  99.7 22.5 %copy-start.2 = (bf16[1024,512]{1,0:T(8,128)(2,1)}, bf16[1024,512]{1,0:T(8,128)(2,1)S(1)}, u32[]{:S(2)}) copy-start(bf16[1024,512]{1,0:T(8,128)(2,1)S(1)} %get-tuple-element.90.refs_9_.refs_5_) | copy-start | bytes 3145732
  99.7 4.6 %collective-permute-start.16 = (bf16[1024,512]{1,0:T(8,128)(2,1)S(1)}, bf16[1024,512]{1,0:T(8,128)(2,1)S(1)}, u32[]{:S(2)}, u32[]{:S(2)}) collective-permute-start(bf16[1024,512]{1,0:T(8,128)(2,1)S(1)} %get-tuple-element.88.refs_7_.refs_3_), channel_id=1, source_target_pairs={{0,4},{4,0},{8,12},{12,8},{16,20},{20,16},{24,28},{28,24},{32,36},... | collective-permute-start | bytes 3145736 | tf_op jit(solution)/shard_map/ppermute | solution.py:746
  101.1 3.8 %collective-permute-start.17 = (bf16[1024,512]{1,0:T(8,128)(2,1)S(1)}, bf16[1024,512]{1,0:T(8,128)(2,1)S(1)}, u32[]{:S(2)}, u32[]{:S(2)}) collective-permute-start(bf16[1024,512]{1,0:T(8,128)(2,1)S(1)} %get-tuple-element.89.refs_8_.refs_4_), channel_id=1, source_target_pairs={{0,4},{4,0},{8,12},{12,8},{16,20},{20,16},{24,28},{28,24},{32,36},... | collective-permute-start | bytes 3145736 | tf_op jit(solution)/shard_map/ppermute | solution.py:746
  101.2 5.2 %collective-permute-start.18 = (bf16[1024,512]{1,0:T(8,128)(2,1)S(1)}, bf16[1024,512]{1,0:T(8,128)(2,1)S(1)}, u32[]{:S(2)}, u32[]{:S(2)}) collective-permute-start(bf16[1024,512]{1,0:T(8,128)(2,1)S(1)} %get-tuple-element.90.refs_9_.refs_5_), channel_id=1, source_target_pairs={{0,4},{4,0},{8,12},{12,8},{16,20},{20,16},{24,28},{28,24},{32,36},... | collective-permute-start | bytes 3145736 | tf_op jit(solution)/shard_map/ppermute | solution.py:746
  101.6 12.0 %collective-permute-start.11 = (bf16[192,1024]{1,0:T(8,128)(2,1)S(1)}, bf16[192,1024]{1,0:T(8,128)(2,1)}, u32[]{:S(2)}, u32[]{:S(2)}) collective-permute-start(bf16[192,1024]{1,0:T(8,128)(2,1)S(1)} %get-tuple-element.80.refs_3_.refs_0_), channel_id=1, source_target_pairs={{0,1},{1,2},{2,3},{3,0},{4,5},{5,6},{6,7},{7,4},{8,9},{9,10},{10,1... | collective-permute-start | bytes 1179656 | tf_op jit(solution)/shard_map/ppermute | solution.py:20
  102.1 11.4 %collective-permute-start.12 = (bf16[192,1024]{1,0:T(8,128)(2,1)S(1)}, bf16[192,1024]{1,0:T(8,128)(2,1)}, u32[]{:S(2)}, u32[]{:S(2)}) collective-permute-start(bf16[192,1024]{1,0:T(8,128)(2,1)S(1)} %get-tuple-element.81.refs_1_), channel_id=1, source_target_pairs={{0,3},{1,0},{2,1},{3,2},{4,7},{5,4},{6,5},{7,6},{8,11},{9,8},{10,9... | collective-permute-start | bytes 1179656 | tf_op jit(solution)/shard_map/ppermute | solution.py:20
  106.4 1.0 copy-start.3
  107.3 1.0 copy-start.4
  108.3 1.1 copy-start.5
  110.3 11.9 %collective-permute-start.21 = (bf16[192,1024]{1,0:T(8,128)(2,1)}, bf16[192,1024]{1,0:T(8,128)(2,1)}, u32[]{:S(2)}, u32[]{:S(2)}) collective-permute-start(bf16[192,1024]{1,0:T(8,128)(2,1)} %get-tuple-element.92.refs_2_), channel_id=1, source_target_pairs={{0,1},{1,2},{2,3},{3,0},{4,5},{5,6},{6,7},{7,4},{8,9},{9,10},{10,1... | collective-permute-start | bytes 1179656 | tf_op jit(solution)/shard_map/ppermute | solution.py:20
  110.9 11.3 %collective-permute-start.22 = (bf16[192,1024]{1,0:T(8,128)(2,1)}, bf16[192,1024]{1,0:T(8,128)(2,1)}, u32[]{:S(2)}, u32[]{:S(2)}) collective-permute-start(bf16[192,1024]{1,0:T(8,128)(2,1)} %get-tuple-element.98), channel_id=1, source_target_pairs={{0,3},{1,0},{2,1},{3,2},{4,7},{5,4},{6,5},{7,6},{8,11},{9,8},{10,9... | collective-permute-start | bytes 1179656 | tf_op jit(solution)/shard_map/ppermute | solution.py:20
  113.6 17.0 %collective-permute-start.19 = (bf16[192,1024]{1,0:T(8,128)(2,1)}, bf16[192,1024]{1,0:T(8,128)(2,1)}, u32[]{:S(2)}, u32[]{:S(2)}) collective-permute-start(bf16[192,1024]{1,0:T(8,128)(2,1)} %get-tuple-element.93.refs_2_), channel_id=1, source_target_pairs={{0,1},{1,2},{2,3},{3,0},{4,5},{5,6},{6,7},{7,4},{8,9},{9,10},{10,1... | collective-permute-start | bytes 1179656 | tf_op jit(solution)/shard_map/ppermute | solution.py:20
  114.4 16.2 %collective-permute-start.20 = (bf16[192,1024]{1,0:T(8,128)(2,1)}, bf16[192,1024]{1,0:T(8,128)(2,1)}, u32[]{:S(2)}, u32[]{:S(2)}) collective-permute-start(bf16[192,1024]{1,0:T(8,128)(2,1)} %get-tuple-element.94.refs_5_), channel_id=1, source_target_pairs={{0,3},{1,0},{2,1},{3,2},{4,7},{5,4},{6,5},{7,6},{8,11},{9,8},{10,9... | collective-permute-start | bytes 1179656 | tf_op jit(solution)/shard_map/ppermute | solution.py:20
